TPU v7x, 32 devices: a whole 2x2x4 slice. The times are simulated.
32 devices in a mesh: scene: 2 (over y), tok: 8 (over z, x), hid: 2 (over core).
Axes of the slice: x: 2, y: 2, z: 4, core: 2. Of those that a mesh axis runs over, the one named last changes fastest.
Arguments:
- input_keys: bfloat16 [16384, 384], P(('scene', 'tok'), 'hid'), parts along dimension 0, may hold values from -6 to 6
- input_values: bfloat16 [16384, 384], P(('scene', 'tok'), 'hid'), parts along dimension 0, may hold values from -6 to 6
- input_lr: float32 [16384], P(('scene', 'tok')), parts along dimension 0, may hold values from 0.1 to 1
- gate_weight: bfloat16 [384, 1536], P('tok', 'hid'), may hold values from -0.3125 to 0.3125
- up_weight: bfloat16 [384, 1536], P('tok', 'hid'), may hold values from -0.3125 to 0.3125
- down_weight: bfloat16 [384, 1536], P('tok', 'hid'), may hold values from -0.15625 to 0.15625
- queries: bfloat16 [2048, 384], P(('scene', 'tok'), 'hid'), parts along dimension 0, may hold values from -6 to 6
- out_grad: bfloat16 [2048, 384], P(('scene', 'tok'), 'hid'), parts along dimension 0, may hold values from -6 to 6
Outputs:
- target_out: bfloat16 [2048, 384], P(('scene', 'tok'), 'hid'), parts along dimension 0
- query_grad: bfloat16 [2048, 384], P(('scene', 'tok'), 'hid'), parts along dimension 0
There are 2 independent parts, one for each index of `scene`. A program takes and returns all parts, laid end to end along the dimension named above; an argument that names none is the same for every part. Nothing has to cross between parts.
All inputs are finite; a program needn't handle non-finite values.
Results may differ from a plain program's by a relative error of at most 0.009.
Values may be sent and summed in bfloat16 or wider, within the bound.
No kernel may reach another device: no remote copies, remote signals or barrier semaphores. Data moves between devices by JAX's collectives and lax.ppermute only.
A program may use at most 64 MiB of HBM per device.

v0:
```python
import jax
import jax.numpy as jnp
from jax import lax
from jax.sharding import PartitionSpec as P

HID = 1536


step_ratio = 0.5
epsilon = 1e-06


def silu_slope(pre):
    sigma = jax.nn.sigmoid(pre)
    return sigma * (1.0 + pre * (1.0 - sigma))


def contract_rows(left, right):
    return lax.dot_general(
        left, right, (((0,), (0,)), ((), ())), preferred_element_type=jnp.float32
    )


def contract_cols(left, right):
    return lax.dot_general(
        left, right, (((1,), (1,)), ((), ())), preferred_element_type=jnp.float32
    )


def finish(moved, wsq, msq):
    return (moved * (jnp.sqrt(wsq) / jnp.sqrt(msq + epsilon))[:, None]).astype(jnp.bfloat16)


def shards(
    input_keys, input_values, input_lr, gate_weight, up_weight, down_weight, queries, out_grad
):
    keys, values = (
        lax.all_gather(input_keys, "hid", axis=1, tiled=True),
        lax.all_gather(input_values, "hid", axis=1, tiled=True),
    )
    w_gate, w_up, w_down = (
        lax.all_gather(gate_weight, "tok", axis=0, tiled=True),
        lax.all_gather(up_weight, "tok", axis=0, tiled=True),
        lax.all_gather(down_weight, "tok", axis=0, tiled=True),
    )
    scaled = (input_lr[:, None] * values.astype(jnp.float32)).astype(jnp.bfloat16)
    key_gate = jnp.dot(keys, w_gate, preferred_element_type=jnp.float32)
    key_up = jnp.dot(keys, w_up, preferred_element_type=jnp.float32)
    gate_act = jax.nn.silu(key_gate)
    key_act = (gate_act * key_up).astype(jnp.bfloat16)
    back = jnp.dot(scaled, w_down, preferred_element_type=jnp.float32)
    d_gate = (-back * key_up * silu_slope(key_gate)).astype(jnp.bfloat16)
    d_up = (-back * gate_act).astype(jnp.bfloat16)
    width = gate_weight.shape[1]
    grads = lax.psum(
        jnp.concatenate(
            [
                contract_rows(keys, d_gate),
                contract_rows(keys, d_up),
                -contract_rows(scaled, key_act),
            ],
            axis=1,
        ),
        "tok",
    )
    olds = (w_gate, w_up, w_down)
    pieces = [grads[:, :width], grads[:, width : 2 * width], grads[:, 2 * width :]]
    weights = [old.astype(jnp.float32) for old in olds]
    renewed = []
    stats = []
    for weight, grad in zip(weights, pieces):
        stats.append(jnp.sum(weight * weight, axis=1))
        stats.append(jnp.sum(weight * grad, axis=1))
        stats.append(jnp.sum(grad * grad, axis=1))
    totals = lax.psum(
        (stats[0], stats[1], stats[2], stats[3], stats[4], stats[5], stats[6], stats[7], stats[8]),
        "hid",
    )
    for index in range(3):
        wsq = totals[3 * index] / HID
        cross = totals[3 * index + 1] / HID
        gsq = totals[3 * index + 2] / HID
        scale = step_ratio * jnp.sqrt(wsq) / jnp.sqrt(gsq + epsilon)
        moved = weights[index] - scale[:, None] * pieces[index]
        msq = wsq - 2.0 * scale * cross + scale * scale * gsq
        renewed.append(finish(moved, wsq, msq))
    new_gate, new_up, new_down = (renewed[0], renewed[1], renewed[2])
    query_rows, grad_rows = (
        lax.all_gather(queries, "hid", axis=1, tiled=True),
        lax.all_gather(out_grad, "hid", axis=1, tiled=True),
    )
    query_gate = jnp.dot(query_rows, new_gate, preferred_element_type=jnp.float32)
    query_up = jnp.dot(query_rows, new_up, preferred_element_type=jnp.float32)
    query_silu = jax.nn.silu(query_gate)
    query_act = (query_silu * query_up).astype(jnp.bfloat16)
    out_part = contract_cols(query_act, new_down)
    query_back = jnp.dot(grad_rows, new_down, preferred_element_type=jnp.float32)
    q_gate_grad = (query_back * query_up * silu_slope(query_gate)).astype(jnp.bfloat16)
    q_up_grad = (query_back * query_silu).astype(jnp.bfloat16)
    grad_part = contract_cols(q_gate_grad, new_gate) + contract_cols(q_up_grad, new_up)
    out_sum, grad_sum = (
        lax.psum_scatter(
            out_part.astype(jnp.bfloat16), "hid", scatter_dimension=1, tiled=True
        ).astype(jnp.float32),
        lax.psum_scatter(
            grad_part.astype(jnp.bfloat16), "hid", scatter_dimension=1, tiled=True
        ).astype(jnp.float32),
    )
    return (out_sum.astype(jnp.bfloat16), grad_sum.astype(jnp.bfloat16))


def solution(mesh):
    return jax.shard_map(
        shards,
        mesh=mesh,
        in_specs=(
            P(("scene", "tok"), "hid"),
            P(("scene", "tok"), "hid"),
            P(("scene", "tok")),
            P("tok", "hid"),
            P("tok", "hid"),
            P("tok", "hid"),
            P(("scene", "tok"), "hid"),
            P(("scene", "tok"), "hid"),
        ),
        out_specs=(P(("scene", "tok"), "hid"), P(("scene", "tok"), "hid")),
        check_vma=False,
    )
```

profile of v0, /device:TPU:0, one launch (start us, length us, event | category | flops | bytes accessed | tf_op | source)
XLA Modules:
  0.0 298.4 jit_solution(15559393787212214560)
XLA Ops:
  7.2 2.7 all_gather.24
  9.9 33.4 %all_gather.21 = bf16[384,768]{1,0:T(8,128)(2,1)S(1)} all-gather(bf16[48,768]{1,0:T(8,128)(2,1)} %param.11), channel_id=1, replica_groups=mesh['scene'=2,'tok'=8,'hid'=2] {'tok'}, dimensions={0}, use_global_device_ids=true | all-gather | bytes 663552 | tf_op jit(solution)/shard_map/all_gather | solution.py:42
  43.3 31.3 %all_gather.25 = bf16[384,768]{1,0:T(8,128)(2,1)S(1)} all-gather(bf16[48,768]{1,0:T(8,128)(2,1)S(1)} %copy-done.6), channel_id=1, replica_groups=mesh['scene'=2,'tok'=8,'hid'=2] {'tok'}, dimensions={0}, use_global_device_ids=true | all-gather | bytes 663552 | tf_op jit(solution)/shard_map/all_gather | solution.py:43
  74.6 1.0 fusion.34
  75.7 1.0 fusion.33
  76.7 2.4 all_gather.22
  79.1 31.4 %all_gather.23 = bf16[384,768]{1,0:T(8,128)(2,1)S(1)} all-gather(bf16[48,768]{1,0:T(8,128)(2,1)S(1)} %copy-done.7), channel_id=1, replica_groups=mesh['scene'=2,'tok'=8,'hid'=2] {'tok'}, dimensions={0}, use_global_device_ids=true | all-gather | bytes 663552 | tf_op jit(solution)/shard_map/all_gather | solution.py:44
  110.5 1.0 fusion.20
  111.6 1.2 fusion.6
  112.8 1.5 fusion.4
  114.2 1.3 fusion.5
  115.6 2.0 pad_maximum_fusion
  117.7 1.1 copy.14
  118.8 1.1 copy.16
  119.8 1.1 copy.17
  120.9 2.0 all_gather.27
  122.9 2.0 all_gather.26
  124.9 133.6 %all-reduce.3.cloned.1.call-done = f32[384,2304]{0,1:T(8,128)} async-done(((f32[384,2304]{0,1:T(8,128)}), f32[384,2304]{0,1:T(8,128)}) %all-reduce.3.cloned.1.call-update) | async-done | bytes 3538960 | tf_op jit(solution)/shard_map/psum | solution.py:55
  258.6 4.1 %multiply_reduce_fusion.2 = (f32[384]{0:T(512)S(1)}, f32[384]{0:T(512)S(1)}, f32[384]{0:T(512)S(1)}, f32[384]{0:T(512)S(1)}, f32[384]{0:T(512)}, /*index=5*/f32[...) fusion(f32[384,2304]{0,1:T(8,128)} %all-reduce.3.cloned.1.call-done, bf16[384,768]{0,1:T(8,128)(2,1)} %copy.14, ...), kind=kLoop, calls=%fused_computation.39 | loop fusion | flops 6189696 | bytes 5322240 | tf_op jit(solution)/shard_map/reduce_sum | solution.py:74
  262.6 4.6 %all-reduce = (f32[384]{0:T(512)}, f32[384]{0:T(512)}, f32[384]{0:T(512)}, f32[384]{0:T(512)}, f32[384]{0:T(512)}, /*index=5*/f32[384]{0:T(512)}, f32[384]{0:T(512)}, f32[384]{0:T(512)}, f32[384]{0:T(512)}) all-reduce(f32[384]{0:T(512)S(1)} %get-tuple-element.5, ...), channel_id=1, replica_groups=mesh['scene'=2,'tok'=8,'hid'=2] {'hid'}, use_global_device_ids=true, to_apply=%region_18.19 | all-reduce | flops 3456 | bytes 27648 | tf_op jit(solution)/shard_map/psum | solution.py:75
  267.2 0.7 rsqrt_multiply_fusion.5
  267.9 0.8 rsqrt_multiply_fusion.1
  268.7 2.0 fusion.9
  270.8 0.3 convolution_bitcast_fusion.1
  271.1 0.3 convolution_bitcast_fusion.2
  271.4 0.3 copy-done.4
  271.8 0.3 convolution_bitcast_fusion
  272.1 0.5 fusion.24
  272.6 1.1 fusion.19
  273.7 1.0 convolution_convert_fusion
  274.8 5.6 %reduce-scatter.5.cloned.1.call-done = bf16[128,192]{0,1:T(8,128)(2,1)} async-done(((bf16[128,384]{0,1:T(8,128)(2,1)}), bf16[128,192]{0,1:T(8,128)(2,1)}) %reduce-scatter.5.cloned.1.call-update) | async-done | bytes 49168 | tf_op jit(solution)/shard_map/reduce_scatter | solution.py:105
  280.3 11.5 %reduce-scatter.3.cloned.1.call-done = bf16[128,192]{0,1:T(8,128)(2,1)} async-done(((bf16[128,384]{0,1:T(8,128)(2,1)}), bf16[128,192]{0,1:T(8,128)(2,1)}) %reduce-scatter.3.cloned.1.call-update) | async-done | bytes 49168 | tf_op jit(solution)/shard_map/reduce_scatter | solution.py:102
  (27 shorter events, 0.2 us)
Async XLA Ops:
  7.2 36.2 %copy-start.6 = (bf16[48,768]{1,0:T(8,128)(2,1)S(1)}, bf16[48,768]{1,0:T(8,128)(2,1)}, u32[]{:S(2)}) copy-start(bf16[48,768]{1,0:T(8,128)(2,1)} %param.12) | copy-start | bytes 221188
  7.2 251.4 %all-reduce.3.cloned.1.call-start = ((), (), s32[]{:S(2)}) async-start(), calls=%async_computation.2 | async-start | bytes 7077888 | tf_op jit(solution)/shard_map/psum | solution.py:55
  75.6 1.1 copy-start.5
  75.7 3.4 %copy-start.7 = (bf16[48,768]{1,0:T(8,128)(2,1)S(1)}, bf16[48,768]{1,0:T(8,128)(2,1)}, u32[]{:S(2)}) copy-start(bf16[48,768]{1,0:T(8,128)(2,1)} %param.13) | copy-start | bytes 221188
  76.7 33.8 %copy-start.10 = (f32[1024]{0:T(1024)S(1)}, f32[1024]{0:T(1024)}, u32[]{:S(2)}) copy-start(f32[1024]{0:T(1024)} %param.10) | copy-start | bytes 12292
  117.6 3.3 %copy-start.8 = (bf16[128,192]{0,1:T(8,128)(2,1)S(1)}, bf16[128,192]{0,1:T(8,128)(2,1)}, u32[]{:S(2)}) copy-start(bf16[128,192]{0,1:T(8,128)(2,1)} %param.15) | copy-start | bytes 147460
  117.6 5.3 %copy-start.9 = (bf16[128,192]{0,1:T(8,128)(2,1)S(1)}, bf16[128,192]{0,1:T(8,128)(2,1)}, u32[]{:S(2)}) copy-start(bf16[128,192]{0,1:T(8,128)(2,1)} %param.14) | copy-start | bytes 147460
  117.7 162.7 %reduce-scatter.5.cloned.1.call-start = ((), (), s32[]{:S(2)}) async-start(), calls=%async_computation.4 | async-start | bytes 147456 | tf_op jit(solution)/shard_map/reduce_scatter | solution.py:105
  258.6 10.2 %copy-start = (f32[384,2304]{0,1:T(8,128)S(1)}, f32[384,2304]{0,1:T(8,128)}, u32[]{:S(2)}) copy-start(f32[384,2304]{0,1:T(8,128)} %all-reduce.3.cloned.1.call-done) | copy-start | bytes 10616836
  268.7 2.1 copy-start.3
  270.8 1.3 copy-start.1
  270.8 1.0 copy-start.4
  272.5 1.2 copy-start.2
  273.6 18.2 %reduce-scatter.3.cloned.1.call-start = ((), (), s32[]{:S(2)}) async-start(), calls=%async_computation.3 | async-start | bytes 147456 | tf_op jit(solution)/shard_map/reduce_scatter | solution.py:102
Sparse Core Ops, SparseCore 0:
  117.8 140.7 all-reduce.2
  273.8 6.5 reduce-scatter.4
  283.2 8.6 reduce-scatter.2
where the time goes:
time: 299 us; the launch traced here: 298 us
  waiting for transfers between devices  151 us (51%)
  blocking collectives  110 us (37%)
  between operations  13.9 us (5%)
  matrix products  10.6 us (4%)
  other arithmetic  9.59 us (3%)
  local copies, waits for them, and re-layouts  3.61 us (1%)
    psum x1, waiting for transfers between devices, shards(): lax.psum(jnp.concatenate([contract_rows(keys, d_gate), contract_rows(keys...  134 us
    all_gather x1, blocking collectives, shards(): lax.all_gather(gate_weight, 'tok', axis=0, tiled=True)  33.4 us
    all_gather x1, blocking collectives, shards(): lax.all_gather(down_weight, 'tok', axis=0, tiled=True)  31.4 us
    all_gather x1, blocking collectives, shards(): lax.all_gather(up_weight, 'tok', axis=0, tiled=True)  31.3 us
    reduce_scatter x1, waiting for transfers between devices, shards(): lax.psum_scatter(out_part.astype(jnp.bfloat16), 'hid', scatter_dimension=...  11.5 us
  transfers between devices with their start and end apart: 3, of which 3 were waited for; matrix products, arithmetic and copies ran while one was open for 1% of the time, Pallas kernels for 0%

commit v1 on v0

--- a/solution.py
+++ b/solution.py
@@ -1,13 +1,257 @@
+import functools
+
 import jax
 import jax.numpy as jnp
 from jax import lax
+from jax.experimental import pallas as pl
+from jax.experimental.pallas import tpu as pltpu
 from jax.sharding import PartitionSpec as P
-
-HID = 1536
-
 
 step_ratio = 0.5
 epsilon = 1e-06
+f32, bf16 = jnp.float32, jnp.bfloat16
+
+
+def contract(left, right, left_dim, right_dim):
+    return lax.dot_general(
+        left, right, (((left_dim,), (right_dim,)), ((), ())), preferred_element_type=f32
+    )
+
+
+def gated(gate, up):
+    sigma = jax.nn.sigmoid(gate)
+    silu = gate * sigma
+    slope = sigma * (1.0 + gate * (1.0 - sigma))
+    return silu, slope * up, silu * up
+
+
+def token_kernel(groups, place, *refs):
+    (key_a, key_b, key_c, key_d, val_a, val_b, val_c, val_d), refs = refs[:8], refs[8:]
+    own_w, pair_w, refs = refs[0], refs[1], refs[2:]
+    first, second, refs = refs[: groups - 1], refs[groups - 1 : 2 * groups - 2], refs[2 * groups - 2 :]
+    weights, own_grad, sends, (keys, vals, grads) = refs[0], refs[1], refs[2 : groups + 1], refs[groups + 1 :]
+    group, side, half = place[0], place[1], place[2]
+    feats, toks = key_a.shape
+    rows = own_w.shape[1]
+
+    for full, parts in ((keys, (key_a, key_b, key_c, key_d)), (vals, (val_a, val_b, val_c, val_d))):
+        here = pl.ds(pl.multiple_of(half * feats, feats), feats)
+        there = pl.ds(pl.multiple_of((1 - half) * feats, feats), feats)
+        full[here, :toks] = parts[0][...]
+        full[there, :toks] = parts[1][...]
+        full[here, toks:] = parts[2][...]
+        full[there, toks:] = parts[3][...]
+
+    def place_rows(source, owner, sided):
+        start = pl.multiple_of((owner * 2 + sided) * rows, rows)
+        weights[:, pl.ds(start, rows), :] = source[...]
+
+    place_rows(own_w, group, side)
+    place_rows(pair_w, group, 1 - side)
+    for step in range(1, groups):
+        place_rows(first[step - 1], group ^ step, side)
+        place_rows(second[step - 1], group ^ step, 1 - side)
+
+    total = 2 * toks
+    chunk = min(512, total)
+    for start in range(0, total, chunk):
+        key = keys[:, start : start + chunk]
+        val = vals[:, start : start + chunk]
+        gate = contract(weights[0], key, 0, 0)
+        up = contract(weights[1], key, 0, 0)
+        back = contract(weights[2], val, 0, 0)
+        silu, slope_up, act = gated(gate, up)
+        d_gate = (back * slope_up).astype(bf16)
+        d_up = (back * silu).astype(bf16)
+        parts = (
+            contract(key, d_gate, 1, 1),
+            contract(key, d_up, 1, 1),
+            contract(val, act.astype(bf16), 1, 1),
+        )
+        for index, part in enumerate(parts):
+            if start == 0:
+                grads[index] = part
+            else:
+                grads[index] += part
+
+    def rows_of(owner):
+        return grads[:, pl.ds(pl.multiple_of(owner * 2 * rows, 2 * rows), 2 * rows), :]
+
+    own_grad[...] = rows_of(group)
+    for step in range(1, groups):
+        sends[step - 1][...] = rows_of(group ^ step).astype(bf16)
+
+
+def sum_kernel(groups, place, weights, own, *refs):
+    arrived, (total_out, stats_out) = refs[: groups - 1], refs[groups - 1 :]
+    rows = own.shape[1]
+    mine = pl.ds(pl.multiple_of(place[0] * rows, rows), rows)
+    lane = lax.broadcasted_iota(jnp.int32, stats_out.shape, 1)
+    stats = jnp.zeros(stats_out.shape, f32)
+    for index in range(3):
+        grad = own[index]
+        for other in arrived:
+            grad = grad + other[index].astype(f32)
+        total_out[index] = grad.astype(bf16)
+        weight = weights[index, mine, :].astype(f32)
+        for slot, product in enumerate((weight * weight, weight * grad, grad * grad)):
+            row_sum = jnp.sum(product, axis=1, keepdims=True)
+            stats = jnp.where(lane == 3 * index + slot, row_sum, stats)
+    stats_out[...] = stats
+
+
+def query_kernel(groups, hidden, place, weights, *refs):
+    grads, refs = refs[:groups], refs[groups:]
+    stats, refs = refs[:groups], refs[groups:]
+    quests, refs = refs[:4], refs[4:]
+    own_out, sends, (renewed, query, cotangent) = refs[0], refs[1:4], refs[4:]
+    group, side, half = place[0], place[1], place[2]
+    rows = grads[0].shape[1]
+    feats, count = quests[0].shape[1:]
+
+    for step in range(groups):
+        where = pl.ds(pl.multiple_of((group ^ step) * rows, rows), rows)
+        sums = stats[step][...] * (1.0 / hidden)
+        for index in range(3):
+            wsq = sums[:, 3 * index : 3 * index + 1]
+            cross = sums[:, 3 * index + 1 : 3 * index + 2]
+            gsq = sums[:, 3 * index + 2 : 3 * index + 3]
+            scale = step_ratio * jnp.sqrt(wsq) / jnp.sqrt(gsq + epsilon)
+            msq = wsq + 2.0 * scale * cross + scale * scale * gsq
+            factor = jnp.sqrt(wsq) / jnp.sqrt(msq + epsilon)
+            moved = weights[index, where, :].astype(f32) + scale * grads[step][index].astype(f32)
+            renewed[index, where, :] = (moved * factor).astype(bf16)
+
+    for flip in range(4):
+        feat = pl.ds(pl.multiple_of((half ^ (flip & 1)) * feats, feats), feats)
+        span = pl.ds(pl.multiple_of((side ^ (flip >> 1)) * count, count), count)
+        query[feat, span] = quests[flip][0]
+        cotangent[feat, span] = quests[flip][1]
+
+    gate = contract(renewed[0], query[...], 0, 0)
+    up = contract(renewed[1], query[...], 0, 0)
+    back = contract(renewed[2], cotangent[...], 0, 0)
+    silu, slope_up, act = gated(gate, up)
+    out = contract(renewed[2], act.astype(bf16), 1, 0)
+    grad = contract(renewed[0], (back * slope_up).astype(bf16), 1, 0) + contract(
+        renewed[1], (back * silu).astype(bf16), 1, 0
+    )
+    query_out = (out, grad)
+    for index in range(2):
+        stage = query_out[index]
+        result_at(stage, index, own_out, sends, side, half, feats, count)
+
+
+def result_at(stage, index, own_out, sends, side, half, feats, count):
+    def pick(sided, halved):
+        left = jnp.where(halved == 0, stage[:feats], stage[feats:])
+        return jnp.where(sided == 0, left[:, :count], left[:, count:])
+
+    own_out[index] = pick(side, half)
+    for flip in range(1, 4):
+        sends[flip - 1][index] = pick(side ^ (flip >> 1), half ^ (flip & 1)).astype(bf16)
+
+
+def call(body, n_in, outs, scratch, flops, moved):
+    return pl.pallas_call(
+        body,
+        out_shape=outs,
+        in_specs=[pl.BlockSpec(memory_space=pltpu.SMEM)]
+        + [pl.BlockSpec(memory_space=pltpu.VMEM)] * n_in,
+        out_specs=[pl.BlockSpec(memory_space=pltpu.VMEM)] * len(outs),
+        scratch_shapes=scratch,
+        compiler_params=pltpu.CompilerParams(vmem_limit_bytes=48 * 1024 * 1024),
+        cost_estimate=pl.CostEstimate(flops=flops, bytes_accessed=moved, transcendentals=0),
+    )
+
+
+def direct(
+    input_keys, input_values, input_lr, gate_weight, up_weight, down_weight, queries, out_grad,
+    n_tok, n_hid,
+):
+    groups = n_tok // 2
+    tok, half = lax.axis_index("tok"), lax.axis_index("hid")
+    group, side = tok // 2, tok % 2
+    place = jnp.stack([group, side, half]).astype(jnp.int32)
+
+    def swap(array, flip):
+        pairs = [(i, i ^ flip) for i in range(n_tok * n_hid)]
+        return lax.ppermute(array, ("tok", "hid"), pairs)
+
+    core, pair = 1, 2
+    zed = [4 * step for step in range(1, groups)]
+
+    keys = input_keys.T
+    vals = (input_lr[None, :] * input_values.T.astype(f32)).astype(bf16)
+    stacked = jnp.stack([gate_weight, up_weight, down_weight])
+    cols = stacked.shape[2] // 2
+    own_w = lax.dynamic_slice_in_dim(stacked, side * cols, cols, 2)
+    give_w = lax.dynamic_slice_in_dim(stacked, (1 - side) * cols, cols, 2)
+    pair_w = swap(give_w, pair)
+    first = [swap(own_w, flip) for flip in zed]
+    key_c = swap(keys, pair)
+    val_c = swap(vals, pair)
+    second = [swap(pair_w, flip) for flip in zed]
+    key_b, val_b = swap(keys, core), swap(vals, core)
+    key_d, val_d = swap(key_c, core), swap(val_c, core)
+
+    feats, toks = keys.shape
+    width = n_hid * feats
+    rows = width // groups
+    block = (3, rows, cols)
+    token_flops = 6 * 2 * 2 * toks * width * cols
+    token_step = call(
+        functools.partial(token_kernel, groups),
+        8 + 2 + 2 * (groups - 1),
+        [jax.ShapeDtypeStruct((3, width, cols), bf16), jax.ShapeDtypeStruct(block, f32)]
+        + [jax.ShapeDtypeStruct(block, bf16)] * (groups - 1),
+        [
+            pltpu.VMEM((width, 2 * toks), bf16),
+            pltpu.VMEM((width, 2 * toks), bf16),
+            pltpu.VMEM((3, width, cols), f32),
+        ],
+        token_flops,
+        8 * feats * toks * 2 + 3 * width * cols * 4,
+    )
+    weights, own_grad, *sends = token_step(
+        place, keys, key_b, key_c, key_d, vals, val_b, val_c, val_d, own_w, pair_w, *first, *second
+    )
+    arrived = [swap(send, flip) for send, flip in zip(sends, zed)]
+
+    quest = jnp.stack([queries.T, out_grad.T])
+    quest, _ = lax.optimization_barrier((quest, sends[0]))
+    quests = [quest] + [swap(quest, flip) for flip in (1, 2, 3)]
+
+    grad, stats = call(
+        functools.partial(sum_kernel, groups),
+        groups + 1,
+        [jax.ShapeDtypeStruct(block, bf16), jax.ShapeDtypeStruct((rows, 128), f32)],
+        [],
+        30 * 3 * rows * cols,
+        3 * rows * cols * 16,
+    )(place, weights, own_grad, *arrived)
+    grads = [grad] + [swap(grad, flip) for flip in zed]
+    stats = stats + swap(stats, 1) + swap(stats, 2) + swap(stats, 3)
+    stats = [stats] + [swap(stats, flip) for flip in zed]
+
+    count = queries.shape[0]
+    piece = (2, feats, count)
+    own_out, *out_sends = call(
+        functools.partial(query_kernel, groups, 2 * n_hid * cols),
+        1 + 2 * groups + 4,
+        [jax.ShapeDtypeStruct(piece, f32)] + [jax.ShapeDtypeStruct(piece, bf16)] * 3,
+        [
+            pltpu.VMEM((3, width, cols), bf16),
+            pltpu.VMEM((width, 2 * count), bf16),
+            pltpu.VMEM((width, 2 * count), bf16),
+        ],
+        6 * 2 * 2 * count * width * cols,
+        6 * width * cols * 2,
+    )(place, weights, *grads, *stats, *quests)
+    total = own_out
+    for send, flip in zip(out_sends, (1, 2, 3)):
+        total = total + swap(send, flip).astype(f32)
+    return total[0].astype(bf16).T, total[1].astype(bf16).T
 
 
 def silu_slope(pre):
@@ -31,8 +275,8 @@
     return (moved * (jnp.sqrt(wsq) / jnp.sqrt(msq + epsilon))[:, None]).astype(jnp.bfloat16)
 
 
-def shards(
-    input_keys, input_values, input_lr, gate_weight, up_weight, down_weight, queries, out_grad
+def general(
+    input_keys, input_values, input_lr, gate_weight, up_weight, down_weight, queries, out_grad, n_hid
 ):
     keys, values = (
         lax.all_gather(input_keys, "hid", axis=1, tiled=True),
@@ -52,6 +296,7 @@
     d_gate = (-back * key_up * silu_slope(key_gate)).astype(jnp.bfloat16)
     d_up = (-back * gate_act).astype(jnp.bfloat16)
     width = gate_weight.shape[1]
+    hidden = width * n_hid
     grads = lax.psum(
         jnp.concatenate(
             [
@@ -77,9 +322,9 @@
         "hid",
     )
     for index in range(3):
-        wsq = totals[3 * index] / HID
-        cross = totals[3 * index + 1] / HID
-        gsq = totals[3 * index + 2] / HID
+        wsq = totals[3 * index] / hidden
+        cross = totals[3 * index + 1] / hidden
+        gsq = totals[3 * index + 2] / hidden
         scale = step_ratio * jnp.sqrt(wsq) / jnp.sqrt(gsq + epsilon)
         moved = weights[index] - scale[:, None] * pieces[index]
         msq = wsq - 2.0 * scale * cross + scale * scale * gsq
@@ -110,6 +355,24 @@
 
 
 def solution(mesh):
+    n_tok, n_hid = mesh.shape["tok"], mesh.shape["hid"]
+
+    def shards(*args):
+        rows, cols = args[3].shape
+        toks, count = args[0].shape[0], args[6].shape[0]
+        fits = (
+            n_hid == 2
+            and 2 <= n_tok <= 8
+            and n_tok & (n_tok - 1) == 0
+            and rows % 16 == 0
+            and cols % 256 == 0
+            and toks % 256 == 0
+            and count % 128 == 0
+        )
+        if fits:
+            return direct(*args, n_tok, n_hid)
+        return general(*args, n_hid)
+
     return jax.shard_map(
         shards,
         mesh=mesh,

time: 299 us -> 122 us (0.41)
  blocking collectives: 110 us -> 0 us
  waiting for transfers between devices: 151 us -> 61.8 us
  starting transfers between devices: 0.12 us -> 41.9 us
  between operations: 13.9 us -> 0.83 us
  matrix products: 10.6 us -> 0 us
  Pallas kernels: 0 us -> 10.4 us
  other arithmetic: 9.59 us -> 1.31 us
    psum x1 -> x0, waiting for transfers between devices: 134 us -> none  [shards(): lax.psum(jnp.concatenate([contract_rows(keys, d_gate), contract_rows(keys...]
    all_gather x7 -> x0, blocking collectives: 105 us -> none  [the longest x1 33.4 us: shards(): lax.all_gather(gate_weight, 'tok', axis=0, tiled=True)]
    ppermute x0 -> x31, waiting for transfers between devices: none -> 61.8 us  [swap(): return lax.ppermute(array, ('tok', 'hid'), pairs)]
    ppermute x0 -> x31, starting transfers between devices: none -> 41.9 us  [swap(): return lax.ppermute(array, ('tok', 'hid'), pairs)]
    reduce_scatter x2 -> x0, waiting for transfers between devices: 17.1 us -> none  [the longest x1 11.5 us: shards(): lax.psum_scatter(out_part.astype(jnp.bfloat16), 'hid', scatter_dimension=...]
    dot_general x12 -> x0, matrix products: 10.6 us -> none  [the longest x3 4 us: contract_rows(): lax.dot_general(left, right, (((0,), (0,)), ((), ())), preferred_element_...]
    pallas_call x0 -> x3, Pallas kernels: none -> 10.4 us  [the longest x1 7.24 us: direct(): token_step(place, keys, key_b, key_c, key_d, vals, val_b, val_c, val_d, o...]
    psum x1 -> x0, blocking collectives: 4.62 us -> none  [shards(): lax.psum((stats[0], stats[1], stats[2], stats[3], stats[4], stats[5], sta...]
  transfers between devices with their start and end apart: 3 -> 31, of which waited for: 3 -> 11; matrix products, arithmetic and copies ran while one was open for 1% -> 0% of each run, Pallas kernels for 0% -> 1%
where the time goes in v1:
time: 122 us
  waiting for transfers between devices  61.8 us (51%)
  starting transfers between devices  41.9 us (34%)
  Pallas kernels  10.4 us (9%)
  local copies, waits for them, and re-layouts  5.32 us (4%)
  other arithmetic  1.31 us (1%)
    ppermute x31, waiting for transfers between devices, swap(): return lax.ppermute(array, ('tok', 'hid'), pairs)  61.8 us
    ppermute x31, starting transfers between devices, swap(): return lax.ppermute(array, ('tok', 'hid'), pairs)  41.9 us
    pallas_call x1, Pallas kernels, direct(): token_step(place, keys, key_b, key_c, key_d, vals, val_b, val_c, val_d, o...  7.24 us
    unnamed x24, local copies, waits for them, and re-layouts  4.64 us
  transfers between devices with their start and end apart: 31, of which 11 were waited for; matrix products, arithmetic and copies ran while one was open for 0% of the time, Pallas kernels for 1%

profile of v1, /device:TPU:0, one launch (start us, length us, event | category | flops | bytes accessed | tf_op | source)
XLA Modules:
  0.0 121.6 jit_solution(700000258850751890)
XLA Ops:
  0.7 1.1 fusion.refs_4_
  1.8 3.0 %collective-permute-start.4 = (bf16[192,1024]{1,0:T(8,128)(2,1)S(1)}, bf16[192,1024]{1,0:T(8,128)(2,1)S(1)}, u32[]{:S(2)}, u32[]{:S(2)}) collective-permute-start(bf16[192,1024]{1,0:T(8,128)(2,1)S(1)} %fusion.refs_4_), channel_id=1, source_target_pairs={{0,2},{1,3},{2,0},{3,1},{4,6},{5,7},{6,4},{7,5},{8,10},{9,11},{10,... | collective-permute-start | bytes 1179656 | tf_op jit(solution)/shard_map/ppermute | solution.py:179
  5.0 2.0 %collective-permute-start.6 = (bf16[3,48,384]{2,1,0:T(8,128)(2,1)S(1)}, bf16[3,48,384]{2,1,0:T(8,128)(2,1)S(1)}, u32[]{:S(2)}, u32[]{:S(2)}) collective-permute-start(bf16[3,48,384]{2,1,0:T(8,128)(2,1)S(1)} %get-tuple-element.26), channel_id=1, source_target_pairs={{0,2},{1,3},{2,0},{3,1},{4,6},{5,7},{6,4},{7,5},{8,10},{9,11},{10,... | collective-permute-start | bytes 331784 | tf_op jit(solution)/shard_map/ppermute | solution.py:179
  7.0 1.6 %collective-permute-start.7 = (bf16[3,48,384]{2,1,0:T(8,128)(2,1)S(1)}, bf16[3,48,384]{2,1,0:T(8,128)(2,1)S(1)}, u32[]{:S(2)}, u32[]{:S(2)}) collective-permute-start(bf16[3,48,384]{2,1,0:T(8,128)(2,1)S(1)} %get-tuple-element.27.refs_8_), channel_id=1, source_target_pairs={{0,4},{1,5},{2,6},{3,7},{4,0},{5,1},{6,2},{7,3},{8,12},{9,13},{10,... | collective-permute-start | bytes 331784 | tf_op jit(solution)/shard_map/ppermute | solution.py:179
  8.6 2.6 %collective-permute-start.8 = (bf16[3,48,384]{2,1,0:T(8,128)(2,1)S(1)}, bf16[3,48,384]{2,1,0:T(8,128)(2,1)S(1)}, u32[]{:S(2)}, u32[]{:S(2)}) collective-permute-start(bf16[3,48,384]{2,1,0:T(8,128)(2,1)S(1)} %get-tuple-element.27.refs_8_), channel_id=1, source_target_pairs={{0,8},{1,9},{2,10},{3,11},{4,12},{5,13},{6,14},{7,15},{8,0},{9,1},... | collective-permute-start | bytes 331784 | tf_op jit(solution)/shard_map/ppermute | solution.py:179
  11.2 13.6 %collective-permute-done.6.refs_9_ = bf16[3,48,384]{2,1,0:T(8,128)(2,1)S(1)} collective-permute-done((bf16[3,48,384]{2,1,0:T(8,128)(2,1)S(1)}, bf16[3,48,384]{2,1,0:T(8,128)(2,1)S(1)}, u32[]{:S(2)}, u32[]{:S(2)}) %collective-permute-start.6) | collective-permute-done | bytes 110624 | tf_op jit(solution)/shard_map/ppermute | solution.py:179
  24.7 3.9 %collective-permute-start.9 = (bf16[3,48,384]{2,1,0:T(8,128)(2,1)S(1)}, bf16[3,48,384]{2,1,0:T(8,128)(2,1)S(1)}, u32[]{:S(2)}, u32[]{:S(2)}) collective-permute-start(bf16[3,48,384]{2,1,0:T(8,128)(2,1)S(1)} %get-tuple-element.27.refs_8_), channel_id=1, source_target_pairs={{0,12},{1,13},{2,14},{3,15},{4,8},{5,9},{6,10},{7,11},{8,4},{9,5},... | collective-permute-start | bytes 331784 | tf_op jit(solution)/shard_map/ppermute | solution.py:179
  30.3 1.1 collective-permute-done.9.refs_12_
  32.0 1.5 %collective-permute-start.10 = (bf16[3,48,384]{2,1,0:T(8,128)(2,1)S(1)}, bf16[3,48,384]{2,1,0:T(8,128)(2,1)S(1)}, u32[]{:S(2)}, u32[]{:S(2)}) collective-permute-start(bf16[3,48,384]{2,1,0:T(8,128)(2,1)S(1)} %collective-permute-done.6.refs_9_), channel_id=1, source_target_pairs={{0,4},{1,5},{2,6},{3,7},{4,0},{5,1},{6,2},{7,3},{8,12},{9,13},{10,... | collective-permute-start | bytes 331784 | tf_op jit(solution)/shard_map/ppermute | solution.py:179
  33.5 3.3 %collective-permute-done.10.refs_13_ = bf16[3,48,384]{2,1,0:T(8,128)(2,1)S(1)} collective-permute-done((bf16[3,48,384]{2,1,0:T(8,128)(2,1)S(1)}, bf16[3,48,384]{2,1,0:T(8,128)(2,1)S(1)}, u32[]{:S(2)}, u32[]{:S(2)}) %collective-permute-start.10) | collective-permute-done | bytes 110624 | tf_op jit(solution)/shard_map/ppermute | solution.py:179
  37.4 3.9 %collective-permute-start.11 = (bf16[3,48,384]{2,1,0:T(8,128)(2,1)S(1)}, bf16[3,48,384]{2,1,0:T(8,128)(2,1)}, u32[]{:S(2)}, u32[]{:S(2)}) collective-permute-start(bf16[3,48,384]{2,1,0:T(8,128)(2,1)S(1)} %collective-permute-done.6.refs_9_), channel_id=1, source_target_pairs={{0,8},{1,9},{2,10},{3,11},{4,12},{5,13},{6,14},{7,15},{8,0},{9,1},... | collective-permute-start | bytes 331784 | tf_op jit(solution)/shard_map/ppermute | solution.py:179
  41.3 6.3 %collective-permute-done.11.refs_14_ = bf16[3,48,384]{2,1,0:T(8,128)(2,1)} collective-permute-done((bf16[3,48,384]{2,1,0:T(8,128)(2,1)S(1)}, bf16[3,48,384]{2,1,0:T(8,128)(2,1)}, u32[]{:S(2)}, u32[]{:S(2)}) %collective-permute-start.11) | collective-permute-done | bytes 110624 | tf_op jit(solution)/shard_map/ppermute | solution.py:179
  47.6 2.2 %collective-permute-start.12 = (bf16[3,48,384]{2,1,0:T(8,128)(2,1)S(1)}, bf16[3,48,384]{2,1,0:T(8,128)(2,1)S(1)}, u32[]{:S(2)}, u32[]{:S(2)}) collective-permute-start(bf16[3,48,384]{2,1,0:T(8,128)(2,1)S(1)} %collective-permute-done.6.refs_9_), channel_id=1, source_target_pairs={{0,12},{1,13},{2,14},{3,15},{4,8},{5,9},{6,10},{7,11},{8,4},{9,5},... | collective-permute-start | bytes 331784 | tf_op jit(solution)/shard_map/ppermute | solution.py:179
  49.9 4.3 %collective-permute-done.12.refs_15_ = bf16[3,48,384]{2,1,0:T(8,128)(2,1)S(1)} collective-permute-done((bf16[3,48,384]{2,1,0:T(8,128)(2,1)S(1)}, bf16[3,48,384]{2,1,0:T(8,128)(2,1)S(1)}, u32[]{:S(2)}, u32[]{:S(2)}) %collective-permute-start.12) | collective-permute-done | bytes 110624 | tf_op jit(solution)/shard_map/ppermute | solution.py:179
  56.9 7.2 %shard_map.95 = (bf16[3,384,384]{2,1,0:T(8,128)(2,1)S(1)}, f32[3,96,384]{2,1,0:T(8,128)S(1)}, bf16[3,96,384]{2,1,0:T(8,128)(2,1)S(1)}, bf16[3,96,384]{2,1,0:T(8,128)(2,1)S(1)}, bf16[3,96,384]{2,1,0:T(8,128)(2,1)S(1)}) custom-call(s32[3]{0:T(128)S(1)} %pad_add_fusion.place, bf16[192,1024]{1,0:T(8,128)(2,1)S(1)} %bitcast.25, ...), custom_call_target="tpu_custom_call" | custom-call | flops 3623878656 | bytes 4915200 | tf_op jit(solution)/shard_map/pallas_call | solution.py:216
  64.2 2.7 %collective-permute-start.14 = (bf16[3,96,384]{2,1,0:T(8,128)(2,1)S(1)}, bf16[3,96,384]{2,1,0:T(8,128)(2,1)S(1)}, u32[]{:S(2)}, u32[]{:S(2)}) collective-permute-start(bf16[3,96,384]{2,1,0:T(8,128)(2,1)S(1)} %get-tuple-element.17), channel_id=1, source_target_pairs={{0,8},{1,9},{2,10},{3,11},{4,12},{5,13},{6,14},{7,15},{8,0},{9,1},... | collective-permute-start | bytes 663560 | tf_op jit(solution)/shard_map/ppermute | solution.py:179
  66.9 1.7 %collective-permute-start.15 = (bf16[3,96,384]{2,1,0:T(8,128)(2,1)S(1)}, bf16[3,96,384]{2,1,0:T(8,128)(2,1)S(1)}, u32[]{:S(2)}, u32[]{:S(2)}) collective-permute-start(bf16[3,96,384]{2,1,0:T(8,128)(2,1)S(1)} %get-tuple-element.18), channel_id=1, source_target_pairs={{0,12},{1,13},{2,14},{3,15},{4,8},{5,9},{6,10},{7,11},{8,4},{9,5},... | collective-permute-start | bytes 663560 | tf_op jit(solution)/shard_map/ppermute | solution.py:179
  68.7 2.8 %collective-permute-done.13.refs_0_ = bf16[3,96,384]{2,1,0:T(8,128)(2,1)S(1)} collective-permute-done((bf16[3,96,384]{2,1,0:T(8,128)(2,1)S(1)}, bf16[3,96,384]{2,1,0:T(8,128)(2,1)S(1)}, u32[]{:S(2)}, u32[]{:S(2)}) %collective-permute-start.13) | collective-permute-done | bytes 221216 | tf_op jit(solution)/shard_map/ppermute | solution.py:179
  71.5 6.3 %collective-permute-done.14.refs_1_ = bf16[3,96,384]{2,1,0:T(8,128)(2,1)S(1)} collective-permute-done((bf16[3,96,384]{2,1,0:T(8,128)(2,1)S(1)}, bf16[3,96,384]{2,1,0:T(8,128)(2,1)S(1)}, u32[]{:S(2)}, u32[]{:S(2)}) %collective-permute-start.14) | collective-permute-done | bytes 221216 | tf_op jit(solution)/shard_map/ppermute | solution.py:179
  78.7 1.6 %collective-permute-start.20 = (f32[96,128]{1,0:T(8,128)S(1)}, f32[96,128]{1,0:T(8,128)S(1)}, u32[]{:S(2)}, u32[]{:S(2)}) collective-permute-start(f32[96,128]{1,0:T(8,128)S(1)} %get-tuple-element.20), channel_id=1, source_target_pairs={{0,2},{1,3},{2,0},{3,1},{4,6},{5,7},{6,4},{7,5},{8,10},{9,11},{10,... | collective-permute-start | bytes 147464 | tf_op jit(solution)/shard_map/ppermute | solution.py:179
  80.6 1.5 %collective-permute-start.26 = (bf16[2,192,128]{2,1,0:T(8,128)(2,1)S(1)}, bf16[2,192,128]{2,1,0:T(8,128)(2,1)S(1)}, u32[]{:S(2)}, u32[]{:S(2)}) collective-permute-start(bf16[2,192,128]{2,1,0:T(8,128)(2,1)S(1)} %pad_maximum_fusion.1.refs_8_), channel_id=1, source_target_pairs={{0,2},{1,3},{2,0},{3,1},{4,6},{5,7},{6,4},{7,5},{8,10},{9,11},{10,... | collective-permute-start | bytes 294920 | tf_op jit(solution)/shard_map/ppermute | solution.py:179
  82.3 2.9 %collective-permute-start.16 = (bf16[3,96,384]{2,1,0:T(8,128)(2,1)S(1)}, bf16[3,96,384]{2,1,0:T(8,128)(2,1)S(1)}, u32[]{:S(2)}, u32[]{:S(2)}) collective-permute-start(bf16[3,96,384]{2,1,0:T(8,128)(2,1)S(1)} %get-tuple-element.19.refs_0_), channel_id=1, source_target_pairs={{0,4},{1,5},{2,6},{3,7},{4,0},{5,1},{6,2},{7,3},{8,12},{9,13},{10,... | collective-permute-start | bytes 663560 | tf_op jit(solution)/shard_map/ppermute | solution.py:179
  85.7 2.4 %collective-permute-start.18 = (bf16[3,96,384]{2,1,0:T(8,128)(2,1)S(1)}, bf16[3,96,384]{2,1,0:T(8,128)(2,1)S(1)}, u32[]{:S(2)}, u32[]{:S(2)}) collective-permute-start(bf16[3,96,384]{2,1,0:T(8,128)(2,1)S(1)} %get-tuple-element.19.refs_0_), channel_id=1, source_target_pairs={{0,12},{1,13},{2,14},{3,15},{4,8},{5,9},{6,10},{7,11},{8,4},{9,5},... | collective-permute-start | bytes 663560 | tf_op jit(solution)/shard_map/ppermute | solution.py:179
  88.2 1.5 %collective-permute-start.22 = (f32[96,128]{1,0:T(8,128)S(1)}, f32[96,128]{1,0:T(8,128)S(1)}, u32[]{:S(2)}, u32[]{:S(2)}) collective-permute-start(f32[96,128]{1,0:T(8,128)S(1)} %add_add_fusion.refs_4_), channel_id=1, source_target_pairs={{0,4},{1,5},{2,6},{3,7},{4,0},{5,1},{6,2},{7,3},{8,12},{9,13},{10,... | collective-permute-start | bytes 147464 | tf_op jit(solution)/shard_map/ppermute | solution.py:179
  89.7 1.3 %collective-permute-start.23 = (f32[96,128]{1,0:T(8,128)S(1)}, f32[96,128]{1,0:T(8,128)S(1)}, u32[]{:S(2)}, u32[]{:S(2)}) collective-permute-start(f32[96,128]{1,0:T(8,128)S(1)} %add_add_fusion.refs_4_), channel_id=1, source_target_pairs={{0,8},{1,9},{2,10},{3,11},{4,12},{5,13},{6,14},{7,15},{8,0},{9,1},... | collective-permute-start | bytes 147464 | tf_op jit(solution)/shard_map/ppermute | solution.py:179
  91.0 10.5 %collective-permute-done.22.refs_5_ = f32[96,128]{1,0:T(8,128)S(1)} collective-permute-done((f32[96,128]{1,0:T(8,128)S(1)}, f32[96,128]{1,0:T(8,128)S(1)}, u32[]{:S(2)}, u32[]{:S(2)}) %collective-permute-start.22) | collective-permute-done | bytes 49184 | tf_op jit(solution)/shard_map/ppermute | solution.py:179
  101.5 1.4 %collective-permute-start.24 = (f32[96,128]{1,0:T(8,128)S(1)}, f32[96,128]{1,0:T(8,128)S(1)}, u32[]{:S(2)}, u32[]{:S(2)}) collective-permute-start(f32[96,128]{1,0:T(8,128)S(1)} %add_add_fusion.refs_4_), channel_id=1, source_target_pairs={{0,12},{1,13},{2,14},{3,15},{4,8},{5,9},{6,10},{7,11},{8,4},{9,5},... | collective-permute-start | bytes 147464 | tf_op jit(solution)/shard_map/ppermute | solution.py:179
  102.9 8.6 %collective-permute-done.23.refs_6_ = f32[96,128]{1,0:T(8,128)S(1)} collective-permute-done((f32[96,128]{1,0:T(8,128)S(1)}, f32[96,128]{1,0:T(8,128)S(1)}, u32[]{:S(2)}, u32[]{:S(2)}) %collective-permute-start.23) | collective-permute-done | bytes 49184 | tf_op jit(solution)/shard_map/ppermute | solution.py:179
  111.6 2.3 %shard_map.97 = (f32[2,192,128]{2,1,0:T(8,128)S(1)}, bf16[2,192,128]{2,1,0:T(8,128)(2,1)S(1)}, bf16[2,192,128]{2,1,0:T(8,128)(2,1)S(1)}, bf16[2,192,128]{2,1,0:T(8,128)(2,1)S(1)}) custom-call(s32[3]{0:T(128)S(1)} %pad_add_fusion.place, bf16[3,384,384]{2,1,0:T(8,128)(2,1)S(1)} %get-tuple-element.14.weights, ...), custom_call_target="tpu_custom_call" | custom-call | flops 452984832 | bytes 1769472 | tf_op jit(solution)/shard_map/pallas_call | solution.py:239
  114.0 1.6 %collective-permute-start.29 = (bf16[2,192,128]{2,1,0:T(8,128)(2,1)S(1)}, bf16[2,192,128]{2,1,0:T(8,128)(2,1)S(1)}, u32[]{:S(2)}, u32[]{:S(2)}) collective-permute-start(bf16[2,192,128]{2,1,0:T(8,128)(2,1)S(1)} %get-tuple-element.24), channel_id=1, source_target_pairs={{0,2},{1,3},{2,0},{3,1},{4,6},{5,7},{6,4},{7,5},{8,10},{9,11},{10,... | collective-permute-start | bytes 294920 | tf_op jit(solution)/shard_map/ppermute | solution.py:179
  115.9 3.8 %collective-permute-done.29 = bf16[2,192,128]{2,1,0:T(8,128)(2,1)S(1)} collective-permute-done((bf16[2,192,128]{2,1,0:T(8,128)(2,1)S(1)}, bf16[2,192,128]{2,1,0:T(8,128)(2,1)S(1)}, u32[]{:S(2)}, u32[]{:S(2)}) %collective-permute-start.29) | collective-permute-done | bytes 98336 | tf_op jit(solution)/shard_map/ppermute | solution.py:179
  119.7 1.2 collective-permute-done.30
  (65 shorter events, 9.1 us)
Async XLA Ops:
  1.8 27.9 %collective-permute-start.4 = (bf16[192,1024]{1,0:T(8,128)(2,1)S(1)}, bf16[192,1024]{1,0:T(8,128)(2,1)S(1)}, u32[]{:S(2)}, u32[]{:S(2)}) collective-permute-start(bf16[192,1024]{1,0:T(8,128)(2,1)S(1)} %fusion.refs_4_), channel_id=1, source_target_pairs={{0,2},{1,3},{2,0},{3,1},{4,6},{5,7},{6,4},{7,5},{8,10},{9,11},{10,... | collective-permute-start | bytes 1179656 | tf_op jit(solution)/shard_map/ppermute | solution.py:179
  4.8 24.9 %collective-permute-start.1 = (bf16[192,1024]{1,0:T(8,128)(2,1)S(1)}, bf16[192,1024]{1,0:T(8,128)(2,1)S(1)}, u32[]{:S(2)}, u32[]{:S(2)}) collective-permute-start(bf16[192,1024]{1,0:T(8,128)(2,1)S(1)} %bitcast.23), channel_id=1, source_target_pairs={{0,2},{1,3},{2,0},{3,1},{4,6},{5,7},{6,4},{7,5},{8,10},{9,11},{10,... | collective-permute-start | bytes 1179656 | tf_op jit(solution)/shard_map/ppermute | solution.py:179
  5.0 19.7 %collective-permute-start.6 = (bf16[3,48,384]{2,1,0:T(8,128)(2,1)S(1)}, bf16[3,48,384]{2,1,0:T(8,128)(2,1)S(1)}, u32[]{:S(2)}, u32[]{:S(2)}) collective-permute-start(bf16[3,48,384]{2,1,0:T(8,128)(2,1)S(1)} %get-tuple-element.26), channel_id=1, source_target_pairs={{0,2},{1,3},{2,0},{3,1},{4,6},{5,7},{6,4},{7,5},{8,10},{9,11},{10,... | collective-permute-start | bytes 331784 | tf_op jit(solution)/shard_map/ppermute | solution.py:179
  7.0 21.6 %collective-permute-start.7 = (bf16[3,48,384]{2,1,0:T(8,128)(2,1)S(1)}, bf16[3,48,384]{2,1,0:T(8,128)(2,1)S(1)}, u32[]{:S(2)}, u32[]{:S(2)}) collective-permute-start(bf16[3,48,384]{2,1,0:T(8,128)(2,1)S(1)} %get-tuple-element.27.refs_8_), channel_id=1, source_target_pairs={{0,4},{1,5},{2,6},{3,7},{4,0},{5,1},{6,2},{7,3},{8,12},{9,13},{10,... | collective-permute-start | bytes 331784 | tf_op jit(solution)/shard_map/ppermute | solution.py:179
  8.6 20.0 %collective-permute-start.8 = (bf16[3,48,384]{2,1,0:T(8,128)(2,1)S(1)}, bf16[3,48,384]{2,1,0:T(8,128)(2,1)S(1)}, u32[]{:S(2)}, u32[]{:S(2)}) collective-permute-start(bf16[3,48,384]{2,1,0:T(8,128)(2,1)S(1)} %get-tuple-element.27.refs_8_), channel_id=1, source_target_pairs={{0,8},{1,9},{2,10},{3,11},{4,12},{5,13},{6,14},{7,15},{8,0},{9,1},... | collective-permute-start | bytes 331784 | tf_op jit(solution)/shard_map/ppermute | solution.py:179
  24.7 6.6 %collective-permute-start.9 = (bf16[3,48,384]{2,1,0:T(8,128)(2,1)S(1)}, bf16[3,48,384]{2,1,0:T(8,128)(2,1)S(1)}, u32[]{:S(2)}, u32[]{:S(2)}) collective-permute-start(bf16[3,48,384]{2,1,0:T(8,128)(2,1)S(1)} %get-tuple-element.27.refs_8_), channel_id=1, source_target_pairs={{0,12},{1,13},{2,14},{3,15},{4,8},{5,9},{6,10},{7,11},{8,4},{9,5},... | collective-permute-start | bytes 331784 | tf_op jit(solution)/shard_map/ppermute | solution.py:179
  28.6 25.6 %collective-permute-start.3 = (bf16[192,1024]{1,0:T(8,128)(2,1)S(1)}, bf16[192,1024]{1,0:T(8,128)(2,1)S(1)}, u32[]{:S(2)}, u32[]{:S(2)}) collective-permute-start(bf16[192,1024]{1,0:T(8,128)(2,1)S(1)} %fusion.refs_4_), channel_id=1, source_target_pairs={{0,1},{1,0},{2,3},{3,2},{4,5},{5,4},{6,7},{7,6},{8,9},{9,8},{10,11... | collective-permute-start | bytes 1179656 | tf_op jit(solution)/shard_map/ppermute | solution.py:179
  29.2 25.0 %collective-permute-start = (bf16[192,1024]{1,0:T(8,128)(2,1)S(1)}, bf16[192,1024]{1,0:T(8,128)(2,1)S(1)}, u32[]{:S(2)}, u32[]{:S(2)}) collective-permute-start(bf16[192,1024]{1,0:T(8,128)(2,1)S(1)} %bitcast.24), channel_id=1, source_target_pairs={{0,1},{1,0},{2,3},{3,2},{4,5},{5,4},{6,7},{7,6},{8,9},{9,8},{10,11... | collective-permute-start | bytes 1179656 | tf_op jit(solution)/shard_map/ppermute | solution.py:179
  29.7 24.5 %collective-permute-start.5 = (bf16[192,1024]{1,0:T(8,128)(2,1)S(1)}, bf16[192,1024]{1,0:T(8,128)(2,1)S(1)}, u32[]{:S(2)}, u32[]{:S(2)}) collective-permute-start(bf16[192,1024]{1,0:T(8,128)(2,1)S(1)} %collective-permute-done.4.refs_6_), channel_id=1, source_target_pairs={{0,1},{1,0},{2,3},{3,2},{4,5},{5,4},{6,7},{7,6},{8,9},{9,8},{10,11... | collective-permute-start | bytes 1179656 | tf_op jit(solution)/shard_map/ppermute | solution.py:179
  29.8 24.4 %collective-permute-start.2 = (bf16[192,1024]{1,0:T(8,128)(2,1)S(1)}, bf16[192,1024]{1,0:T(8,128)(2,1)S(1)}, u32[]{:S(2)}, u32[]{:S(2)}) collective-permute-start(bf16[192,1024]{1,0:T(8,128)(2,1)S(1)} %collective-permute-done.1.refs_2_), channel_id=1, source_target_pairs={{0,1},{1,0},{2,3},{3,2},{4,5},{5,4},{6,7},{7,6},{8,9},{9,8},{10,11... | collective-permute-start | bytes 1179656 | tf_op jit(solution)/shard_map/ppermute | solution.py:179
  32.0 4.7 %collective-permute-start.10 = (bf16[3,48,384]{2,1,0:T(8,128)(2,1)S(1)}, bf16[3,48,384]{2,1,0:T(8,128)(2,1)S(1)}, u32[]{:S(2)}, u32[]{:S(2)}) collective-permute-start(bf16[3,48,384]{2,1,0:T(8,128)(2,1)S(1)} %collective-permute-done.6.refs_9_), channel_id=1, source_target_pairs={{0,4},{1,5},{2,6},{3,7},{4,0},{5,1},{6,2},{7,3},{8,12},{9,13},{10,... | collective-permute-start | bytes 331784 | tf_op jit(solution)/shard_map/ppermute | solution.py:179
  37.4 10.2 %collective-permute-start.11 = (bf16[3,48,384]{2,1,0:T(8,128)(2,1)S(1)}, bf16[3,48,384]{2,1,0:T(8,128)(2,1)}, u32[]{:S(2)}, u32[]{:S(2)}) collective-permute-start(bf16[3,48,384]{2,1,0:T(8,128)(2,1)S(1)} %collective-permute-done.6.refs_9_), channel_id=1, source_target_pairs={{0,8},{1,9},{2,10},{3,11},{4,12},{5,13},{6,14},{7,15},{8,0},{9,1},... | collective-permute-start | bytes 331784 | tf_op jit(solution)/shard_map/ppermute | solution.py:179
  47.6 6.5 %collective-permute-start.12 = (bf16[3,48,384]{2,1,0:T(8,128)(2,1)S(1)}, bf16[3,48,384]{2,1,0:T(8,128)(2,1)S(1)}, u32[]{:S(2)}, u32[]{:S(2)}) collective-permute-start(bf16[3,48,384]{2,1,0:T(8,128)(2,1)S(1)} %collective-permute-done.6.refs_9_), channel_id=1, source_target_pairs={{0,12},{1,13},{2,14},{3,15},{4,8},{5,9},{6,10},{7,11},{8,4},{9,5},... | collective-permute-start | bytes 331784 | tf_op jit(solution)/shard_map/ppermute | solution.py:179
  56.9 11.7 %copy-start.11 = (bf16[128,192]{0,1:T(8,128)(2,1)S(1)}, bf16[128,192]{0,1:T(8,128)(2,1)}, u32[]{:S(2)}) copy-start(bf16[128,192]{0,1:T(8,128)(2,1)} %param.14) | copy-start | bytes 147460
  64.2 7.3 %collective-permute-start.13 = (bf16[3,96,384]{2,1,0:T(8,128)(2,1)S(1)}, bf16[3,96,384]{2,1,0:T(8,128)(2,1)S(1)}, u32[]{:S(2)}, u32[]{:S(2)}) collective-permute-start(bf16[3,96,384]{2,1,0:T(8,128)(2,1)S(1)} %get-tuple-element.16), channel_id=1, source_target_pairs={{0,4},{1,5},{2,6},{3,7},{4,0},{5,1},{6,2},{7,3},{8,12},{9,13},{10,... | collective-permute-start | bytes 663560 | tf_op jit(solution)/shard_map/ppermute | solution.py:179
  64.2 13.6 %collective-permute-start.14 = (bf16[3,96,384]{2,1,0:T(8,128)(2,1)S(1)}, bf16[3,96,384]{2,1,0:T(8,128)(2,1)S(1)}, u32[]{:S(2)}, u32[]{:S(2)}) collective-permute-start(bf16[3,96,384]{2,1,0:T(8,128)(2,1)S(1)} %get-tuple-element.17), channel_id=1, source_target_pairs={{0,8},{1,9},{2,10},{3,11},{4,12},{5,13},{6,14},{7,15},{8,0},{9,1},... | collective-permute-start | bytes 663560 | tf_op jit(solution)/shard_map/ppermute | solution.py:179
  66.9 10.9 %collective-permute-start.15 = (bf16[3,96,384]{2,1,0:T(8,128)(2,1)S(1)}, bf16[3,96,384]{2,1,0:T(8,128)(2,1)S(1)}, u32[]{:S(2)}, u32[]{:S(2)}) collective-permute-start(bf16[3,96,384]{2,1,0:T(8,128)(2,1)S(1)} %get-tuple-element.18), channel_id=1, source_target_pairs={{0,12},{1,13},{2,14},{3,15},{4,8},{5,9},{6,10},{7,11},{8,4},{9,5},... | collective-permute-start | bytes 663560 | tf_op jit(solution)/shard_map/ppermute | solution.py:179
  68.6 13.5 %collective-permute-start.25 = (bf16[2,192,128]{2,1,0:T(8,128)(2,1)S(1)}, bf16[2,192,128]{2,1,0:T(8,128)(2,1)S(1)}, u32[]{:S(2)}, u32[]{:S(2)}) collective-permute-start(bf16[2,192,128]{2,1,0:T(8,128)(2,1)S(1)} %pad_maximum_fusion.1.refs_8_), channel_id=1, source_target_pairs={{0,1},{1,0},{2,3},{3,2},{4,5},{5,4},{6,7},{7,6},{8,9},{9,8},{10,11... | collective-permute-start | bytes 294920 | tf_op jit(solution)/shard_map/ppermute | solution.py:179
  78.6 3.6 %collective-permute-start.19 = (f32[96,128]{1,0:T(8,128)S(1)}, f32[96,128]{1,0:T(8,128)S(1)}, u32[]{:S(2)}, u32[]{:S(2)}) collective-permute-start(f32[96,128]{1,0:T(8,128)S(1)} %get-tuple-element.20), channel_id=1, source_target_pairs={{0,1},{1,0},{2,3},{3,2},{4,5},{5,4},{6,7},{7,6},{8,9},{9,8},{10,11... | collective-permute-start | bytes 147464 | tf_op jit(solution)/shard_map/ppermute | solution.py:179
  78.7 6.5 %collective-permute-start.20 = (f32[96,128]{1,0:T(8,128)S(1)}, f32[96,128]{1,0:T(8,128)S(1)}, u32[]{:S(2)}, u32[]{:S(2)}) collective-permute-start(f32[96,128]{1,0:T(8,128)S(1)} %get-tuple-element.20), channel_id=1, source_target_pairs={{0,2},{1,3},{2,0},{3,1},{4,6},{5,7},{6,4},{7,5},{8,10},{9,11},{10,... | collective-permute-start | bytes 147464 | tf_op jit(solution)/shard_map/ppermute | solution.py:179
  80.3 5.5 %collective-permute-start.21 = (f32[96,128]{1,0:T(8,128)S(1)}, f32[96,128]{1,0:T(8,128)S(1)}, u32[]{:S(2)}, u32[]{:S(2)}) collective-permute-start(f32[96,128]{1,0:T(8,128)S(1)} %get-tuple-element.20), channel_id=1, source_target_pairs={{0,3},{1,2},{2,1},{3,0},{4,7},{5,6},{6,5},{7,4},{8,11},{9,10},{10,... | collective-permute-start | bytes 147464 | tf_op jit(solution)/shard_map/ppermute | solution.py:179
  80.6 7.6 %collective-permute-start.26 = (bf16[2,192,128]{2,1,0:T(8,128)(2,1)S(1)}, bf16[2,192,128]{2,1,0:T(8,128)(2,1)S(1)}, u32[]{:S(2)}, u32[]{:S(2)}) collective-permute-start(bf16[2,192,128]{2,1,0:T(8,128)(2,1)S(1)} %pad_maximum_fusion.1.refs_8_), channel_id=1, source_target_pairs={{0,2},{1,3},{2,0},{3,1},{4,6},{5,7},{6,4},{7,5},{8,10},{9,11},{10,... | collective-permute-start | bytes 294920 | tf_op jit(solution)/shard_map/ppermute | solution.py:179
  82.1 7.6 %collective-permute-start.27 = (bf16[2,192,128]{2,1,0:T(8,128)(2,1)S(1)}, bf16[2,192,128]{2,1,0:T(8,128)(2,1)S(1)}, u32[]{:S(2)}, u32[]{:S(2)}) collective-permute-start(bf16[2,192,128]{2,1,0:T(8,128)(2,1)S(1)} %pad_maximum_fusion.1.refs_8_), channel_id=1, source_target_pairs={{0,3},{1,2},{2,1},{3,0},{4,7},{5,6},{6,5},{7,4},{8,11},{9,10},{10,... | collective-permute-start | bytes 294920 | tf_op jit(solution)/shard_map/ppermute | solution.py:179
  82.3 29.3 %collective-permute-start.16 = (bf16[3,96,384]{2,1,0:T(8,128)(2,1)S(1)}, bf16[3,96,384]{2,1,0:T(8,128)(2,1)S(1)}, u32[]{:S(2)}, u32[]{:S(2)}) collective-permute-start(bf16[3,96,384]{2,1,0:T(8,128)(2,1)S(1)} %get-tuple-element.19.refs_0_), channel_id=1, source_target_pairs={{0,4},{1,5},{2,6},{3,7},{4,0},{5,1},{6,2},{7,3},{8,12},{9,13},{10,... | collective-permute-start | bytes 663560 | tf_op jit(solution)/shard_map/ppermute | solution.py:179
  85.2 26.4 %collective-permute-start.17 = (bf16[3,96,384]{2,1,0:T(8,128)(2,1)S(1)}, bf16[3,96,384]{2,1,0:T(8,128)(2,1)S(1)}, u32[]{:S(2)}, u32[]{:S(2)}) collective-permute-start(bf16[3,96,384]{2,1,0:T(8,128)(2,1)S(1)} %get-tuple-element.19.refs_0_), channel_id=1, source_target_pairs={{0,8},{1,9},{2,10},{3,11},{4,12},{5,13},{6,14},{7,15},{8,0},{9,1},... | collective-permute-start | bytes 663560 | tf_op jit(solution)/shard_map/ppermute | solution.py:179
  85.7 25.8 %collective-permute-start.18 = (bf16[3,96,384]{2,1,0:T(8,128)(2,1)S(1)}, bf16[3,96,384]{2,1,0:T(8,128)(2,1)S(1)}, u32[]{:S(2)}, u32[]{:S(2)}) collective-permute-start(bf16[3,96,384]{2,1,0:T(8,128)(2,1)S(1)} %get-tuple-element.19.refs_0_), channel_id=1, source_target_pairs={{0,12},{1,13},{2,14},{3,15},{4,8},{5,9},{6,10},{7,11},{8,4},{9,5},... | collective-permute-start | bytes 663560 | tf_op jit(solution)/shard_map/ppermute | solution.py:179
  88.2 13.3 %collective-permute-start.22 = (f32[96,128]{1,0:T(8,128)S(1)}, f32[96,128]{1,0:T(8,128)S(1)}, u32[]{:S(2)}, u32[]{:S(2)}) collective-permute-start(f32[96,128]{1,0:T(8,128)S(1)} %add_add_fusion.refs_4_), channel_id=1, source_target_pairs={{0,4},{1,5},{2,6},{3,7},{4,0},{5,1},{6,2},{7,3},{8,12},{9,13},{10,... | collective-permute-start | bytes 147464 | tf_op jit(solution)/shard_map/ppermute | solution.py:179
  89.7 21.9 %collective-permute-start.23 = (f32[96,128]{1,0:T(8,128)S(1)}, f32[96,128]{1,0:T(8,128)S(1)}, u32[]{:S(2)}, u32[]{:S(2)}) collective-permute-start(f32[96,128]{1,0:T(8,128)S(1)} %add_add_fusion.refs_4_), channel_id=1, source_target_pairs={{0,8},{1,9},{2,10},{3,11},{4,12},{5,13},{6,14},{7,15},{8,0},{9,1},... | collective-permute-start | bytes 147464 | tf_op jit(solution)/shard_map/ppermute | solution.py:179
  101.5 10.0 %collective-permute-start.24 = (f32[96,128]{1,0:T(8,128)S(1)}, f32[96,128]{1,0:T(8,128)S(1)}, u32[]{:S(2)}, u32[]{:S(2)}) collective-permute-start(f32[96,128]{1,0:T(8,128)S(1)} %add_add_fusion.refs_4_), channel_id=1, source_target_pairs={{0,12},{1,13},{2,14},{3,15},{4,8},{5,9},{6,10},{7,11},{8,4},{9,5},... | collective-permute-start | bytes 147464 | tf_op jit(solution)/shard_map/ppermute | solution.py:179
  113.9 1.9 %collective-permute-start.28 = (bf16[2,192,128]{2,1,0:T(8,128)(2,1)S(1)}, bf16[2,192,128]{2,1,0:T(8,128)(2,1)S(1)}, u32[]{:S(2)}, u32[]{:S(2)}) collective-permute-start(bf16[2,192,128]{2,1,0:T(8,128)(2,1)S(1)} %get-tuple-element.23), channel_id=1, source_target_pairs={{0,1},{1,0},{2,3},{3,2},{4,5},{5,4},{6,7},{7,6},{8,9},{9,8},{10,11... | collective-permute-start | bytes 294920 | tf_op jit(solution)/shard_map/ppermute | solution.py:179
  114.0 5.7 %collective-permute-start.29 = (bf16[2,192,128]{2,1,0:T(8,128)(2,1)S(1)}, bf16[2,192,128]{2,1,0:T(8,128)(2,1)S(1)}, u32[]{:S(2)}, u32[]{:S(2)}) collective-permute-start(bf16[2,192,128]{2,1,0:T(8,128)(2,1)S(1)} %get-tuple-element.24), channel_id=1, source_target_pairs={{0,2},{1,3},{2,0},{3,1},{4,6},{5,7},{6,4},{7,5},{8,10},{9,11},{10,... | collective-permute-start | bytes 294920 | tf_op jit(solution)/shard_map/ppermute | solution.py:179
  115.6 5.3 %collective-permute-start.30 = (bf16[2,192,128]{2,1,0:T(8,128)(2,1)S(1)}, bf16[2,192,128]{2,1,0:T(8,128)(2,1)S(1)}, u32[]{:S(2)}, u32[]{:S(2)}) collective-permute-start(bf16[2,192,128]{2,1,0:T(8,128)(2,1)S(1)} %get-tuple-element.25), channel_id=1, source_target_pairs={{0,3},{1,2},{2,1},{3,0},{4,7},{5,6},{6,5},{7,4},{8,11},{9,10},{10,... | collective-permute-start | bytes 294920 | tf_op jit(solution)/shard_map/ppermute | solution.py:179
  (11 other events, 33.3 us)

commit v2 on v0

--- a/solution.py
+++ b/solution.py
@@ -1,13 +1,268 @@
+import functools
+
 import jax
 import jax.numpy as jnp
 from jax import lax
+from jax.experimental import pallas as pl
+from jax.experimental.pallas import tpu as pltpu
 from jax.sharding import PartitionSpec as P
-
-HID = 1536
-
 
 step_ratio = 0.5
 epsilon = 1e-06
+f32, bf16 = jnp.float32, jnp.bfloat16
+
+
+def contract(left, right, left_dim, right_dim):
+    return lax.dot_general(
+        left, right, (((left_dim,), (right_dim,)), ((), ())), preferred_element_type=f32
+    )
+
+
+def gated(gate, up):
+    sigma = jax.nn.sigmoid(gate)
+    silu = gate * sigma
+    slope = sigma * (1.0 + gate * (1.0 - sigma))
+    return silu, slope * up, silu * up
+
+
+def join(full, mine, other, half):
+    feats = mine.shape[-2]
+    full[:, pl.ds(pl.multiple_of(half * feats, feats), feats), :] = mine[...]
+    full[:, pl.ds(pl.multiple_of((1 - half) * feats, feats), feats), :] = other[...]
+
+
+def add_grads(tokens, weights, grads, fresh):
+    total = tokens.shape[2]
+    chunk = min(512, total)
+    for start in range(0, total, chunk):
+        key = tokens[0, :, start : start + chunk]
+        val = tokens[1, :, start : start + chunk]
+        gate = contract(weights[0], key, 0, 0)
+        up = contract(weights[1], key, 0, 0)
+        back = contract(weights[2], val, 0, 0)
+        silu, slope_up, act = gated(gate, up)
+        parts = (
+            contract(key, (back * slope_up).astype(bf16), 1, 1),
+            contract(key, (back * silu).astype(bf16), 1, 1),
+            contract(val, act.astype(bf16), 1, 1),
+        )
+        for index, part in enumerate(parts):
+            if fresh and start == 0:
+                grads[index] = part
+            else:
+                grads[index] += part
+
+
+def rows_kernel(groups, place, *refs):
+    blocks, (weights,) = refs[: 2 * groups], refs[2 * groups :]
+    group, side = place[0], place[1]
+    for index, block in enumerate(blocks):
+        flip, sided = index % groups, (side if index < groups else 1 - side)
+        weights[:, rows_of((group ^ flip) * 2 + sided, block.shape[1]), :] = block[...]
+
+
+def own_kernel(place, mine, other, weights, grads, tokens):
+    join(tokens, mine, other, place[2])
+    add_grads(tokens, weights, grads, True)
+
+
+def pair_kernel(groups, place, mine, other, weights, before, *refs):
+    outs, (grads, tokens) = refs[:groups], refs[groups:]
+    group, half = place[0], place[2]
+    grads[...] = before[...]
+    join(tokens, mine, other, half)
+    add_grads(tokens, weights, grads, False)
+    for flip, out in enumerate(outs):
+        out[...] = grads[:, rows_of(group ^ flip, out.shape[1]), :].astype(out.dtype)
+
+
+def rows_of(owner, rows):
+    return pl.ds(pl.multiple_of(owner * rows, rows), rows)
+
+
+def sum_kernel(arrivals, place, weights, own, *refs):
+    arrived, (grad_out, stats_out) = refs[:arrivals], refs[arrivals:]
+    where = rows_of(place[0], own.shape[1])
+    lane = lax.broadcasted_iota(jnp.int32, stats_out.shape, 1)
+    stats = jnp.zeros(stats_out.shape, f32)
+    for index in range(3):
+        grad = own[index]
+        for other in arrived:
+            grad = grad + other[index].astype(f32)
+        grad_out[index] = grad.astype(bf16)
+        weight = weights[index, where, :].astype(f32)
+        for slot, product in enumerate((weight * weight, weight * grad, grad * grad)):
+            row_sum = jnp.sum(product, axis=1, keepdims=True)
+            stats = jnp.where(lane == 3 * index + slot, row_sum, stats)
+    stats_out[...] = stats
+
+
+def query_kernel(groups, hidden, place, weights, *refs):
+    grads, stats, quests, refs = (
+        refs[:groups],
+        refs[groups : 2 * groups],
+        refs[2 * groups : 2 * groups + 4],
+        refs[2 * groups + 4 :],
+    )
+    own_out, sends, (renewed, query) = refs[0], refs[1:4], refs[4:]
+    group, side, half = place[0], place[1], place[2]
+    feats, count = quests[0].shape[1:]
+
+    for flip in range(groups):
+        where = rows_of(group ^ flip, grads[0].shape[1])
+        sums = stats[flip][...] * (1.0 / hidden)
+        for index in range(3):
+            wsq = sums[:, 3 * index : 3 * index + 1]
+            cross = sums[:, 3 * index + 1 : 3 * index + 2]
+            gsq = sums[:, 3 * index + 2 : 3 * index + 3]
+            scale = step_ratio * jnp.sqrt(wsq) / jnp.sqrt(gsq + epsilon)
+            msq = wsq + 2.0 * scale * cross + scale * scale * gsq
+            factor = jnp.sqrt(wsq) / jnp.sqrt(msq + epsilon)
+            moved = weights[index, where, :].astype(f32) + scale * grads[flip][index].astype(f32)
+            renewed[index, where, :] = (moved * factor).astype(bf16)
+    for flip in range(4):
+        feat = pl.ds(pl.multiple_of((half ^ (flip & 1)) * feats, feats), feats)
+        span = pl.ds(pl.multiple_of((side ^ (flip >> 1)) * count, count), count)
+        query[:, feat, span] = quests[flip][...]
+
+    gate = contract(renewed[0], query[0], 0, 0)
+    up = contract(renewed[1], query[0], 0, 0)
+    back = contract(renewed[2], query[1], 0, 0)
+    silu, slope_up, act = gated(gate, up)
+    out = contract(renewed[2], act.astype(bf16), 1, 0)
+    grad = contract(renewed[0], (back * slope_up).astype(bf16), 1, 0) + contract(
+        renewed[1], (back * silu).astype(bf16), 1, 0
+    )
+    for index, whole in enumerate((out, grad)):
+        for flip, target in enumerate((own_out, *sends)):
+            left = jnp.where((half ^ (flip & 1)) == 0, whole[:feats], whole[feats:])
+            piece = jnp.where((side ^ (flip >> 1)) == 0, left[:, :count], left[:, count:])
+            target[index] = piece.astype(target.dtype)
+
+
+def last_kernel(own, first, second, third, out, grad):
+    for index, target in enumerate((out, grad)):
+        total = own[index] + first[index].astype(f32) + second[index].astype(f32)
+        target[...] = (total + third[index].astype(f32)).astype(bf16)
+
+
+def call(body, operands, outs, scratch=(), flops=0, place=None, mib=4):
+    specs = [pl.BlockSpec(memory_space=pltpu.VMEM)] * len(operands)
+    if place is not None:
+        specs, operands = [pl.BlockSpec(memory_space=pltpu.SMEM)] + specs, (place, *operands)
+    moved = sum(4 * leaf.size for leaf in (*operands, *outs))
+    return pl.pallas_call(
+        body,
+        out_shape=list(outs),
+        in_specs=specs,
+        out_specs=[pl.BlockSpec(memory_space=pltpu.VMEM)] * len(outs),
+        scratch_shapes=list(scratch),
+        compiler_params=pltpu.CompilerParams(vmem_limit_bytes=mib * 1024 * 1024),
+        cost_estimate=pl.CostEstimate(flops=flops, bytes_accessed=moved, transcendentals=0),
+    )(*operands)
+
+
+def direct(
+    input_keys, input_values, input_lr, gate_weight, up_weight, down_weight, queries, out_grad,
+    n_tok, n_hid,
+):
+    groups = n_tok // 2
+    tok, half = lax.axis_index("tok"), lax.axis_index("hid")
+    group, side = tok // 2, tok % 2
+    place = jnp.stack([group, side, half]).astype(jnp.int32)
+    core, pair, zed = 1, 2, 4
+
+    def swap(array, flip):
+        pairs = [(i, i ^ flip) for i in range(n_tok * n_hid)]
+        return lax.ppermute(array, ("tok", "hid"), pairs)
+
+    def gather(block, beside=()):
+        bits = [1 << place for place in range(groups.bit_length() - 1)]
+        came = {bit: swap(block, zed * bit) for bit in reversed(bits)}
+        came, _ = lax.optimization_barrier((came, beside))
+        held = {0: block, **came}
+        for flip in range(groups):
+            if flip not in held:
+                low = flip & -flip
+                held[flip] = swap(held[flip ^ low], zed * low)
+        return [held[flip] for flip in range(groups)]
+
+    stacked = jnp.stack([gate_weight, up_weight, down_weight])
+    cols = stacked.shape[2] // 2
+    own_w = lax.dynamic_slice_in_dim(stacked, side * cols, cols, 2)
+    give_w = lax.dynamic_slice_in_dim(stacked, (1 - side) * cols, cols, 2)
+    vals = (input_lr[None, :] * input_values.T.astype(f32)).astype(bf16)
+    tokens = jnp.stack([input_keys.T, vals])
+    _, feats, toks = tokens.shape
+    tokens, pair_w = lax.optimization_barrier((tokens, swap(give_w, pair)))
+    first = gather(own_w)
+    pair_w, _ = lax.optimization_barrier((pair_w, first[1]))
+    second = gather(pair_w)
+    pair_tokens = swap(tokens, pair)
+
+    width = n_hid * feats
+    rows = width // groups
+    whole = (3, width, cols)
+    block = (3, rows, cols)
+    token_flops = 6 * 2 * toks * width * cols
+    joined = pltpu.VMEM((2, width, toks), bf16)
+    (weights,) = call(
+        functools.partial(rows_kernel, groups),
+        (*first, *second),
+        (jax.ShapeDtypeStruct(whole, bf16),),
+        place=place,
+    )
+    pair_tokens, weights = lax.optimization_barrier((pair_tokens, weights))
+    (grads,) = call(
+        own_kernel,
+        (tokens, swap(tokens, core), weights),
+        (jax.ShapeDtypeStruct(whole, f32),),
+        [joined],
+        token_flops,
+        place,
+        16,
+    )
+    shares = call(
+        functools.partial(pair_kernel, groups),
+        (pair_tokens, swap(pair_tokens, core), weights, grads),
+        [jax.ShapeDtypeStruct(block, bf16 if flip else f32) for flip in range(groups)],
+        [pltpu.VMEM(whole, f32), joined],
+        token_flops,
+        place,
+        16,
+    )
+    quest = jnp.stack([queries.T, out_grad.T])
+    quest, shares = lax.optimization_barrier((quest, shares))
+    quests = [quest] + [swap(quest, flip) for flip in (1, 2, 3)]
+
+    arrived = [swap(shares[flip], zed * flip) for flip in range(1, groups)]
+    arrived, quests = lax.optimization_barrier((arrived, quests))
+    grad, stats = call(
+        functools.partial(sum_kernel, len(arrived)),
+        (weights, shares[0], *arrived),
+        (jax.ShapeDtypeStruct(block, bf16), jax.ShapeDtypeStruct((rows, 128), f32)),
+        place=place,
+    )
+    stats = stats + swap(stats, core)
+    stats = stats + swap(stats, pair)
+    all_stats = [stats] + [swap(stats, zed * flip) for flip in range(1, groups)]
+
+    count = queries.shape[0]
+    piece = (2, feats, count)
+    own_out, *sends = call(
+        functools.partial(query_kernel, groups, 2 * n_hid * cols),
+        (weights, *gather(grad, stats), *all_stats, *quests),
+        [jax.ShapeDtypeStruct(piece, f32)] + [jax.ShapeDtypeStruct(piece, bf16)] * 3,
+        [pltpu.VMEM(whole, bf16), pltpu.VMEM((2, width, 2 * count), bf16)],
+        6 * 2 * 2 * count * width * cols,
+        place,
+        16,
+    )
+    arrived = [swap(send, flip) for send, flip in zip(sends, (1, 2, 3))]
+    out, grad = call(
+        last_kernel, (own_out, *arrived), [jax.ShapeDtypeStruct(piece[1:], bf16)] * 2
+    )
+    return out.T, grad.T
 
 
 def silu_slope(pre):
@@ -31,8 +286,8 @@
     return (moved * (jnp.sqrt(wsq) / jnp.sqrt(msq + epsilon))[:, None]).astype(jnp.bfloat16)
 
 
-def shards(
-    input_keys, input_values, input_lr, gate_weight, up_weight, down_weight, queries, out_grad
+def general(
+    input_keys, input_values, input_lr, gate_weight, up_weight, down_weight, queries, out_grad, n_hid
 ):
     keys, values = (
         lax.all_gather(input_keys, "hid", axis=1, tiled=True),
@@ -52,6 +307,7 @@
     d_gate = (-back * key_up * silu_slope(key_gate)).astype(jnp.bfloat16)
     d_up = (-back * gate_act).astype(jnp.bfloat16)
     width = gate_weight.shape[1]
+    hidden = width * n_hid
     grads = lax.psum(
         jnp.concatenate(
             [
@@ -77,9 +333,9 @@
         "hid",
     )
     for index in range(3):
-        wsq = totals[3 * index] / HID
-        cross = totals[3 * index + 1] / HID
-        gsq = totals[3 * index + 2] / HID
+        wsq = totals[3 * index] / hidden
+        cross = totals[3 * index + 1] / hidden
+        gsq = totals[3 * index + 2] / hidden
         scale = step_ratio * jnp.sqrt(wsq) / jnp.sqrt(gsq + epsilon)
         moved = weights[index] - scale[:, None] * pieces[index]
         msq = wsq - 2.0 * scale * cross + scale * scale * gsq
@@ -110,6 +366,24 @@
 
 
 def solution(mesh):
+    n_tok, n_hid = mesh.shape["tok"], mesh.shape["hid"]
+
+    def shards(*args):
+        rows, cols = args[3].shape
+        toks, count = args[0].shape[0], args[6].shape[0]
+        fits = (
+            n_hid == 2
+            and 2 <= n_tok <= 8
+            and n_tok & (n_tok - 1) == 0
+            and rows % 16 == 0
+            and cols % 256 == 0
+            and toks % 256 == 0
+            and count % 128 == 0
+        )
+        if fits:
+            return direct(*args, n_tok, n_hid)
+        return general(*args, n_hid)
+
     return jax.shard_map(
         shards,
         mesh=mesh,

time: 299 us -> 96.7 us (0.32)
  blocking collectives: 110 us -> 0 us
  waiting for transfers between devices: 151 us -> 44.4 us
  starting transfers between devices: 0.12 us -> 37 us
  between operations: 13.9 us -> 0.83 us
  Pallas kernels: 0 us -> 12 us
  matrix products: 10.6 us -> 0 us
  other arithmetic: 9.59 us -> 2.28 us
  local copies, waits for them, and re-layouts: 3.61 us -> 0.06 us
    psum x1 -> x0, waiting for transfers between devices: 134 us -> none  [shards(): lax.psum(jnp.concatenate([contract_rows(keys, d_gate), contract_rows(keys...]
    all_gather x7 -> x0, blocking collectives: 105 us -> none  [the longest x1 33.4 us: shards(): lax.all_gather(gate_weight, 'tok', axis=0, tiled=True)]
    ppermute x0 -> x27, waiting for transfers between devices: none -> 44.4 us  [swap(): return lax.ppermute(array, ('tok', 'hid'), pairs)]
    ppermute x0 -> x27, starting transfers between devices: none -> 37 us  [swap(): return lax.ppermute(array, ('tok', 'hid'), pairs)]
    reduce_scatter x2 -> x0, waiting for transfers between devices: 17.1 us -> none  [the longest x1 11.5 us: shards(): lax.psum_scatter(out_part.astype(jnp.bfloat16), 'hid', scatter_dimension=...]
    pallas_call x0 -> x6, Pallas kernels: none -> 12 us  [call(): pl.pallas_call(body, out_shape=list(outs), in_specs=specs, out_specs=[pl....]
    dot_general x12 -> x0, matrix products: 10.6 us -> none  [the longest x3 4 us: contract_rows(): lax.dot_general(left, right, (((0,), (0,)), ((), ())), preferred_element_...]
    psum x1 -> x0, blocking collectives: 4.62 us -> none  [shards(): lax.psum((stats[0], stats[1], stats[2], stats[3], stats[4], stats[5], sta...]
  transfers between devices with their start and end apart: 3 -> 27, of which waited for: 3 -> 19; matrix products, arithmetic and copies ran while one was open for 1% -> 1% of each run, Pallas kernels for 0% -> 4%
where the time goes in v2:
time: 96.7 us; the launch traced here: 96.6 us
  waiting for transfers between devices  44.4 us (46%)
  starting transfers between devices  37 us (38%)
  Pallas kernels  12 us (12%)
  other arithmetic  2.28 us (2%)
    ppermute x27, waiting for transfers between devices, swap(): return lax.ppermute(array, ('tok', 'hid'), pairs)  44.4 us
    ppermute x27, starting transfers between devices, swap(): return lax.ppermute(array, ('tok', 'hid'), pairs)  37 us
    pallas_call x6, Pallas kernels, call(): pl.pallas_call(body, out_shape=list(outs), in_specs=specs, out_specs=[pl....  12 us
  transfers between devices with their start and end apart: 27, of which 19 were waited for; matrix products, arithmetic and copies ran while one was open for 1% of the time, Pallas kernels for 4%

profile of v2, /device:TPU:0, one launch (start us, length us, event | category | flops | bytes accessed | tf_op | source)
XLA Modules:
  0.0 96.6 jit_solution(895287237588811854)
XLA Ops:
  1.7 3.0 %collective-permute-start = (bf16[3,48,384]{2,1,0:T(8,128)(2,1)S(1)}, bf16[3,48,384]{2,1,0:T(8,128)(2,1)S(1)}, u32[]{:S(2)}, u32[]{:S(2)}) collective-permute-start(bf16[3,48,384]{2,1,0:T(8,128)(2,1)S(1)} %get-tuple-element.73), channel_id=1, source_target_pairs={{0,2},{1,3},{2,0},{3,1},{4,6},{5,7},{6,4},{7,5},{8,10},{9,11},{10,... | collective-permute-start | bytes 331784 | tf_op jit(solution)/shard_map/ppermute | solution.py:177
  5.9 1.9 %collective-permute-done.refs_4_ = bf16[3,48,384]{2,1,0:T(8,128)(2,1)S(1)} collective-permute-done((bf16[3,48,384]{2,1,0:T(8,128)(2,1)S(1)}, bf16[3,48,384]{2,1,0:T(8,128)(2,1)S(1)}, u32[]{:S(2)}, u32[]{:S(2)}) %collective-permute-start) | collective-permute-done | bytes 110624 | tf_op jit(solution)/shard_map/ppermute | solution.py:177
  7.8 1.7 %collective-permute-start.1 = (bf16[2,192,1024]{2,1,0:T(8,128)(2,1)S(1)}, bf16[2,192,1024]{2,1,0:T(8,128)(2,1)S(1)}, u32[]{:S(2)}, u32[]{:S(2)}) collective-permute-start(bf16[2,192,1024]{2,1,0:T(8,128)(2,1)S(1)} %pad_maximum_fusion.mine), channel_id=1, source_target_pairs={{0,2},{1,3},{2,0},{3,1},{4,6},{5,7},{6,4},{7,5},{8,10},{9,11},{10,... | collective-permute-start | bytes 2359304 | tf_op jit(solution)/shard_map/ppermute | solution.py:177
  9.5 1.6 %collective-permute-start.2 = (bf16[3,48,384]{2,1,0:T(8,128)(2,1)S(1)}, bf16[3,48,384]{2,1,0:T(8,128)(2,1)S(1)}, u32[]{:S(2)}, u32[]{:S(2)}) collective-permute-start(bf16[3,48,384]{2,1,0:T(8,128)(2,1)S(1)} %get-tuple-element.72.refs_0_), channel_id=1, source_target_pairs={{0,4},{1,5},{2,6},{3,7},{4,0},{5,1},{6,2},{7,3},{8,12},{9,13},{10,... | collective-permute-start | bytes 331784 | tf_op jit(solution)/shard_map/ppermute | solution.py:177
  11.1 2.6 %collective-permute-start.3 = (bf16[3,48,384]{2,1,0:T(8,128)(2,1)S(1)}, bf16[3,48,384]{2,1,0:T(8,128)(2,1)S(1)}, u32[]{:S(2)}, u32[]{:S(2)}) collective-permute-start(bf16[3,48,384]{2,1,0:T(8,128)(2,1)S(1)} %get-tuple-element.72.refs_0_), channel_id=1, source_target_pairs={{0,8},{1,9},{2,10},{3,11},{4,12},{5,13},{6,14},{7,15},{8,0},{9,1},... | collective-permute-start | bytes 331784 | tf_op jit(solution)/shard_map/ppermute | solution.py:177
  13.7 1.6 %collective-permute-done.2.refs_1_ = bf16[3,48,384]{2,1,0:T(8,128)(2,1)S(1)} collective-permute-done((bf16[3,48,384]{2,1,0:T(8,128)(2,1)S(1)}, bf16[3,48,384]{2,1,0:T(8,128)(2,1)S(1)}, u32[]{:S(2)}, u32[]{:S(2)}) %collective-permute-start.2) | collective-permute-done | bytes 110624 | tf_op jit(solution)/shard_map/ppermute | solution.py:177
  15.3 2.6 %collective-permute-done.3.refs_2_ = bf16[3,48,384]{2,1,0:T(8,128)(2,1)S(1)} collective-permute-done((bf16[3,48,384]{2,1,0:T(8,128)(2,1)S(1)}, bf16[3,48,384]{2,1,0:T(8,128)(2,1)S(1)}, u32[]{:S(2)}, u32[]{:S(2)}) %collective-permute-start.3) | collective-permute-done | bytes 110624 | tf_op jit(solution)/shard_map/ppermute | solution.py:177
  18.3 3.2 %collective-permute-start.6 = (bf16[3,48,384]{2,1,0:T(8,128)(2,1)S(1)}, bf16[3,48,384]{2,1,0:T(8,128)(2,1)S(1)}, u32[]{:S(2)}, u32[]{:S(2)}) collective-permute-start(bf16[3,48,384]{2,1,0:T(8,128)(2,1)S(1)} %collective-permute-done.refs_4_), channel_id=1, source_target_pairs={{0,8},{1,9},{2,10},{3,11},{4,12},{5,13},{6,14},{7,15},{8,0},{9,1},... | collective-permute-start | bytes 331784 | tf_op jit(solution)/shard_map/ppermute | solution.py:177
  22.7 2.2 %collective-permute-done.6.refs_6_ = bf16[3,48,384]{2,1,0:T(8,128)(2,1)S(1)} collective-permute-done((bf16[3,48,384]{2,1,0:T(8,128)(2,1)S(1)}, bf16[3,48,384]{2,1,0:T(8,128)(2,1)S(1)}, u32[]{:S(2)}, u32[]{:S(2)}) %collective-permute-start.6) | collective-permute-done | bytes 110624 | tf_op jit(solution)/shard_map/ppermute | solution.py:177
  25.0 1.7 %collective-permute-start.7 = (bf16[3,48,384]{2,1,0:T(8,128)(2,1)S(1)}, bf16[3,48,384]{2,1,0:T(8,128)(2,1)S(1)}, u32[]{:S(2)}, u32[]{:S(2)}) collective-permute-start(bf16[3,48,384]{2,1,0:T(8,128)(2,1)S(1)} %collective-permute-done.6.refs_6_), channel_id=1, source_target_pairs={{0,4},{1,5},{2,6},{3,7},{4,0},{5,1},{6,2},{7,3},{8,12},{9,13},{10,... | collective-permute-start | bytes 331784 | tf_op jit(solution)/shard_map/ppermute | solution.py:177
  27.4 2.3 %collective-permute-done.7.refs_7_ = bf16[3,48,384]{2,1,0:T(8,128)(2,1)S(1)} collective-permute-done((bf16[3,48,384]{2,1,0:T(8,128)(2,1)S(1)}, bf16[3,48,384]{2,1,0:T(8,128)(2,1)S(1)}, u32[]{:S(2)}, u32[]{:S(2)}) %collective-permute-start.7) | collective-permute-done | bytes 110624 | tf_op jit(solution)/shard_map/ppermute | solution.py:177
  30.5 3.7 %shard_map.96.before = f32[3,384,384]{2,1,0:T(8,128)S(1)} custom-call(s32[3]{0:T(128)S(1)} %pad_add_fusion.place, bf16[2,192,1024]{2,1,0:T(8,128)(2,1)S(1)} %pad_maximum_fusion.mine, bf16[2,192,1024]{2,1,0:T(8,128)(2,1)S(1)} %collective-permute-done.9.other, bf16[3,384,384]{2,1,0:T(8,128)(2,1)S(1)} %shard_map.95.weights), custom_call_target="tpu_custom_call" | custom-call | flops 1811939328 | bytes 6684684 | tf_op jit(solution)/shard_map/pallas_call | solution.py:154
  34.2 3.8 %shard_map.97 = (f32[3,96,384]{2,1,0:T(8,128)S(1)}, bf16[3,96,384]{2,1,0:T(8,128)(2,1)S(1)}, bf16[3,96,384]{2,1,0:T(8,128)(2,1)S(1)}, bf16[3,96,384]{2,1,0:T(8,128)(2,1)S(1)}) custom-call(s32[3]{0:T(128)S(1)} %pad_add_fusion.place, bf16[2,192,1024]{2,1,0:T(8,128)(2,1)S(1)} %collective-permute-done.1.mine, ...), custom_call_target="tpu_custom_call" | custom-call | flops 1811939328 | bytes 8454156 | tf_op jit(solution)/shard_map/pallas_call | solution.py:154
  38.0 1.8 %collective-permute-start.10 = (bf16[3,96,384]{2,1,0:T(8,128)(2,1)S(1)}, bf16[3,96,384]{2,1,0:T(8,128)(2,1)S(1)}, u32[]{:S(2)}, u32[]{:S(2)}) collective-permute-start(bf16[3,96,384]{2,1,0:T(8,128)(2,1)S(1)} %get-tuple-element.51), channel_id=1, source_target_pairs={{0,4},{1,5},{2,6},{3,7},{4,0},{5,1},{6,2},{7,3},{8,12},{9,13},{10,... | collective-permute-start | bytes 663560 | tf_op jit(solution)/shard_map/ppermute | solution.py:177
  39.8 1.8 %collective-permute-start.11 = (bf16[3,96,384]{2,1,0:T(8,128)(2,1)S(1)}, bf16[3,96,384]{2,1,0:T(8,128)(2,1)S(1)}, u32[]{:S(2)}, u32[]{:S(2)}) collective-permute-start(bf16[3,96,384]{2,1,0:T(8,128)(2,1)S(1)} %get-tuple-element.52), channel_id=1, source_target_pairs={{0,8},{1,9},{2,10},{3,11},{4,12},{5,13},{6,14},{7,15},{8,0},{9,1},... | collective-permute-start | bytes 663560 | tf_op jit(solution)/shard_map/ppermute | solution.py:177
  41.6 1.4 %collective-permute-start.12 = (bf16[3,96,384]{2,1,0:T(8,128)(2,1)S(1)}, bf16[3,96,384]{2,1,0:T(8,128)(2,1)S(1)}, u32[]{:S(2)}, u32[]{:S(2)}) collective-permute-start(bf16[3,96,384]{2,1,0:T(8,128)(2,1)S(1)} %get-tuple-element.53), channel_id=1, source_target_pairs={{0,12},{1,13},{2,14},{3,15},{4,8},{5,9},{6,10},{7,11},{8,4},{9,5},... | collective-permute-start | bytes 663560 | tf_op jit(solution)/shard_map/ppermute | solution.py:177
  44.8 3.7 %collective-permute-done.14.refs_10_ = bf16[2,192,128]{2,1,0:T(8,128)(2,1)S(1)} collective-permute-done((bf16[2,192,128]{2,1,0:T(8,128)(2,1)S(1)}, bf16[2,192,128]{2,1,0:T(8,128)(2,1)S(1)}, u32[]{:S(2)}, u32[]{:S(2)}) %collective-permute-start.14) | collective-permute-done | bytes 98336 | tf_op jit(solution)/shard_map/ppermute | solution.py:177
  48.6 1.3 %collective-permute-done.15.refs_11_ = bf16[2,192,128]{2,1,0:T(8,128)(2,1)S(1)} collective-permute-done((bf16[2,192,128]{2,1,0:T(8,128)(2,1)S(1)}, bf16[2,192,128]{2,1,0:T(8,128)(2,1)S(1)}, u32[]{:S(2)}, u32[]{:S(2)}) %collective-permute-start.15) | collective-permute-done | bytes 98336 | tf_op jit(solution)/shard_map/ppermute | solution.py:177
  50.6 7.9 %collective-permute-done.11.refs_1_ = bf16[3,96,384]{2,1,0:T(8,128)(2,1)S(1)} collective-permute-done((bf16[3,96,384]{2,1,0:T(8,128)(2,1)S(1)}, bf16[3,96,384]{2,1,0:T(8,128)(2,1)S(1)}, u32[]{:S(2)}, u32[]{:S(2)}) %collective-permute-start.11) | collective-permute-done | bytes 221216 | tf_op jit(solution)/shard_map/ppermute | solution.py:177
  59.4 4.6 %collective-permute-start.16 = (bf16[3,96,384]{2,1,0:T(8,128)(2,1)S(1)}, bf16[3,96,384]{2,1,0:T(8,128)(2,1)S(1)}, u32[]{:S(2)}, u32[]{:S(2)}) collective-permute-start(bf16[3,96,384]{2,1,0:T(8,128)(2,1)S(1)} %get-tuple-element.58.refs_0_), channel_id=1, source_target_pairs={{0,4},{1,5},{2,6},{3,7},{4,0},{5,1},{6,2},{7,3},{8,12},{9,13},{10,... | collective-permute-start | bytes 663560 | tf_op jit(solution)/shard_map/ppermute | solution.py:177
  64.0 1.8 %collective-permute-start.17 = (bf16[3,96,384]{2,1,0:T(8,128)(2,1)S(1)}, bf16[3,96,384]{2,1,0:T(8,128)(2,1)S(1)}, u32[]{:S(2)}, u32[]{:S(2)}) collective-permute-start(bf16[3,96,384]{2,1,0:T(8,128)(2,1)S(1)} %get-tuple-element.58.refs_0_), channel_id=1, source_target_pairs={{0,8},{1,9},{2,10},{3,11},{4,12},{5,13},{6,14},{7,15},{8,0},{9,1},... | collective-permute-start | bytes 663560 | tf_op jit(solution)/shard_map/ppermute | solution.py:177
  65.7 1.2 %collective-permute-done.18 = f32[96,128]{1,0:T(8,128)S(1)} collective-permute-done((f32[96,128]{1,0:T(8,128)S(1)}, f32[96,128]{1,0:T(8,128)S(1)}, u32[]{:S(2)}, u32[]{:S(2)}) %collective-permute-start.18) | collective-permute-done | bytes 49184 | tf_op jit(solution)/shard_map/ppermute | solution.py:177
  67.6 3.6 %collective-permute-done.19 = f32[96,128]{1,0:T(8,128)S(1)} collective-permute-done((f32[96,128]{1,0:T(8,128)S(1)}, f32[96,128]{1,0:T(8,128)S(1)}, u32[]{:S(2)}, u32[]{:S(2)}) %collective-permute-start.19) | collective-permute-done | bytes 49184 | tf_op jit(solution)/shard_map/ppermute | solution.py:177
  71.1 2.5 %collective-permute-done.16.refs_1_ = bf16[3,96,384]{2,1,0:T(8,128)(2,1)S(1)} collective-permute-done((bf16[3,96,384]{2,1,0:T(8,128)(2,1)S(1)}, bf16[3,96,384]{2,1,0:T(8,128)(2,1)S(1)}, u32[]{:S(2)}, u32[]{:S(2)}) %collective-permute-start.16) | collective-permute-done | bytes 221216 | tf_op jit(solution)/shard_map/ppermute | solution.py:177
  73.7 3.4 %collective-permute-start.20 = (bf16[3,96,384]{2,1,0:T(8,128)(2,1)S(1)}, bf16[3,96,384]{2,1,0:T(8,128)(2,1)S(1)}, u32[]{:S(2)}, u32[]{:S(2)}) collective-permute-start(bf16[3,96,384]{2,1,0:T(8,128)(2,1)S(1)} %collective-permute-done.17.refs_2_), channel_id=1, source_target_pairs={{0,4},{1,5},{2,6},{3,7},{4,0},{5,1},{6,2},{7,3},{8,12},{9,13},{10,... | collective-permute-start | bytes 663560 | tf_op jit(solution)/shard_map/ppermute | solution.py:177
  77.1 2.7 %collective-permute-start.22 = (f32[96,128]{1,0:T(8,128)S(1)}, f32[96,128]{1,0:T(8,128)S(1)}, u32[]{:S(2)}, u32[]{:S(2)}) collective-permute-start(f32[96,128]{1,0:T(8,128)S(1)} %add.21.refs_4_), channel_id=1, source_target_pairs={{0,8},{1,9},{2,10},{3,11},{4,12},{5,13},{6,14},{7,15},{8,0},{9,1},... | collective-permute-start | bytes 147464 | tf_op jit(solution)/shard_map/ppermute | solution.py:177
  79.8 1.7 %collective-permute-start.23 = (f32[96,128]{1,0:T(8,128)S(1)}, f32[96,128]{1,0:T(8,128)S(1)}, u32[]{:S(2)}, u32[]{:S(2)}) collective-permute-start(f32[96,128]{1,0:T(8,128)S(1)} %add.21.refs_4_), channel_id=1, source_target_pairs={{0,12},{1,13},{2,14},{3,15},{4,8},{5,9},{6,10},{7,11},{8,4},{9,5},... | collective-permute-start | bytes 147464 | tf_op jit(solution)/shard_map/ppermute | solution.py:177
  81.5 1.8 %collective-permute-done.21.refs_5_ = f32[96,128]{1,0:T(8,128)S(1)} collective-permute-done((f32[96,128]{1,0:T(8,128)S(1)}, f32[96,128]{1,0:T(8,128)S(1)}, u32[]{:S(2)}, u32[]{:S(2)}) %collective-permute-start.21) | collective-permute-done | bytes 49184 | tf_op jit(solution)/shard_map/ppermute | solution.py:177
  83.3 3.3 %collective-permute-done.23.refs_7_ = f32[96,128]{1,0:T(8,128)S(1)} collective-permute-done((f32[96,128]{1,0:T(8,128)S(1)}, f32[96,128]{1,0:T(8,128)S(1)}, u32[]{:S(2)}, u32[]{:S(2)}) %collective-permute-start.23) | collective-permute-done | bytes 49184 | tf_op jit(solution)/shard_map/ppermute | solution.py:177
  86.6 2.3 %shard_map.99 = (f32[2,192,128]{2,1,0:T(8,128)S(1)}, bf16[2,192,128]{2,1,0:T(8,128)(2,1)S(1)}, bf16[2,192,128]{2,1,0:T(8,128)(2,1)S(1)}, bf16[2,192,128]{2,1,0:T(8,128)(2,1)S(1)}) custom-call(s32[3]{0:T(128)S(1)} %pad_add_fusion.place, bf16[3,384,384]{2,1,0:T(8,128)(2,1)S(1)} %shard_map.95.weights, bf16[3,96,384]{2,1,0:T(8,128)(2,1)S(1)} %get-tuple-element.58.refs_0_, ...), custom_call_target="tpu_custom_call" | custom-call | flops 452984832 | bytes 5308428 | tf_op jit(solution)/shard_map/pallas_call | solution.py:154
  89.6 1.2 %collective-permute-start.26 = (bf16[2,192,128]{2,1,0:T(8,128)(2,1)S(1)}, bf16[2,192,128]{2,1,0:T(8,128)(2,1)S(1)}, u32[]{:S(2)}, u32[]{:S(2)}) collective-permute-start(bf16[2,192,128]{2,1,0:T(8,128)(2,1)S(1)} %get-tuple-element.69), channel_id=1, source_target_pairs={{0,3},{1,2},{2,1},{3,0},{4,7},{5,6},{6,5},{7,4},{8,11},{9,10},{10,... | collective-permute-start | bytes 294920 | tf_op jit(solution)/shard_map/ppermute | solution.py:177
  90.9 3.8 %collective-permute-done.25.second = bf16[2,192,128]{2,1,0:T(8,128)(2,1)S(1)} collective-permute-done((bf16[2,192,128]{2,1,0:T(8,128)(2,1)S(1)}, bf16[2,192,128]{2,1,0:T(8,128)(2,1)S(1)}, u32[]{:S(2)}, u32[]{:S(2)}) %collective-permute-start.25) | collective-permute-done | bytes 98336 | tf_op jit(solution)/shard_map/ppermute | solution.py:177
  (42 shorter events, 11.8 us)
Async XLA Ops:
  0.6 5.2 %copy-start = (bf16[1024,192]{0,1:T(8,128)(2,1)S(1)}, bf16[1024,192]{0,1:T(8,128)(2,1)}, u32[]{:S(2)}) copy-start(bf16[1024,192]{0,1:T(8,128)(2,1)} %param.8) | copy-start | bytes 1179652
  1.7 6.1 %collective-permute-start = (bf16[3,48,384]{2,1,0:T(8,128)(2,1)S(1)}, bf16[3,48,384]{2,1,0:T(8,128)(2,1)S(1)}, u32[]{:S(2)}, u32[]{:S(2)}) collective-permute-start(bf16[3,48,384]{2,1,0:T(8,128)(2,1)S(1)} %get-tuple-element.73), channel_id=1, source_target_pairs={{0,2},{1,3},{2,0},{3,1},{4,6},{5,7},{6,4},{7,5},{8,10},{9,11},{10,... | collective-permute-start | bytes 331784 | tf_op jit(solution)/shard_map/ppermute | solution.py:177
  5.8 24.6 %copy-start.1 = (bf16[128,192]{0,1:T(8,128)(2,1)S(1)}, bf16[128,192]{0,1:T(8,128)(2,1)}, u32[]{:S(2)}) copy-start(bf16[128,192]{0,1:T(8,128)(2,1)} %param.15) | copy-start | bytes 147460
  5.8 24.6 %copy-start.2 = (bf16[128,192]{0,1:T(8,128)(2,1)S(1)}, bf16[128,192]{0,1:T(8,128)(2,1)}, u32[]{:S(2)}) copy-start(bf16[128,192]{0,1:T(8,128)(2,1)} %param.14) | copy-start | bytes 147460
  7.8 22.5 %collective-permute-start.1 = (bf16[2,192,1024]{2,1,0:T(8,128)(2,1)S(1)}, bf16[2,192,1024]{2,1,0:T(8,128)(2,1)S(1)}, u32[]{:S(2)}, u32[]{:S(2)}) collective-permute-start(bf16[2,192,1024]{2,1,0:T(8,128)(2,1)S(1)} %pad_maximum_fusion.mine), channel_id=1, source_target_pairs={{0,2},{1,3},{2,0},{3,1},{4,6},{5,7},{6,4},{7,5},{8,10},{9,11},{10,... | collective-permute-start | bytes 2359304 | tf_op jit(solution)/shard_map/ppermute | solution.py:177
  9.5 5.8 %collective-permute-start.2 = (bf16[3,48,384]{2,1,0:T(8,128)(2,1)S(1)}, bf16[3,48,384]{2,1,0:T(8,128)(2,1)S(1)}, u32[]{:S(2)}, u32[]{:S(2)}) collective-permute-start(bf16[3,48,384]{2,1,0:T(8,128)(2,1)S(1)} %get-tuple-element.72.refs_0_), channel_id=1, source_target_pairs={{0,4},{1,5},{2,6},{3,7},{4,0},{5,1},{6,2},{7,3},{8,12},{9,13},{10,... | collective-permute-start | bytes 331784 | tf_op jit(solution)/shard_map/ppermute | solution.py:177
  11.1 6.8 %collective-permute-start.3 = (bf16[3,48,384]{2,1,0:T(8,128)(2,1)S(1)}, bf16[3,48,384]{2,1,0:T(8,128)(2,1)S(1)}, u32[]{:S(2)}, u32[]{:S(2)}) collective-permute-start(bf16[3,48,384]{2,1,0:T(8,128)(2,1)S(1)} %get-tuple-element.72.refs_0_), channel_id=1, source_target_pairs={{0,8},{1,9},{2,10},{3,11},{4,12},{5,13},{6,14},{7,15},{8,0},{9,1},... | collective-permute-start | bytes 331784 | tf_op jit(solution)/shard_map/ppermute | solution.py:177
  18.0 4.7 %collective-permute-start.5 = (bf16[3,48,384]{2,1,0:T(8,128)(2,1)S(1)}, bf16[3,48,384]{2,1,0:T(8,128)(2,1)S(1)}, u32[]{:S(2)}, u32[]{:S(2)}) collective-permute-start(bf16[3,48,384]{2,1,0:T(8,128)(2,1)S(1)} %collective-permute-done.refs_4_), channel_id=1, source_target_pairs={{0,4},{1,5},{2,6},{3,7},{4,0},{5,1},{6,2},{7,3},{8,12},{9,13},{10,... | collective-permute-start | bytes 331784 | tf_op jit(solution)/shard_map/ppermute | solution.py:177
  18.3 6.7 %collective-permute-start.6 = (bf16[3,48,384]{2,1,0:T(8,128)(2,1)S(1)}, bf16[3,48,384]{2,1,0:T(8,128)(2,1)S(1)}, u32[]{:S(2)}, u32[]{:S(2)}) collective-permute-start(bf16[3,48,384]{2,1,0:T(8,128)(2,1)S(1)} %collective-permute-done.refs_4_), channel_id=1, source_target_pairs={{0,8},{1,9},{2,10},{3,11},{4,12},{5,13},{6,14},{7,15},{8,0},{9,1},... | collective-permute-start | bytes 331784 | tf_op jit(solution)/shard_map/ppermute | solution.py:177
  21.5 9.0 %collective-permute-start.9 = (bf16[2,192,1024]{2,1,0:T(8,128)(2,1)S(1)}, bf16[2,192,1024]{2,1,0:T(8,128)(2,1)S(1)}, u32[]{:S(2)}, u32[]{:S(2)}) collective-permute-start(bf16[2,192,1024]{2,1,0:T(8,128)(2,1)S(1)} %pad_maximum_fusion.mine), channel_id=1, source_target_pairs={{0,1},{1,0},{2,3},{3,2},{4,5},{5,4},{6,7},{7,6},{8,9},{9,8},{10,11... | collective-permute-start | bytes 2359304 | tf_op jit(solution)/shard_map/ppermute | solution.py:177
  21.5 5.9 %collective-permute-start.4 = (bf16[3,48,384]{2,1,0:T(8,128)(2,1)S(1)}, bf16[3,48,384]{2,1,0:T(8,128)(2,1)S(1)}, u32[]{:S(2)}, u32[]{:S(2)}) collective-permute-start(bf16[3,48,384]{2,1,0:T(8,128)(2,1)S(1)} %collective-permute-done.3.refs_2_), channel_id=1, source_target_pairs={{0,4},{1,5},{2,6},{3,7},{4,0},{5,1},{6,2},{7,3},{8,12},{9,13},{10,... | collective-permute-start | bytes 331784 | tf_op jit(solution)/shard_map/ppermute | solution.py:177
  25.0 4.7 %collective-permute-start.7 = (bf16[3,48,384]{2,1,0:T(8,128)(2,1)S(1)}, bf16[3,48,384]{2,1,0:T(8,128)(2,1)S(1)}, u32[]{:S(2)}, u32[]{:S(2)}) collective-permute-start(bf16[3,48,384]{2,1,0:T(8,128)(2,1)S(1)} %collective-permute-done.6.refs_6_), channel_id=1, source_target_pairs={{0,4},{1,5},{2,6},{3,7},{4,0},{5,1},{6,2},{7,3},{8,12},{9,13},{10,... | collective-permute-start | bytes 331784 | tf_op jit(solution)/shard_map/ppermute | solution.py:177
  30.3 3.8 %collective-permute-start.8 = (bf16[2,192,1024]{2,1,0:T(8,128)(2,1)S(1)}, bf16[2,192,1024]{2,1,0:T(8,128)(2,1)S(1)}, u32[]{:S(2)}, u32[]{:S(2)}) collective-permute-start(bf16[2,192,1024]{2,1,0:T(8,128)(2,1)S(1)} %collective-permute-done.1.mine), channel_id=1, source_target_pairs={{0,1},{1,0},{2,3},{3,2},{4,5},{5,4},{6,7},{7,6},{8,9},{9,8},{10,11... | collective-permute-start | bytes 2359304 | tf_op jit(solution)/shard_map/ppermute | solution.py:177
  38.0 12.5 %collective-permute-start.10 = (bf16[3,96,384]{2,1,0:T(8,128)(2,1)S(1)}, bf16[3,96,384]{2,1,0:T(8,128)(2,1)S(1)}, u32[]{:S(2)}, u32[]{:S(2)}) collective-permute-start(bf16[3,96,384]{2,1,0:T(8,128)(2,1)S(1)} %get-tuple-element.51), channel_id=1, source_target_pairs={{0,4},{1,5},{2,6},{3,7},{4,0},{5,1},{6,2},{7,3},{8,12},{9,13},{10,... | collective-permute-start | bytes 663560 | tf_op jit(solution)/shard_map/ppermute | solution.py:177
  39.8 18.7 %collective-permute-start.11 = (bf16[3,96,384]{2,1,0:T(8,128)(2,1)S(1)}, bf16[3,96,384]{2,1,0:T(8,128)(2,1)S(1)}, u32[]{:S(2)}, u32[]{:S(2)}) collective-permute-start(bf16[3,96,384]{2,1,0:T(8,128)(2,1)S(1)} %get-tuple-element.52), channel_id=1, source_target_pairs={{0,8},{1,9},{2,10},{3,11},{4,12},{5,13},{6,14},{7,15},{8,0},{9,1},... | collective-permute-start | bytes 663560 | tf_op jit(solution)/shard_map/ppermute | solution.py:177
  41.6 16.9 %collective-permute-start.12 = (bf16[3,96,384]{2,1,0:T(8,128)(2,1)S(1)}, bf16[3,96,384]{2,1,0:T(8,128)(2,1)S(1)}, u32[]{:S(2)}, u32[]{:S(2)}) collective-permute-start(bf16[3,96,384]{2,1,0:T(8,128)(2,1)S(1)} %get-tuple-element.53), channel_id=1, source_target_pairs={{0,12},{1,13},{2,14},{3,15},{4,8},{5,9},{6,10},{7,11},{8,4},{9,5},... | collective-permute-start | bytes 663560 | tf_op jit(solution)/shard_map/ppermute | solution.py:177
  43.0 1.3 %collective-permute-start.13 = (bf16[2,192,128]{2,1,0:T(8,128)(2,1)S(1)}, bf16[2,192,128]{2,1,0:T(8,128)(2,1)S(1)}, u32[]{:S(2)}, u32[]{:S(2)}) collective-permute-start(bf16[2,192,128]{2,1,0:T(8,128)(2,1)S(1)} %pad_maximum_fusion.2.refs_8_), channel_id=1, source_target_pairs={{0,1},{1,0},{2,3},{3,2},{4,5},{5,4},{6,7},{7,6},{8,9},{9,8},{10,11... | collective-permute-start | bytes 294920 | tf_op jit(solution)/shard_map/ppermute | solution.py:177
  43.0 5.6 %collective-permute-start.14 = (bf16[2,192,128]{2,1,0:T(8,128)(2,1)S(1)}, bf16[2,192,128]{2,1,0:T(8,128)(2,1)S(1)}, u32[]{:S(2)}, u32[]{:S(2)}) collective-permute-start(bf16[2,192,128]{2,1,0:T(8,128)(2,1)S(1)} %pad_maximum_fusion.2.refs_8_), channel_id=1, source_target_pairs={{0,2},{1,3},{2,0},{3,1},{4,6},{5,7},{6,4},{7,5},{8,10},{9,11},{10,... | collective-permute-start | bytes 294920 | tf_op jit(solution)/shard_map/ppermute | solution.py:177
  44.3 5.6 %collective-permute-start.15 = (bf16[2,192,128]{2,1,0:T(8,128)(2,1)S(1)}, bf16[2,192,128]{2,1,0:T(8,128)(2,1)S(1)}, u32[]{:S(2)}, u32[]{:S(2)}) collective-permute-start(bf16[2,192,128]{2,1,0:T(8,128)(2,1)S(1)} %pad_maximum_fusion.2.refs_8_), channel_id=1, source_target_pairs={{0,3},{1,2},{2,1},{3,0},{4,7},{5,6},{6,5},{7,4},{8,11},{9,10},{10,... | collective-permute-start | bytes 294920 | tf_op jit(solution)/shard_map/ppermute | solution.py:177
  59.4 14.3 %collective-permute-start.16 = (bf16[3,96,384]{2,1,0:T(8,128)(2,1)S(1)}, bf16[3,96,384]{2,1,0:T(8,128)(2,1)S(1)}, u32[]{:S(2)}, u32[]{:S(2)}) collective-permute-start(bf16[3,96,384]{2,1,0:T(8,128)(2,1)S(1)} %get-tuple-element.58.refs_0_), channel_id=1, source_target_pairs={{0,4},{1,5},{2,6},{3,7},{4,0},{5,1},{6,2},{7,3},{8,12},{9,13},{10,... | collective-permute-start | bytes 663560 | tf_op jit(solution)/shard_map/ppermute | solution.py:177
  64.0 9.7 %collective-permute-start.17 = (bf16[3,96,384]{2,1,0:T(8,128)(2,1)S(1)}, bf16[3,96,384]{2,1,0:T(8,128)(2,1)S(1)}, u32[]{:S(2)}, u32[]{:S(2)}) collective-permute-start(bf16[3,96,384]{2,1,0:T(8,128)(2,1)S(1)} %get-tuple-element.58.refs_0_), channel_id=1, source_target_pairs={{0,8},{1,9},{2,10},{3,11},{4,12},{5,13},{6,14},{7,15},{8,0},{9,1},... | collective-permute-start | bytes 663560 | tf_op jit(solution)/shard_map/ppermute | solution.py:177
  65.7 1.2 %collective-permute-start.18 = (f32[96,128]{1,0:T(8,128)S(1)}, f32[96,128]{1,0:T(8,128)S(1)}, u32[]{:S(2)}, u32[]{:S(2)}) collective-permute-start(f32[96,128]{1,0:T(8,128)S(1)} %get-tuple-element.59), channel_id=1, source_target_pairs={{0,1},{1,0},{2,3},{3,2},{4,5},{5,4},{6,7},{7,6},{8,9},{9,8},{10,11... | collective-permute-start | bytes 147464 | tf_op jit(solution)/shard_map/ppermute | solution.py:177
  67.0 4.2 %collective-permute-start.19 = (f32[96,128]{1,0:T(8,128)S(1)}, f32[96,128]{1,0:T(8,128)S(1)}, u32[]{:S(2)}, u32[]{:S(2)}) collective-permute-start(f32[96,128]{1,0:T(8,128)S(1)} %add.20), channel_id=1, source_target_pairs={{0,2},{1,3},{2,0},{3,1},{4,6},{5,7},{6,4},{7,5},{8,10},{9,11},{10,... | collective-permute-start | bytes 147464 | tf_op jit(solution)/shard_map/ppermute | solution.py:177
  73.7 12.9 %collective-permute-start.20 = (bf16[3,96,384]{2,1,0:T(8,128)(2,1)S(1)}, bf16[3,96,384]{2,1,0:T(8,128)(2,1)S(1)}, u32[]{:S(2)}, u32[]{:S(2)}) collective-permute-start(bf16[3,96,384]{2,1,0:T(8,128)(2,1)S(1)} %collective-permute-done.17.refs_2_), channel_id=1, source_target_pairs={{0,4},{1,5},{2,6},{3,7},{4,0},{5,1},{6,2},{7,3},{8,12},{9,13},{10,... | collective-permute-start | bytes 663560 | tf_op jit(solution)/shard_map/ppermute | solution.py:177
  77.1 6.2 %collective-permute-start.21 = (f32[96,128]{1,0:T(8,128)S(1)}, f32[96,128]{1,0:T(8,128)S(1)}, u32[]{:S(2)}, u32[]{:S(2)}) collective-permute-start(f32[96,128]{1,0:T(8,128)S(1)} %add.21.refs_4_), channel_id=1, source_target_pairs={{0,4},{1,5},{2,6},{3,7},{4,0},{5,1},{6,2},{7,3},{8,12},{9,13},{10,... | collective-permute-start | bytes 147464 | tf_op jit(solution)/shard_map/ppermute | solution.py:177
  77.1 6.1 %collective-permute-start.22 = (f32[96,128]{1,0:T(8,128)S(1)}, f32[96,128]{1,0:T(8,128)S(1)}, u32[]{:S(2)}, u32[]{:S(2)}) collective-permute-start(f32[96,128]{1,0:T(8,128)S(1)} %add.21.refs_4_), channel_id=1, source_target_pairs={{0,8},{1,9},{2,10},{3,11},{4,12},{5,13},{6,14},{7,15},{8,0},{9,1},... | collective-permute-start | bytes 147464 | tf_op jit(solution)/shard_map/ppermute | solution.py:177
  79.8 6.8 %collective-permute-start.23 = (f32[96,128]{1,0:T(8,128)S(1)}, f32[96,128]{1,0:T(8,128)S(1)}, u32[]{:S(2)}, u32[]{:S(2)}) collective-permute-start(f32[96,128]{1,0:T(8,128)S(1)} %add.21.refs_4_), channel_id=1, source_target_pairs={{0,12},{1,13},{2,14},{3,15},{4,8},{5,9},{6,10},{7,11},{8,4},{9,5},... | collective-permute-start | bytes 147464 | tf_op jit(solution)/shard_map/ppermute | solution.py:177
  88.9 1.9 %collective-permute-start.24 = (bf16[2,192,128]{2,1,0:T(8,128)(2,1)S(1)}, bf16[2,192,128]{2,1,0:T(8,128)(2,1)S(1)}, u32[]{:S(2)}, u32[]{:S(2)}) collective-permute-start(bf16[2,192,128]{2,1,0:T(8,128)(2,1)S(1)} %get-tuple-element.67), channel_id=1, source_target_pairs={{0,1},{1,0},{2,3},{3,2},{4,5},{5,4},{6,7},{7,6},{8,9},{9,8},{10,11... | collective-permute-start | bytes 294920 | tf_op jit(solution)/shard_map/ppermute | solution.py:177
  89.0 5.7 %collective-permute-start.25 = (bf16[2,192,128]{2,1,0:T(8,128)(2,1)S(1)}, bf16[2,192,128]{2,1,0:T(8,128)(2,1)S(1)}, u32[]{:S(2)}, u32[]{:S(2)}) collective-permute-start(bf16[2,192,128]{2,1,0:T(8,128)(2,1)S(1)} %get-tuple-element.68), channel_id=1, source_target_pairs={{0,2},{1,3},{2,0},{3,1},{4,6},{5,7},{6,4},{7,5},{8,10},{9,11},{10,... | collective-permute-start | bytes 294920 | tf_op jit(solution)/shard_map/ppermute | solution.py:177
  89.6 6.2 %collective-permute-start.26 = (bf16[2,192,128]{2,1,0:T(8,128)(2,1)S(1)}, bf16[2,192,128]{2,1,0:T(8,128)(2,1)S(1)}, u32[]{:S(2)}, u32[]{:S(2)}) collective-permute-start(bf16[2,192,128]{2,1,0:T(8,128)(2,1)S(1)} %get-tuple-element.69), channel_id=1, source_target_pairs={{0,3},{1,2},{2,1},{3,0},{4,7},{5,6},{6,5},{7,4},{8,11},{9,10},{10,... | collective-permute-start | bytes 294920 | tf_op jit(solution)/shard_map/ppermute | solution.py:177

commit v3 on v2

--- a/solution.py
+++ b/solution.py
@@ -98,19 +98,15 @@
 
 
 def query_kernel(groups, hidden, place, weights, *refs):
-    grads, stats, quests, refs = (
-        refs[:groups],
-        refs[groups : 2 * groups],
-        refs[2 * groups : 2 * groups + 4],
-        refs[2 * groups + 4 :],
-    )
+    grads, stats, refs = refs[:groups], refs[groups], refs[groups + 1 :]
+    quests, refs = refs[:4], refs[4:]
     own_out, sends, (renewed, query) = refs[0], refs[1:4], refs[4:]
     group, side, half = place[0], place[1], place[2]
     feats, count = quests[0].shape[1:]
 
     for flip in range(groups):
         where = rows_of(group ^ flip, grads[0].shape[1])
-        sums = stats[flip][...] * (1.0 / hidden)
+        sums = stats[flip] / hidden
         for index in range(3):
             wsq = sums[:, 3 * index : 3 * index + 1]
             cross = sums[:, 3 * index + 1 : 3 * index + 2]
@@ -176,15 +172,18 @@
         pairs = [(i, i ^ flip) for i in range(n_tok * n_hid)]
         return lax.ppermute(array, ("tok", "hid"), pairs)
 
-    def gather(block, beside=()):
-        bits = [1 << place for place in range(groups.bit_length() - 1)]
-        came = {bit: swap(block, zed * bit) for bit in reversed(bits)}
-        came, _ = lax.optimization_barrier((came, beside))
-        held = {0: block, **came}
-        for flip in range(groups):
-            if flip not in held:
-                low = flip & -flip
-                held[flip] = swap(held[flip ^ low], zed * low)
+    def gather(block, soon=(), late=()):
+        held, bit = {0: block}, groups // 2
+        while bit > 1:
+            held.update({flip | bit: swap(held[flip], zed * bit) for flip in list(held)})
+            bit //= 2
+        if soon:
+            block, _ = lax.optimization_barrier((block, soon))
+        near = swap(block, zed)
+        if late:
+            held, near, _ = lax.optimization_barrier((held, near, late))
+        held.update({flip | 1: swap(held[flip], zed) for flip in list(held) if flip})
+        held[1] = near
         return [held[flip] for flip in range(groups)]
 
     stacked = jnp.stack([gate_weight, up_weight, down_weight])
@@ -194,9 +193,8 @@
     vals = (input_lr[None, :] * input_values.T.astype(f32)).astype(bf16)
     tokens = jnp.stack([input_keys.T, vals])
     _, feats, toks = tokens.shape
-    tokens, pair_w = lax.optimization_barrier((tokens, swap(give_w, pair)))
     first = gather(own_w)
-    pair_w, _ = lax.optimization_barrier((pair_w, first[1]))
+    tokens, pair_w, _ = lax.optimization_barrier((tokens, swap(give_w, pair), first[1]))
     second = gather(pair_w)
     pair_tokens = swap(tokens, pair)
 
@@ -225,33 +223,44 @@
     shares = call(
         functools.partial(pair_kernel, groups),
         (pair_tokens, swap(pair_tokens, core), weights, grads),
-        [jax.ShapeDtypeStruct(block, bf16 if flip else f32) for flip in range(groups)],
+        [jax.ShapeDtypeStruct(block, bf16 if flip & 1 else f32) for flip in range(groups)],
         [pltpu.VMEM(whole, f32), joined],
         token_flops,
         place,
         16,
     )
-    quest = jnp.stack([queries.T, out_grad.T])
-    quest, shares = lax.optimization_barrier((quest, shares))
+    quest, shares = lax.optimization_barrier((jnp.stack([queries.T, out_grad.T]), shares))
     quests = [quest] + [swap(quest, flip) for flip in (1, 2, 3)]
-
-    arrived = [swap(shares[flip], zed * flip) for flip in range(1, groups)]
-    arrived, quests = lax.optimization_barrier((arrived, quests))
+    held, arrived, bit = dict(enumerate(shares)), [], 1
+    while bit < groups:
+        for flip in sorted((f for f in held if f & bit), reverse=True):
+            came = swap(held.pop(flip), zed * bit)
+            if flip == bit:
+                arrived.append(came)
+            else:
+                came, quests = lax.optimization_barrier((came, quests))
+                other = (held[flip ^ bit].astype(f32) + came.astype(f32)).astype(bf16)
+                held, held[flip ^ bit] = lax.optimization_barrier((held, other))
+        bit *= 2
     grad, stats = call(
         functools.partial(sum_kernel, len(arrived)),
-        (weights, shares[0], *arrived),
+        (weights, held[0], *arrived),
         (jax.ShapeDtypeStruct(block, bf16), jax.ShapeDtypeStruct((rows, 128), f32)),
         place=place,
     )
-    stats = stats + swap(stats, core)
+    stats = near_stats = stats + swap(stats, core)
     stats = stats + swap(stats, pair)
-    all_stats = [stats] + [swap(stats, zed * flip) for flip in range(1, groups)]
+    all_stats, bit = stats[None], groups // 2
+    while bit:
+        all_stats = jnp.stack([all_stats, swap(all_stats, zed * bit)], axis=1)
+        all_stats = all_stats.reshape(-1, *stats.shape)
+        bit //= 2
 
     count = queries.shape[0]
     piece = (2, feats, count)
     own_out, *sends = call(
         functools.partial(query_kernel, groups, 2 * n_hid * cols),
-        (weights, *gather(grad, stats), *all_stats, *quests),
+        (weights, *gather(grad, [near_stats], [stats]), all_stats, *quests),
         [jax.ShapeDtypeStruct(piece, f32)] + [jax.ShapeDtypeStruct(piece, bf16)] * 3,
         [pltpu.VMEM(whole, bf16), pltpu.VMEM((2, width, 2 * count), bf16)],
         6 * 2 * 2 * count * width * cols,

time: 96.7 us -> 91.4 us (0.945); the launches traced: 96.6 us -> 89.7 us
  starting transfers between devices: 37 us -> 32.3 us
  waiting for transfers between devices: 44.4 us -> 42.2 us
    ppermute x27 -> x26, starting transfers between devices: 37 us -> 32.3 us  [swap(): return lax.ppermute(array, ('tok', 'hid'), pairs)]
    ppermute x27 -> x26, waiting for transfers between devices: 44.4 us -> 42.2 us  [swap(): return lax.ppermute(array, ('tok', 'hid'), pairs)]
  transfers between devices with their start and end apart: 27 -> 26, of which waited for: 19 -> 17; matrix products, arithmetic and copies ran while one was open for 1% -> 1% of each run, Pallas kernels for 4% -> 5%
where the time goes in v3:
time: 91.4 us; the launch traced here: 89.7 us
  waiting for transfers between devices  42.2 us (46%)
  starting transfers between devices  32.3 us (35%)
  Pallas kernels  11.9 us (13%)
  other arithmetic  2.36 us (3%)
    ppermute x26, waiting for transfers between devices, swap(): return lax.ppermute(array, ('tok', 'hid'), pairs)  42.2 us
    ppermute x26, starting transfers between devices, swap(): return lax.ppermute(array, ('tok', 'hid'), pairs)  32.3 us
    pallas_call x6, Pallas kernels, call(): pl.pallas_call(body, out_shape=list(outs), in_specs=specs, out_specs=[pl....  11.9 us
  transfers between devices with their start and end apart: 26, of which 17 were waited for; matrix products, arithmetic and copies ran while one was open for 1% of the time, Pallas kernels for 5%

profile of v3, /device:TPU:0, one launch (start us, length us, event | category | flops | bytes accessed | tf_op | source)
XLA Modules:
  0.0 89.7 jit_solution(2629846015497758838)
XLA Ops:
  0.7 1.0 %pad_maximum_fusion.1 = bf16[3,48,768]{2,1,0:T(8,128)(2,1)S(1)} fusion(bf16[1,48,768]{2,1,0:T(8,128)(2,1)} %bitcast.35, bf16[1,48,768]{2,1,0:T(8,128)(2,1)} %bitcast.36, bf16[1,48,768]{2,1,0:T(8,128)(2,1)} %bitcast.37), kind=kLoop, calls=%fused_computation.4 | loop fusion | flops 221184 | bytes 442368 | tf_op jit(solution)/shard_map/stack | solution.py:189
  1.7 3.0 %collective-permute-start = (bf16[3,48,384]{2,1,0:T(8,128)(2,1)S(1)}, bf16[3,48,384]{2,1,0:T(8,128)(2,1)S(1)}, u32[]{:S(2)}, u32[]{:S(2)}) collective-permute-start(bf16[3,48,384]{2,1,0:T(8,128)(2,1)S(1)} %get-tuple-element.69), channel_id=1, source_target_pairs={{0,2},{1,3},{2,0},{3,1},{4,6},{5,7},{6,4},{7,5},{8,10},{9,11},{10,... | collective-permute-start | bytes 331784 | tf_op jit(solution)/shard_map/ppermute | solution.py:173
  4.7 1.6 %collective-permute-start.1 = (bf16[3,48,384]{2,1,0:T(8,128)(2,1)S(1)}, bf16[3,48,384]{2,1,0:T(8,128)(2,1)S(1)}, u32[]{:S(2)}, u32[]{:S(2)}) collective-permute-start(bf16[3,48,384]{2,1,0:T(8,128)(2,1)S(1)} %get-tuple-element.68.refs_0_), channel_id=1, source_target_pairs={{0,4},{1,5},{2,6},{3,7},{4,0},{5,1},{6,2},{7,3},{8,12},{9,13},{10,... | collective-permute-start | bytes 331784 | tf_op jit(solution)/shard_map/ppermute | solution.py:173
  6.3 1.1 %fusion = bf16[1,192,1024]{2,1,0:T(8,128)(2,1)S(1)} fusion(bf16[1024,192]{0,1:T(8,128)(2,1)} %param.9, f32[1024]{0:T(1024)} %param.10), kind=kLoop, calls=%fused_computation.3 | loop fusion | flops 589824 | bytes 790528 | tf_op jit(solution)/shard_map/stack | solution.py:194
  7.8 1.7 %collective-permute-done.1.refs_1_ = bf16[3,48,384]{2,1,0:T(8,128)(2,1)S(1)} collective-permute-done((bf16[3,48,384]{2,1,0:T(8,128)(2,1)S(1)}, bf16[3,48,384]{2,1,0:T(8,128)(2,1)S(1)}, u32[]{:S(2)}, u32[]{:S(2)}) %collective-permute-start.1) | collective-permute-done | bytes 110624 | tf_op jit(solution)/shard_map/ppermute | solution.py:173
  9.6 3.0 %collective-permute-start.3 = (bf16[3,48,384]{2,1,0:T(8,128)(2,1)S(1)}, bf16[3,48,384]{2,1,0:T(8,128)(2,1)S(1)}, u32[]{:S(2)}, u32[]{:S(2)}) collective-permute-start(bf16[3,48,384]{2,1,0:T(8,128)(2,1)S(1)} %get-tuple-element.68.refs_0_), channel_id=1, source_target_pairs={{0,8},{1,9},{2,10},{3,11},{4,12},{5,13},{6,14},{7,15},{8,0},{9,1},... | collective-permute-start | bytes 331784 | tf_op jit(solution)/shard_map/ppermute | solution.py:173
  12.7 1.9 %collective-permute-start.5 = (bf16[3,48,384]{2,1,0:T(8,128)(2,1)S(1)}, bf16[3,48,384]{2,1,0:T(8,128)(2,1)S(1)}, u32[]{:S(2)}, u32[]{:S(2)}) collective-permute-start(bf16[3,48,384]{2,1,0:T(8,128)(2,1)S(1)} %collective-permute-done.refs_4_), channel_id=1, source_target_pairs={{0,4},{1,5},{2,6},{3,7},{4,0},{5,1},{6,2},{7,3},{8,12},{9,13},{10,... | collective-permute-start | bytes 331784 | tf_op jit(solution)/shard_map/ppermute | solution.py:173
  14.5 5.4 %collective-permute-done.3.refs_2_ = bf16[3,48,384]{2,1,0:T(8,128)(2,1)S(1)} collective-permute-done((bf16[3,48,384]{2,1,0:T(8,128)(2,1)S(1)}, bf16[3,48,384]{2,1,0:T(8,128)(2,1)S(1)}, u32[]{:S(2)}, u32[]{:S(2)}) %collective-permute-start.3) | collective-permute-done | bytes 110624 | tf_op jit(solution)/shard_map/ppermute | solution.py:173
  19.9 1.5 %collective-permute-done.6.refs_6_ = bf16[3,48,384]{2,1,0:T(8,128)(2,1)S(1)} collective-permute-done((bf16[3,48,384]{2,1,0:T(8,128)(2,1)S(1)}, bf16[3,48,384]{2,1,0:T(8,128)(2,1)S(1)}, u32[]{:S(2)}, u32[]{:S(2)}) %collective-permute-start.6) | collective-permute-done | bytes 110624 | tf_op jit(solution)/shard_map/ppermute | solution.py:173
  22.2 3.1 %collective-permute-done.4.refs_3_ = bf16[3,48,384]{2,1,0:T(8,128)(2,1)S(1)} collective-permute-done((bf16[3,48,384]{2,1,0:T(8,128)(2,1)S(1)}, bf16[3,48,384]{2,1,0:T(8,128)(2,1)S(1)}, u32[]{:S(2)}, u32[]{:S(2)}) %collective-permute-start.4) | collective-permute-done | bytes 110624 | tf_op jit(solution)/shard_map/ppermute | solution.py:173
  25.3 1.2 %collective-permute-done.7.refs_7_ = bf16[3,48,384]{2,1,0:T(8,128)(2,1)S(1)} collective-permute-done((bf16[3,48,384]{2,1,0:T(8,128)(2,1)S(1)}, bf16[3,48,384]{2,1,0:T(8,128)(2,1)S(1)}, u32[]{:S(2)}, u32[]{:S(2)}) %collective-permute-start.7) | collective-permute-done | bytes 110624 | tf_op jit(solution)/shard_map/ppermute | solution.py:173
  27.4 3.7 %shard_map.96.before = f32[3,384,384]{2,1,0:T(8,128)S(1)} custom-call(s32[3]{0:T(128)S(1)} %pad_add_fusion.place, bf16[2,192,1024]{2,1,0:T(8,128)(2,1)S(1)} %pad_maximum_fusion.mine, bf16[2,192,1024]{2,1,0:T(8,128)(2,1)S(1)} %collective-permute-done.9.other, bf16[3,384,384]{2,1,0:T(8,128)(2,1)S(1)} %shard_map.95.weights), custom_call_target="tpu_custom_call" | custom-call | flops 1811939328 | bytes 6684684 | tf_op jit(solution)/shard_map/pallas_call | solution.py:150
  31.1 3.8 %shard_map.97 = (f32[3,96,384]{2,1,0:T(8,128)S(1)}, bf16[3,96,384]{2,1,0:T(8,128)(2,1)S(1)}, f32[3,96,384]{2,1,0:T(8,128)S(1)}, bf16[3,96,384]{2,1,0:T(8,128)(2,1)S(1)}) custom-call(s32[3]{0:T(128)S(1)} %pad_add_fusion.place, bf16[2,192,1024]{2,1,0:T(8,128)(2,1)S(1)} %collective-permute-done.2.mine, bf16[2,192,1024]{2,1,0:T(8,128)(2,1)S(1)} %collective-permute-done.8.other, ...), custom_call_target="tpu_custom_call" | custom-call | flops 1811939328 | bytes 8454156 | tf_op jit(solution)/shard_map/pallas_call | solution.py:150
  35.0 1.9 %collective-permute-start.10 = (bf16[3,96,384]{2,1,0:T(8,128)(2,1)S(1)}, bf16[3,96,384]{2,1,0:T(8,128)(2,1)S(1)}, u32[]{:S(2)}, u32[]{:S(2)}) collective-permute-start(bf16[3,96,384]{2,1,0:T(8,128)(2,1)S(1)} %get-tuple-element.46), channel_id=1, source_target_pairs={{0,4},{1,5},{2,6},{3,7},{4,0},{5,1},{6,2},{7,3},{8,12},{9,13},{10,... | collective-permute-start | bytes 663560 | tf_op jit(solution)/shard_map/ppermute | solution.py:173
  37.6 1.1 %collective-permute-start.13 = (bf16[2,192,128]{2,1,0:T(8,128)(2,1)S(1)}, bf16[2,192,128]{2,1,0:T(8,128)(2,1)S(1)}, u32[]{:S(2)}, u32[]{:S(2)}) collective-permute-start(bf16[2,192,128]{2,1,0:T(8,128)(2,1)S(1)} %pad_maximum_fusion.3.refs_5_), channel_id=1, source_target_pairs={{0,3},{1,2},{2,1},{3,0},{4,7},{5,6},{6,5},{7,4},{8,11},{9,10},{10,... | collective-permute-start | bytes 294920 | tf_op jit(solution)/shard_map/ppermute | solution.py:173
  38.7 4.0 %collective-permute-done.12.refs_7_ = bf16[2,192,128]{2,1,0:T(8,128)(2,1)S(1)} collective-permute-done((bf16[2,192,128]{2,1,0:T(8,128)(2,1)S(1)}, bf16[2,192,128]{2,1,0:T(8,128)(2,1)S(1)}, u32[]{:S(2)}, u32[]{:S(2)}) %collective-permute-start.12) | collective-permute-done | bytes 98336 | tf_op jit(solution)/shard_map/ppermute | solution.py:173
  42.7 0.9 collective-permute-done.13.refs_8_
  43.6 1.2 %collective-permute-start.14 = (bf16[3,96,384]{2,1,0:T(8,128)(2,1)S(1)}, bf16[3,96,384]{2,1,0:T(8,128)(2,1)S(1)}, u32[]{:S(2)}, u32[]{:S(2)}) collective-permute-start(bf16[3,96,384]{2,1,0:T(8,128)(2,1)S(1)} %get-tuple-element.50), channel_id=1, source_target_pairs={{0,4},{1,5},{2,6},{3,7},{4,0},{5,1},{6,2},{7,3},{8,12},{9,13},{10,... | collective-permute-start | bytes 663560 | tf_op jit(solution)/shard_map/ppermute | solution.py:173
  44.8 3.3 %collective-permute-start.15 = (bf16[3,96,384]{2,1,0:T(8,128)(2,1)S(1)}, bf16[3,96,384]{2,1,0:T(8,128)(2,1)S(1)}, u32[]{:S(2)}, u32[]{:S(2)}) collective-permute-start(bf16[3,96,384]{2,1,0:T(8,128)(2,1)S(1)} %add_convert_fusion), channel_id=1, source_target_pairs={{0,8},{1,9},{2,10},{3,11},{4,12},{5,13},{6,14},{7,15},{8,0},{9,1},... | collective-permute-start | bytes 663560 | tf_op jit(solution)/shard_map/ppermute | solution.py:173
  48.1 8.1 %collective-permute-done.14.refs_0_ = bf16[3,96,384]{2,1,0:T(8,128)(2,1)S(1)} collective-permute-done((bf16[3,96,384]{2,1,0:T(8,128)(2,1)S(1)}, bf16[3,96,384]{2,1,0:T(8,128)(2,1)S(1)}, u32[]{:S(2)}, u32[]{:S(2)}) %collective-permute-start.14) | collective-permute-done | bytes 221216 | tf_op jit(solution)/shard_map/ppermute | solution.py:173
  57.1 1.5 %collective-permute-start.16 = (bf16[3,96,384]{2,1,0:T(8,128)(2,1)S(1)}, bf16[3,96,384]{2,1,0:T(8,128)(2,1)S(1)}, u32[]{:S(2)}, u32[]{:S(2)}) collective-permute-start(bf16[3,96,384]{2,1,0:T(8,128)(2,1)S(1)} %get-tuple-element.55.refs_0_), channel_id=1, source_target_pairs={{0,8},{1,9},{2,10},{3,11},{4,12},{5,13},{6,14},{7,15},{8,0},{9,1},... | collective-permute-start | bytes 663560 | tf_op jit(solution)/shard_map/ppermute | solution.py:173
  58.6 4.6 %collective-permute-start.18 = (bf16[3,96,384]{2,1,0:T(8,128)(2,1)S(1)}, bf16[3,96,384]{2,1,0:T(8,128)(2,1)S(1)}, u32[]{:S(2)}, u32[]{:S(2)}) collective-permute-start(bf16[3,96,384]{2,1,0:T(8,128)(2,1)S(1)} %get-tuple-element.55.refs_0_), channel_id=1, source_target_pairs={{0,4},{1,5},{2,6},{3,7},{4,0},{5,1},{6,2},{7,3},{8,12},{9,13},{10,... | collective-permute-start | bytes 663560 | tf_op jit(solution)/shard_map/ppermute | solution.py:173
  63.2 1.5 %collective-permute-start.19 = (f32[96,128]{1,0:T(8,128)S(1)}, f32[96,128]{1,0:T(8,128)S(1)}, u32[]{:S(2)}, u32[]{:S(2)}) collective-permute-start(f32[96,128]{1,0:T(8,128)S(1)} %add.24), channel_id=1, source_target_pairs={{0,2},{1,3},{2,0},{3,1},{4,6},{5,7},{6,4},{7,5},{8,10},{9,11},{10,... | collective-permute-start | bytes 147464 | tf_op jit(solution)/shard_map/ppermute | solution.py:173
  64.7 2.6 %collective-permute-done.19 = f32[96,128]{1,0:T(8,128)S(1)} collective-permute-done((f32[96,128]{1,0:T(8,128)S(1)}, f32[96,128]{1,0:T(8,128)S(1)}, u32[]{:S(2)}, u32[]{:S(2)}) %collective-permute-start.19) | collective-permute-done | bytes 49184 | tf_op jit(solution)/shard_map/ppermute | solution.py:173
  67.3 1.2 %collective-permute-start.21 = (f32[1,96,128]{2,1,0:T(8,128)S(1)}, f32[1,96,128]{2,1,0:T(8,128)S(1)}, u32[]{:S(2)}, u32[]{:S(2)}) collective-permute-start(f32[1,96,128]{2,1,0:T(8,128)S(1)} %bitcast.32), channel_id=1, source_target_pairs={{0,8},{1,9},{2,10},{3,11},{4,12},{5,13},{6,14},{7,15},{8,0},{9,1},... | collective-permute-start | bytes 147464 | tf_op jit(solution)/shard_map/ppermute | solution.py:173
  68.5 2.6 %collective-permute-done.16.refs_2_ = bf16[3,96,384]{2,1,0:T(8,128)(2,1)S(1)} collective-permute-done((bf16[3,96,384]{2,1,0:T(8,128)(2,1)S(1)}, bf16[3,96,384]{2,1,0:T(8,128)(2,1)S(1)}, u32[]{:S(2)}, u32[]{:S(2)}) %collective-permute-start.16) | collective-permute-done | bytes 221216 | tf_op jit(solution)/shard_map/ppermute | solution.py:173
  72.4 2.7 %collective-permute-start.22 = (f32[2,96,128]{2,1,0:T(8,128)S(1)}, f32[2,96,128]{2,1,0:T(8,128)S(1)}, u32[]{:S(2)}, u32[]{:S(2)}) collective-permute-start(f32[2,96,128]{2,1,0:T(8,128)S(1)} %get-tuple-element.71), channel_id=1, source_target_pairs={{0,4},{1,5},{2,6},{3,7},{4,0},{5,1},{6,2},{7,3},{8,12},{9,13},{10,... | collective-permute-start | bytes 294920 | tf_op jit(solution)/shard_map/ppermute | solution.py:173
  75.1 4.6 %collective-permute-done.22 = f32[2,96,128]{2,1,0:T(8,128)S(1)} collective-permute-done((f32[2,96,128]{2,1,0:T(8,128)S(1)}, f32[2,96,128]{2,1,0:T(8,128)S(1)}, u32[]{:S(2)}, u32[]{:S(2)}) %collective-permute-start.22) | collective-permute-done | bytes 98336 | tf_op jit(solution)/shard_map/ppermute | solution.py:173
  79.7 2.3 %shard_map.99 = (f32[2,192,128]{2,1,0:T(8,128)S(1)}, bf16[2,192,128]{2,1,0:T(8,128)(2,1)S(1)}, bf16[2,192,128]{2,1,0:T(8,128)(2,1)S(1)}, bf16[2,192,128]{2,1,0:T(8,128)(2,1)S(1)}) custom-call(s32[3]{0:T(128)S(1)} %pad_add_fusion.place, bf16[3,384,384]{2,1,0:T(8,128)(2,1)S(1)} %shard_map.95.weights, bf16[3,96,384]{2,1,0:T(8,128)(2,1)S(1)} %get-tuple-element.55.refs_0_, ...), custom_call_target="tpu_custom_call" | custom-call | flops 452984832 | bytes 5308428 | tf_op jit(solution)/shard_map/pallas_call | solution.py:150
  82.2 1.0 %collective-permute-start.24 = (bf16[2,192,128]{2,1,0:T(8,128)(2,1)S(1)}, bf16[2,192,128]{2,1,0:T(8,128)(2,1)S(1)}, u32[]{:S(2)}, u32[]{:S(2)}) collective-permute-start(bf16[2,192,128]{2,1,0:T(8,128)(2,1)S(1)} %get-tuple-element.64), channel_id=1, source_target_pairs={{0,2},{1,3},{2,0},{3,1},{4,6},{5,7},{6,4},{7,5},{8,10},{9,11},{10,... | collective-permute-start | bytes 294920 | tf_op jit(solution)/shard_map/ppermute | solution.py:173
  84.0 3.8 %collective-permute-done.24.second = bf16[2,192,128]{2,1,0:T(8,128)(2,1)S(1)} collective-permute-done((bf16[2,192,128]{2,1,0:T(8,128)(2,1)S(1)}, bf16[2,192,128]{2,1,0:T(8,128)(2,1)S(1)}, u32[]{:S(2)}, u32[]{:S(2)}) %collective-permute-start.24) | collective-permute-done | bytes 98336 | tf_op jit(solution)/shard_map/ppermute | solution.py:173
  87.8 1.2 %collective-permute-done.25.third = bf16[2,192,128]{2,1,0:T(8,128)(2,1)S(1)} collective-permute-done((bf16[2,192,128]{2,1,0:T(8,128)(2,1)S(1)}, bf16[2,192,128]{2,1,0:T(8,128)(2,1)S(1)}, u32[]{:S(2)}, u32[]{:S(2)}) %collective-permute-start.25) | collective-permute-done | bytes 98336 | tf_op jit(solution)/shard_map/ppermute | solution.py:173
  (44 shorter events, 6.9 us)
Async XLA Ops:
  0.6 6.8 %copy-start = (bf16[1024,192]{0,1:T(8,128)(2,1)S(1)}, bf16[1024,192]{0,1:T(8,128)(2,1)}, u32[]{:S(2)}) copy-start(bf16[1024,192]{0,1:T(8,128)(2,1)} %param.8) | copy-start | bytes 1179652
  1.7 6.1 %collective-permute-start = (bf16[3,48,384]{2,1,0:T(8,128)(2,1)S(1)}, bf16[3,48,384]{2,1,0:T(8,128)(2,1)S(1)}, u32[]{:S(2)}, u32[]{:S(2)}) collective-permute-start(bf16[3,48,384]{2,1,0:T(8,128)(2,1)S(1)} %get-tuple-element.69), channel_id=1, source_target_pairs={{0,2},{1,3},{2,0},{3,1},{4,6},{5,7},{6,4},{7,5},{8,10},{9,11},{10,... | collective-permute-start | bytes 331784 | tf_op jit(solution)/shard_map/ppermute | solution.py:173
  4.7 4.7 %collective-permute-start.1 = (bf16[3,48,384]{2,1,0:T(8,128)(2,1)S(1)}, bf16[3,48,384]{2,1,0:T(8,128)(2,1)S(1)}, u32[]{:S(2)}, u32[]{:S(2)}) collective-permute-start(bf16[3,48,384]{2,1,0:T(8,128)(2,1)S(1)} %get-tuple-element.68.refs_0_), channel_id=1, source_target_pairs={{0,4},{1,5},{2,6},{3,7},{4,0},{5,1},{6,2},{7,3},{8,12},{9,13},{10,... | collective-permute-start | bytes 331784 | tf_op jit(solution)/shard_map/ppermute | solution.py:173
  7.4 20.0 %copy-start.1 = (bf16[128,192]{0,1:T(8,128)(2,1)S(1)}, bf16[128,192]{0,1:T(8,128)(2,1)}, u32[]{:S(2)}) copy-start(bf16[128,192]{0,1:T(8,128)(2,1)} %param.15) | copy-start | bytes 147460
  7.4 20.0 %copy-start.2 = (bf16[128,192]{0,1:T(8,128)(2,1)S(1)}, bf16[128,192]{0,1:T(8,128)(2,1)}, u32[]{:S(2)}) copy-start(bf16[128,192]{0,1:T(8,128)(2,1)} %param.14) | copy-start | bytes 147460
  9.5 17.9 %collective-permute-start.2 = (bf16[2,192,1024]{2,1,0:T(8,128)(2,1)S(1)}, bf16[2,192,1024]{2,1,0:T(8,128)(2,1)S(1)}, u32[]{:S(2)}, u32[]{:S(2)}) collective-permute-start(bf16[2,192,1024]{2,1,0:T(8,128)(2,1)S(1)} %pad_maximum_fusion.mine), channel_id=1, source_target_pairs={{0,2},{1,3},{2,0},{3,1},{4,6},{5,7},{6,4},{7,5},{8,10},{9,11},{10,... | collective-permute-start | bytes 2359304 | tf_op jit(solution)/shard_map/ppermute | solution.py:173
  9.6 10.3 %collective-permute-start.3 = (bf16[3,48,384]{2,1,0:T(8,128)(2,1)S(1)}, bf16[3,48,384]{2,1,0:T(8,128)(2,1)S(1)}, u32[]{:S(2)}, u32[]{:S(2)}) collective-permute-start(bf16[3,48,384]{2,1,0:T(8,128)(2,1)S(1)} %get-tuple-element.68.refs_0_), channel_id=1, source_target_pairs={{0,8},{1,9},{2,10},{3,11},{4,12},{5,13},{6,14},{7,15},{8,0},{9,1},... | collective-permute-start | bytes 331784 | tf_op jit(solution)/shard_map/ppermute | solution.py:173
  12.6 8.8 %collective-permute-start.6 = (bf16[3,48,384]{2,1,0:T(8,128)(2,1)S(1)}, bf16[3,48,384]{2,1,0:T(8,128)(2,1)S(1)}, u32[]{:S(2)}, u32[]{:S(2)}) collective-permute-start(bf16[3,48,384]{2,1,0:T(8,128)(2,1)S(1)} %collective-permute-done.refs_4_), channel_id=1, source_target_pairs={{0,8},{1,9},{2,10},{3,11},{4,12},{5,13},{6,14},{7,15},{8,0},{9,1},... | collective-permute-start | bytes 331784 | tf_op jit(solution)/shard_map/ppermute | solution.py:173
  12.7 14.7 %collective-permute-start.9 = (bf16[2,192,1024]{2,1,0:T(8,128)(2,1)S(1)}, bf16[2,192,1024]{2,1,0:T(8,128)(2,1)S(1)}, u32[]{:S(2)}, u32[]{:S(2)}) collective-permute-start(bf16[2,192,1024]{2,1,0:T(8,128)(2,1)S(1)} %pad_maximum_fusion.mine), channel_id=1, source_target_pairs={{0,1},{1,0},{2,3},{3,2},{4,5},{5,4},{6,7},{7,6},{8,9},{9,8},{10,11... | collective-permute-start | bytes 2359304 | tf_op jit(solution)/shard_map/ppermute | solution.py:173
  12.7 9.6 %collective-permute-start.5 = (bf16[3,48,384]{2,1,0:T(8,128)(2,1)S(1)}, bf16[3,48,384]{2,1,0:T(8,128)(2,1)S(1)}, u32[]{:S(2)}, u32[]{:S(2)}) collective-permute-start(bf16[3,48,384]{2,1,0:T(8,128)(2,1)S(1)} %collective-permute-done.refs_4_), channel_id=1, source_target_pairs={{0,4},{1,5},{2,6},{3,7},{4,0},{5,1},{6,2},{7,3},{8,12},{9,13},{10,... | collective-permute-start | bytes 331784 | tf_op jit(solution)/shard_map/ppermute | solution.py:173
  19.9 5.4 %collective-permute-start.4 = (bf16[3,48,384]{2,1,0:T(8,128)(2,1)S(1)}, bf16[3,48,384]{2,1,0:T(8,128)(2,1)S(1)}, u32[]{:S(2)}, u32[]{:S(2)}) collective-permute-start(bf16[3,48,384]{2,1,0:T(8,128)(2,1)S(1)} %collective-permute-done.3.refs_2_), channel_id=1, source_target_pairs={{0,4},{1,5},{2,6},{3,7},{4,0},{5,1},{6,2},{7,3},{8,12},{9,13},{10,... | collective-permute-start | bytes 331784 | tf_op jit(solution)/shard_map/ppermute | solution.py:173
  21.4 5.0 %collective-permute-start.7 = (bf16[3,48,384]{2,1,0:T(8,128)(2,1)S(1)}, bf16[3,48,384]{2,1,0:T(8,128)(2,1)S(1)}, u32[]{:S(2)}, u32[]{:S(2)}) collective-permute-start(bf16[3,48,384]{2,1,0:T(8,128)(2,1)S(1)} %collective-permute-done.6.refs_6_), channel_id=1, source_target_pairs={{0,4},{1,5},{2,6},{3,7},{4,0},{5,1},{6,2},{7,3},{8,12},{9,13},{10,... | collective-permute-start | bytes 331784 | tf_op jit(solution)/shard_map/ppermute | solution.py:173
  27.4 3.8 %collective-permute-start.8 = (bf16[2,192,1024]{2,1,0:T(8,128)(2,1)S(1)}, bf16[2,192,1024]{2,1,0:T(8,128)(2,1)S(1)}, u32[]{:S(2)}, u32[]{:S(2)}) collective-permute-start(bf16[2,192,1024]{2,1,0:T(8,128)(2,1)S(1)} %collective-permute-done.2.mine), channel_id=1, source_target_pairs={{0,1},{1,0},{2,3},{3,2},{4,5},{5,4},{6,7},{7,6},{8,9},{9,8},{10,11... | collective-permute-start | bytes 2359304 | tf_op jit(solution)/shard_map/ppermute | solution.py:173
  35.0 8.6 %collective-permute-start.10 = (bf16[3,96,384]{2,1,0:T(8,128)(2,1)S(1)}, bf16[3,96,384]{2,1,0:T(8,128)(2,1)S(1)}, u32[]{:S(2)}, u32[]{:S(2)}) collective-permute-start(bf16[3,96,384]{2,1,0:T(8,128)(2,1)S(1)} %get-tuple-element.46), channel_id=1, source_target_pairs={{0,4},{1,5},{2,6},{3,7},{4,0},{5,1},{6,2},{7,3},{8,12},{9,13},{10,... | collective-permute-start | bytes 663560 | tf_op jit(solution)/shard_map/ppermute | solution.py:173
  36.9 1.9 %collective-permute-start.11 = (bf16[2,192,128]{2,1,0:T(8,128)(2,1)S(1)}, bf16[2,192,128]{2,1,0:T(8,128)(2,1)S(1)}, u32[]{:S(2)}, u32[]{:S(2)}) collective-permute-start(bf16[2,192,128]{2,1,0:T(8,128)(2,1)S(1)} %pad_maximum_fusion.3.refs_5_), channel_id=1, source_target_pairs={{0,1},{1,0},{2,3},{3,2},{4,5},{5,4},{6,7},{7,6},{8,9},{9,8},{10,11... | collective-permute-start | bytes 294920 | tf_op jit(solution)/shard_map/ppermute | solution.py:173
  37.1 5.6 %collective-permute-start.12 = (bf16[2,192,128]{2,1,0:T(8,128)(2,1)S(1)}, bf16[2,192,128]{2,1,0:T(8,128)(2,1)S(1)}, u32[]{:S(2)}, u32[]{:S(2)}) collective-permute-start(bf16[2,192,128]{2,1,0:T(8,128)(2,1)S(1)} %pad_maximum_fusion.3.refs_5_), channel_id=1, source_target_pairs={{0,2},{1,3},{2,0},{3,1},{4,6},{5,7},{6,4},{7,5},{8,10},{9,11},{10,... | collective-permute-start | bytes 294920 | tf_op jit(solution)/shard_map/ppermute | solution.py:173
  37.6 5.9 %collective-permute-start.13 = (bf16[2,192,128]{2,1,0:T(8,128)(2,1)S(1)}, bf16[2,192,128]{2,1,0:T(8,128)(2,1)S(1)}, u32[]{:S(2)}, u32[]{:S(2)}) collective-permute-start(bf16[2,192,128]{2,1,0:T(8,128)(2,1)S(1)} %pad_maximum_fusion.3.refs_5_), channel_id=1, source_target_pairs={{0,3},{1,2},{2,1},{3,0},{4,7},{5,6},{6,5},{7,4},{8,11},{9,10},{10,... | collective-permute-start | bytes 294920 | tf_op jit(solution)/shard_map/ppermute | solution.py:173
  43.6 12.6 %collective-permute-start.14 = (bf16[3,96,384]{2,1,0:T(8,128)(2,1)S(1)}, bf16[3,96,384]{2,1,0:T(8,128)(2,1)S(1)}, u32[]{:S(2)}, u32[]{:S(2)}) collective-permute-start(bf16[3,96,384]{2,1,0:T(8,128)(2,1)S(1)} %get-tuple-element.50), channel_id=1, source_target_pairs={{0,4},{1,5},{2,6},{3,7},{4,0},{5,1},{6,2},{7,3},{8,12},{9,13},{10,... | collective-permute-start | bytes 663560 | tf_op jit(solution)/shard_map/ppermute | solution.py:173
  44.8 11.4 %collective-permute-start.15 = (bf16[3,96,384]{2,1,0:T(8,128)(2,1)S(1)}, bf16[3,96,384]{2,1,0:T(8,128)(2,1)S(1)}, u32[]{:S(2)}, u32[]{:S(2)}) collective-permute-start(bf16[3,96,384]{2,1,0:T(8,128)(2,1)S(1)} %add_convert_fusion), channel_id=1, source_target_pairs={{0,8},{1,9},{2,10},{3,11},{4,12},{5,13},{6,14},{7,15},{8,0},{9,1},... | collective-permute-start | bytes 663560 | tf_op jit(solution)/shard_map/ppermute | solution.py:173
  57.0 1.6 %collective-permute-start.17 = (f32[96,128]{1,0:T(8,128)S(1)}, f32[96,128]{1,0:T(8,128)S(1)}, u32[]{:S(2)}, u32[]{:S(2)}) collective-permute-start(f32[96,128]{1,0:T(8,128)S(1)} %get-tuple-element.53), channel_id=1, source_target_pairs={{0,1},{1,0},{2,3},{3,2},{4,5},{5,4},{6,7},{7,6},{8,9},{9,8},{10,11... | collective-permute-start | bytes 147464 | tf_op jit(solution)/shard_map/ppermute | solution.py:173
  57.1 14.0 %collective-permute-start.16 = (bf16[3,96,384]{2,1,0:T(8,128)(2,1)S(1)}, bf16[3,96,384]{2,1,0:T(8,128)(2,1)S(1)}, u32[]{:S(2)}, u32[]{:S(2)}) collective-permute-start(bf16[3,96,384]{2,1,0:T(8,128)(2,1)S(1)} %get-tuple-element.55.refs_0_), channel_id=1, source_target_pairs={{0,8},{1,9},{2,10},{3,11},{4,12},{5,13},{6,14},{7,15},{8,0},{9,1},... | collective-permute-start | bytes 663560 | tf_op jit(solution)/shard_map/ppermute | solution.py:173
  58.6 12.7 %collective-permute-start.18 = (bf16[3,96,384]{2,1,0:T(8,128)(2,1)S(1)}, bf16[3,96,384]{2,1,0:T(8,128)(2,1)S(1)}, u32[]{:S(2)}, u32[]{:S(2)}) collective-permute-start(bf16[3,96,384]{2,1,0:T(8,128)(2,1)S(1)} %get-tuple-element.55.refs_0_), channel_id=1, source_target_pairs={{0,4},{1,5},{2,6},{3,7},{4,0},{5,1},{6,2},{7,3},{8,12},{9,13},{10,... | collective-permute-start | bytes 663560 | tf_op jit(solution)/shard_map/ppermute | solution.py:173
  63.2 4.1 %collective-permute-start.19 = (f32[96,128]{1,0:T(8,128)S(1)}, f32[96,128]{1,0:T(8,128)S(1)}, u32[]{:S(2)}, u32[]{:S(2)}) collective-permute-start(f32[96,128]{1,0:T(8,128)S(1)} %add.24), channel_id=1, source_target_pairs={{0,2},{1,3},{2,0},{3,1},{4,6},{5,7},{6,4},{7,5},{8,10},{9,11},{10,... | collective-permute-start | bytes 147464 | tf_op jit(solution)/shard_map/ppermute | solution.py:173
  67.3 5.0 %collective-permute-start.21 = (f32[1,96,128]{2,1,0:T(8,128)S(1)}, f32[1,96,128]{2,1,0:T(8,128)S(1)}, u32[]{:S(2)}, u32[]{:S(2)}) collective-permute-start(f32[1,96,128]{2,1,0:T(8,128)S(1)} %bitcast.32), channel_id=1, source_target_pairs={{0,8},{1,9},{2,10},{3,11},{4,12},{5,13},{6,14},{7,15},{8,0},{9,1},... | collective-permute-start | bytes 147464 | tf_op jit(solution)/shard_map/ppermute | solution.py:173
  71.3 8.4 %collective-permute-start.20 = (bf16[3,96,384]{2,1,0:T(8,128)(2,1)S(1)}, bf16[3,96,384]{2,1,0:T(8,128)(2,1)S(1)}, u32[]{:S(2)}, u32[]{:S(2)}) collective-permute-start(bf16[3,96,384]{2,1,0:T(8,128)(2,1)S(1)} %collective-permute-done.16.refs_2_), channel_id=1, source_target_pairs={{0,4},{1,5},{2,6},{3,7},{4,0},{5,1},{6,2},{7,3},{8,12},{9,13},{10,... | collective-permute-start | bytes 663560 | tf_op jit(solution)/shard_map/ppermute | solution.py:173
  72.4 7.3 %collective-permute-start.22 = (f32[2,96,128]{2,1,0:T(8,128)S(1)}, f32[2,96,128]{2,1,0:T(8,128)S(1)}, u32[]{:S(2)}, u32[]{:S(2)}) collective-permute-start(f32[2,96,128]{2,1,0:T(8,128)S(1)} %get-tuple-element.71), channel_id=1, source_target_pairs={{0,4},{1,5},{2,6},{3,7},{4,0},{5,1},{6,2},{7,3},{8,12},{9,13},{10,... | collective-permute-start | bytes 294920 | tf_op jit(solution)/shard_map/ppermute | solution.py:173
  82.1 1.9 %collective-permute-start.23 = (bf16[2,192,128]{2,1,0:T(8,128)(2,1)S(1)}, bf16[2,192,128]{2,1,0:T(8,128)(2,1)S(1)}, u32[]{:S(2)}, u32[]{:S(2)}) collective-permute-start(bf16[2,192,128]{2,1,0:T(8,128)(2,1)S(1)} %get-tuple-element.63), channel_id=1, source_target_pairs={{0,1},{1,0},{2,3},{3,2},{4,5},{5,4},{6,7},{7,6},{8,9},{9,8},{10,11... | collective-permute-start | bytes 294920 | tf_op jit(solution)/shard_map/ppermute | solution.py:173
  82.2 5.7 %collective-permute-start.24 = (bf16[2,192,128]{2,1,0:T(8,128)(2,1)S(1)}, bf16[2,192,128]{2,1,0:T(8,128)(2,1)S(1)}, u32[]{:S(2)}, u32[]{:S(2)}) collective-permute-start(bf16[2,192,128]{2,1,0:T(8,128)(2,1)S(1)} %get-tuple-element.64), channel_id=1, source_target_pairs={{0,2},{1,3},{2,0},{3,1},{4,6},{5,7},{6,4},{7,5},{8,10},{9,11},{10,... | collective-permute-start | bytes 294920 | tf_op jit(solution)/shard_map/ppermute | solution.py:173
  83.2 5.8 %collective-permute-start.25 = (bf16[2,192,128]{2,1,0:T(8,128)(2,1)S(1)}, bf16[2,192,128]{2,1,0:T(8,128)(2,1)S(1)}, u32[]{:S(2)}, u32[]{:S(2)}) collective-permute-start(bf16[2,192,128]{2,1,0:T(8,128)(2,1)S(1)} %get-tuple-element.65), channel_id=1, source_target_pairs={{0,3},{1,2},{2,1},{3,0},{4,7},{5,6},{6,5},{7,4},{8,11},{9,10},{10,... | collective-permute-start | bytes 294920 | tf_op jit(solution)/shard_map/ppermute | solution.py:173

commit v4 on v3

--- a/solution.py
+++ b/solution.py
@@ -97,15 +97,29 @@
     stats_out[...] = stats
 
 
-def query_kernel(groups, hidden, place, weights, *refs):
-    grads, stats, refs = refs[:groups], refs[groups], refs[groups + 1 :]
-    quests, refs = refs[:4], refs[4:]
-    own_out, sends, (renewed, query) = refs[0], refs[1:4], refs[4:]
-    group, side, half = place[0], place[1], place[2]
-    feats, count = quests[0].shape[1:]
-
+def answer(renewed, query, quests, half, kept, given):
+    mine, other = quests
+    feats = mine.shape[1]
+    join(query, mine, other, half)
+    gate = contract(renewed[0], query[0], 0, 0)
+    up = contract(renewed[1], query[0], 0, 0)
+    back = contract(renewed[2], query[1], 0, 0)
+    silu, slope_up, act = gated(gate, up)
+    out = contract(renewed[2], act.astype(bf16), 1, 0)
+    grad = contract(renewed[0], (back * slope_up).astype(bf16), 1, 0) + contract(
+        renewed[1], (back * silu).astype(bf16), 1, 0
+    )
+    for index, whole in enumerate((out, grad)):
+        first, second = whole[:feats], whole[feats:]
+        kept[index] = jnp.where(half == 0, first, second)
+        given[index] = jnp.where(half == 0, second, first).astype(bf16)
+
+
+def renew_kernel(groups, hidden, place, weights, *refs):
+    grads, stats, quests, refs = refs[:groups], refs[groups], refs[groups + 1 : groups + 3], refs[groups + 3 :]
+    renewed, kept, given, query = refs
     for flip in range(groups):
-        where = rows_of(group ^ flip, grads[0].shape[1])
+        where = rows_of(place[0] ^ flip, grads[0].shape[1])
         sums = stats[flip] / hidden
         for index in range(3):
             wsq = sums[:, 3 * index : 3 * index + 1]
@@ -116,30 +130,16 @@
             factor = jnp.sqrt(wsq) / jnp.sqrt(msq + epsilon)
             moved = weights[index, where, :].astype(f32) + scale * grads[flip][index].astype(f32)
             renewed[index, where, :] = (moved * factor).astype(bf16)
-    for flip in range(4):
-        feat = pl.ds(pl.multiple_of((half ^ (flip & 1)) * feats, feats), feats)
-        span = pl.ds(pl.multiple_of((side ^ (flip >> 1)) * count, count), count)
-        query[:, feat, span] = quests[flip][...]
-
-    gate = contract(renewed[0], query[0], 0, 0)
-    up = contract(renewed[1], query[0], 0, 0)
-    back = contract(renewed[2], query[1], 0, 0)
-    silu, slope_up, act = gated(gate, up)
-    out = contract(renewed[2], act.astype(bf16), 1, 0)
-    grad = contract(renewed[0], (back * slope_up).astype(bf16), 1, 0) + contract(
-        renewed[1], (back * silu).astype(bf16), 1, 0
-    )
-    for index, whole in enumerate((out, grad)):
-        for flip, target in enumerate((own_out, *sends)):
-            left = jnp.where((half ^ (flip & 1)) == 0, whole[:feats], whole[feats:])
-            piece = jnp.where((side ^ (flip >> 1)) == 0, left[:, :count], left[:, count:])
-            target[index] = piece.astype(target.dtype)
-
-
-def last_kernel(own, first, second, third, out, grad):
+    answer(renewed, query, quests, place[2], kept, given)
+
+
+def query_kernel(place, renewed, mine, other, kept, given, query):
+    answer(renewed, query, (mine, other), place[2], kept, given)
+
+
+def last_kernel(kept, core, pair, out, grad):
     for index, target in enumerate((out, grad)):
-        total = own[index] + first[index].astype(f32) + second[index].astype(f32)
-        target[...] = (total + third[index].astype(f32)).astype(bf16)
+        target[...] = (kept[index] + core[index].astype(f32) + pair[index].astype(f32)).astype(bf16)
 
 
 def call(body, operands, outs, scratch=(), flops=0, place=None, mib=4):
@@ -194,7 +194,8 @@
     tokens = jnp.stack([input_keys.T, vals])
     _, feats, toks = tokens.shape
     first = gather(own_w)
-    tokens, pair_w, _ = lax.optimization_barrier((tokens, swap(give_w, pair), first[1]))
+    tokens, pair_w = lax.optimization_barrier((tokens, swap(give_w, pair)))
+    pair_w, _ = lax.optimization_barrier((pair_w, first[1]))
     second = gather(pair_w)
     pair_tokens = swap(tokens, pair)
 
@@ -258,18 +259,27 @@
 
     count = queries.shape[0]
     piece = (2, feats, count)
-    own_out, *sends = call(
-        functools.partial(query_kernel, groups, 2 * n_hid * cols),
-        (weights, *gather(grad, [near_stats], [stats]), all_stats, *quests),
-        [jax.ShapeDtypeStruct(piece, f32)] + [jax.ShapeDtypeStruct(piece, bf16)] * 3,
-        [pltpu.VMEM(whole, bf16), pltpu.VMEM((2, width, 2 * count), bf16)],
-        6 * 2 * 2 * count * width * cols,
+    kept_given = [jax.ShapeDtypeStruct(piece, f32), jax.ShapeDtypeStruct(piece, bf16)]
+    query = pltpu.VMEM((2, width, count), bf16)
+    query_flops = 6 * 2 * count * width * cols
+    renewed, kept, given = call(
+        functools.partial(renew_kernel, groups, 2 * n_hid * cols),
+        (weights, *gather(grad, [near_stats], [stats]), all_stats, *quests[2:]),
+        [jax.ShapeDtypeStruct(whole, bf16), *kept_given],
+        [query],
+        query_flops,
         place,
         16,
     )
-    arrived = [swap(send, flip) for send, flip in zip(sends, (1, 2, 3))]
+    from_core, quests = lax.optimization_barrier((swap(given, core), quests))
+    from_pair = swap((kept + from_core.astype(f32)).astype(bf16), pair)
+    kept, given = call(
+        query_kernel, (renewed, *quests[:2]), kept_given, [query], query_flops, place, 16
+    )
     out, grad = call(
-        last_kernel, (own_out, *arrived), [jax.ShapeDtypeStruct(piece[1:], bf16)] * 2
+        last_kernel,
+        (kept, swap(given, core), from_pair),
+        [jax.ShapeDtypeStruct(piece[1:], bf16)] * 2,
     )
     return out.T, grad.T
 

time: 91.4 us -> 89.8 us (0.982); the launches traced: 89.7 us -> 89.7 us
  Pallas kernels: 11.9 us -> 13.1 us
  starting transfers between devices: 32.3 us -> 31.3 us
    pallas_call x6 -> x7, Pallas kernels: 11.9 us -> 13.1 us  [call(): pl.pallas_call(body, out_shape=list(outs), in_specs=specs, out_specs=[pl....]
    ppermute x26, starting transfers between devices: 32.3 us -> 31.3 us  [swap(): return lax.ppermute(array, ('tok', 'hid'), pairs)]
  transfers between devices with their start and end apart: 26 -> 26, of which waited for: 17 -> 16; matrix products, arithmetic and copies ran while one was open for 1% -> 1% of each run, Pallas kernels for 5% -> 6%
where the time goes in v4:
time: 89.8 us; the launch traced here: 89.7 us
  waiting for transfers between devices  42 us (47%)
  starting transfers between devices  31.3 us (35%)
  Pallas kernels  13.1 us (15%)
  other arithmetic  2.39 us (3%)
    ppermute x26, waiting for transfers between devices, swap(): return lax.ppermute(array, ('tok', 'hid'), pairs)  42 us
    ppermute x26, starting transfers between devices, swap(): return lax.ppermute(array, ('tok', 'hid'), pairs)  31.3 us
    pallas_call x7, Pallas kernels, call(): pl.pallas_call(body, out_shape=list(outs), in_specs=specs, out_specs=[pl....  13.1 us
  transfers between devices with their start and end apart: 26, of which 16 were waited for; matrix products, arithmetic and copies ran while one was open for 1% of the time, Pallas kernels for 6%

profile of v4, /device:TPU:0, one launch (start us, length us, event | category | flops | bytes accessed | tf_op | source)
XLA Modules:
  0.0 89.7 jit_solution(2819779931285665436)
XLA Ops:
  1.7 3.0 %collective-permute-start = (bf16[3,48,384]{2,1,0:T(8,128)(2,1)S(1)}, bf16[3,48,384]{2,1,0:T(8,128)(2,1)S(1)}, u32[]{:S(2)}, u32[]{:S(2)}) collective-permute-start(bf16[3,48,384]{2,1,0:T(8,128)(2,1)S(1)} %get-tuple-element.79), channel_id=1, source_target_pairs={{0,2},{1,3},{2,0},{3,1},{4,6},{5,7},{6,4},{7,5},{8,10},{9,11},{10,... | collective-permute-start | bytes 331784 | tf_op jit(solution)/shard_map/ppermute | solution.py:173
  4.7 1.1 %fusion = bf16[1,192,1024]{2,1,0:T(8,128)(2,1)S(1)} fusion(bf16[1024,192]{0,1:T(8,128)(2,1)} %param.9, f32[1024]{0:T(1024)} %param.10), kind=kLoop, calls=%fused_computation.3 | loop fusion | flops 589824 | bytes 790528 | tf_op jit(solution)/shard_map/stack | solution.py:194
  5.9 1.9 %collective-permute-done.refs_4_ = bf16[3,48,384]{2,1,0:T(8,128)(2,1)S(1)} collective-permute-done((bf16[3,48,384]{2,1,0:T(8,128)(2,1)S(1)}, bf16[3,48,384]{2,1,0:T(8,128)(2,1)S(1)}, u32[]{:S(2)}, u32[]{:S(2)}) %collective-permute-start) | collective-permute-done | bytes 110624 | tf_op jit(solution)/shard_map/ppermute | solution.py:173
  7.8 1.7 %collective-permute-start.1 = (bf16[2,192,1024]{2,1,0:T(8,128)(2,1)S(1)}, bf16[2,192,1024]{2,1,0:T(8,128)(2,1)S(1)}, u32[]{:S(2)}, u32[]{:S(2)}) collective-permute-start(bf16[2,192,1024]{2,1,0:T(8,128)(2,1)S(1)} %pad_maximum_fusion.mine), channel_id=1, source_target_pairs={{0,2},{1,3},{2,0},{3,1},{4,6},{5,7},{6,4},{7,5},{8,10},{9,11},{10,... | collective-permute-start | bytes 2359304 | tf_op jit(solution)/shard_map/ppermute | solution.py:173
  9.5 1.6 %collective-permute-start.2 = (bf16[3,48,384]{2,1,0:T(8,128)(2,1)S(1)}, bf16[3,48,384]{2,1,0:T(8,128)(2,1)S(1)}, u32[]{:S(2)}, u32[]{:S(2)}) collective-permute-start(bf16[3,48,384]{2,1,0:T(8,128)(2,1)S(1)} %get-tuple-element.78.refs_0_), channel_id=1, source_target_pairs={{0,4},{1,5},{2,6},{3,7},{4,0},{5,1},{6,2},{7,3},{8,12},{9,13},{10,... | collective-permute-start | bytes 331784 | tf_op jit(solution)/shard_map/ppermute | solution.py:173
  11.1 2.6 %collective-permute-start.3 = (bf16[3,48,384]{2,1,0:T(8,128)(2,1)S(1)}, bf16[3,48,384]{2,1,0:T(8,128)(2,1)S(1)}, u32[]{:S(2)}, u32[]{:S(2)}) collective-permute-start(bf16[3,48,384]{2,1,0:T(8,128)(2,1)S(1)} %get-tuple-element.78.refs_0_), channel_id=1, source_target_pairs={{0,8},{1,9},{2,10},{3,11},{4,12},{5,13},{6,14},{7,15},{8,0},{9,1},... | collective-permute-start | bytes 331784 | tf_op jit(solution)/shard_map/ppermute | solution.py:173
  13.7 1.6 %collective-permute-done.2.refs_1_ = bf16[3,48,384]{2,1,0:T(8,128)(2,1)S(1)} collective-permute-done((bf16[3,48,384]{2,1,0:T(8,128)(2,1)S(1)}, bf16[3,48,384]{2,1,0:T(8,128)(2,1)S(1)}, u32[]{:S(2)}, u32[]{:S(2)}) %collective-permute-start.2) | collective-permute-done | bytes 110624 | tf_op jit(solution)/shard_map/ppermute | solution.py:173
  15.3 1.7 %collective-permute-start.6 = (bf16[3,48,384]{2,1,0:T(8,128)(2,1)S(1)}, bf16[3,48,384]{2,1,0:T(8,128)(2,1)S(1)}, u32[]{:S(2)}, u32[]{:S(2)}) collective-permute-start(bf16[3,48,384]{2,1,0:T(8,128)(2,1)S(1)} %collective-permute-done.refs_4_), channel_id=1, source_target_pairs={{0,8},{1,9},{2,10},{3,11},{4,12},{5,13},{6,14},{7,15},{8,0},{9,1},... | collective-permute-start | bytes 331784 | tf_op jit(solution)/shard_map/ppermute | solution.py:173
  17.0 1.6 %collective-permute-start.5 = (bf16[3,48,384]{2,1,0:T(8,128)(2,1)S(1)}, bf16[3,48,384]{2,1,0:T(8,128)(2,1)S(1)}, u32[]{:S(2)}, u32[]{:S(2)}) collective-permute-start(bf16[3,48,384]{2,1,0:T(8,128)(2,1)S(1)} %collective-permute-done.refs_4_), channel_id=1, source_target_pairs={{0,4},{1,5},{2,6},{3,7},{4,0},{5,1},{6,2},{7,3},{8,12},{9,13},{10,... | collective-permute-start | bytes 331784 | tf_op jit(solution)/shard_map/ppermute | solution.py:173
  18.6 1.7 %collective-permute-done.3.refs_2_ = bf16[3,48,384]{2,1,0:T(8,128)(2,1)S(1)} collective-permute-done((bf16[3,48,384]{2,1,0:T(8,128)(2,1)S(1)}, bf16[3,48,384]{2,1,0:T(8,128)(2,1)S(1)}, u32[]{:S(2)}, u32[]{:S(2)}) %collective-permute-start.3) | collective-permute-done | bytes 110624 | tf_op jit(solution)/shard_map/ppermute | solution.py:173
  20.3 1.8 %collective-permute-done.6.refs_6_ = bf16[3,48,384]{2,1,0:T(8,128)(2,1)S(1)} collective-permute-done((bf16[3,48,384]{2,1,0:T(8,128)(2,1)S(1)}, bf16[3,48,384]{2,1,0:T(8,128)(2,1)S(1)}, u32[]{:S(2)}, u32[]{:S(2)}) %collective-permute-start.6) | collective-permute-done | bytes 110624 | tf_op jit(solution)/shard_map/ppermute | solution.py:173
  22.1 1.8 %collective-permute-start.7 = (bf16[3,48,384]{2,1,0:T(8,128)(2,1)S(1)}, bf16[3,48,384]{2,1,0:T(8,128)(2,1)S(1)}, u32[]{:S(2)}, u32[]{:S(2)}) collective-permute-start(bf16[3,48,384]{2,1,0:T(8,128)(2,1)S(1)} %collective-permute-done.6.refs_6_), channel_id=1, source_target_pairs={{0,4},{1,5},{2,6},{3,7},{4,0},{5,1},{6,2},{7,3},{8,12},{9,13},{10,... | collective-permute-start | bytes 331784 | tf_op jit(solution)/shard_map/ppermute | solution.py:173
  23.9 2.3 %collective-permute-done.4.refs_3_ = bf16[3,48,384]{2,1,0:T(8,128)(2,1)S(1)} collective-permute-done((bf16[3,48,384]{2,1,0:T(8,128)(2,1)S(1)}, bf16[3,48,384]{2,1,0:T(8,128)(2,1)S(1)}, u32[]{:S(2)}, u32[]{:S(2)}) %collective-permute-start.4) | collective-permute-done | bytes 110624 | tf_op jit(solution)/shard_map/ppermute | solution.py:173
  26.3 2.3 %collective-permute-done.7.refs_7_ = bf16[3,48,384]{2,1,0:T(8,128)(2,1)S(1)} collective-permute-done((bf16[3,48,384]{2,1,0:T(8,128)(2,1)S(1)}, bf16[3,48,384]{2,1,0:T(8,128)(2,1)S(1)}, u32[]{:S(2)}, u32[]{:S(2)}) %collective-permute-start.7) | collective-permute-done | bytes 110624 | tf_op jit(solution)/shard_map/ppermute | solution.py:173
  29.4 3.7 %shard_map.96.before = f32[3,384,384]{2,1,0:T(8,128)S(1)} custom-call(s32[3]{0:T(128)S(1)} %pad_add_fusion.place, bf16[2,192,1024]{2,1,0:T(8,128)(2,1)S(1)} %pad_maximum_fusion.mine, bf16[2,192,1024]{2,1,0:T(8,128)(2,1)S(1)} %collective-permute-done.9.other, bf16[3,384,384]{2,1,0:T(8,128)(2,1)S(1)} %shard_map.95.weights), custom_call_target="tpu_custom_call" | custom-call | flops 1811939328 | bytes 6684684 | tf_op jit(solution)/shard_map/pallas_call | solution.py:150
  33.1 3.8 %shard_map.97 = (f32[3,96,384]{2,1,0:T(8,128)S(1)}, bf16[3,96,384]{2,1,0:T(8,128)(2,1)S(1)}, f32[3,96,384]{2,1,0:T(8,128)S(1)}, bf16[3,96,384]{2,1,0:T(8,128)(2,1)S(1)}) custom-call(s32[3]{0:T(128)S(1)} %pad_add_fusion.place, bf16[2,192,1024]{2,1,0:T(8,128)(2,1)S(1)} %collective-permute-done.1.mine, bf16[2,192,1024]{2,1,0:T(8,128)(2,1)S(1)} %collective-permute-done.8.other, ...), custom_call_target="tpu_custom_call" | custom-call | flops 1811939328 | bytes 8454156 | tf_op jit(solution)/shard_map/pallas_call | solution.py:150
  38.0 1.1 %collective-permute-start.13 = (bf16[2,192,128]{2,1,0:T(8,128)(2,1)S(1)}, bf16[2,192,128]{2,1,0:T(8,128)(2,1)S(1)}, u32[]{:S(2)}, u32[]{:S(2)}) collective-permute-start(bf16[2,192,128]{2,1,0:T(8,128)(2,1)S(1)} %pad_maximum_fusion.3.mine), channel_id=1, source_target_pairs={{0,3},{1,2},{2,1},{3,0},{4,7},{5,6},{6,5},{7,4},{8,11},{9,10},{10,... | collective-permute-start | bytes 294920 | tf_op jit(solution)/shard_map/ppermute | solution.py:173
  39.2 4.0 %collective-permute-done.12.refs_5_ = bf16[2,192,128]{2,1,0:T(8,128)(2,1)S(1)} collective-permute-done((bf16[2,192,128]{2,1,0:T(8,128)(2,1)S(1)}, bf16[2,192,128]{2,1,0:T(8,128)(2,1)S(1)}, u32[]{:S(2)}, u32[]{:S(2)}) %collective-permute-start.12) | collective-permute-done | bytes 98336 | tf_op jit(solution)/shard_map/ppermute | solution.py:173
  45.9 2.5 %collective-permute-start.15 = (bf16[3,96,384]{2,1,0:T(8,128)(2,1)S(1)}, bf16[3,96,384]{2,1,0:T(8,128)(2,1)S(1)}, u32[]{:S(2)}, u32[]{:S(2)}) collective-permute-start(bf16[3,96,384]{2,1,0:T(8,128)(2,1)S(1)} %add_convert_fusion), channel_id=1, source_target_pairs={{0,8},{1,9},{2,10},{3,11},{4,12},{5,13},{6,14},{7,15},{8,0},{9,1},... | collective-permute-start | bytes 663560 | tf_op jit(solution)/shard_map/ppermute | solution.py:173
  48.4 8.5 %collective-permute-done.14.refs_0_ = bf16[3,96,384]{2,1,0:T(8,128)(2,1)S(1)} collective-permute-done((bf16[3,96,384]{2,1,0:T(8,128)(2,1)S(1)}, bf16[3,96,384]{2,1,0:T(8,128)(2,1)S(1)}, u32[]{:S(2)}, u32[]{:S(2)}) %collective-permute-start.14) | collective-permute-done | bytes 221216 | tf_op jit(solution)/shard_map/ppermute | solution.py:173
  57.8 2.6 %collective-permute-start.16 = (bf16[3,96,384]{2,1,0:T(8,128)(2,1)S(1)}, bf16[3,96,384]{2,1,0:T(8,128)(2,1)S(1)}, u32[]{:S(2)}, u32[]{:S(2)}) collective-permute-start(bf16[3,96,384]{2,1,0:T(8,128)(2,1)S(1)} %get-tuple-element.61.refs_0_), channel_id=1, source_target_pairs={{0,8},{1,9},{2,10},{3,11},{4,12},{5,13},{6,14},{7,15},{8,0},{9,1},... | collective-permute-start | bytes 663560 | tf_op jit(solution)/shard_map/ppermute | solution.py:173
  60.4 3.1 %collective-permute-start.18 = (bf16[3,96,384]{2,1,0:T(8,128)(2,1)S(1)}, bf16[3,96,384]{2,1,0:T(8,128)(2,1)S(1)}, u32[]{:S(2)}, u32[]{:S(2)}) collective-permute-start(bf16[3,96,384]{2,1,0:T(8,128)(2,1)S(1)} %get-tuple-element.61.refs_0_), channel_id=1, source_target_pairs={{0,4},{1,5},{2,6},{3,7},{4,0},{5,1},{6,2},{7,3},{8,12},{9,13},{10,... | collective-permute-start | bytes 663560 | tf_op jit(solution)/shard_map/ppermute | solution.py:173
  64.1 3.6 %collective-permute-done.19 = f32[96,128]{1,0:T(8,128)S(1)} collective-permute-done((f32[96,128]{1,0:T(8,128)S(1)}, f32[96,128]{1,0:T(8,128)S(1)}, u32[]{:S(2)}, u32[]{:S(2)}) %collective-permute-start.19) | collective-permute-done | bytes 49184 | tf_op jit(solution)/shard_map/ppermute | solution.py:173
  67.6 1.2 %collective-permute-start.21 = (f32[1,96,128]{2,1,0:T(8,128)S(1)}, f32[1,96,128]{2,1,0:T(8,128)S(1)}, u32[]{:S(2)}, u32[]{:S(2)}) collective-permute-start(f32[1,96,128]{2,1,0:T(8,128)S(1)} %bitcast.32), channel_id=1, source_target_pairs={{0,8},{1,9},{2,10},{3,11},{4,12},{5,13},{6,14},{7,15},{8,0},{9,1},... | collective-permute-start | bytes 147464 | tf_op jit(solution)/shard_map/ppermute | solution.py:173
  68.8 3.0 %collective-permute-done.16.refs_2_ = bf16[3,96,384]{2,1,0:T(8,128)(2,1)S(1)} collective-permute-done((bf16[3,96,384]{2,1,0:T(8,128)(2,1)S(1)}, bf16[3,96,384]{2,1,0:T(8,128)(2,1)S(1)}, u32[]{:S(2)}, u32[]{:S(2)}) %collective-permute-start.16) | collective-permute-done | bytes 221216 | tf_op jit(solution)/shard_map/ppermute | solution.py:173
  72.1 1.3 %collective-permute-start.20 = (bf16[3,96,384]{2,1,0:T(8,128)(2,1)S(1)}, bf16[3,96,384]{2,1,0:T(8,128)(2,1)S(1)}, u32[]{:S(2)}, u32[]{:S(2)}) collective-permute-start(bf16[3,96,384]{2,1,0:T(8,128)(2,1)S(1)} %collective-permute-done.16.refs_2_), channel_id=1, source_target_pairs={{0,4},{1,5},{2,6},{3,7},{4,0},{5,1},{6,2},{7,3},{8,12},{9,13},{10,... | collective-permute-start | bytes 663560 | tf_op jit(solution)/shard_map/ppermute | solution.py:173
  73.4 2.0 %collective-permute-start.22 = (f32[2,96,128]{2,1,0:T(8,128)S(1)}, f32[2,96,128]{2,1,0:T(8,128)S(1)}, u32[]{:S(2)}, u32[]{:S(2)}) collective-permute-start(f32[2,96,128]{2,1,0:T(8,128)S(1)} %get-tuple-element.81), channel_id=1, source_target_pairs={{0,4},{1,5},{2,6},{3,7},{4,0},{5,1},{6,2},{7,3},{8,12},{9,13},{10,... | collective-permute-start | bytes 294920 | tf_op jit(solution)/shard_map/ppermute | solution.py:173
  75.4 5.1 %collective-permute-done.22 = f32[2,96,128]{2,1,0:T(8,128)S(1)} collective-permute-done((f32[2,96,128]{2,1,0:T(8,128)S(1)}, f32[2,96,128]{2,1,0:T(8,128)S(1)}, u32[]{:S(2)}, u32[]{:S(2)}) %collective-permute-start.22) | collective-permute-done | bytes 98336 | tf_op jit(solution)/shard_map/ppermute | solution.py:173
  80.5 2.2 %shard_map.99 = (bf16[3,384,384]{2,1,0:T(8,128)(2,1)S(1)}, f32[2,192,128]{2,1,0:T(8,128)S(1)}, bf16[2,192,128]{2,1,0:T(8,128)(2,1)S(1)}) custom-call(s32[3]{0:T(128)S(1)} %pad_add_fusion.place, bf16[3,384,384]{2,1,0:T(8,128)(2,1)S(1)} %shard_map.95.weights, bf16[3,96,384]{2,1,0:T(8,128)(2,1)S(1)} %get-tuple-element.61.refs_0_, ...), custom_call_target="tpu_custom_call" | custom-call | flops 226492416 | bytes 6291468 | tf_op jit(solution)/shard_map/pallas_call | solution.py:150
  82.8 1.3 %collective-permute-done.23 = bf16[2,192,128]{2,1,0:T(8,128)(2,1)S(1)} collective-permute-done((bf16[2,192,128]{2,1,0:T(8,128)(2,1)S(1)}, bf16[2,192,128]{2,1,0:T(8,128)(2,1)S(1)}, u32[]{:S(2)}, u32[]{:S(2)}) %collective-permute-start.23) | collective-permute-done | bytes 98336 | tf_op jit(solution)/shard_map/ppermute | solution.py:173
  84.7 1.3 %shard_map.100 = (f32[2,192,128]{2,1,0:T(8,128)S(1)}, bf16[2,192,128]{2,1,0:T(8,128)(2,1)S(1)}) custom-call(s32[3]{0:T(128)S(1)} %pad_add_fusion.place, bf16[3,384,384]{2,1,0:T(8,128)(2,1)S(1)} %get-tuple-element.66.renewed, bf16[2,192,128]{2,1,0:T(8,128)(2,1)S(1)} %pad_maximum_fusion.3.mine, bf16[2,192,128]{2,1,0:T(8,128)(2,1)S(1)} %collective-permute-done.11.other), custom_call_target="tpu_custom_call" | custom-call | flops 226492416 | bytes 2555916 | tf_op jit(solution)/shard_map/pallas_call | solution.py:150
  86.1 3.0 %collective-permute-done.25.pair = bf16[2,192,128]{2,1,0:T(8,128)(2,1)S(1)} collective-permute-done((bf16[2,192,128]{2,1,0:T(8,128)(2,1)S(1)}, bf16[2,192,128]{2,1,0:T(8,128)(2,1)S(1)}, u32[]{:S(2)}, u32[]{:S(2)}) %collective-permute-start.25) | collective-permute-done | bytes 98336 | tf_op jit(solution)/shard_map/ppermute | solution.py:173
  (46 shorter events, 8.9 us)
Async XLA Ops:
  0.6 5.2 %copy-start = (bf16[1024,192]{0,1:T(8,128)(2,1)S(1)}, bf16[1024,192]{0,1:T(8,128)(2,1)}, u32[]{:S(2)}) copy-start(bf16[1024,192]{0,1:T(8,128)(2,1)} %param.8) | copy-start | bytes 1179652
  1.7 6.1 %collective-permute-start = (bf16[3,48,384]{2,1,0:T(8,128)(2,1)S(1)}, bf16[3,48,384]{2,1,0:T(8,128)(2,1)S(1)}, u32[]{:S(2)}, u32[]{:S(2)}) collective-permute-start(bf16[3,48,384]{2,1,0:T(8,128)(2,1)S(1)} %get-tuple-element.79), channel_id=1, source_target_pairs={{0,2},{1,3},{2,0},{3,1},{4,6},{5,7},{6,4},{7,5},{8,10},{9,11},{10,... | collective-permute-start | bytes 331784 | tf_op jit(solution)/shard_map/ppermute | solution.py:173
  5.8 23.6 %copy-start.1 = (bf16[128,192]{0,1:T(8,128)(2,1)S(1)}, bf16[128,192]{0,1:T(8,128)(2,1)}, u32[]{:S(2)}) copy-start(bf16[128,192]{0,1:T(8,128)(2,1)} %param.15) | copy-start | bytes 147460
  5.8 23.6 %copy-start.2 = (bf16[128,192]{0,1:T(8,128)(2,1)S(1)}, bf16[128,192]{0,1:T(8,128)(2,1)}, u32[]{:S(2)}) copy-start(bf16[128,192]{0,1:T(8,128)(2,1)} %param.14) | copy-start | bytes 147460
  7.8 21.4 %collective-permute-start.1 = (bf16[2,192,1024]{2,1,0:T(8,128)(2,1)S(1)}, bf16[2,192,1024]{2,1,0:T(8,128)(2,1)S(1)}, u32[]{:S(2)}, u32[]{:S(2)}) collective-permute-start(bf16[2,192,1024]{2,1,0:T(8,128)(2,1)S(1)} %pad_maximum_fusion.mine), channel_id=1, source_target_pairs={{0,2},{1,3},{2,0},{3,1},{4,6},{5,7},{6,4},{7,5},{8,10},{9,11},{10,... | collective-permute-start | bytes 2359304 | tf_op jit(solution)/shard_map/ppermute | solution.py:173
  9.5 5.8 %collective-permute-start.2 = (bf16[3,48,384]{2,1,0:T(8,128)(2,1)S(1)}, bf16[3,48,384]{2,1,0:T(8,128)(2,1)S(1)}, u32[]{:S(2)}, u32[]{:S(2)}) collective-permute-start(bf16[3,48,384]{2,1,0:T(8,128)(2,1)S(1)} %get-tuple-element.78.refs_0_), channel_id=1, source_target_pairs={{0,4},{1,5},{2,6},{3,7},{4,0},{5,1},{6,2},{7,3},{8,12},{9,13},{10,... | collective-permute-start | bytes 331784 | tf_op jit(solution)/shard_map/ppermute | solution.py:173
  11.1 9.2 %collective-permute-start.3 = (bf16[3,48,384]{2,1,0:T(8,128)(2,1)S(1)}, bf16[3,48,384]{2,1,0:T(8,128)(2,1)S(1)}, u32[]{:S(2)}, u32[]{:S(2)}) collective-permute-start(bf16[3,48,384]{2,1,0:T(8,128)(2,1)S(1)} %get-tuple-element.78.refs_0_), channel_id=1, source_target_pairs={{0,8},{1,9},{2,10},{3,11},{4,12},{5,13},{6,14},{7,15},{8,0},{9,1},... | collective-permute-start | bytes 331784 | tf_op jit(solution)/shard_map/ppermute | solution.py:173
  15.3 6.8 %collective-permute-start.6 = (bf16[3,48,384]{2,1,0:T(8,128)(2,1)S(1)}, bf16[3,48,384]{2,1,0:T(8,128)(2,1)S(1)}, u32[]{:S(2)}, u32[]{:S(2)}) collective-permute-start(bf16[3,48,384]{2,1,0:T(8,128)(2,1)S(1)} %collective-permute-done.refs_4_), channel_id=1, source_target_pairs={{0,8},{1,9},{2,10},{3,11},{4,12},{5,13},{6,14},{7,15},{8,0},{9,1},... | collective-permute-start | bytes 331784 | tf_op jit(solution)/shard_map/ppermute | solution.py:173
  17.0 12.4 %collective-permute-start.9 = (bf16[2,192,1024]{2,1,0:T(8,128)(2,1)S(1)}, bf16[2,192,1024]{2,1,0:T(8,128)(2,1)S(1)}, u32[]{:S(2)}, u32[]{:S(2)}) collective-permute-start(bf16[2,192,1024]{2,1,0:T(8,128)(2,1)S(1)} %pad_maximum_fusion.mine), channel_id=1, source_target_pairs={{0,1},{1,0},{2,3},{3,2},{4,5},{5,4},{6,7},{7,6},{8,9},{9,8},{10,11... | collective-permute-start | bytes 2359304 | tf_op jit(solution)/shard_map/ppermute | solution.py:173
  17.0 6.9 %collective-permute-start.5 = (bf16[3,48,384]{2,1,0:T(8,128)(2,1)S(1)}, bf16[3,48,384]{2,1,0:T(8,128)(2,1)S(1)}, u32[]{:S(2)}, u32[]{:S(2)}) collective-permute-start(bf16[3,48,384]{2,1,0:T(8,128)(2,1)S(1)} %collective-permute-done.refs_4_), channel_id=1, source_target_pairs={{0,4},{1,5},{2,6},{3,7},{4,0},{5,1},{6,2},{7,3},{8,12},{9,13},{10,... | collective-permute-start | bytes 331784 | tf_op jit(solution)/shard_map/ppermute | solution.py:173
  20.3 6.0 %collective-permute-start.4 = (bf16[3,48,384]{2,1,0:T(8,128)(2,1)S(1)}, bf16[3,48,384]{2,1,0:T(8,128)(2,1)S(1)}, u32[]{:S(2)}, u32[]{:S(2)}) collective-permute-start(bf16[3,48,384]{2,1,0:T(8,128)(2,1)S(1)} %collective-permute-done.3.refs_2_), channel_id=1, source_target_pairs={{0,4},{1,5},{2,6},{3,7},{4,0},{5,1},{6,2},{7,3},{8,12},{9,13},{10,... | collective-permute-start | bytes 331784 | tf_op jit(solution)/shard_map/ppermute | solution.py:173
  22.1 6.5 %collective-permute-start.7 = (bf16[3,48,384]{2,1,0:T(8,128)(2,1)S(1)}, bf16[3,48,384]{2,1,0:T(8,128)(2,1)S(1)}, u32[]{:S(2)}, u32[]{:S(2)}) collective-permute-start(bf16[3,48,384]{2,1,0:T(8,128)(2,1)S(1)} %collective-permute-done.6.refs_6_), channel_id=1, source_target_pairs={{0,4},{1,5},{2,6},{3,7},{4,0},{5,1},{6,2},{7,3},{8,12},{9,13},{10,... | collective-permute-start | bytes 331784 | tf_op jit(solution)/shard_map/ppermute | solution.py:173
  29.3 3.9 %collective-permute-start.8 = (bf16[2,192,1024]{2,1,0:T(8,128)(2,1)S(1)}, bf16[2,192,1024]{2,1,0:T(8,128)(2,1)S(1)}, u32[]{:S(2)}, u32[]{:S(2)}) collective-permute-start(bf16[2,192,1024]{2,1,0:T(8,128)(2,1)S(1)} %collective-permute-done.1.mine), channel_id=1, source_target_pairs={{0,1},{1,0},{2,3},{3,2},{4,5},{5,4},{6,7},{7,6},{8,9},{9,8},{10,11... | collective-permute-start | bytes 2359304 | tf_op jit(solution)/shard_map/ppermute | solution.py:173
  37.0 7.9 %collective-permute-start.10 = (bf16[3,96,384]{2,1,0:T(8,128)(2,1)S(1)}, bf16[3,96,384]{2,1,0:T(8,128)(2,1)S(1)}, u32[]{:S(2)}, u32[]{:S(2)}) collective-permute-start(bf16[3,96,384]{2,1,0:T(8,128)(2,1)S(1)} %get-tuple-element.52), channel_id=1, source_target_pairs={{0,4},{1,5},{2,6},{3,7},{4,0},{5,1},{6,2},{7,3},{8,12},{9,13},{10,... | collective-permute-start | bytes 663560 | tf_op jit(solution)/shard_map/ppermute | solution.py:173
  37.3 1.9 %collective-permute-start.11 = (bf16[2,192,128]{2,1,0:T(8,128)(2,1)S(1)}, bf16[2,192,128]{2,1,0:T(8,128)(2,1)S(1)}, u32[]{:S(2)}, u32[]{:S(2)}) collective-permute-start(bf16[2,192,128]{2,1,0:T(8,128)(2,1)S(1)} %pad_maximum_fusion.3.mine), channel_id=1, source_target_pairs={{0,1},{1,0},{2,3},{3,2},{4,5},{5,4},{6,7},{7,6},{8,9},{9,8},{10,11... | collective-permute-start | bytes 294920 | tf_op jit(solution)/shard_map/ppermute | solution.py:173
  37.6 5.6 %collective-permute-start.12 = (bf16[2,192,128]{2,1,0:T(8,128)(2,1)S(1)}, bf16[2,192,128]{2,1,0:T(8,128)(2,1)S(1)}, u32[]{:S(2)}, u32[]{:S(2)}) collective-permute-start(bf16[2,192,128]{2,1,0:T(8,128)(2,1)S(1)} %pad_maximum_fusion.3.mine), channel_id=1, source_target_pairs={{0,2},{1,3},{2,0},{3,1},{4,6},{5,7},{6,4},{7,5},{8,10},{9,11},{10,... | collective-permute-start | bytes 294920 | tf_op jit(solution)/shard_map/ppermute | solution.py:173
  38.0 5.9 %collective-permute-start.13 = (bf16[2,192,128]{2,1,0:T(8,128)(2,1)S(1)}, bf16[2,192,128]{2,1,0:T(8,128)(2,1)S(1)}, u32[]{:S(2)}, u32[]{:S(2)}) collective-permute-start(bf16[2,192,128]{2,1,0:T(8,128)(2,1)S(1)} %pad_maximum_fusion.3.mine), channel_id=1, source_target_pairs={{0,3},{1,2},{2,1},{3,0},{4,7},{5,6},{6,5},{7,4},{8,11},{9,10},{10,... | collective-permute-start | bytes 294920 | tf_op jit(solution)/shard_map/ppermute | solution.py:173
  44.9 12.1 %collective-permute-start.14 = (bf16[3,96,384]{2,1,0:T(8,128)(2,1)S(1)}, bf16[3,96,384]{2,1,0:T(8,128)(2,1)S(1)}, u32[]{:S(2)}, u32[]{:S(2)}) collective-permute-start(bf16[3,96,384]{2,1,0:T(8,128)(2,1)S(1)} %get-tuple-element.56), channel_id=1, source_target_pairs={{0,4},{1,5},{2,6},{3,7},{4,0},{5,1},{6,2},{7,3},{8,12},{9,13},{10,... | collective-permute-start | bytes 663560 | tf_op jit(solution)/shard_map/ppermute | solution.py:173
  45.9 11.0 %collective-permute-start.15 = (bf16[3,96,384]{2,1,0:T(8,128)(2,1)S(1)}, bf16[3,96,384]{2,1,0:T(8,128)(2,1)S(1)}, u32[]{:S(2)}, u32[]{:S(2)}) collective-permute-start(bf16[3,96,384]{2,1,0:T(8,128)(2,1)S(1)} %add_convert_fusion), channel_id=1, source_target_pairs={{0,8},{1,9},{2,10},{3,11},{4,12},{5,13},{6,14},{7,15},{8,0},{9,1},... | collective-permute-start | bytes 663560 | tf_op jit(solution)/shard_map/ppermute | solution.py:173
  57.7 2.6 %collective-permute-start.17 = (f32[96,128]{1,0:T(8,128)S(1)}, f32[96,128]{1,0:T(8,128)S(1)}, u32[]{:S(2)}, u32[]{:S(2)}) collective-permute-start(f32[96,128]{1,0:T(8,128)S(1)} %get-tuple-element.59), channel_id=1, source_target_pairs={{0,1},{1,0},{2,3},{3,2},{4,5},{5,4},{6,7},{7,6},{8,9},{9,8},{10,11... | collective-permute-start | bytes 147464 | tf_op jit(solution)/shard_map/ppermute | solution.py:173
  57.8 14.0 %collective-permute-start.16 = (bf16[3,96,384]{2,1,0:T(8,128)(2,1)S(1)}, bf16[3,96,384]{2,1,0:T(8,128)(2,1)S(1)}, u32[]{:S(2)}, u32[]{:S(2)}) collective-permute-start(bf16[3,96,384]{2,1,0:T(8,128)(2,1)S(1)} %get-tuple-element.61.refs_0_), channel_id=1, source_target_pairs={{0,8},{1,9},{2,10},{3,11},{4,12},{5,13},{6,14},{7,15},{8,0},{9,1},... | collective-permute-start | bytes 663560 | tf_op jit(solution)/shard_map/ppermute | solution.py:173
  60.4 11.7 %collective-permute-start.18 = (bf16[3,96,384]{2,1,0:T(8,128)(2,1)S(1)}, bf16[3,96,384]{2,1,0:T(8,128)(2,1)S(1)}, u32[]{:S(2)}, u32[]{:S(2)}) collective-permute-start(bf16[3,96,384]{2,1,0:T(8,128)(2,1)S(1)} %get-tuple-element.61.refs_0_), channel_id=1, source_target_pairs={{0,4},{1,5},{2,6},{3,7},{4,0},{5,1},{6,2},{7,3},{8,12},{9,13},{10,... | collective-permute-start | bytes 663560 | tf_op jit(solution)/shard_map/ppermute | solution.py:173
  63.5 4.1 %collective-permute-start.19 = (f32[96,128]{1,0:T(8,128)S(1)}, f32[96,128]{1,0:T(8,128)S(1)}, u32[]{:S(2)}, u32[]{:S(2)}) collective-permute-start(f32[96,128]{1,0:T(8,128)S(1)} %add.27), channel_id=1, source_target_pairs={{0,2},{1,3},{2,0},{3,1},{4,6},{5,7},{6,4},{7,5},{8,10},{9,11},{10,... | collective-permute-start | bytes 147464 | tf_op jit(solution)/shard_map/ppermute | solution.py:173
  67.6 5.8 %collective-permute-start.21 = (f32[1,96,128]{2,1,0:T(8,128)S(1)}, f32[1,96,128]{2,1,0:T(8,128)S(1)}, u32[]{:S(2)}, u32[]{:S(2)}) collective-permute-start(f32[1,96,128]{2,1,0:T(8,128)S(1)} %bitcast.32), channel_id=1, source_target_pairs={{0,8},{1,9},{2,10},{3,11},{4,12},{5,13},{6,14},{7,15},{8,0},{9,1},... | collective-permute-start | bytes 147464 | tf_op jit(solution)/shard_map/ppermute | solution.py:173
  72.1 8.4 %collective-permute-start.20 = (bf16[3,96,384]{2,1,0:T(8,128)(2,1)S(1)}, bf16[3,96,384]{2,1,0:T(8,128)(2,1)S(1)}, u32[]{:S(2)}, u32[]{:S(2)}) collective-permute-start(bf16[3,96,384]{2,1,0:T(8,128)(2,1)S(1)} %collective-permute-done.16.refs_2_), channel_id=1, source_target_pairs={{0,4},{1,5},{2,6},{3,7},{4,0},{5,1},{6,2},{7,3},{8,12},{9,13},{10,... | collective-permute-start | bytes 663560 | tf_op jit(solution)/shard_map/ppermute | solution.py:173
  73.4 7.0 %collective-permute-start.22 = (f32[2,96,128]{2,1,0:T(8,128)S(1)}, f32[2,96,128]{2,1,0:T(8,128)S(1)}, u32[]{:S(2)}, u32[]{:S(2)}) collective-permute-start(f32[2,96,128]{2,1,0:T(8,128)S(1)} %get-tuple-element.81), channel_id=1, source_target_pairs={{0,4},{1,5},{2,6},{3,7},{4,0},{5,1},{6,2},{7,3},{8,12},{9,13},{10,... | collective-permute-start | bytes 294920 | tf_op jit(solution)/shard_map/ppermute | solution.py:173
  82.7 1.4 %collective-permute-start.23 = (bf16[2,192,128]{2,1,0:T(8,128)(2,1)S(1)}, bf16[2,192,128]{2,1,0:T(8,128)(2,1)S(1)}, u32[]{:S(2)}, u32[]{:S(2)}) collective-permute-start(bf16[2,192,128]{2,1,0:T(8,128)(2,1)S(1)} %get-tuple-element.67), channel_id=1, source_target_pairs={{0,1},{1,0},{2,3},{3,2},{4,5},{5,4},{6,7},{7,6},{8,9},{9,8},{10,11... | collective-permute-start | bytes 294920 | tf_op jit(solution)/shard_map/ppermute | solution.py:173
  84.1 4.9 %collective-permute-start.25 = (bf16[2,192,128]{2,1,0:T(8,128)(2,1)S(1)}, bf16[2,192,128]{2,1,0:T(8,128)(2,1)S(1)}, u32[]{:S(2)}, u32[]{:S(2)}) collective-permute-start(bf16[2,192,128]{2,1,0:T(8,128)(2,1)S(1)} %add_convert_fusion.1), channel_id=1, source_target_pairs={{0,2},{1,3},{2,0},{3,1},{4,6},{5,7},{6,4},{7,5},{8,10},{9,11},{10,... | collective-permute-start | bytes 294920 | tf_op jit(solution)/shard_map/ppermute | solution.py:173
  86.0 3.1 %collective-permute-start.24 = (bf16[2,192,128]{2,1,0:T(8,128)(2,1)S(1)}, bf16[2,192,128]{2,1,0:T(8,128)(2,1)S(1)}, u32[]{:S(2)}, u32[]{:S(2)}) collective-permute-start(bf16[2,192,128]{2,1,0:T(8,128)(2,1)S(1)} %get-tuple-element.73), channel_id=1, source_target_pairs={{0,1},{1,0},{2,3},{3,2},{4,5},{5,4},{6,7},{7,6},{8,9},{9,8},{10,11... | collective-permute-start | bytes 294920 | tf_op jit(solution)/shard_map/ppermute | solution.py:173

commit v5 on v4

--- a/solution.py
+++ b/solution.py
@@ -31,26 +31,20 @@
     full[:, pl.ds(pl.multiple_of((1 - half) * feats, feats), feats), :] = other[...]
 
 
-def add_grads(tokens, weights, grads, fresh):
-    total = tokens.shape[2]
+def gradients(tokens, weights, deltas, acts):
+    cols, total = acts.shape
     chunk = min(512, total)
     for start in range(0, total, chunk):
-        key = tokens[0, :, start : start + chunk]
-        val = tokens[1, :, start : start + chunk]
-        gate = contract(weights[0], key, 0, 0)
-        up = contract(weights[1], key, 0, 0)
-        back = contract(weights[2], val, 0, 0)
+        span = slice(start, start + chunk)
+        gate = contract(weights[0], tokens[0, :, span], 0, 0)
+        up = contract(weights[1], tokens[0, :, span], 0, 0)
+        back = contract(weights[2], tokens[1, :, span], 0, 0)
         silu, slope_up, act = gated(gate, up)
-        parts = (
-            contract(key, (back * slope_up).astype(bf16), 1, 1),
-            contract(key, (back * silu).astype(bf16), 1, 1),
-            contract(val, act.astype(bf16), 1, 1),
-        )
-        for index, part in enumerate(parts):
-            if fresh and start == 0:
-                grads[index] = part
-            else:
-                grads[index] += part
+        deltas[:cols, span] = (back * slope_up).astype(bf16)
+        deltas[cols:, span] = (back * silu).astype(bf16)
+        acts[:, span] = act.astype(bf16)
+    both = contract(tokens[0], deltas[...], 1, 1)
+    return both[:, :cols], both[:, cols:], contract(tokens[1], acts[...], 1, 1)
 
 
 def rows_kernel(groups, place, *refs):
@@ -61,19 +55,19 @@
         weights[:, rows_of((group ^ flip) * 2 + sided, block.shape[1]), :] = block[...]
 
 
-def own_kernel(place, mine, other, weights, grads, tokens):
+def own_kernel(place, mine, other, weights, grads, tokens, deltas, acts):
     join(tokens, mine, other, place[2])
-    add_grads(tokens, weights, grads, True)
+    for index, grad in enumerate(gradients(tokens, weights, deltas, acts)):
+        grads[index] = grad
 
 
 def pair_kernel(groups, place, mine, other, weights, before, *refs):
-    outs, (grads, tokens) = refs[:groups], refs[groups:]
-    group, half = place[0], place[2]
-    grads[...] = before[...]
-    join(tokens, mine, other, half)
-    add_grads(tokens, weights, grads, False)
+    outs, (grads, tokens, deltas, acts) = refs[:groups], refs[groups:]
+    join(tokens, mine, other, place[2])
+    for index, grad in enumerate(gradients(tokens, weights, deltas, acts)):
+        grads[index] = before[index] + grad
     for flip, out in enumerate(outs):
-        out[...] = grads[:, rows_of(group ^ flip, out.shape[1]), :].astype(out.dtype)
+        out[...] = grads[:, rows_of(place[0] ^ flip, out.shape[1]), :].astype(out.dtype)
 
 
 def rows_of(owner, rows):
@@ -93,8 +87,19 @@
         weight = weights[index, where, :].astype(f32)
         for slot, product in enumerate((weight * weight, weight * grad, grad * grad)):
             row_sum = jnp.sum(product, axis=1, keepdims=True)
-            stats = jnp.where(lane == 3 * index + slot, row_sum, stats)
+            stats = jnp.where(lane == 3 * slot + index, row_sum, stats)
     stats_out[...] = stats
+
+
+def factor_kernel(hidden, here, there, factors):
+    wsq = (here[...] + there[...]) / hidden
+    lane = lax.broadcasted_iota(jnp.int32, wsq.shape, 1)
+    lanes = wsq.shape[1]
+    cross, gsq = pltpu.roll(wsq, lanes - 3, 1), pltpu.roll(wsq, lanes - 6, 1)
+    scale = step_ratio * jnp.sqrt(wsq) / jnp.sqrt(gsq + epsilon)
+    msq = wsq + 2.0 * scale * cross + scale * scale * gsq
+    factor = jnp.sqrt(wsq) / jnp.sqrt(msq + epsilon)
+    factors[...] = jnp.where(lane < 3, factor, pltpu.roll(scale * factor, 3, 1))
 
 
 def answer(renewed, query, quests, half, kept, given):
@@ -115,21 +120,15 @@
         given[index] = jnp.where(half == 0, second, first).astype(bf16)
 
 
-def renew_kernel(groups, hidden, place, weights, *refs):
-    grads, stats, quests, refs = refs[:groups], refs[groups], refs[groups + 1 : groups + 3], refs[groups + 3 :]
+def renew_kernel(groups, place, weights, *refs):
+    grads, factors, quests, refs = refs[:groups], refs[groups], refs[groups + 1 : groups + 3], refs[groups + 3 :]
     renewed, kept, given, query = refs
     for flip in range(groups):
         where = rows_of(place[0] ^ flip, grads[0].shape[1])
-        sums = stats[flip] / hidden
         for index in range(3):
-            wsq = sums[:, 3 * index : 3 * index + 1]
-            cross = sums[:, 3 * index + 1 : 3 * index + 2]
-            gsq = sums[:, 3 * index + 2 : 3 * index + 3]
-            scale = step_ratio * jnp.sqrt(wsq) / jnp.sqrt(gsq + epsilon)
-            msq = wsq + 2.0 * scale * cross + scale * scale * gsq
-            factor = jnp.sqrt(wsq) / jnp.sqrt(msq + epsilon)
-            moved = weights[index, where, :].astype(f32) + scale * grads[flip][index].astype(f32)
-            renewed[index, where, :] = (moved * factor).astype(bf16)
+            old = weights[index, where, :].astype(f32) * factors[flip, :, index : index + 1]
+            step = grads[flip][index].astype(f32) * factors[flip, :, 3 + index : 4 + index]
+            renewed[index, where, :] = (old + step).astype(bf16)
     answer(renewed, query, quests, place[2], kept, given)
 
 
@@ -195,7 +194,6 @@
     _, feats, toks = tokens.shape
     first = gather(own_w)
     tokens, pair_w = lax.optimization_barrier((tokens, swap(give_w, pair)))
-    pair_w, _ = lax.optimization_barrier((pair_w, first[1]))
     second = gather(pair_w)
     pair_tokens = swap(tokens, pair)
 
@@ -204,7 +202,11 @@
     whole = (3, width, cols)
     block = (3, rows, cols)
     token_flops = 6 * 2 * toks * width * cols
-    joined = pltpu.VMEM((2, width, toks), bf16)
+    joined = [
+        pltpu.VMEM((2, width, toks), bf16),
+        pltpu.VMEM((2 * cols, toks), bf16),
+        pltpu.VMEM((cols, toks), bf16),
+    ]
     (weights,) = call(
         functools.partial(rows_kernel, groups),
         (*first, *second),
@@ -216,7 +218,7 @@
         own_kernel,
         (tokens, swap(tokens, core), weights),
         (jax.ShapeDtypeStruct(whole, f32),),
-        [joined],
+        joined,
         token_flops,
         place,
         16,
@@ -225,7 +227,7 @@
         functools.partial(pair_kernel, groups),
         (pair_tokens, swap(pair_tokens, core), weights, grads),
         [jax.ShapeDtypeStruct(block, bf16 if flip & 1 else f32) for flip in range(groups)],
-        [pltpu.VMEM(whole, f32), joined],
+        [pltpu.VMEM(whole, f32), *joined],
         token_flops,
         place,
         16,
@@ -249,12 +251,16 @@
         (jax.ShapeDtypeStruct(block, bf16), jax.ShapeDtypeStruct((rows, 128), f32)),
         place=place,
     )
-    stats = near_stats = stats + swap(stats, core)
-    stats = stats + swap(stats, pair)
-    all_stats, bit = stats[None], groups // 2
+    stats = stats + swap(stats, core)
+    (factors,) = call(
+        functools.partial(factor_kernel, 2 * n_hid * cols),
+        (stats, swap(stats, pair)),
+        (jax.ShapeDtypeStruct(stats.shape, f32),),
+    )
+    all_factors, bit = factors[None], groups // 2
     while bit:
-        all_stats = jnp.stack([all_stats, swap(all_stats, zed * bit)], axis=1)
-        all_stats = all_stats.reshape(-1, *stats.shape)
+        all_factors = jnp.stack([all_factors, swap(all_factors, zed * bit)], axis=1)
+        all_factors = all_factors.reshape(-1, *stats.shape)
         bit //= 2
 
     count = queries.shape[0]
@@ -263,8 +269,8 @@
     query = pltpu.VMEM((2, width, count), bf16)
     query_flops = 6 * 2 * count * width * cols
     renewed, kept, given = call(
-        functools.partial(renew_kernel, groups, 2 * n_hid * cols),
-        (weights, *gather(grad, [near_stats], [stats]), all_stats, *quests[2:]),
+        functools.partial(renew_kernel, groups),
+        (weights, *gather(grad, [stats], [factors]), all_factors, *quests[2:]),
         [jax.ShapeDtypeStruct(whole, bf16), *kept_given],
         [query],
         query_flops,

time: 89.8 us -> 88.5 us (0.986); the launches traced: 89.7 us -> 87.5 us
  waiting for transfers between devices: 42 us -> 40 us
    ppermute x26, waiting for transfers between devices: 42 us -> 40 us  [swap(): return lax.ppermute(array, ('tok', 'hid'), pairs)]
    pallas_call x7 -> x8, Pallas kernels: 13.1 us -> 12.3 us  [call(): pl.pallas_call(body, out_shape=list(outs), in_specs=specs, out_specs=[pl....]
where the time goes in v5:
time: 88.5 us; the launch traced here: 87.5 us
  waiting for transfers between devices  40 us (45%)
  starting transfers between devices  31.8 us (36%)
  Pallas kernels  12.3 us (14%)
  other arithmetic  2.38 us (3%)
  between operations  0.9 us (1%)
    ppermute x26, waiting for transfers between devices, swap(): return lax.ppermute(array, ('tok', 'hid'), pairs)  40 us
    ppermute x26, starting transfers between devices, swap(): return lax.ppermute(array, ('tok', 'hid'), pairs)  31.8 us
    pallas_call x8, Pallas kernels, call(): pl.pallas_call(body, out_shape=list(outs), in_specs=specs, out_specs=[pl....  12.3 us
  transfers between devices with their start and end apart: 26, of which 16 were waited for; matrix products, arithmetic and copies ran while one was open for 1% of the time, Pallas kernels for 6%

profile of v5, /device:TPU:0, one launch (start us, length us, event | category | flops | bytes accessed | tf_op | source)
XLA Modules:
  0.0 87.5 jit_solution(6908631178569274251)
XLA Ops:
  0.7 1.0 %pad_maximum_fusion.1 = bf16[3,48,768]{2,1,0:T(8,128)(2,1)S(1)} fusion(bf16[1,48,768]{2,1,0:T(8,128)(2,1)} %bitcast.35, bf16[1,48,768]{2,1,0:T(8,128)(2,1)} %bitcast.36, bf16[1,48,768]{2,1,0:T(8,128)(2,1)} %bitcast.37), kind=kLoop, calls=%fused_computation.4 | loop fusion | flops 221184 | bytes 442368 | tf_op jit(solution)/shard_map/stack | solution.py:188
  1.7 3.0 %collective-permute-start = (bf16[3,48,384]{2,1,0:T(8,128)(2,1)S(1)}, bf16[3,48,384]{2,1,0:T(8,128)(2,1)S(1)}, u32[]{:S(2)}, u32[]{:S(2)}) collective-permute-start(bf16[3,48,384]{2,1,0:T(8,128)(2,1)S(1)} %get-tuple-element.77), channel_id=1, source_target_pairs={{0,2},{1,3},{2,0},{3,1},{4,6},{5,7},{6,4},{7,5},{8,10},{9,11},{10,... | collective-permute-start | bytes 331784 | tf_op jit(solution)/shard_map/ppermute | solution.py:172
  4.7 1.1 %fusion = bf16[1,192,1024]{2,1,0:T(8,128)(2,1)S(1)} fusion(bf16[1024,192]{0,1:T(8,128)(2,1)} %param.9, f32[1024]{0:T(1024)} %param.10), kind=kLoop, calls=%fused_computation.3 | loop fusion | flops 589824 | bytes 790528 | tf_op jit(solution)/shard_map/stack | solution.py:193
  5.9 1.9 %collective-permute-done.refs_4_ = bf16[3,48,384]{2,1,0:T(8,128)(2,1)S(1)} collective-permute-done((bf16[3,48,384]{2,1,0:T(8,128)(2,1)S(1)}, bf16[3,48,384]{2,1,0:T(8,128)(2,1)S(1)}, u32[]{:S(2)}, u32[]{:S(2)}) %collective-permute-start) | collective-permute-done | bytes 110624 | tf_op jit(solution)/shard_map/ppermute | solution.py:172
  7.8 1.7 %collective-permute-start.1 = (bf16[2,192,1024]{2,1,0:T(8,128)(2,1)S(1)}, bf16[2,192,1024]{2,1,0:T(8,128)(2,1)S(1)}, u32[]{:S(2)}, u32[]{:S(2)}) collective-permute-start(bf16[2,192,1024]{2,1,0:T(8,128)(2,1)S(1)} %pad_maximum_fusion.mine), channel_id=1, source_target_pairs={{0,2},{1,3},{2,0},{3,1},{4,6},{5,7},{6,4},{7,5},{8,10},{9,11},{10,... | collective-permute-start | bytes 2359304 | tf_op jit(solution)/shard_map/ppermute | solution.py:172
  9.5 2.6 %collective-permute-start.3 = (bf16[3,48,384]{2,1,0:T(8,128)(2,1)S(1)}, bf16[3,48,384]{2,1,0:T(8,128)(2,1)S(1)}, u32[]{:S(2)}, u32[]{:S(2)}) collective-permute-start(bf16[3,48,384]{2,1,0:T(8,128)(2,1)S(1)} %get-tuple-element.76.refs_0_), channel_id=1, source_target_pairs={{0,8},{1,9},{2,10},{3,11},{4,12},{5,13},{6,14},{7,15},{8,0},{9,1},... | collective-permute-start | bytes 331784 | tf_op jit(solution)/shard_map/ppermute | solution.py:172
  12.1 1.6 %collective-permute-start.2 = (bf16[3,48,384]{2,1,0:T(8,128)(2,1)S(1)}, bf16[3,48,384]{2,1,0:T(8,128)(2,1)S(1)}, u32[]{:S(2)}, u32[]{:S(2)}) collective-permute-start(bf16[3,48,384]{2,1,0:T(8,128)(2,1)S(1)} %get-tuple-element.76.refs_0_), channel_id=1, source_target_pairs={{0,4},{1,5},{2,6},{3,7},{4,0},{5,1},{6,2},{7,3},{8,12},{9,13},{10,... | collective-permute-start | bytes 331784 | tf_op jit(solution)/shard_map/ppermute | solution.py:172
  14.0 3.8 %collective-permute-done.3.refs_2_ = bf16[3,48,384]{2,1,0:T(8,128)(2,1)S(1)} collective-permute-done((bf16[3,48,384]{2,1,0:T(8,128)(2,1)S(1)}, bf16[3,48,384]{2,1,0:T(8,128)(2,1)S(1)}, u32[]{:S(2)}, u32[]{:S(2)}) %collective-permute-start.3) | collective-permute-done | bytes 110624 | tf_op jit(solution)/shard_map/ppermute | solution.py:172
  17.8 1.8 %collective-permute-start.5 = (bf16[3,48,384]{2,1,0:T(8,128)(2,1)S(1)}, bf16[3,48,384]{2,1,0:T(8,128)(2,1)S(1)}, u32[]{:S(2)}, u32[]{:S(2)}) collective-permute-start(bf16[3,48,384]{2,1,0:T(8,128)(2,1)S(1)} %collective-permute-done.refs_4_), channel_id=1, source_target_pairs={{0,4},{1,5},{2,6},{3,7},{4,0},{5,1},{6,2},{7,3},{8,12},{9,13},{10,... | collective-permute-start | bytes 331784 | tf_op jit(solution)/shard_map/ppermute | solution.py:172
  20.4 1.0 %collective-permute-done.6.refs_6_ = bf16[3,48,384]{2,1,0:T(8,128)(2,1)S(1)} collective-permute-done((bf16[3,48,384]{2,1,0:T(8,128)(2,1)S(1)}, bf16[3,48,384]{2,1,0:T(8,128)(2,1)S(1)}, u32[]{:S(2)}, u32[]{:S(2)}) %collective-permute-start.6) | collective-permute-done | bytes 110624 | tf_op jit(solution)/shard_map/ppermute | solution.py:172
  22.0 1.2 %collective-permute-done.5.refs_5_ = bf16[3,48,384]{2,1,0:T(8,128)(2,1)S(1)} collective-permute-done((bf16[3,48,384]{2,1,0:T(8,128)(2,1)S(1)}, bf16[3,48,384]{2,1,0:T(8,128)(2,1)S(1)}, u32[]{:S(2)}, u32[]{:S(2)}) %collective-permute-start.5) | collective-permute-done | bytes 110624 | tf_op jit(solution)/shard_map/ppermute | solution.py:172
  23.2 2.2 %collective-permute-done.4.refs_3_ = bf16[3,48,384]{2,1,0:T(8,128)(2,1)S(1)} collective-permute-done((bf16[3,48,384]{2,1,0:T(8,128)(2,1)S(1)}, bf16[3,48,384]{2,1,0:T(8,128)(2,1)S(1)}, u32[]{:S(2)}, u32[]{:S(2)}) %collective-permute-start.4) | collective-permute-done | bytes 110624 | tf_op jit(solution)/shard_map/ppermute | solution.py:172
  25.3 1.4 %collective-permute-done.7.refs_7_ = bf16[3,48,384]{2,1,0:T(8,128)(2,1)S(1)} collective-permute-done((bf16[3,48,384]{2,1,0:T(8,128)(2,1)S(1)}, bf16[3,48,384]{2,1,0:T(8,128)(2,1)S(1)}, u32[]{:S(2)}, u32[]{:S(2)}) %collective-permute-start.7) | collective-permute-done | bytes 110624 | tf_op jit(solution)/shard_map/ppermute | solution.py:172
  27.5 3.3 %shard_map.96.before = f32[3,384,384]{2,1,0:T(8,128)S(1)} custom-call(s32[3]{0:T(128)S(1)} %pad_add_fusion.place, bf16[2,192,1024]{2,1,0:T(8,128)(2,1)S(1)} %pad_maximum_fusion.mine, bf16[2,192,1024]{2,1,0:T(8,128)(2,1)S(1)} %collective-permute-done.9.other, bf16[3,384,384]{2,1,0:T(8,128)(2,1)S(1)} %shard_map.95.weights), custom_call_target="tpu_custom_call" | custom-call | flops 1811939328 | bytes 6684684 | tf_op jit(solution)/shard_map/pallas_call | solution.py:149
  30.9 3.5 %shard_map.97 = (f32[3,96,384]{2,1,0:T(8,128)S(1)}, bf16[3,96,384]{2,1,0:T(8,128)(2,1)S(1)}, f32[3,96,384]{2,1,0:T(8,128)S(1)}, bf16[3,96,384]{2,1,0:T(8,128)(2,1)S(1)}) custom-call(s32[3]{0:T(128)S(1)} %pad_add_fusion.place, bf16[2,192,1024]{2,1,0:T(8,128)(2,1)S(1)} %collective-permute-done.1.mine, bf16[2,192,1024]{2,1,0:T(8,128)(2,1)S(1)} %collective-permute-done.8.other, ...), custom_call_target="tpu_custom_call" | custom-call | flops 1811939328 | bytes 8454156 | tf_op jit(solution)/shard_map/pallas_call | solution.py:149
  34.4 1.2 %collective-permute-start.10 = (bf16[3,96,384]{2,1,0:T(8,128)(2,1)S(1)}, bf16[3,96,384]{2,1,0:T(8,128)(2,1)S(1)}, u32[]{:S(2)}, u32[]{:S(2)}) collective-permute-start(bf16[3,96,384]{2,1,0:T(8,128)(2,1)S(1)} %get-tuple-element.50), channel_id=1, source_target_pairs={{0,4},{1,5},{2,6},{3,7},{4,0},{5,1},{6,2},{7,3},{8,12},{9,13},{10,... | collective-permute-start | bytes 663560 | tf_op jit(solution)/shard_map/ppermute | solution.py:172
  37.5 3.9 %collective-permute-done.12.refs_5_ = bf16[2,192,128]{2,1,0:T(8,128)(2,1)S(1)} collective-permute-done((bf16[2,192,128]{2,1,0:T(8,128)(2,1)S(1)}, bf16[2,192,128]{2,1,0:T(8,128)(2,1)S(1)}, u32[]{:S(2)}, u32[]{:S(2)}) %collective-permute-start.12) | collective-permute-done | bytes 98336 | tf_op jit(solution)/shard_map/ppermute | solution.py:172
  42.5 1.2 %collective-permute-start.14 = (bf16[3,96,384]{2,1,0:T(8,128)(2,1)S(1)}, bf16[3,96,384]{2,1,0:T(8,128)(2,1)S(1)}, u32[]{:S(2)}, u32[]{:S(2)}) collective-permute-start(bf16[3,96,384]{2,1,0:T(8,128)(2,1)S(1)} %get-tuple-element.54), channel_id=1, source_target_pairs={{0,4},{1,5},{2,6},{3,7},{4,0},{5,1},{6,2},{7,3},{8,12},{9,13},{10,... | collective-permute-start | bytes 663560 | tf_op jit(solution)/shard_map/ppermute | solution.py:172
  43.6 3.1 %collective-permute-start.15 = (bf16[3,96,384]{2,1,0:T(8,128)(2,1)S(1)}, bf16[3,96,384]{2,1,0:T(8,128)(2,1)S(1)}, u32[]{:S(2)}, u32[]{:S(2)}) collective-permute-start(bf16[3,96,384]{2,1,0:T(8,128)(2,1)S(1)} %add_convert_fusion), channel_id=1, source_target_pairs={{0,8},{1,9},{2,10},{3,11},{4,12},{5,13},{6,14},{7,15},{8,0},{9,1},... | collective-permute-start | bytes 663560 | tf_op jit(solution)/shard_map/ppermute | solution.py:172
  46.8 8.3 %collective-permute-done.14.refs_0_ = bf16[3,96,384]{2,1,0:T(8,128)(2,1)S(1)} collective-permute-done((bf16[3,96,384]{2,1,0:T(8,128)(2,1)S(1)}, bf16[3,96,384]{2,1,0:T(8,128)(2,1)S(1)}, u32[]{:S(2)}, u32[]{:S(2)}) %collective-permute-start.14) | collective-permute-done | bytes 221216 | tf_op jit(solution)/shard_map/ppermute | solution.py:172
  55.9 1.9 %collective-permute-start.16 = (bf16[3,96,384]{2,1,0:T(8,128)(2,1)S(1)}, bf16[3,96,384]{2,1,0:T(8,128)(2,1)S(1)}, u32[]{:S(2)}, u32[]{:S(2)}) collective-permute-start(bf16[3,96,384]{2,1,0:T(8,128)(2,1)S(1)} %get-tuple-element.59.refs_0_), channel_id=1, source_target_pairs={{0,8},{1,9},{2,10},{3,11},{4,12},{5,13},{6,14},{7,15},{8,0},{9,1},... | collective-permute-start | bytes 663560 | tf_op jit(solution)/shard_map/ppermute | solution.py:172
  57.8 4.1 %collective-permute-start.18 = (bf16[3,96,384]{2,1,0:T(8,128)(2,1)S(1)}, bf16[3,96,384]{2,1,0:T(8,128)(2,1)S(1)}, u32[]{:S(2)}, u32[]{:S(2)}) collective-permute-start(bf16[3,96,384]{2,1,0:T(8,128)(2,1)S(1)} %get-tuple-element.59.refs_0_), channel_id=1, source_target_pairs={{0,4},{1,5},{2,6},{3,7},{4,0},{5,1},{6,2},{7,3},{8,12},{9,13},{10,... | collective-permute-start | bytes 663560 | tf_op jit(solution)/shard_map/ppermute | solution.py:172
  62.4 3.6 %collective-permute-done.19.there = f32[96,128]{1,0:T(8,128)S(1)} collective-permute-done((f32[96,128]{1,0:T(8,128)S(1)}, f32[96,128]{1,0:T(8,128)S(1)}, u32[]{:S(2)}, u32[]{:S(2)}) %collective-permute-start.19) | collective-permute-done | bytes 49184 | tf_op jit(solution)/shard_map/ppermute | solution.py:172
  66.2 1.2 %collective-permute-start.21 = (f32[1,96,128]{2,1,0:T(8,128)S(1)}, f32[1,96,128]{2,1,0:T(8,128)S(1)}, u32[]{:S(2)}, u32[]{:S(2)}) collective-permute-start(f32[1,96,128]{2,1,0:T(8,128)S(1)} %bitcast.31), channel_id=1, source_target_pairs={{0,8},{1,9},{2,10},{3,11},{4,12},{5,13},{6,14},{7,15},{8,0},{9,1},... | collective-permute-start | bytes 147464 | tf_op jit(solution)/shard_map/ppermute | solution.py:172
  67.4 2.6 %collective-permute-done.16.refs_2_ = bf16[3,96,384]{2,1,0:T(8,128)(2,1)S(1)} collective-permute-done((bf16[3,96,384]{2,1,0:T(8,128)(2,1)S(1)}, bf16[3,96,384]{2,1,0:T(8,128)(2,1)S(1)}, u32[]{:S(2)}, u32[]{:S(2)}) %collective-permute-start.16) | collective-permute-done | bytes 221216 | tf_op jit(solution)/shard_map/ppermute | solution.py:172
  71.2 2.5 %collective-permute-start.22 = (f32[2,96,128]{2,1,0:T(8,128)S(1)}, f32[2,96,128]{2,1,0:T(8,128)S(1)}, u32[]{:S(2)}, u32[]{:S(2)}) collective-permute-start(f32[2,96,128]{2,1,0:T(8,128)S(1)} %get-tuple-element.79), channel_id=1, source_target_pairs={{0,4},{1,5},{2,6},{3,7},{4,0},{5,1},{6,2},{7,3},{8,12},{9,13},{10,... | collective-permute-start | bytes 294920 | tf_op jit(solution)/shard_map/ppermute | solution.py:172
  73.7 4.8 %collective-permute-done.22 = f32[2,96,128]{2,1,0:T(8,128)S(1)} collective-permute-done((f32[2,96,128]{2,1,0:T(8,128)S(1)}, f32[2,96,128]{2,1,0:T(8,128)S(1)}, u32[]{:S(2)}, u32[]{:S(2)}) %collective-permute-start.22) | collective-permute-done | bytes 98336 | tf_op jit(solution)/shard_map/ppermute | solution.py:172
  78.6 1.9 %shard_map.100 = (bf16[3,384,384]{2,1,0:T(8,128)(2,1)S(1)}, f32[2,192,128]{2,1,0:T(8,128)S(1)}, bf16[2,192,128]{2,1,0:T(8,128)(2,1)S(1)}) custom-call(s32[3]{0:T(128)S(1)} %pad_add_fusion.place, bf16[3,384,384]{2,1,0:T(8,128)(2,1)S(1)} %shard_map.95.weights, bf16[3,96,384]{2,1,0:T(8,128)(2,1)S(1)} %get-tuple-element.59.refs_0_, ...), custom_call_target="tpu_custom_call" | custom-call | flops 226492416 | bytes 6291468 | tf_op jit(solution)/shard_map/pallas_call | solution.py:149
  80.6 1.3 %collective-permute-done.23 = bf16[2,192,128]{2,1,0:T(8,128)(2,1)S(1)} collective-permute-done((bf16[2,192,128]{2,1,0:T(8,128)(2,1)S(1)}, bf16[2,192,128]{2,1,0:T(8,128)(2,1)S(1)}, u32[]{:S(2)}, u32[]{:S(2)}) %collective-permute-start.23) | collective-permute-done | bytes 98336 | tf_op jit(solution)/shard_map/ppermute | solution.py:172
  81.9 0.9 %collective-permute-start.25 = (bf16[2,192,128]{2,1,0:T(8,128)(2,1)S(1)}, bf16[2,192,128]{2,1,0:T(8,128)(2,1)S(1)}, u32[]{:S(2)}, u32[]{:S(2)}) collective-permute-start(bf16[2,192,128]{2,1,0:T(8,128)(2,1)S(1)} %add_convert_fusion.1), channel_id=1, source_target_pairs={{0,2},{1,3},{2,0},{3,1},{4,6},{5,7},{6,4},{7,5},{8,10},{9,11},{10,... | collective-permute-start | bytes 294920 | tf_op jit(solution)/shard_map/ppermute | solution.py:172
  82.8 1.3 %shard_map.101 = (f32[2,192,128]{2,1,0:T(8,128)S(1)}, bf16[2,192,128]{2,1,0:T(8,128)(2,1)S(1)}) custom-call(s32[3]{0:T(128)S(1)} %pad_add_fusion.place, bf16[3,384,384]{2,1,0:T(8,128)(2,1)S(1)} %get-tuple-element.64.renewed, bf16[2,192,128]{2,1,0:T(8,128)(2,1)S(1)} %pad_maximum_fusion.3.mine, bf16[2,192,128]{2,1,0:T(8,128)(2,1)S(1)} %collective-permute-done.11.other), custom_call_target="tpu_custom_call" | custom-call | flops 226492416 | bytes 2555916 | tf_op jit(solution)/shard_map/pallas_call | solution.py:149
  84.2 2.6 %collective-permute-done.25.pair = bf16[2,192,128]{2,1,0:T(8,128)(2,1)S(1)} collective-permute-done((bf16[2,192,128]{2,1,0:T(8,128)(2,1)S(1)}, bf16[2,192,128]{2,1,0:T(8,128)(2,1)S(1)}, u32[]{:S(2)}, u32[]{:S(2)}) %collective-permute-start.25) | collective-permute-done | bytes 98336 | tf_op jit(solution)/shard_map/ppermute | solution.py:172
  (46 shorter events, 9.1 us)
Async XLA Ops:
  0.6 5.2 %copy-start = (bf16[1024,192]{0,1:T(8,128)(2,1)S(1)}, bf16[1024,192]{0,1:T(8,128)(2,1)}, u32[]{:S(2)}) copy-start(bf16[1024,192]{0,1:T(8,128)(2,1)} %param.8) | copy-start | bytes 1179652
  1.7 6.1 %collective-permute-start = (bf16[3,48,384]{2,1,0:T(8,128)(2,1)S(1)}, bf16[3,48,384]{2,1,0:T(8,128)(2,1)S(1)}, u32[]{:S(2)}, u32[]{:S(2)}) collective-permute-start(bf16[3,48,384]{2,1,0:T(8,128)(2,1)S(1)} %get-tuple-element.77), channel_id=1, source_target_pairs={{0,2},{1,3},{2,0},{3,1},{4,6},{5,7},{6,4},{7,5},{8,10},{9,11},{10,... | collective-permute-start | bytes 331784 | tf_op jit(solution)/shard_map/ppermute | solution.py:172
  5.8 21.6 %copy-start.1 = (bf16[128,192]{0,1:T(8,128)(2,1)S(1)}, bf16[128,192]{0,1:T(8,128)(2,1)}, u32[]{:S(2)}) copy-start(bf16[128,192]{0,1:T(8,128)(2,1)} %param.15) | copy-start | bytes 147460
  5.8 21.6 %copy-start.2 = (bf16[128,192]{0,1:T(8,128)(2,1)S(1)}, bf16[128,192]{0,1:T(8,128)(2,1)}, u32[]{:S(2)}) copy-start(bf16[128,192]{0,1:T(8,128)(2,1)} %param.14) | copy-start | bytes 147460
  7.8 19.6 %collective-permute-start.1 = (bf16[2,192,1024]{2,1,0:T(8,128)(2,1)S(1)}, bf16[2,192,1024]{2,1,0:T(8,128)(2,1)S(1)}, u32[]{:S(2)}, u32[]{:S(2)}) collective-permute-start(bf16[2,192,1024]{2,1,0:T(8,128)(2,1)S(1)} %pad_maximum_fusion.mine), channel_id=1, source_target_pairs={{0,2},{1,3},{2,0},{3,1},{4,6},{5,7},{6,4},{7,5},{8,10},{9,11},{10,... | collective-permute-start | bytes 2359304 | tf_op jit(solution)/shard_map/ppermute | solution.py:172
  9.5 8.3 %collective-permute-start.3 = (bf16[3,48,384]{2,1,0:T(8,128)(2,1)S(1)}, bf16[3,48,384]{2,1,0:T(8,128)(2,1)S(1)}, u32[]{:S(2)}, u32[]{:S(2)}) collective-permute-start(bf16[3,48,384]{2,1,0:T(8,128)(2,1)S(1)} %get-tuple-element.76.refs_0_), channel_id=1, source_target_pairs={{0,8},{1,9},{2,10},{3,11},{4,12},{5,13},{6,14},{7,15},{8,0},{9,1},... | collective-permute-start | bytes 331784 | tf_op jit(solution)/shard_map/ppermute | solution.py:172
  12.1 7.5 %collective-permute-start.2 = (bf16[3,48,384]{2,1,0:T(8,128)(2,1)S(1)}, bf16[3,48,384]{2,1,0:T(8,128)(2,1)S(1)}, u32[]{:S(2)}, u32[]{:S(2)}) collective-permute-start(bf16[3,48,384]{2,1,0:T(8,128)(2,1)S(1)} %get-tuple-element.76.refs_0_), channel_id=1, source_target_pairs={{0,4},{1,5},{2,6},{3,7},{4,0},{5,1},{6,2},{7,3},{8,12},{9,13},{10,... | collective-permute-start | bytes 331784 | tf_op jit(solution)/shard_map/ppermute | solution.py:172
  13.7 7.7 %collective-permute-start.6 = (bf16[3,48,384]{2,1,0:T(8,128)(2,1)S(1)}, bf16[3,48,384]{2,1,0:T(8,128)(2,1)S(1)}, u32[]{:S(2)}, u32[]{:S(2)}) collective-permute-start(bf16[3,48,384]{2,1,0:T(8,128)(2,1)S(1)} %collective-permute-done.refs_4_), channel_id=1, source_target_pairs={{0,8},{1,9},{2,10},{3,11},{4,12},{5,13},{6,14},{7,15},{8,0},{9,1},... | collective-permute-start | bytes 331784 | tf_op jit(solution)/shard_map/ppermute | solution.py:172
  14.0 13.5 %collective-permute-start.9 = (bf16[2,192,1024]{2,1,0:T(8,128)(2,1)S(1)}, bf16[2,192,1024]{2,1,0:T(8,128)(2,1)S(1)}, u32[]{:S(2)}, u32[]{:S(2)}) collective-permute-start(bf16[2,192,1024]{2,1,0:T(8,128)(2,1)S(1)} %pad_maximum_fusion.mine), channel_id=1, source_target_pairs={{0,1},{1,0},{2,3},{3,2},{4,5},{5,4},{6,7},{7,6},{8,9},{9,8},{10,11... | collective-permute-start | bytes 2359304 | tf_op jit(solution)/shard_map/ppermute | solution.py:172
  17.8 5.3 %collective-permute-start.5 = (bf16[3,48,384]{2,1,0:T(8,128)(2,1)S(1)}, bf16[3,48,384]{2,1,0:T(8,128)(2,1)S(1)}, u32[]{:S(2)}, u32[]{:S(2)}) collective-permute-start(bf16[3,48,384]{2,1,0:T(8,128)(2,1)S(1)} %collective-permute-done.refs_4_), channel_id=1, source_target_pairs={{0,4},{1,5},{2,6},{3,7},{4,0},{5,1},{6,2},{7,3},{8,12},{9,13},{10,... | collective-permute-start | bytes 331784 | tf_op jit(solution)/shard_map/ppermute | solution.py:172
  19.6 5.7 %collective-permute-start.4 = (bf16[3,48,384]{2,1,0:T(8,128)(2,1)S(1)}, bf16[3,48,384]{2,1,0:T(8,128)(2,1)S(1)}, u32[]{:S(2)}, u32[]{:S(2)}) collective-permute-start(bf16[3,48,384]{2,1,0:T(8,128)(2,1)S(1)} %collective-permute-done.3.refs_2_), channel_id=1, source_target_pairs={{0,4},{1,5},{2,6},{3,7},{4,0},{5,1},{6,2},{7,3},{8,12},{9,13},{10,... | collective-permute-start | bytes 331784 | tf_op jit(solution)/shard_map/ppermute | solution.py:172
  21.4 5.4 %collective-permute-start.7 = (bf16[3,48,384]{2,1,0:T(8,128)(2,1)S(1)}, bf16[3,48,384]{2,1,0:T(8,128)(2,1)S(1)}, u32[]{:S(2)}, u32[]{:S(2)}) collective-permute-start(bf16[3,48,384]{2,1,0:T(8,128)(2,1)S(1)} %collective-permute-done.6.refs_6_), channel_id=1, source_target_pairs={{0,4},{1,5},{2,6},{3,7},{4,0},{5,1},{6,2},{7,3},{8,12},{9,13},{10,... | collective-permute-start | bytes 331784 | tf_op jit(solution)/shard_map/ppermute | solution.py:172
  27.4 3.5 %collective-permute-start.8 = (bf16[2,192,1024]{2,1,0:T(8,128)(2,1)S(1)}, bf16[2,192,1024]{2,1,0:T(8,128)(2,1)S(1)}, u32[]{:S(2)}, u32[]{:S(2)}) collective-permute-start(bf16[2,192,1024]{2,1,0:T(8,128)(2,1)S(1)} %collective-permute-done.1.mine), channel_id=1, source_target_pairs={{0,1},{1,0},{2,3},{3,2},{4,5},{5,4},{6,7},{7,6},{8,9},{9,8},{10,11... | collective-permute-start | bytes 2359304 | tf_op jit(solution)/shard_map/ppermute | solution.py:172
  34.4 8.0 %collective-permute-start.10 = (bf16[3,96,384]{2,1,0:T(8,128)(2,1)S(1)}, bf16[3,96,384]{2,1,0:T(8,128)(2,1)S(1)}, u32[]{:S(2)}, u32[]{:S(2)}) collective-permute-start(bf16[3,96,384]{2,1,0:T(8,128)(2,1)S(1)} %get-tuple-element.50), channel_id=1, source_target_pairs={{0,4},{1,5},{2,6},{3,7},{4,0},{5,1},{6,2},{7,3},{8,12},{9,13},{10,... | collective-permute-start | bytes 663560 | tf_op jit(solution)/shard_map/ppermute | solution.py:172
  35.7 1.9 %collective-permute-start.11 = (bf16[2,192,128]{2,1,0:T(8,128)(2,1)S(1)}, bf16[2,192,128]{2,1,0:T(8,128)(2,1)S(1)}, u32[]{:S(2)}, u32[]{:S(2)}) collective-permute-start(bf16[2,192,128]{2,1,0:T(8,128)(2,1)S(1)} %pad_maximum_fusion.3.mine), channel_id=1, source_target_pairs={{0,1},{1,0},{2,3},{3,2},{4,5},{5,4},{6,7},{7,6},{8,9},{9,8},{10,11... | collective-permute-start | bytes 294920 | tf_op jit(solution)/shard_map/ppermute | solution.py:172
  35.9 5.6 %collective-permute-start.12 = (bf16[2,192,128]{2,1,0:T(8,128)(2,1)S(1)}, bf16[2,192,128]{2,1,0:T(8,128)(2,1)S(1)}, u32[]{:S(2)}, u32[]{:S(2)}) collective-permute-start(bf16[2,192,128]{2,1,0:T(8,128)(2,1)S(1)} %pad_maximum_fusion.3.mine), channel_id=1, source_target_pairs={{0,2},{1,3},{2,0},{3,1},{4,6},{5,7},{6,4},{7,5},{8,10},{9,11},{10,... | collective-permute-start | bytes 294920 | tf_op jit(solution)/shard_map/ppermute | solution.py:172
  36.8 5.6 %collective-permute-start.13 = (bf16[2,192,128]{2,1,0:T(8,128)(2,1)S(1)}, bf16[2,192,128]{2,1,0:T(8,128)(2,1)S(1)}, u32[]{:S(2)}, u32[]{:S(2)}) collective-permute-start(bf16[2,192,128]{2,1,0:T(8,128)(2,1)S(1)} %pad_maximum_fusion.3.mine), channel_id=1, source_target_pairs={{0,3},{1,2},{2,1},{3,0},{4,7},{5,6},{6,5},{7,4},{8,11},{9,10},{10,... | collective-permute-start | bytes 294920 | tf_op jit(solution)/shard_map/ppermute | solution.py:172
  42.5 12.6 %collective-permute-start.14 = (bf16[3,96,384]{2,1,0:T(8,128)(2,1)S(1)}, bf16[3,96,384]{2,1,0:T(8,128)(2,1)S(1)}, u32[]{:S(2)}, u32[]{:S(2)}) collective-permute-start(bf16[3,96,384]{2,1,0:T(8,128)(2,1)S(1)} %get-tuple-element.54), channel_id=1, source_target_pairs={{0,4},{1,5},{2,6},{3,7},{4,0},{5,1},{6,2},{7,3},{8,12},{9,13},{10,... | collective-permute-start | bytes 663560 | tf_op jit(solution)/shard_map/ppermute | solution.py:172
  43.6 11.4 %collective-permute-start.15 = (bf16[3,96,384]{2,1,0:T(8,128)(2,1)S(1)}, bf16[3,96,384]{2,1,0:T(8,128)(2,1)S(1)}, u32[]{:S(2)}, u32[]{:S(2)}) collective-permute-start(bf16[3,96,384]{2,1,0:T(8,128)(2,1)S(1)} %add_convert_fusion), channel_id=1, source_target_pairs={{0,8},{1,9},{2,10},{3,11},{4,12},{5,13},{6,14},{7,15},{8,0},{9,1},... | collective-permute-start | bytes 663560 | tf_op jit(solution)/shard_map/ppermute | solution.py:172
  55.8 2.0 %collective-permute-start.17 = (f32[96,128]{1,0:T(8,128)S(1)}, f32[96,128]{1,0:T(8,128)S(1)}, u32[]{:S(2)}, u32[]{:S(2)}) collective-permute-start(f32[96,128]{1,0:T(8,128)S(1)} %get-tuple-element.57), channel_id=1, source_target_pairs={{0,1},{1,0},{2,3},{3,2},{4,5},{5,4},{6,7},{7,6},{8,9},{9,8},{10,11... | collective-permute-start | bytes 147464 | tf_op jit(solution)/shard_map/ppermute | solution.py:172
  55.9 14.0 %collective-permute-start.16 = (bf16[3,96,384]{2,1,0:T(8,128)(2,1)S(1)}, bf16[3,96,384]{2,1,0:T(8,128)(2,1)S(1)}, u32[]{:S(2)}, u32[]{:S(2)}) collective-permute-start(bf16[3,96,384]{2,1,0:T(8,128)(2,1)S(1)} %get-tuple-element.59.refs_0_), channel_id=1, source_target_pairs={{0,8},{1,9},{2,10},{3,11},{4,12},{5,13},{6,14},{7,15},{8,0},{9,1},... | collective-permute-start | bytes 663560 | tf_op jit(solution)/shard_map/ppermute | solution.py:172
  57.8 12.4 %collective-permute-start.18 = (bf16[3,96,384]{2,1,0:T(8,128)(2,1)S(1)}, bf16[3,96,384]{2,1,0:T(8,128)(2,1)S(1)}, u32[]{:S(2)}, u32[]{:S(2)}) collective-permute-start(bf16[3,96,384]{2,1,0:T(8,128)(2,1)S(1)} %get-tuple-element.59.refs_0_), channel_id=1, source_target_pairs={{0,4},{1,5},{2,6},{3,7},{4,0},{5,1},{6,2},{7,3},{8,12},{9,13},{10,... | collective-permute-start | bytes 663560 | tf_op jit(solution)/shard_map/ppermute | solution.py:172
  61.9 4.1 %collective-permute-start.19 = (f32[96,128]{1,0:T(8,128)S(1)}, f32[96,128]{1,0:T(8,128)S(1)}, u32[]{:S(2)}, u32[]{:S(2)}) collective-permute-start(f32[96,128]{1,0:T(8,128)S(1)} %add.24.here), channel_id=1, source_target_pairs={{0,2},{1,3},{2,0},{3,1},{4,6},{5,7},{6,4},{7,5},{8,10},{9,11},{10,... | collective-permute-start | bytes 147464 | tf_op jit(solution)/shard_map/ppermute | solution.py:172
  66.2 5.1 %collective-permute-start.21 = (f32[1,96,128]{2,1,0:T(8,128)S(1)}, f32[1,96,128]{2,1,0:T(8,128)S(1)}, u32[]{:S(2)}, u32[]{:S(2)}) collective-permute-start(f32[1,96,128]{2,1,0:T(8,128)S(1)} %bitcast.31), channel_id=1, source_target_pairs={{0,8},{1,9},{2,10},{3,11},{4,12},{5,13},{6,14},{7,15},{8,0},{9,1},... | collective-permute-start | bytes 147464 | tf_op jit(solution)/shard_map/ppermute | solution.py:172
  70.2 8.4 %collective-permute-start.20 = (bf16[3,96,384]{2,1,0:T(8,128)(2,1)S(1)}, bf16[3,96,384]{2,1,0:T(8,128)(2,1)S(1)}, u32[]{:S(2)}, u32[]{:S(2)}) collective-permute-start(bf16[3,96,384]{2,1,0:T(8,128)(2,1)S(1)} %collective-permute-done.16.refs_2_), channel_id=1, source_target_pairs={{0,4},{1,5},{2,6},{3,7},{4,0},{5,1},{6,2},{7,3},{8,12},{9,13},{10,... | collective-permute-start | bytes 663560 | tf_op jit(solution)/shard_map/ppermute | solution.py:172
  71.2 7.3 %collective-permute-start.22 = (f32[2,96,128]{2,1,0:T(8,128)S(1)}, f32[2,96,128]{2,1,0:T(8,128)S(1)}, u32[]{:S(2)}, u32[]{:S(2)}) collective-permute-start(f32[2,96,128]{2,1,0:T(8,128)S(1)} %get-tuple-element.79), channel_id=1, source_target_pairs={{0,4},{1,5},{2,6},{3,7},{4,0},{5,1},{6,2},{7,3},{8,12},{9,13},{10,... | collective-permute-start | bytes 294920 | tf_op jit(solution)/shard_map/ppermute | solution.py:172
  80.5 1.4 %collective-permute-start.23 = (bf16[2,192,128]{2,1,0:T(8,128)(2,1)S(1)}, bf16[2,192,128]{2,1,0:T(8,128)(2,1)S(1)}, u32[]{:S(2)}, u32[]{:S(2)}) collective-permute-start(bf16[2,192,128]{2,1,0:T(8,128)(2,1)S(1)} %get-tuple-element.65), channel_id=1, source_target_pairs={{0,1},{1,0},{2,3},{3,2},{4,5},{5,4},{6,7},{7,6},{8,9},{9,8},{10,11... | collective-permute-start | bytes 294920 | tf_op jit(solution)/shard_map/ppermute | solution.py:172
  81.9 4.9 %collective-permute-start.25 = (bf16[2,192,128]{2,1,0:T(8,128)(2,1)S(1)}, bf16[2,192,128]{2,1,0:T(8,128)(2,1)S(1)}, u32[]{:S(2)}, u32[]{:S(2)}) collective-permute-start(bf16[2,192,128]{2,1,0:T(8,128)(2,1)S(1)} %add_convert_fusion.1), channel_id=1, source_target_pairs={{0,2},{1,3},{2,0},{3,1},{4,6},{5,7},{6,4},{7,5},{8,10},{9,11},{10,... | collective-permute-start | bytes 294920 | tf_op jit(solution)/shard_map/ppermute | solution.py:172
  84.1 2.7 %collective-permute-start.24 = (bf16[2,192,128]{2,1,0:T(8,128)(2,1)S(1)}, bf16[2,192,128]{2,1,0:T(8,128)(2,1)S(1)}, u32[]{:S(2)}, u32[]{:S(2)}) collective-permute-start(bf16[2,192,128]{2,1,0:T(8,128)(2,1)S(1)} %get-tuple-element.71), channel_id=1, source_target_pairs={{0,1},{1,0},{2,3},{3,2},{4,5},{5,4},{6,7},{7,6},{8,9},{9,8},{10,11... | collective-permute-start | bytes 294920 | tf_op jit(solution)/shard_map/ppermute | solution.py:172

commit v6 on v5

--- a/solution.py
+++ b/solution.py
@@ -10,6 +10,7 @@
 step_ratio = 0.5
 epsilon = 1e-06
 f32, bf16 = jnp.float32, jnp.bfloat16
+LANES = 128
 
 
 def contract(left, right, left_dim, right_dim):
@@ -61,45 +62,49 @@
         grads[index] = grad
 
 
-def pair_kernel(groups, place, mine, other, weights, before, *refs):
-    outs, (grads, tokens, deltas, acts) = refs[:groups], refs[groups:]
+def pair_kernel(parts, place, mine, other, weights, before, *refs):
+    outs, (grads, tokens, deltas, acts) = refs[: 2 * parts], refs[2 * parts :]
     join(tokens, mine, other, place[2])
     for index, grad in enumerate(gradients(tokens, weights, deltas, acts)):
         grads[index] = before[index] + grad
-    for flip, out in enumerate(outs):
-        out[...] = grads[:, rows_of(place[0] ^ flip, out.shape[1]), :].astype(out.dtype)
+    for index, out in enumerate(outs):
+        part, given = index % parts, index // parts
+        for spot in range(2):
+            where = rows_of((place[0] ^ ((3 * spot) ^ given)) * parts + part, out.shape[2])
+            out[spot] = grads[:, where, :].astype(out.dtype)
 
 
 def rows_of(owner, rows):
     return pl.ds(pl.multiple_of(owner * rows, rows), rows)
 
 
-def sum_kernel(arrivals, place, weights, own, *refs):
-    arrived, (grad_out, stats_out) = refs[:arrivals], refs[arrivals:]
-    where = rows_of(place[0], own.shape[1])
-    lane = lax.broadcasted_iota(jnp.int32, stats_out.shape, 1)
-    stats = jnp.zeros(stats_out.shape, f32)
-    for index in range(3):
-        grad = own[index]
-        for other in arrived:
-            grad = grad + other[index].astype(f32)
-        grad_out[index] = grad.astype(bf16)
-        weight = weights[index, where, :].astype(f32)
-        for slot, product in enumerate((weight * weight, weight * grad, grad * grad)):
-            row_sum = jnp.sum(product, axis=1, keepdims=True)
-            stats = jnp.where(lane == 3 * slot + index, row_sum, stats)
-    stats_out[...] = stats
+def sum_kernel(parts, part, place, weights, kept, came, crossed, grad_out, stats_out):
+    rows = kept.shape[2]
+    lane = lax.broadcasted_iota(jnp.int32, (rows, LANES), 1)
+    both = []
+    for spot in range(2):
+        where = rows_of((place[0] ^ (3 * spot)) * parts + part, rows)
+        stats = jnp.zeros((rows, LANES), f32)
+        for index in range(3):
+            near = kept[spot, index] + came[spot, index].astype(f32)
+            grad = near + crossed[1 - spot, index].astype(f32)
+            grad_out[spot, index] = grad.astype(bf16)
+            weight = weights[index, where, :].astype(f32)
+            for slot, product in enumerate((weight * weight, weight * grad, grad * grad)):
+                row_sum = jnp.sum(product, axis=1, keepdims=True)
+                stats = jnp.where(lane == 8 * slot + index, row_sum, stats)
+        both.append(stats)
+    stats_out[...] = jnp.concatenate(both, axis=0).T[: stats_out.shape[0]]
 
 
 def factor_kernel(hidden, here, there, factors):
-    wsq = (here[...] + there[...]) / hidden
-    lane = lax.broadcasted_iota(jnp.int32, wsq.shape, 1)
-    lanes = wsq.shape[1]
-    cross, gsq = pltpu.roll(wsq, lanes - 3, 1), pltpu.roll(wsq, lanes - 6, 1)
+    sums = (here[...] + there[...]) / hidden
+    wsq, cross, gsq = sums[:, :8], sums[:, 8:16], sums[:, 16:]
     scale = step_ratio * jnp.sqrt(wsq) / jnp.sqrt(gsq + epsilon)
     msq = wsq + 2.0 * scale * cross + scale * scale * gsq
     factor = jnp.sqrt(wsq) / jnp.sqrt(msq + epsilon)
-    factors[...] = jnp.where(lane < 3, factor, pltpu.roll(scale * factor, 3, 1))
+    factors[:, :8] = factor
+    factors[:, 8:] = scale * factor
 
 
 def answer(renewed, query, quests, half, kept, given):
@@ -120,15 +125,20 @@
         given[index] = jnp.where(half == 0, second, first).astype(bf16)
 
 
-def renew_kernel(groups, place, weights, *refs):
-    grads, factors, quests, refs = refs[:groups], refs[groups], refs[groups + 1 : groups + 3], refs[groups + 3 :]
+def renew_kernel(parts, place, weights, *refs):
+    grads, factors, quests, refs = refs[: 2 * parts], refs[2 * parts : 2 * parts + 2], refs[-6:-4], refs[-4:]
     renewed, kept, given, query = refs
-    for flip in range(groups):
-        where = rows_of(place[0] ^ flip, grads[0].shape[1])
-        for index in range(3):
-            old = weights[index, where, :].astype(f32) * factors[flip, :, index : index + 1]
-            step = grads[flip][index].astype(f32) * factors[flip, :, 3 + index : 4 + index]
-            renewed[index, where, :] = (old + step).astype(bf16)
+    for spot in range(2):
+        for near in range(2):
+            for part in range(parts):
+                grad = grads[near * parts + part]
+                rows = grad.shape[2]
+                where = rows_of((place[0] ^ ((3 * spot) ^ near)) * parts + part, rows)
+                scales = factors[near][part].T[spot * rows : (spot + 1) * rows]
+                for index in range(3):
+                    old = weights[index, where, :].astype(f32) * scales[:, index : index + 1]
+                    step = grad[spot, index].astype(f32) * scales[:, 8 + index : 9 + index]
+                    renewed[index, where, :] = (old + step).astype(bf16)
     answer(renewed, query, quests, place[2], kept, given)
 
 
@@ -171,19 +181,9 @@
         pairs = [(i, i ^ flip) for i in range(n_tok * n_hid)]
         return lax.ppermute(array, ("tok", "hid"), pairs)
 
-    def gather(block, soon=(), late=()):
-        held, bit = {0: block}, groups // 2
-        while bit > 1:
-            held.update({flip | bit: swap(held[flip], zed * bit) for flip in list(held)})
-            bit //= 2
-        if soon:
-            block, _ = lax.optimization_barrier((block, soon))
-        near = swap(block, zed)
-        if late:
-            held, near, _ = lax.optimization_barrier((held, near, late))
-        held.update({flip | 1: swap(held[flip], zed) for flip in list(held) if flip})
-        held[1] = near
-        return [held[flip] for flip in range(groups)]
+    def gather(block):
+        near, across = swap(block, zed), swap(block, 2 * zed)
+        return [block, near, across, swap(across, zed)]
 
     stacked = jnp.stack([gate_weight, up_weight, down_weight])
     cols = stacked.shape[2] // 2
@@ -223,10 +223,13 @@
         place,
         16,
     )
+    parts = 2
+    block = (2, 3, rows // parts, cols)
+    kept_given = [jax.ShapeDtypeStruct(block, f32)] * parts + [jax.ShapeDtypeStruct(block, bf16)] * parts
     shares = call(
-        functools.partial(pair_kernel, groups),
+        functools.partial(pair_kernel, parts),
         (pair_tokens, swap(pair_tokens, core), weights, grads),
-        [jax.ShapeDtypeStruct(block, bf16 if flip & 1 else f32) for flip in range(groups)],
+        kept_given,
         [pltpu.VMEM(whole, f32), *joined],
         token_flops,
         place,
@@ -234,34 +237,32 @@
     )
     quest, shares = lax.optimization_barrier((jnp.stack([queries.T, out_grad.T]), shares))
     quests = [quest] + [swap(quest, flip) for flip in (1, 2, 3)]
-    held, arrived, bit = dict(enumerate(shares)), [], 1
-    while bit < groups:
-        for flip in sorted((f for f in held if f & bit), reverse=True):
-            came = swap(held.pop(flip), zed * bit)
-            if flip == bit:
-                arrived.append(came)
-            else:
-                came, quests = lax.optimization_barrier((came, quests))
-                other = (held[flip ^ bit].astype(f32) + came.astype(f32)).astype(bf16)
-                held, held[flip ^ bit] = lax.optimization_barrier((held, other))
-        bit *= 2
-    grad, stats = call(
-        functools.partial(sum_kernel, len(arrived)),
-        (weights, held[0], *arrived),
-        (jax.ShapeDtypeStruct(block, bf16), jax.ShapeDtypeStruct((rows, 128), f32)),
-        place=place,
-    )
-    stats = stats + swap(stats, core)
+    kept, came = shares[:parts], [swap(share, zed) for share in shares[parts:]]
+    came[0], quests = lax.optimization_barrier((came[0], quests))
+    crossed = [swap((k + c.astype(f32)).astype(bf16), 3 * zed) for k, c in zip(kept, came)]
+    sums, stats = zip(
+        *(
+            call(
+                functools.partial(sum_kernel, parts, part),
+                (weights, kept[part], came[part], crossed[part]),
+                (
+                    jax.ShapeDtypeStruct(block, bf16),
+                    jax.ShapeDtypeStruct((24, 2 * rows // parts), f32),
+                ),
+                place=place,
+            )
+            for part in range(parts)
+        )
+    )
+    backs = [swap(part, zed) for part in sums]
+    stats = jnp.stack(stats)
+    there, backs[0] = lax.optimization_barrier((swap(stats, core), backs[0]))
+    stats = stats + there
     (factors,) = call(
         functools.partial(factor_kernel, 2 * n_hid * cols),
         (stats, swap(stats, pair)),
-        (jax.ShapeDtypeStruct(stats.shape, f32),),
-    )
-    all_factors, bit = factors[None], groups // 2
-    while bit:
-        all_factors = jnp.stack([all_factors, swap(all_factors, zed * bit)], axis=1)
-        all_factors = all_factors.reshape(-1, *stats.shape)
-        bit //= 2
+        (jax.ShapeDtypeStruct((parts, 16, 2 * rows // parts), f32),),
+    )
 
     count = queries.shape[0]
     piece = (2, feats, count)
@@ -269,8 +270,8 @@
     query = pltpu.VMEM((2, width, count), bf16)
     query_flops = 6 * 2 * count * width * cols
     renewed, kept, given = call(
-        functools.partial(renew_kernel, groups),
-        (weights, *gather(grad, [stats], [factors]), all_factors, *quests[2:]),
+        functools.partial(renew_kernel, parts),
+        (weights, *sums, *backs, factors, swap(factors, zed), *quests[2:]),
         [jax.ShapeDtypeStruct(whole, bf16), *kept_given],
         [query],
         query_flops,
@@ -398,8 +399,7 @@
         toks, count = args[0].shape[0], args[6].shape[0]
         fits = (
             n_hid == 2
-            and 2 <= n_tok <= 8
-            and n_tok & (n_tok - 1) == 0
+            and n_tok == 8
             and rows % 16 == 0
             and cols % 256 == 0
             and toks % 256 == 0

time: 88.5 us -> 84.6 us (0.956); the launches traced: 87.5 us -> 84.5 us
  waiting for transfers between devices: 40 us -> 28.3 us
  starting transfers between devices: 31.8 us -> 39.7 us
    ppermute x26 -> x25, waiting for transfers between devices: 40 us -> 28.3 us  [swap(): return lax.ppermute(array, ('tok', 'hid'), pairs)]
    ppermute x26 -> x25, starting transfers between devices: 31.8 us -> 39.7 us  [swap(): return lax.ppermute(array, ('tok', 'hid'), pairs)]
    pallas_call x8 -> x9, Pallas kernels: 12.3 us -> 13.1 us  [call(): pl.pallas_call(body, out_shape=list(outs), in_specs=specs, out_specs=[pl....]
  transfers between devices with their start and end apart: 26 -> 25, of which waited for: 16 -> 16; matrix products, arithmetic and copies ran while one was open for 1% -> 2% of each run, Pallas kernels for 6% -> 8%
where the time goes in v6:
time: 84.6 us; the launch traced here: 84.5 us
  starting transfers between devices  39.7 us (47%)
  waiting for transfers between devices  28.3 us (33%)
  Pallas kernels  13.1 us (15%)
  other arithmetic  2.41 us (3%)
  between operations  0.87 us (1%)
    ppermute x25, starting transfers between devices, swap(): return lax.ppermute(array, ('tok', 'hid'), pairs)  39.7 us
    ppermute x25, waiting for transfers between devices, swap(): return lax.ppermute(array, ('tok', 'hid'), pairs)  28.3 us
    pallas_call x9, Pallas kernels, call(): pl.pallas_call(body, out_shape=list(outs), in_specs=specs, out_specs=[pl....  13.1 us
  transfers between devices with their start and end apart: 25, of which 16 were waited for; matrix products, arithmetic and copies ran while one was open for 2% of the time, Pallas kernels for 8%

profile of v6, /device:TPU:0, one launch (start us, length us, event | category | flops | bytes accessed | tf_op | source)
XLA Modules:
  0.0 84.5 jit_solution(7652216843818630229)
XLA Ops:
  0.7 1.0 %pad_maximum_fusion.1 = bf16[3,48,768]{2,1,0:T(8,128)(2,1)S(1)} fusion(bf16[1,48,768]{2,1,0:T(8,128)(2,1)} %bitcast.28, bf16[1,48,768]{2,1,0:T(8,128)(2,1)} %bitcast.29, bf16[1,48,768]{2,1,0:T(8,128)(2,1)} %bitcast.30), kind=kLoop, calls=%fused_computation.5 | loop fusion | flops 221184 | bytes 442368 | tf_op jit(solution)/shard_map/stack | solution.py:188
  1.7 3.0 %collective-permute-start = (bf16[3,48,384]{2,1,0:T(8,128)(2,1)S(1)}, bf16[3,48,384]{2,1,0:T(8,128)(2,1)S(1)}, u32[]{:S(2)}, u32[]{:S(2)}) collective-permute-start(bf16[3,48,384]{2,1,0:T(8,128)(2,1)S(1)} %get-tuple-element.71), channel_id=1, source_target_pairs={{0,2},{1,3},{2,0},{3,1},{4,6},{5,7},{6,4},{7,5},{8,10},{9,11},{10,... | collective-permute-start | bytes 331784 | tf_op jit(solution)/shard_map/ppermute | solution.py:182
  4.7 1.1 %fusion = bf16[1,192,1024]{2,1,0:T(8,128)(2,1)S(1)} fusion(bf16[1024,192]{0,1:T(8,128)(2,1)} %param.9, f32[1024]{0:T(1024)} %param.10), kind=kLoop, calls=%fused_computation.4 | loop fusion | flops 589824 | bytes 790528 | tf_op jit(solution)/shard_map/stack | solution.py:193
  5.9 1.9 %collective-permute-done.refs_4_ = bf16[3,48,384]{2,1,0:T(8,128)(2,1)S(1)} collective-permute-done((bf16[3,48,384]{2,1,0:T(8,128)(2,1)S(1)}, bf16[3,48,384]{2,1,0:T(8,128)(2,1)S(1)}, u32[]{:S(2)}, u32[]{:S(2)}) %collective-permute-start) | collective-permute-done | bytes 110624 | tf_op jit(solution)/shard_map/ppermute | solution.py:182
  7.8 1.7 %collective-permute-start.1 = (bf16[2,192,1024]{2,1,0:T(8,128)(2,1)S(1)}, bf16[2,192,1024]{2,1,0:T(8,128)(2,1)S(1)}, u32[]{:S(2)}, u32[]{:S(2)}) collective-permute-start(bf16[2,192,1024]{2,1,0:T(8,128)(2,1)S(1)} %pad_maximum_fusion.mine), channel_id=1, source_target_pairs={{0,2},{1,3},{2,0},{3,1},{4,6},{5,7},{6,4},{7,5},{8,10},{9,11},{10,... | collective-permute-start | bytes 2359304 | tf_op jit(solution)/shard_map/ppermute | solution.py:182
  9.5 2.6 %collective-permute-start.3 = (bf16[3,48,384]{2,1,0:T(8,128)(2,1)S(1)}, bf16[3,48,384]{2,1,0:T(8,128)(2,1)S(1)}, u32[]{:S(2)}, u32[]{:S(2)}) collective-permute-start(bf16[3,48,384]{2,1,0:T(8,128)(2,1)S(1)} %get-tuple-element.70.refs_0_), channel_id=1, source_target_pairs={{0,8},{1,9},{2,10},{3,11},{4,12},{5,13},{6,14},{7,15},{8,0},{9,1},... | collective-permute-start | bytes 331784 | tf_op jit(solution)/shard_map/ppermute | solution.py:182
  12.1 1.6 %collective-permute-start.2 = (bf16[3,48,384]{2,1,0:T(8,128)(2,1)S(1)}, bf16[3,48,384]{2,1,0:T(8,128)(2,1)S(1)}, u32[]{:S(2)}, u32[]{:S(2)}) collective-permute-start(bf16[3,48,384]{2,1,0:T(8,128)(2,1)S(1)} %get-tuple-element.70.refs_0_), channel_id=1, source_target_pairs={{0,4},{1,5},{2,6},{3,7},{4,0},{5,1},{6,2},{7,3},{8,12},{9,13},{10,... | collective-permute-start | bytes 331784 | tf_op jit(solution)/shard_map/ppermute | solution.py:182
  14.0 3.8 %collective-permute-done.3.refs_2_ = bf16[3,48,384]{2,1,0:T(8,128)(2,1)S(1)} collective-permute-done((bf16[3,48,384]{2,1,0:T(8,128)(2,1)S(1)}, bf16[3,48,384]{2,1,0:T(8,128)(2,1)S(1)}, u32[]{:S(2)}, u32[]{:S(2)}) %collective-permute-start.3) | collective-permute-done | bytes 110624 | tf_op jit(solution)/shard_map/ppermute | solution.py:182
  17.8 1.8 %collective-permute-start.5 = (bf16[3,48,384]{2,1,0:T(8,128)(2,1)S(1)}, bf16[3,48,384]{2,1,0:T(8,128)(2,1)S(1)}, u32[]{:S(2)}, u32[]{:S(2)}) collective-permute-start(bf16[3,48,384]{2,1,0:T(8,128)(2,1)S(1)} %collective-permute-done.refs_4_), channel_id=1, source_target_pairs={{0,4},{1,5},{2,6},{3,7},{4,0},{5,1},{6,2},{7,3},{8,12},{9,13},{10,... | collective-permute-start | bytes 331784 | tf_op jit(solution)/shard_map/ppermute | solution.py:182
  20.4 1.0 %collective-permute-done.6.refs_6_ = bf16[3,48,384]{2,1,0:T(8,128)(2,1)S(1)} collective-permute-done((bf16[3,48,384]{2,1,0:T(8,128)(2,1)S(1)}, bf16[3,48,384]{2,1,0:T(8,128)(2,1)S(1)}, u32[]{:S(2)}, u32[]{:S(2)}) %collective-permute-start.6) | collective-permute-done | bytes 110624 | tf_op jit(solution)/shard_map/ppermute | solution.py:182
  22.0 1.2 %collective-permute-done.5.refs_5_ = bf16[3,48,384]{2,1,0:T(8,128)(2,1)S(1)} collective-permute-done((bf16[3,48,384]{2,1,0:T(8,128)(2,1)S(1)}, bf16[3,48,384]{2,1,0:T(8,128)(2,1)S(1)}, u32[]{:S(2)}, u32[]{:S(2)}) %collective-permute-start.5) | collective-permute-done | bytes 110624 | tf_op jit(solution)/shard_map/ppermute | solution.py:182
  23.2 2.2 %collective-permute-done.4.refs_3_ = bf16[3,48,384]{2,1,0:T(8,128)(2,1)S(1)} collective-permute-done((bf16[3,48,384]{2,1,0:T(8,128)(2,1)S(1)}, bf16[3,48,384]{2,1,0:T(8,128)(2,1)S(1)}, u32[]{:S(2)}, u32[]{:S(2)}) %collective-permute-start.4) | collective-permute-done | bytes 110624 | tf_op jit(solution)/shard_map/ppermute | solution.py:182
  25.3 1.4 %collective-permute-done.7.refs_7_ = bf16[3,48,384]{2,1,0:T(8,128)(2,1)S(1)} collective-permute-done((bf16[3,48,384]{2,1,0:T(8,128)(2,1)S(1)}, bf16[3,48,384]{2,1,0:T(8,128)(2,1)S(1)}, u32[]{:S(2)}, u32[]{:S(2)}) %collective-permute-start.7) | collective-permute-done | bytes 110624 | tf_op jit(solution)/shard_map/ppermute | solution.py:182
  27.5 3.3 %shard_map.96.before = f32[3,384,384]{2,1,0:T(8,128)S(1)} custom-call(s32[3]{0:T(128)S(1)} %pad_add_fusion.place, bf16[2,192,1024]{2,1,0:T(8,128)(2,1)S(1)} %pad_maximum_fusion.mine, bf16[2,192,1024]{2,1,0:T(8,128)(2,1)S(1)} %collective-permute-done.9.other, bf16[3,384,384]{2,1,0:T(8,128)(2,1)S(1)} %shard_map.95.weights), custom_call_target="tpu_custom_call" | custom-call | flops 1811939328 | bytes 6684684 | tf_op jit(solution)/shard_map/pallas_call | solution.py:159
  30.9 3.5 %shard_map.97 = (f32[2,3,48,384]{3,2,1,0:T(8,128)S(1)}, f32[2,3,48,384]{3,2,1,0:T(8,128)S(1)}, bf16[2,3,48,384]{3,2,1,0:T(8,128)(2,1)S(1)}, bf16[2,3,48,384]{3,2,1,0:T(8,128)(2,1)S(1)}) custom-call(s32[3]{0:T(128)S(1)} %pad_add_fusion.place, bf16[2,192,1024]{2,1,0:T(8,128)(2,1)S(1)} %collective-permute-done.1.mine, ...), custom_call_target="tpu_custom_call" | custom-call | flops 1811939328 | bytes 8454156 | tf_op jit(solution)/shard_map/pallas_call | solution.py:159
  34.4 1.2 %collective-permute-start.10 = (bf16[2,3,48,384]{3,2,1,0:T(8,128)(2,1)S(1)}, bf16[2,3,48,384]{3,2,1,0:T(8,128)(2,1)S(1)}, u32[]{:S(2)}, u32[]{:S(2)}) collective-permute-start(bf16[2,3,48,384]{3,2,1,0:T(8,128)(2,1)S(1)} %get-tuple-element.45), channel_id=1, source_target_pairs={{0,4},{1,5},{2,6},{3,7},{4,0},{5,1},{6,2},{7,3},{8,12},{9,13},{10,... | collective-permute-start | bytes 663560 | tf_op jit(solution)/shard_map/ppermute | solution.py:182
  35.9 0.9 %collective-permute-start.12 = (bf16[2,192,128]{2,1,0:T(8,128)(2,1)S(1)}, bf16[2,192,128]{2,1,0:T(8,128)(2,1)S(1)}, u32[]{:S(2)}, u32[]{:S(2)}) collective-permute-start(bf16[2,192,128]{2,1,0:T(8,128)(2,1)S(1)} %pad_maximum_fusion.2.mine), channel_id=1, source_target_pairs={{0,2},{1,3},{2,0},{3,1},{4,6},{5,7},{6,4},{7,5},{8,10},{9,11},{10,... | collective-permute-start | bytes 294920 | tf_op jit(solution)/shard_map/ppermute | solution.py:182
  38.4 3.1 %collective-permute-done.12.refs_6_ = bf16[2,192,128]{2,1,0:T(8,128)(2,1)S(1)} collective-permute-done((bf16[2,192,128]{2,1,0:T(8,128)(2,1)S(1)}, bf16[2,192,128]{2,1,0:T(8,128)(2,1)S(1)}, u32[]{:S(2)}, u32[]{:S(2)}) %collective-permute-start.12) | collective-permute-done | bytes 98336 | tf_op jit(solution)/shard_map/ppermute | solution.py:182
  41.5 0.9 %collective-permute-done.13.refs_7_ = bf16[2,192,128]{2,1,0:T(8,128)(2,1)S(1)} collective-permute-done((bf16[2,192,128]{2,1,0:T(8,128)(2,1)S(1)}, bf16[2,192,128]{2,1,0:T(8,128)(2,1)S(1)}, u32[]{:S(2)}, u32[]{:S(2)}) %collective-permute-start.13) | collective-permute-done | bytes 98336 | tf_op jit(solution)/shard_map/ppermute | solution.py:182
  42.8 3.8 %collective-permute-start.14 = (bf16[2,3,48,384]{3,2,1,0:T(8,128)(2,1)S(1)}, bf16[2,3,48,384]{3,2,1,0:T(8,128)(2,1)S(1)}, u32[]{:S(2)}, u32[]{:S(2)}) collective-permute-start(bf16[2,3,48,384]{3,2,1,0:T(8,128)(2,1)S(1)} %add_convert_fusion.1), channel_id=1, source_target_pairs={{0,12},{1,13},{2,14},{3,15},{4,8},{5,9},{6,10},{7,11},{8,4},{9,5},... | collective-permute-start | bytes 663560 | tf_op jit(solution)/shard_map/ppermute | solution.py:182
  47.1 10.9 %collective-permute-start.16 = (bf16[2,3,48,384]{3,2,1,0:T(8,128)(2,1)S(1)}, bf16[2,3,48,384]{3,2,1,0:T(8,128)(2,1)S(1)}, u32[]{:S(2)}, u32[]{:S(2)}) collective-permute-start(bf16[2,3,48,384]{3,2,1,0:T(8,128)(2,1)S(1)} %add_convert_fusion), channel_id=1, source_target_pairs={{0,12},{1,13},{2,14},{3,15},{4,8},{5,9},{6,10},{7,11},{8,4},{9,5},... | collective-permute-start | bytes 663560 | tf_op jit(solution)/shard_map/ppermute | solution.py:182
  58.9 1.6 %collective-permute-start.18 = (bf16[2,3,48,384]{3,2,1,0:T(8,128)(2,1)S(1)}, bf16[2,3,48,384]{3,2,1,0:T(8,128)(2,1)S(1)}, u32[]{:S(2)}, u32[]{:S(2)}) collective-permute-start(bf16[2,3,48,384]{3,2,1,0:T(8,128)(2,1)S(1)} %get-tuple-element.48.refs_0_), channel_id=1, source_target_pairs={{0,4},{1,5},{2,6},{3,7},{4,0},{5,1},{6,2},{7,3},{8,12},{9,13},{10,... | collective-permute-start | bytes 663560 | tf_op jit(solution)/shard_map/ppermute | solution.py:182
  60.4 1.9 %collective-permute-done.16.crossed = bf16[2,3,48,384]{3,2,1,0:T(8,128)(2,1)S(1)} collective-permute-done((bf16[2,3,48,384]{3,2,1,0:T(8,128)(2,1)S(1)}, bf16[2,3,48,384]{3,2,1,0:T(8,128)(2,1)S(1)}, u32[]{:S(2)}, u32[]{:S(2)}) %collective-permute-start.16) | collective-permute-done | bytes 221216 | tf_op jit(solution)/shard_map/ppermute | solution.py:182
  63.2 4.5 %collective-permute-start.19 = (bf16[2,3,48,384]{3,2,1,0:T(8,128)(2,1)S(1)}, bf16[2,3,48,384]{3,2,1,0:T(8,128)(2,1)S(1)}, u32[]{:S(2)}, u32[]{:S(2)}) collective-permute-start(bf16[2,3,48,384]{3,2,1,0:T(8,128)(2,1)S(1)} %get-tuple-element.51.refs_1_), channel_id=1, source_target_pairs={{0,4},{1,5},{2,6},{3,7},{4,0},{5,1},{6,2},{7,3},{8,12},{9,13},{10,... | collective-permute-start | bytes 663560 | tf_op jit(solution)/shard_map/ppermute | solution.py:182
  68.3 3.3 %collective-permute-done.20.there = f32[2,24,96]{2,1,0:T(8,128)S(1)} collective-permute-done((f32[2,24,96]{2,1,0:T(8,128)S(1)}, f32[2,24,96]{2,1,0:T(8,128)S(1)}, u32[]{:S(2)}, u32[]{:S(2)}) %collective-permute-start.20) | collective-permute-done | bytes 18464 | tf_op jit(solution)/shard_map/ppermute | solution.py:182
  71.7 1.1 %collective-permute-start.21 = (f32[2,16,96]{2,1,0:T(8,128)S(1)}, f32[2,16,96]{2,1,0:T(8,128)S(1)}, u32[]{:S(2)}, u32[]{:S(2)}) collective-permute-start(f32[2,16,96]{2,1,0:T(8,128)S(1)} %shard_map.100.refs_4_), channel_id=1, source_target_pairs={{0,4},{1,5},{2,6},{3,7},{4,0},{5,1},{6,2},{7,3},{8,12},{9,13},{10,... | collective-permute-start | bytes 36872 | tf_op jit(solution)/shard_map/ppermute | solution.py:182
  72.8 0.9 %collective-permute-done.19.refs_3_ = bf16[2,3,48,384]{3,2,1,0:T(8,128)(2,1)S(1)} collective-permute-done((bf16[2,3,48,384]{3,2,1,0:T(8,128)(2,1)S(1)}, bf16[2,3,48,384]{3,2,1,0:T(8,128)(2,1)S(1)}, u32[]{:S(2)}, u32[]{:S(2)}) %collective-permute-start.19) | collective-permute-done | bytes 221216 | tf_op jit(solution)/shard_map/ppermute | solution.py:182
  73.7 1.8 %collective-permute-done.21.refs_5_ = f32[2,16,96]{2,1,0:T(8,128)S(1)} collective-permute-done((f32[2,16,96]{2,1,0:T(8,128)S(1)}, f32[2,16,96]{2,1,0:T(8,128)S(1)}, u32[]{:S(2)}, u32[]{:S(2)}) %collective-permute-start.21) | collective-permute-done | bytes 12320 | tf_op jit(solution)/shard_map/ppermute | solution.py:182
  75.5 2.0 %shard_map.101 = (bf16[3,384,384]{2,1,0:T(8,128)(2,1)S(1)}, f32[2,192,128]{2,1,0:T(8,128)S(1)}, bf16[2,192,128]{2,1,0:T(8,128)(2,1)S(1)}) custom-call(s32[3]{0:T(128)S(1)} %pad_add_fusion.place, bf16[3,384,384]{2,1,0:T(8,128)(2,1)S(1)} %shard_map.95.weights, bf16[2,3,48,384]{3,2,1,0:T(8,128)(2,1)S(1)} %get-tuple-element.48.refs_0_, ...), custom_call_target="tpu_custom_call" | custom-call | flops 226492416 | bytes 6119436 | tf_op jit(solution)/shard_map/pallas_call | solution.py:159
  77.6 1.3 %collective-permute-done.22 = bf16[2,192,128]{2,1,0:T(8,128)(2,1)S(1)} collective-permute-done((bf16[2,192,128]{2,1,0:T(8,128)(2,1)S(1)}, bf16[2,192,128]{2,1,0:T(8,128)(2,1)S(1)}, u32[]{:S(2)}, u32[]{:S(2)}) %collective-permute-start.22) | collective-permute-done | bytes 98336 | tf_op jit(solution)/shard_map/ppermute | solution.py:182
  79.5 1.3 %shard_map.102 = (f32[2,192,128]{2,1,0:T(8,128)S(1)}, bf16[2,192,128]{2,1,0:T(8,128)(2,1)S(1)}) custom-call(s32[3]{0:T(128)S(1)} %pad_add_fusion.place, bf16[3,384,384]{2,1,0:T(8,128)(2,1)S(1)} %get-tuple-element.58.renewed, bf16[2,192,128]{2,1,0:T(8,128)(2,1)S(1)} %pad_maximum_fusion.2.mine, bf16[2,192,128]{2,1,0:T(8,128)(2,1)S(1)} %collective-permute-done.11.other), custom_call_target="tpu_custom_call" | custom-call | flops 226492416 | bytes 2555916 | tf_op jit(solution)/shard_map/pallas_call | solution.py:159
  80.8 3.0 %collective-permute-done.24.pair = bf16[2,192,128]{2,1,0:T(8,128)(2,1)S(1)} collective-permute-done((bf16[2,192,128]{2,1,0:T(8,128)(2,1)S(1)}, bf16[2,192,128]{2,1,0:T(8,128)(2,1)S(1)}, u32[]{:S(2)}, u32[]{:S(2)}) %collective-permute-start.24) | collective-permute-done | bytes 98336 | tf_op jit(solution)/shard_map/ppermute | solution.py:182
  (44 shorter events, 9.0 us)
Async XLA Ops:
  0.6 5.2 %copy-start = (bf16[1024,192]{0,1:T(8,128)(2,1)S(1)}, bf16[1024,192]{0,1:T(8,128)(2,1)}, u32[]{:S(2)}) copy-start(bf16[1024,192]{0,1:T(8,128)(2,1)} %param.8) | copy-start | bytes 1179652
  1.7 6.1 %collective-permute-start = (bf16[3,48,384]{2,1,0:T(8,128)(2,1)S(1)}, bf16[3,48,384]{2,1,0:T(8,128)(2,1)S(1)}, u32[]{:S(2)}, u32[]{:S(2)}) collective-permute-start(bf16[3,48,384]{2,1,0:T(8,128)(2,1)S(1)} %get-tuple-element.71), channel_id=1, source_target_pairs={{0,2},{1,3},{2,0},{3,1},{4,6},{5,7},{6,4},{7,5},{8,10},{9,11},{10,... | collective-permute-start | bytes 331784 | tf_op jit(solution)/shard_map/ppermute | solution.py:182
  5.8 21.6 %copy-start.1 = (bf16[128,192]{0,1:T(8,128)(2,1)S(1)}, bf16[128,192]{0,1:T(8,128)(2,1)}, u32[]{:S(2)}) copy-start(bf16[128,192]{0,1:T(8,128)(2,1)} %param.15) | copy-start | bytes 147460
  5.8 21.6 %copy-start.2 = (bf16[128,192]{0,1:T(8,128)(2,1)S(1)}, bf16[128,192]{0,1:T(8,128)(2,1)}, u32[]{:S(2)}) copy-start(bf16[128,192]{0,1:T(8,128)(2,1)} %param.14) | copy-start | bytes 147460
  7.8 19.6 %collective-permute-start.1 = (bf16[2,192,1024]{2,1,0:T(8,128)(2,1)S(1)}, bf16[2,192,1024]{2,1,0:T(8,128)(2,1)S(1)}, u32[]{:S(2)}, u32[]{:S(2)}) collective-permute-start(bf16[2,192,1024]{2,1,0:T(8,128)(2,1)S(1)} %pad_maximum_fusion.mine), channel_id=1, source_target_pairs={{0,2},{1,3},{2,0},{3,1},{4,6},{5,7},{6,4},{7,5},{8,10},{9,11},{10,... | collective-permute-start | bytes 2359304 | tf_op jit(solution)/shard_map/ppermute | solution.py:182
  9.5 8.3 %collective-permute-start.3 = (bf16[3,48,384]{2,1,0:T(8,128)(2,1)S(1)}, bf16[3,48,384]{2,1,0:T(8,128)(2,1)S(1)}, u32[]{:S(2)}, u32[]{:S(2)}) collective-permute-start(bf16[3,48,384]{2,1,0:T(8,128)(2,1)S(1)} %get-tuple-element.70.refs_0_), channel_id=1, source_target_pairs={{0,8},{1,9},{2,10},{3,11},{4,12},{5,13},{6,14},{7,15},{8,0},{9,1},... | collective-permute-start | bytes 331784 | tf_op jit(solution)/shard_map/ppermute | solution.py:182
  12.1 7.5 %collective-permute-start.2 = (bf16[3,48,384]{2,1,0:T(8,128)(2,1)S(1)}, bf16[3,48,384]{2,1,0:T(8,128)(2,1)S(1)}, u32[]{:S(2)}, u32[]{:S(2)}) collective-permute-start(bf16[3,48,384]{2,1,0:T(8,128)(2,1)S(1)} %get-tuple-element.70.refs_0_), channel_id=1, source_target_pairs={{0,4},{1,5},{2,6},{3,7},{4,0},{5,1},{6,2},{7,3},{8,12},{9,13},{10,... | collective-permute-start | bytes 331784 | tf_op jit(solution)/shard_map/ppermute | solution.py:182
  13.7 7.7 %collective-permute-start.6 = (bf16[3,48,384]{2,1,0:T(8,128)(2,1)S(1)}, bf16[3,48,384]{2,1,0:T(8,128)(2,1)S(1)}, u32[]{:S(2)}, u32[]{:S(2)}) collective-permute-start(bf16[3,48,384]{2,1,0:T(8,128)(2,1)S(1)} %collective-permute-done.refs_4_), channel_id=1, source_target_pairs={{0,8},{1,9},{2,10},{3,11},{4,12},{5,13},{6,14},{7,15},{8,0},{9,1},... | collective-permute-start | bytes 331784 | tf_op jit(solution)/shard_map/ppermute | solution.py:182
  14.0 13.5 %collective-permute-start.9 = (bf16[2,192,1024]{2,1,0:T(8,128)(2,1)S(1)}, bf16[2,192,1024]{2,1,0:T(8,128)(2,1)S(1)}, u32[]{:S(2)}, u32[]{:S(2)}) collective-permute-start(bf16[2,192,1024]{2,1,0:T(8,128)(2,1)S(1)} %pad_maximum_fusion.mine), channel_id=1, source_target_pairs={{0,1},{1,0},{2,3},{3,2},{4,5},{5,4},{6,7},{7,6},{8,9},{9,8},{10,11... | collective-permute-start | bytes 2359304 | tf_op jit(solution)/shard_map/ppermute | solution.py:182
  17.8 5.3 %collective-permute-start.5 = (bf16[3,48,384]{2,1,0:T(8,128)(2,1)S(1)}, bf16[3,48,384]{2,1,0:T(8,128)(2,1)S(1)}, u32[]{:S(2)}, u32[]{:S(2)}) collective-permute-start(bf16[3,48,384]{2,1,0:T(8,128)(2,1)S(1)} %collective-permute-done.refs_4_), channel_id=1, source_target_pairs={{0,4},{1,5},{2,6},{3,7},{4,0},{5,1},{6,2},{7,3},{8,12},{9,13},{10,... | collective-permute-start | bytes 331784 | tf_op jit(solution)/shard_map/ppermute | solution.py:182
  19.6 5.7 %collective-permute-start.4 = (bf16[3,48,384]{2,1,0:T(8,128)(2,1)S(1)}, bf16[3,48,384]{2,1,0:T(8,128)(2,1)S(1)}, u32[]{:S(2)}, u32[]{:S(2)}) collective-permute-start(bf16[3,48,384]{2,1,0:T(8,128)(2,1)S(1)} %collective-permute-done.3.refs_2_), channel_id=1, source_target_pairs={{0,4},{1,5},{2,6},{3,7},{4,0},{5,1},{6,2},{7,3},{8,12},{9,13},{10,... | collective-permute-start | bytes 331784 | tf_op jit(solution)/shard_map/ppermute | solution.py:182
  21.4 5.4 %collective-permute-start.7 = (bf16[3,48,384]{2,1,0:T(8,128)(2,1)S(1)}, bf16[3,48,384]{2,1,0:T(8,128)(2,1)S(1)}, u32[]{:S(2)}, u32[]{:S(2)}) collective-permute-start(bf16[3,48,384]{2,1,0:T(8,128)(2,1)S(1)} %collective-permute-done.6.refs_6_), channel_id=1, source_target_pairs={{0,4},{1,5},{2,6},{3,7},{4,0},{5,1},{6,2},{7,3},{8,12},{9,13},{10,... | collective-permute-start | bytes 331784 | tf_op jit(solution)/shard_map/ppermute | solution.py:182
  27.4 3.5 %collective-permute-start.8 = (bf16[2,192,1024]{2,1,0:T(8,128)(2,1)S(1)}, bf16[2,192,1024]{2,1,0:T(8,128)(2,1)S(1)}, u32[]{:S(2)}, u32[]{:S(2)}) collective-permute-start(bf16[2,192,1024]{2,1,0:T(8,128)(2,1)S(1)} %collective-permute-done.1.mine), channel_id=1, source_target_pairs={{0,1},{1,0},{2,3},{3,2},{4,5},{5,4},{6,7},{7,6},{8,9},{9,8},{10,11... | collective-permute-start | bytes 2359304 | tf_op jit(solution)/shard_map/ppermute | solution.py:182
  34.4 8.3 %collective-permute-start.10 = (bf16[2,3,48,384]{3,2,1,0:T(8,128)(2,1)S(1)}, bf16[2,3,48,384]{3,2,1,0:T(8,128)(2,1)S(1)}, u32[]{:S(2)}, u32[]{:S(2)}) collective-permute-start(bf16[2,3,48,384]{3,2,1,0:T(8,128)(2,1)S(1)} %get-tuple-element.45), channel_id=1, source_target_pairs={{0,4},{1,5},{2,6},{3,7},{4,0},{5,1},{6,2},{7,3},{8,12},{9,13},{10,... | collective-permute-start | bytes 663560 | tf_op jit(solution)/shard_map/ppermute | solution.py:182
  35.7 2.7 %collective-permute-start.11 = (bf16[2,192,128]{2,1,0:T(8,128)(2,1)S(1)}, bf16[2,192,128]{2,1,0:T(8,128)(2,1)S(1)}, u32[]{:S(2)}, u32[]{:S(2)}) collective-permute-start(bf16[2,192,128]{2,1,0:T(8,128)(2,1)S(1)} %pad_maximum_fusion.2.mine), channel_id=1, source_target_pairs={{0,1},{1,0},{2,3},{3,2},{4,5},{5,4},{6,7},{7,6},{8,9},{9,8},{10,11... | collective-permute-start | bytes 294920 | tf_op jit(solution)/shard_map/ppermute | solution.py:182
  35.9 5.6 %collective-permute-start.12 = (bf16[2,192,128]{2,1,0:T(8,128)(2,1)S(1)}, bf16[2,192,128]{2,1,0:T(8,128)(2,1)S(1)}, u32[]{:S(2)}, u32[]{:S(2)}) collective-permute-start(bf16[2,192,128]{2,1,0:T(8,128)(2,1)S(1)} %pad_maximum_fusion.2.mine), channel_id=1, source_target_pairs={{0,2},{1,3},{2,0},{3,1},{4,6},{5,7},{6,4},{7,5},{8,10},{9,11},{10,... | collective-permute-start | bytes 294920 | tf_op jit(solution)/shard_map/ppermute | solution.py:182
  36.8 5.6 %collective-permute-start.13 = (bf16[2,192,128]{2,1,0:T(8,128)(2,1)S(1)}, bf16[2,192,128]{2,1,0:T(8,128)(2,1)S(1)}, u32[]{:S(2)}, u32[]{:S(2)}) collective-permute-start(bf16[2,192,128]{2,1,0:T(8,128)(2,1)S(1)} %pad_maximum_fusion.2.mine), channel_id=1, source_target_pairs={{0,3},{1,2},{2,1},{3,0},{4,7},{5,6},{6,5},{7,4},{8,11},{9,10},{10,... | collective-permute-start | bytes 294920 | tf_op jit(solution)/shard_map/ppermute | solution.py:182
  37.5 9.5 %collective-permute-start.15 = (bf16[2,3,48,384]{3,2,1,0:T(8,128)(2,1)S(1)}, bf16[2,3,48,384]{3,2,1,0:T(8,128)(2,1)S(1)}, u32[]{:S(2)}, u32[]{:S(2)}) collective-permute-start(bf16[2,3,48,384]{3,2,1,0:T(8,128)(2,1)S(1)} %get-tuple-element.50), channel_id=1, source_target_pairs={{0,4},{1,5},{2,6},{3,7},{4,0},{5,1},{6,2},{7,3},{8,12},{9,13},{10,... | collective-permute-start | bytes 663560 | tf_op jit(solution)/shard_map/ppermute | solution.py:182
  42.8 15.3 %collective-permute-start.14 = (bf16[2,3,48,384]{3,2,1,0:T(8,128)(2,1)S(1)}, bf16[2,3,48,384]{3,2,1,0:T(8,128)(2,1)S(1)}, u32[]{:S(2)}, u32[]{:S(2)}) collective-permute-start(bf16[2,3,48,384]{3,2,1,0:T(8,128)(2,1)S(1)} %add_convert_fusion.1), channel_id=1, source_target_pairs={{0,12},{1,13},{2,14},{3,15},{4,8},{5,9},{6,10},{7,11},{8,4},{9,5},... | collective-permute-start | bytes 663560 | tf_op jit(solution)/shard_map/ppermute | solution.py:182
  47.1 15.2 %collective-permute-start.16 = (bf16[2,3,48,384]{3,2,1,0:T(8,128)(2,1)S(1)}, bf16[2,3,48,384]{3,2,1,0:T(8,128)(2,1)S(1)}, u32[]{:S(2)}, u32[]{:S(2)}) collective-permute-start(bf16[2,3,48,384]{3,2,1,0:T(8,128)(2,1)S(1)} %add_convert_fusion), channel_id=1, source_target_pairs={{0,12},{1,13},{2,14},{3,15},{4,8},{5,9},{6,10},{7,11},{8,4},{9,5},... | collective-permute-start | bytes 663560 | tf_op jit(solution)/shard_map/ppermute | solution.py:182
  58.9 8.9 %collective-permute-start.18 = (bf16[2,3,48,384]{3,2,1,0:T(8,128)(2,1)S(1)}, bf16[2,3,48,384]{3,2,1,0:T(8,128)(2,1)S(1)}, u32[]{:S(2)}, u32[]{:S(2)}) collective-permute-start(bf16[2,3,48,384]{3,2,1,0:T(8,128)(2,1)S(1)} %get-tuple-element.48.refs_0_), channel_id=1, source_target_pairs={{0,4},{1,5},{2,6},{3,7},{4,0},{5,1},{6,2},{7,3},{8,12},{9,13},{10,... | collective-permute-start | bytes 663560 | tf_op jit(solution)/shard_map/ppermute | solution.py:182
  63.1 4.6 %collective-permute-start.17 = (f32[2,24,96]{2,1,0:T(8,128)S(1)}, f32[2,24,96]{2,1,0:T(8,128)S(1)}, u32[]{:S(2)}, u32[]{:S(2)}) collective-permute-start(f32[2,24,96]{2,1,0:T(8,128)S(1)} %pad_maximum_fusion.3), channel_id=1, source_target_pairs={{0,1},{1,0},{2,3},{3,2},{4,5},{5,4},{6,7},{7,6},{8,9},{9,8},{10,11... | collective-permute-start | bytes 55304 | tf_op jit(solution)/shard_map/ppermute | solution.py:182
  63.2 10.5 %collective-permute-start.19 = (bf16[2,3,48,384]{3,2,1,0:T(8,128)(2,1)S(1)}, bf16[2,3,48,384]{3,2,1,0:T(8,128)(2,1)S(1)}, u32[]{:S(2)}, u32[]{:S(2)}) collective-permute-start(bf16[2,3,48,384]{3,2,1,0:T(8,128)(2,1)S(1)} %get-tuple-element.51.refs_1_), channel_id=1, source_target_pairs={{0,4},{1,5},{2,6},{3,7},{4,0},{5,1},{6,2},{7,3},{8,12},{9,13},{10,... | collective-permute-start | bytes 663560 | tf_op jit(solution)/shard_map/ppermute | solution.py:182
  67.8 3.9 %collective-permute-start.20 = (f32[2,24,96]{2,1,0:T(8,128)S(1)}, f32[2,24,96]{2,1,0:T(8,128)S(1)}, u32[]{:S(2)}, u32[]{:S(2)}) collective-permute-start(f32[2,24,96]{2,1,0:T(8,128)S(1)} %fusion.1.here), channel_id=1, source_target_pairs={{0,2},{1,3},{2,0},{3,1},{4,6},{5,7},{6,4},{7,5},{8,10},{9,11},{10,... | collective-permute-start | bytes 55304 | tf_op jit(solution)/shard_map/ppermute | solution.py:182
  71.7 3.8 %collective-permute-start.21 = (f32[2,16,96]{2,1,0:T(8,128)S(1)}, f32[2,16,96]{2,1,0:T(8,128)S(1)}, u32[]{:S(2)}, u32[]{:S(2)}) collective-permute-start(f32[2,16,96]{2,1,0:T(8,128)S(1)} %shard_map.100.refs_4_), channel_id=1, source_target_pairs={{0,4},{1,5},{2,6},{3,7},{4,0},{5,1},{6,2},{7,3},{8,12},{9,13},{10,... | collective-permute-start | bytes 36872 | tf_op jit(solution)/shard_map/ppermute | solution.py:182
  77.5 1.4 %collective-permute-start.22 = (bf16[2,192,128]{2,1,0:T(8,128)(2,1)S(1)}, bf16[2,192,128]{2,1,0:T(8,128)(2,1)S(1)}, u32[]{:S(2)}, u32[]{:S(2)}) collective-permute-start(bf16[2,192,128]{2,1,0:T(8,128)(2,1)S(1)} %get-tuple-element.59), channel_id=1, source_target_pairs={{0,1},{1,0},{2,3},{3,2},{4,5},{5,4},{6,7},{7,6},{8,9},{9,8},{10,11... | collective-permute-start | bytes 294920 | tf_op jit(solution)/shard_map/ppermute | solution.py:182
  78.9 4.9 %collective-permute-start.24 = (bf16[2,192,128]{2,1,0:T(8,128)(2,1)S(1)}, bf16[2,192,128]{2,1,0:T(8,128)(2,1)S(1)}, u32[]{:S(2)}, u32[]{:S(2)}) collective-permute-start(bf16[2,192,128]{2,1,0:T(8,128)(2,1)S(1)} %add_convert_fusion.2), channel_id=1, source_target_pairs={{0,2},{1,3},{2,0},{3,1},{4,6},{5,7},{6,4},{7,5},{8,10},{9,11},{10,... | collective-permute-start | bytes 294920 | tf_op jit(solution)/shard_map/ppermute | solution.py:182
  80.8 3.1 %collective-permute-start.23 = (bf16[2,192,128]{2,1,0:T(8,128)(2,1)S(1)}, bf16[2,192,128]{2,1,0:T(8,128)(2,1)S(1)}, u32[]{:S(2)}, u32[]{:S(2)}) collective-permute-start(bf16[2,192,128]{2,1,0:T(8,128)(2,1)S(1)} %get-tuple-element.65), channel_id=1, source_target_pairs={{0,1},{1,0},{2,3},{3,2},{4,5},{5,4},{6,7},{7,6},{8,9},{9,8},{10,11... | collective-permute-start | bytes 294920 | tf_op jit(solution)/shard_map/ppermute | solution.py:182

commit v7 on v6

--- a/solution.py
+++ b/solution.py
@@ -258,11 +258,17 @@
     stats = jnp.stack(stats)
     there, backs[0] = lax.optimization_barrier((swap(stats, core), backs[0]))
     stats = stats + there
-    (factors,) = call(
-        functools.partial(factor_kernel, 2 * n_hid * cols),
-        (stats, swap(stats, pair)),
-        (jax.ShapeDtypeStruct((parts, 16, 2 * rows // parts), f32),),
-    )
+    factors = [
+        call(
+            functools.partial(factor_kernel, 2 * n_hid * cols),
+            (here, there),
+            (jax.ShapeDtypeStruct((parts, 16, 2 * rows // parts), f32),),
+        )[0]
+        for here, there in (
+            (stats, swap(stats, pair)),
+            (swap(stats, zed), swap(stats, zed + pair)),
+        )
+    ]
 
     count = queries.shape[0]
     piece = (2, feats, count)
@@ -271,7 +277,7 @@
     query_flops = 6 * 2 * count * width * cols
     renewed, kept, given = call(
         functools.partial(renew_kernel, parts),
-        (weights, *sums, *backs, factors, swap(factors, zed), *quests[2:]),
+        (weights, *sums, *backs, *factors, *quests[2:]),
         [jax.ShapeDtypeStruct(whole, bf16), *kept_given],
         [query],
         query_flops,

time: 84.6 us -> 84 us (level)
  waiting for transfers between devices: 28.3 us -> 24.8 us
  starting transfers between devices: 39.7 us -> 42.5 us
    ppermute x25 -> x26, waiting for transfers between devices: 28.3 us -> 24.8 us  [swap(): return lax.ppermute(array, ('tok', 'hid'), pairs)]
    ppermute x25 -> x26, starting transfers between devices: 39.7 us -> 42.5 us  [swap(): return lax.ppermute(array, ('tok', 'hid'), pairs)]
    pallas_call x9 -> x10, Pallas kernels: 13.1 us -> 13.2 us  [call(): pl.pallas_call(body, out_shape=list(outs), in_specs=specs, out_specs=[pl....]
  transfers between devices with their start and end apart: 25 -> 26, of which waited for: 16 -> 16; matrix products, arithmetic and copies ran while one was open for 2% -> 2% of each run, Pallas kernels for 8% -> 8%
where the time goes in v7:
time: 84 us; the launch traced here: 83.8 us
  starting transfers between devices  42.5 us (51%)
  waiting for transfers between devices  24.8 us (30%)
  Pallas kernels  13.2 us (16%)
  other arithmetic  2.41 us (3%)
  between operations  0.89 us (1%)
    ppermute x26, starting transfers between devices, swap(): return lax.ppermute(array, ('tok', 'hid'), pairs)  42.5 us
    ppermute x26, waiting for transfers between devices, swap(): return lax.ppermute(array, ('tok', 'hid'), pairs)  24.8 us
    pallas_call x10, Pallas kernels, call(): pl.pallas_call(body, out_shape=list(outs), in_specs=specs, out_specs=[pl....  13.2 us
  transfers between devices with their start and end apart: 26, of which 16 were waited for; matrix products, arithmetic and copies ran while one was open for 2% of the time, Pallas kernels for 8%

profile of v7, /device:TPU:0, one launch (start us, length us, event | category | flops | bytes accessed | tf_op | source)
XLA Modules:
  0.0 83.8 jit_solution(767127035800667779)
XLA Ops:
  0.7 1.0 %pad_maximum_fusion.1 = bf16[3,48,768]{2,1,0:T(8,128)(2,1)S(1)} fusion(bf16[1,48,768]{2,1,0:T(8,128)(2,1)} %bitcast.28, bf16[1,48,768]{2,1,0:T(8,128)(2,1)} %bitcast.29, bf16[1,48,768]{2,1,0:T(8,128)(2,1)} %bitcast.30), kind=kLoop, calls=%fused_computation.5 | loop fusion | flops 221184 | bytes 442368 | tf_op jit(solution)/shard_map/stack | solution.py:188
  1.7 3.0 %collective-permute-start = (bf16[3,48,384]{2,1,0:T(8,128)(2,1)S(1)}, bf16[3,48,384]{2,1,0:T(8,128)(2,1)S(1)}, u32[]{:S(2)}, u32[]{:S(2)}) collective-permute-start(bf16[3,48,384]{2,1,0:T(8,128)(2,1)S(1)} %get-tuple-element.71), channel_id=1, source_target_pairs={{0,2},{1,3},{2,0},{3,1},{4,6},{5,7},{6,4},{7,5},{8,10},{9,11},{10,... | collective-permute-start | bytes 331784 | tf_op jit(solution)/shard_map/ppermute | solution.py:182
  4.7 1.1 %fusion = bf16[1,192,1024]{2,1,0:T(8,128)(2,1)S(1)} fusion(bf16[1024,192]{0,1:T(8,128)(2,1)} %param.9, f32[1024]{0:T(1024)} %param.10), kind=kLoop, calls=%fused_computation.4 | loop fusion | flops 589824 | bytes 790528 | tf_op jit(solution)/shard_map/stack | solution.py:193
  5.9 1.9 %collective-permute-done.refs_4_ = bf16[3,48,384]{2,1,0:T(8,128)(2,1)S(1)} collective-permute-done((bf16[3,48,384]{2,1,0:T(8,128)(2,1)S(1)}, bf16[3,48,384]{2,1,0:T(8,128)(2,1)S(1)}, u32[]{:S(2)}, u32[]{:S(2)}) %collective-permute-start) | collective-permute-done | bytes 110624 | tf_op jit(solution)/shard_map/ppermute | solution.py:182
  7.8 1.7 %collective-permute-start.1 = (bf16[2,192,1024]{2,1,0:T(8,128)(2,1)S(1)}, bf16[2,192,1024]{2,1,0:T(8,128)(2,1)S(1)}, u32[]{:S(2)}, u32[]{:S(2)}) collective-permute-start(bf16[2,192,1024]{2,1,0:T(8,128)(2,1)S(1)} %pad_maximum_fusion.mine), channel_id=1, source_target_pairs={{0,2},{1,3},{2,0},{3,1},{4,6},{5,7},{6,4},{7,5},{8,10},{9,11},{10,... | collective-permute-start | bytes 2359304 | tf_op jit(solution)/shard_map/ppermute | solution.py:182
  9.5 2.6 %collective-permute-start.3 = (bf16[3,48,384]{2,1,0:T(8,128)(2,1)S(1)}, bf16[3,48,384]{2,1,0:T(8,128)(2,1)S(1)}, u32[]{:S(2)}, u32[]{:S(2)}) collective-permute-start(bf16[3,48,384]{2,1,0:T(8,128)(2,1)S(1)} %get-tuple-element.70.refs_0_), channel_id=1, source_target_pairs={{0,8},{1,9},{2,10},{3,11},{4,12},{5,13},{6,14},{7,15},{8,0},{9,1},... | collective-permute-start | bytes 331784 | tf_op jit(solution)/shard_map/ppermute | solution.py:182
  12.1 1.6 %collective-permute-start.2 = (bf16[3,48,384]{2,1,0:T(8,128)(2,1)S(1)}, bf16[3,48,384]{2,1,0:T(8,128)(2,1)S(1)}, u32[]{:S(2)}, u32[]{:S(2)}) collective-permute-start(bf16[3,48,384]{2,1,0:T(8,128)(2,1)S(1)} %get-tuple-element.70.refs_0_), channel_id=1, source_target_pairs={{0,4},{1,5},{2,6},{3,7},{4,0},{5,1},{6,2},{7,3},{8,12},{9,13},{10,... | collective-permute-start | bytes 331784 | tf_op jit(solution)/shard_map/ppermute | solution.py:182
  14.0 3.8 %collective-permute-done.3.refs_2_ = bf16[3,48,384]{2,1,0:T(8,128)(2,1)S(1)} collective-permute-done((bf16[3,48,384]{2,1,0:T(8,128)(2,1)S(1)}, bf16[3,48,384]{2,1,0:T(8,128)(2,1)S(1)}, u32[]{:S(2)}, u32[]{:S(2)}) %collective-permute-start.3) | collective-permute-done | bytes 110624 | tf_op jit(solution)/shard_map/ppermute | solution.py:182
  17.8 1.8 %collective-permute-start.5 = (bf16[3,48,384]{2,1,0:T(8,128)(2,1)S(1)}, bf16[3,48,384]{2,1,0:T(8,128)(2,1)S(1)}, u32[]{:S(2)}, u32[]{:S(2)}) collective-permute-start(bf16[3,48,384]{2,1,0:T(8,128)(2,1)S(1)} %collective-permute-done.refs_4_), channel_id=1, source_target_pairs={{0,4},{1,5},{2,6},{3,7},{4,0},{5,1},{6,2},{7,3},{8,12},{9,13},{10,... | collective-permute-start | bytes 331784 | tf_op jit(solution)/shard_map/ppermute | solution.py:182
  20.4 1.0 %collective-permute-done.6.refs_6_ = bf16[3,48,384]{2,1,0:T(8,128)(2,1)S(1)} collective-permute-done((bf16[3,48,384]{2,1,0:T(8,128)(2,1)S(1)}, bf16[3,48,384]{2,1,0:T(8,128)(2,1)S(1)}, u32[]{:S(2)}, u32[]{:S(2)}) %collective-permute-start.6) | collective-permute-done | bytes 110624 | tf_op jit(solution)/shard_map/ppermute | solution.py:182
  22.0 1.2 %collective-permute-done.5.refs_5_ = bf16[3,48,384]{2,1,0:T(8,128)(2,1)S(1)} collective-permute-done((bf16[3,48,384]{2,1,0:T(8,128)(2,1)S(1)}, bf16[3,48,384]{2,1,0:T(8,128)(2,1)S(1)}, u32[]{:S(2)}, u32[]{:S(2)}) %collective-permute-start.5) | collective-permute-done | bytes 110624 | tf_op jit(solution)/shard_map/ppermute | solution.py:182
  23.2 2.2 %collective-permute-done.4.refs_3_ = bf16[3,48,384]{2,1,0:T(8,128)(2,1)S(1)} collective-permute-done((bf16[3,48,384]{2,1,0:T(8,128)(2,1)S(1)}, bf16[3,48,384]{2,1,0:T(8,128)(2,1)S(1)}, u32[]{:S(2)}, u32[]{:S(2)}) %collective-permute-start.4) | collective-permute-done | bytes 110624 | tf_op jit(solution)/shard_map/ppermute | solution.py:182
  25.3 1.4 %collective-permute-done.7.refs_7_ = bf16[3,48,384]{2,1,0:T(8,128)(2,1)S(1)} collective-permute-done((bf16[3,48,384]{2,1,0:T(8,128)(2,1)S(1)}, bf16[3,48,384]{2,1,0:T(8,128)(2,1)S(1)}, u32[]{:S(2)}, u32[]{:S(2)}) %collective-permute-start.7) | collective-permute-done | bytes 110624 | tf_op jit(solution)/shard_map/ppermute | solution.py:182
  27.5 3.3 %shard_map.96.before = f32[3,384,384]{2,1,0:T(8,128)S(1)} custom-call(s32[3]{0:T(128)S(1)} %pad_add_fusion.place, bf16[2,192,1024]{2,1,0:T(8,128)(2,1)S(1)} %pad_maximum_fusion.mine, bf16[2,192,1024]{2,1,0:T(8,128)(2,1)S(1)} %collective-permute-done.9.other, bf16[3,384,384]{2,1,0:T(8,128)(2,1)S(1)} %shard_map.95.weights), custom_call_target="tpu_custom_call" | custom-call | flops 1811939328 | bytes 6684684 | tf_op jit(solution)/shard_map/pallas_call | solution.py:159
  30.9 3.5 %shard_map.97 = (f32[2,3,48,384]{3,2,1,0:T(8,128)S(1)}, f32[2,3,48,384]{3,2,1,0:T(8,128)S(1)}, bf16[2,3,48,384]{3,2,1,0:T(8,128)(2,1)S(1)}, bf16[2,3,48,384]{3,2,1,0:T(8,128)(2,1)S(1)}) custom-call(s32[3]{0:T(128)S(1)} %pad_add_fusion.place, bf16[2,192,1024]{2,1,0:T(8,128)(2,1)S(1)} %collective-permute-done.1.mine, ...), custom_call_target="tpu_custom_call" | custom-call | flops 1811939328 | bytes 8454156 | tf_op jit(solution)/shard_map/pallas_call | solution.py:159
  34.4 1.2 %collective-permute-start.10 = (bf16[2,3,48,384]{3,2,1,0:T(8,128)(2,1)S(1)}, bf16[2,3,48,384]{3,2,1,0:T(8,128)(2,1)S(1)}, u32[]{:S(2)}, u32[]{:S(2)}) collective-permute-start(bf16[2,3,48,384]{3,2,1,0:T(8,128)(2,1)S(1)} %get-tuple-element.45), channel_id=1, source_target_pairs={{0,4},{1,5},{2,6},{3,7},{4,0},{5,1},{6,2},{7,3},{8,12},{9,13},{10,... | collective-permute-start | bytes 663560 | tf_op jit(solution)/shard_map/ppermute | solution.py:182
  35.9 0.9 %collective-permute-start.12 = (bf16[2,192,128]{2,1,0:T(8,128)(2,1)S(1)}, bf16[2,192,128]{2,1,0:T(8,128)(2,1)S(1)}, u32[]{:S(2)}, u32[]{:S(2)}) collective-permute-start(bf16[2,192,128]{2,1,0:T(8,128)(2,1)S(1)} %pad_maximum_fusion.2.mine), channel_id=1, source_target_pairs={{0,2},{1,3},{2,0},{3,1},{4,6},{5,7},{6,4},{7,5},{8,10},{9,11},{10,... | collective-permute-start | bytes 294920 | tf_op jit(solution)/shard_map/ppermute | solution.py:182
  38.4 3.1 %collective-permute-done.12.refs_6_ = bf16[2,192,128]{2,1,0:T(8,128)(2,1)S(1)} collective-permute-done((bf16[2,192,128]{2,1,0:T(8,128)(2,1)S(1)}, bf16[2,192,128]{2,1,0:T(8,128)(2,1)S(1)}, u32[]{:S(2)}, u32[]{:S(2)}) %collective-permute-start.12) | collective-permute-done | bytes 98336 | tf_op jit(solution)/shard_map/ppermute | solution.py:182
  41.5 0.9 %collective-permute-done.13.refs_7_ = bf16[2,192,128]{2,1,0:T(8,128)(2,1)S(1)} collective-permute-done((bf16[2,192,128]{2,1,0:T(8,128)(2,1)S(1)}, bf16[2,192,128]{2,1,0:T(8,128)(2,1)S(1)}, u32[]{:S(2)}, u32[]{:S(2)}) %collective-permute-start.13) | collective-permute-done | bytes 98336 | tf_op jit(solution)/shard_map/ppermute | solution.py:182
  42.8 3.8 %collective-permute-start.14 = (bf16[2,3,48,384]{3,2,1,0:T(8,128)(2,1)S(1)}, bf16[2,3,48,384]{3,2,1,0:T(8,128)(2,1)S(1)}, u32[]{:S(2)}, u32[]{:S(2)}) collective-permute-start(bf16[2,3,48,384]{3,2,1,0:T(8,128)(2,1)S(1)} %add_convert_fusion.1), channel_id=1, source_target_pairs={{0,12},{1,13},{2,14},{3,15},{4,8},{5,9},{6,10},{7,11},{8,4},{9,5},... | collective-permute-start | bytes 663560 | tf_op jit(solution)/shard_map/ppermute | solution.py:182
  47.1 10.9 %collective-permute-start.16 = (bf16[2,3,48,384]{3,2,1,0:T(8,128)(2,1)S(1)}, bf16[2,3,48,384]{3,2,1,0:T(8,128)(2,1)S(1)}, u32[]{:S(2)}, u32[]{:S(2)}) collective-permute-start(bf16[2,3,48,384]{3,2,1,0:T(8,128)(2,1)S(1)} %add_convert_fusion), channel_id=1, source_target_pairs={{0,12},{1,13},{2,14},{3,15},{4,8},{5,9},{6,10},{7,11},{8,4},{9,5},... | collective-permute-start | bytes 663560 | tf_op jit(solution)/shard_map/ppermute | solution.py:182
  58.9 1.6 %collective-permute-start.18 = (bf16[2,3,48,384]{3,2,1,0:T(8,128)(2,1)S(1)}, bf16[2,3,48,384]{3,2,1,0:T(8,128)(2,1)S(1)}, u32[]{:S(2)}, u32[]{:S(2)}) collective-permute-start(bf16[2,3,48,384]{3,2,1,0:T(8,128)(2,1)S(1)} %get-tuple-element.48.refs_0_), channel_id=1, source_target_pairs={{0,4},{1,5},{2,6},{3,7},{4,0},{5,1},{6,2},{7,3},{8,12},{9,13},{10,... | collective-permute-start | bytes 663560 | tf_op jit(solution)/shard_map/ppermute | solution.py:182
  60.4 1.9 %collective-permute-done.16.crossed = bf16[2,3,48,384]{3,2,1,0:T(8,128)(2,1)S(1)} collective-permute-done((bf16[2,3,48,384]{3,2,1,0:T(8,128)(2,1)S(1)}, bf16[2,3,48,384]{3,2,1,0:T(8,128)(2,1)S(1)}, u32[]{:S(2)}, u32[]{:S(2)}) %collective-permute-start.16) | collective-permute-done | bytes 221216 | tf_op jit(solution)/shard_map/ppermute | solution.py:182
  63.2 4.5 %collective-permute-start.19 = (bf16[2,3,48,384]{3,2,1,0:T(8,128)(2,1)S(1)}, bf16[2,3,48,384]{3,2,1,0:T(8,128)(2,1)S(1)}, u32[]{:S(2)}, u32[]{:S(2)}) collective-permute-start(bf16[2,3,48,384]{3,2,1,0:T(8,128)(2,1)S(1)} %get-tuple-element.51.refs_1_), channel_id=1, source_target_pairs={{0,4},{1,5},{2,6},{3,7},{4,0},{5,1},{6,2},{7,3},{8,12},{9,13},{10,... | collective-permute-start | bytes 663560 | tf_op jit(solution)/shard_map/ppermute | solution.py:182
  68.3 1.1 %collective-permute-start.21 = (f32[2,24,96]{2,1,0:T(8,128)S(1)}, f32[2,24,96]{2,1,0:T(8,128)S(1)}, u32[]{:S(2)}, u32[]{:S(2)}) collective-permute-start(f32[2,24,96]{2,1,0:T(8,128)S(1)} %fusion.1.here), channel_id=1, source_target_pairs={{0,4},{1,5},{2,6},{3,7},{4,0},{5,1},{6,2},{7,3},{8,12},{9,13},{10,... | collective-permute-start | bytes 55304 | tf_op jit(solution)/shard_map/ppermute | solution.py:182
  69.4 1.9 %collective-permute-start.22 = (f32[2,24,96]{2,1,0:T(8,128)S(1)}, f32[2,24,96]{2,1,0:T(8,128)S(1)}, u32[]{:S(2)}, u32[]{:S(2)}) collective-permute-start(f32[2,24,96]{2,1,0:T(8,128)S(1)} %fusion.1.here), channel_id=1, source_target_pairs={{0,6},{1,7},{2,4},{3,5},{4,2},{5,3},{6,0},{7,1},{8,14},{9,15},{10,... | collective-permute-start | bytes 55304 | tf_op jit(solution)/shard_map/ppermute | solution.py:182
  71.7 2.8 %collective-permute-done.21.here = f32[2,24,96]{2,1,0:T(8,128)S(1)} collective-permute-done((f32[2,24,96]{2,1,0:T(8,128)S(1)}, f32[2,24,96]{2,1,0:T(8,128)S(1)}, u32[]{:S(2)}, u32[]{:S(2)}) %collective-permute-start.21) | collective-permute-done | bytes 18464 | tf_op jit(solution)/shard_map/ppermute | solution.py:182
  74.8 2.0 %shard_map.102 = (bf16[3,384,384]{2,1,0:T(8,128)(2,1)S(1)}, f32[2,192,128]{2,1,0:T(8,128)S(1)}, bf16[2,192,128]{2,1,0:T(8,128)(2,1)S(1)}) custom-call(s32[3]{0:T(128)S(1)} %pad_add_fusion.place, bf16[3,384,384]{2,1,0:T(8,128)(2,1)S(1)} %shard_map.95.weights, bf16[2,3,48,384]{3,2,1,0:T(8,128)(2,1)S(1)} %get-tuple-element.48.refs_0_, ...), custom_call_target="tpu_custom_call" | custom-call | flops 226492416 | bytes 6119436 | tf_op jit(solution)/shard_map/pallas_call | solution.py:159
  76.9 1.3 %collective-permute-done.23 = bf16[2,192,128]{2,1,0:T(8,128)(2,1)S(1)} collective-permute-done((bf16[2,192,128]{2,1,0:T(8,128)(2,1)S(1)}, bf16[2,192,128]{2,1,0:T(8,128)(2,1)S(1)}, u32[]{:S(2)}, u32[]{:S(2)}) %collective-permute-start.23) | collective-permute-done | bytes 98336 | tf_op jit(solution)/shard_map/ppermute | solution.py:182
  78.2 1.5 %collective-permute-start.25 = (bf16[2,192,128]{2,1,0:T(8,128)(2,1)S(1)}, bf16[2,192,128]{2,1,0:T(8,128)(2,1)S(1)}, u32[]{:S(2)}, u32[]{:S(2)}) collective-permute-start(bf16[2,192,128]{2,1,0:T(8,128)(2,1)S(1)} %add_convert_fusion.2), channel_id=1, source_target_pairs={{0,2},{1,3},{2,0},{3,1},{4,6},{5,7},{6,4},{7,5},{8,10},{9,11},{10,... | collective-permute-start | bytes 294920 | tf_op jit(solution)/shard_map/ppermute | solution.py:182
  79.7 1.3 %shard_map.103 = (f32[2,192,128]{2,1,0:T(8,128)S(1)}, bf16[2,192,128]{2,1,0:T(8,128)(2,1)S(1)}) custom-call(s32[3]{0:T(128)S(1)} %pad_add_fusion.place, bf16[3,384,384]{2,1,0:T(8,128)(2,1)S(1)} %get-tuple-element.58.renewed, bf16[2,192,128]{2,1,0:T(8,128)(2,1)S(1)} %pad_maximum_fusion.2.mine, bf16[2,192,128]{2,1,0:T(8,128)(2,1)S(1)} %collective-permute-done.11.other), custom_call_target="tpu_custom_call" | custom-call | flops 226492416 | bytes 2555916 | tf_op jit(solution)/shard_map/pallas_call | solution.py:159
  81.1 2.1 %collective-permute-done.25.pair = bf16[2,192,128]{2,1,0:T(8,128)(2,1)S(1)} collective-permute-done((bf16[2,192,128]{2,1,0:T(8,128)(2,1)S(1)}, bf16[2,192,128]{2,1,0:T(8,128)(2,1)S(1)}, u32[]{:S(2)}, u32[]{:S(2)}) %collective-permute-start.25) | collective-permute-done | bytes 98336 | tf_op jit(solution)/shard_map/ppermute | solution.py:182
  (47 shorter events, 9.1 us)
Async XLA Ops:
  0.6 5.2 %copy-start = (bf16[1024,192]{0,1:T(8,128)(2,1)S(1)}, bf16[1024,192]{0,1:T(8,128)(2,1)}, u32[]{:S(2)}) copy-start(bf16[1024,192]{0,1:T(8,128)(2,1)} %param.8) | copy-start | bytes 1179652
  1.7 6.1 %collective-permute-start = (bf16[3,48,384]{2,1,0:T(8,128)(2,1)S(1)}, bf16[3,48,384]{2,1,0:T(8,128)(2,1)S(1)}, u32[]{:S(2)}, u32[]{:S(2)}) collective-permute-start(bf16[3,48,384]{2,1,0:T(8,128)(2,1)S(1)} %get-tuple-element.71), channel_id=1, source_target_pairs={{0,2},{1,3},{2,0},{3,1},{4,6},{5,7},{6,4},{7,5},{8,10},{9,11},{10,... | collective-permute-start | bytes 331784 | tf_op jit(solution)/shard_map/ppermute | solution.py:182
  5.8 21.6 %copy-start.1 = (bf16[128,192]{0,1:T(8,128)(2,1)S(1)}, bf16[128,192]{0,1:T(8,128)(2,1)}, u32[]{:S(2)}) copy-start(bf16[128,192]{0,1:T(8,128)(2,1)} %param.15) | copy-start | bytes 147460
  5.8 21.6 %copy-start.2 = (bf16[128,192]{0,1:T(8,128)(2,1)S(1)}, bf16[128,192]{0,1:T(8,128)(2,1)}, u32[]{:S(2)}) copy-start(bf16[128,192]{0,1:T(8,128)(2,1)} %param.14) | copy-start | bytes 147460
  7.8 19.6 %collective-permute-start.1 = (bf16[2,192,1024]{2,1,0:T(8,128)(2,1)S(1)}, bf16[2,192,1024]{2,1,0:T(8,128)(2,1)S(1)}, u32[]{:S(2)}, u32[]{:S(2)}) collective-permute-start(bf16[2,192,1024]{2,1,0:T(8,128)(2,1)S(1)} %pad_maximum_fusion.mine), channel_id=1, source_target_pairs={{0,2},{1,3},{2,0},{3,1},{4,6},{5,7},{6,4},{7,5},{8,10},{9,11},{10,... | collective-permute-start | bytes 2359304 | tf_op jit(solution)/shard_map/ppermute | solution.py:182
  9.5 8.3 %collective-permute-start.3 = (bf16[3,48,384]{2,1,0:T(8,128)(2,1)S(1)}, bf16[3,48,384]{2,1,0:T(8,128)(2,1)S(1)}, u32[]{:S(2)}, u32[]{:S(2)}) collective-permute-start(bf16[3,48,384]{2,1,0:T(8,128)(2,1)S(1)} %get-tuple-element.70.refs_0_), channel_id=1, source_target_pairs={{0,8},{1,9},{2,10},{3,11},{4,12},{5,13},{6,14},{7,15},{8,0},{9,1},... | collective-permute-start | bytes 331784 | tf_op jit(solution)/shard_map/ppermute | solution.py:182
  12.1 7.5 %collective-permute-start.2 = (bf16[3,48,384]{2,1,0:T(8,128)(2,1)S(1)}, bf16[3,48,384]{2,1,0:T(8,128)(2,1)S(1)}, u32[]{:S(2)}, u32[]{:S(2)}) collective-permute-start(bf16[3,48,384]{2,1,0:T(8,128)(2,1)S(1)} %get-tuple-element.70.refs_0_), channel_id=1, source_target_pairs={{0,4},{1,5},{2,6},{3,7},{4,0},{5,1},{6,2},{7,3},{8,12},{9,13},{10,... | collective-permute-start | bytes 331784 | tf_op jit(solution)/shard_map/ppermute | solution.py:182
  13.7 7.7 %collective-permute-start.6 = (bf16[3,48,384]{2,1,0:T(8,128)(2,1)S(1)}, bf16[3,48,384]{2,1,0:T(8,128)(2,1)S(1)}, u32[]{:S(2)}, u32[]{:S(2)}) collective-permute-start(bf16[3,48,384]{2,1,0:T(8,128)(2,1)S(1)} %collective-permute-done.refs_4_), channel_id=1, source_target_pairs={{0,8},{1,9},{2,10},{3,11},{4,12},{5,13},{6,14},{7,15},{8,0},{9,1},... | collective-permute-start | bytes 331784 | tf_op jit(solution)/shard_map/ppermute | solution.py:182
  14.0 13.5 %collective-permute-start.9 = (bf16[2,192,1024]{2,1,0:T(8,128)(2,1)S(1)}, bf16[2,192,1024]{2,1,0:T(8,128)(2,1)S(1)}, u32[]{:S(2)}, u32[]{:S(2)}) collective-permute-start(bf16[2,192,1024]{2,1,0:T(8,128)(2,1)S(1)} %pad_maximum_fusion.mine), channel_id=1, source_target_pairs={{0,1},{1,0},{2,3},{3,2},{4,5},{5,4},{6,7},{7,6},{8,9},{9,8},{10,11... | collective-permute-start | bytes 2359304 | tf_op jit(solution)/shard_map/ppermute | solution.py:182
  17.8 5.3 %collective-permute-start.5 = (bf16[3,48,384]{2,1,0:T(8,128)(2,1)S(1)}, bf16[3,48,384]{2,1,0:T(8,128)(2,1)S(1)}, u32[]{:S(2)}, u32[]{:S(2)}) collective-permute-start(bf16[3,48,384]{2,1,0:T(8,128)(2,1)S(1)} %collective-permute-done.refs_4_), channel_id=1, source_target_pairs={{0,4},{1,5},{2,6},{3,7},{4,0},{5,1},{6,2},{7,3},{8,12},{9,13},{10,... | collective-permute-start | bytes 331784 | tf_op jit(solution)/shard_map/ppermute | solution.py:182
  19.6 5.7 %collective-permute-start.4 = (bf16[3,48,384]{2,1,0:T(8,128)(2,1)S(1)}, bf16[3,48,384]{2,1,0:T(8,128)(2,1)S(1)}, u32[]{:S(2)}, u32[]{:S(2)}) collective-permute-start(bf16[3,48,384]{2,1,0:T(8,128)(2,1)S(1)} %collective-permute-done.3.refs_2_), channel_id=1, source_target_pairs={{0,4},{1,5},{2,6},{3,7},{4,0},{5,1},{6,2},{7,3},{8,12},{9,13},{10,... | collective-permute-start | bytes 331784 | tf_op jit(solution)/shard_map/ppermute | solution.py:182
  21.4 5.4 %collective-permute-start.7 = (bf16[3,48,384]{2,1,0:T(8,128)(2,1)S(1)}, bf16[3,48,384]{2,1,0:T(8,128)(2,1)S(1)}, u32[]{:S(2)}, u32[]{:S(2)}) collective-permute-start(bf16[3,48,384]{2,1,0:T(8,128)(2,1)S(1)} %collective-permute-done.6.refs_6_), channel_id=1, source_target_pairs={{0,4},{1,5},{2,6},{3,7},{4,0},{5,1},{6,2},{7,3},{8,12},{9,13},{10,... | collective-permute-start | bytes 331784 | tf_op jit(solution)/shard_map/ppermute | solution.py:182
  27.4 3.5 %collective-permute-start.8 = (bf16[2,192,1024]{2,1,0:T(8,128)(2,1)S(1)}, bf16[2,192,1024]{2,1,0:T(8,128)(2,1)S(1)}, u32[]{:S(2)}, u32[]{:S(2)}) collective-permute-start(bf16[2,192,1024]{2,1,0:T(8,128)(2,1)S(1)} %collective-permute-done.1.mine), channel_id=1, source_target_pairs={{0,1},{1,0},{2,3},{3,2},{4,5},{5,4},{6,7},{7,6},{8,9},{9,8},{10,11... | collective-permute-start | bytes 2359304 | tf_op jit(solution)/shard_map/ppermute | solution.py:182
  34.4 8.3 %collective-permute-start.10 = (bf16[2,3,48,384]{3,2,1,0:T(8,128)(2,1)S(1)}, bf16[2,3,48,384]{3,2,1,0:T(8,128)(2,1)S(1)}, u32[]{:S(2)}, u32[]{:S(2)}) collective-permute-start(bf16[2,3,48,384]{3,2,1,0:T(8,128)(2,1)S(1)} %get-tuple-element.45), channel_id=1, source_target_pairs={{0,4},{1,5},{2,6},{3,7},{4,0},{5,1},{6,2},{7,3},{8,12},{9,13},{10,... | collective-permute-start | bytes 663560 | tf_op jit(solution)/shard_map/ppermute | solution.py:182
  35.7 2.7 %collective-permute-start.11 = (bf16[2,192,128]{2,1,0:T(8,128)(2,1)S(1)}, bf16[2,192,128]{2,1,0:T(8,128)(2,1)S(1)}, u32[]{:S(2)}, u32[]{:S(2)}) collective-permute-start(bf16[2,192,128]{2,1,0:T(8,128)(2,1)S(1)} %pad_maximum_fusion.2.mine), channel_id=1, source_target_pairs={{0,1},{1,0},{2,3},{3,2},{4,5},{5,4},{6,7},{7,6},{8,9},{9,8},{10,11... | collective-permute-start | bytes 294920 | tf_op jit(solution)/shard_map/ppermute | solution.py:182
  35.9 5.6 %collective-permute-start.12 = (bf16[2,192,128]{2,1,0:T(8,128)(2,1)S(1)}, bf16[2,192,128]{2,1,0:T(8,128)(2,1)S(1)}, u32[]{:S(2)}, u32[]{:S(2)}) collective-permute-start(bf16[2,192,128]{2,1,0:T(8,128)(2,1)S(1)} %pad_maximum_fusion.2.mine), channel_id=1, source_target_pairs={{0,2},{1,3},{2,0},{3,1},{4,6},{5,7},{6,4},{7,5},{8,10},{9,11},{10,... | collective-permute-start | bytes 294920 | tf_op jit(solution)/shard_map/ppermute | solution.py:182
  36.8 5.6 %collective-permute-start.13 = (bf16[2,192,128]{2,1,0:T(8,128)(2,1)S(1)}, bf16[2,192,128]{2,1,0:T(8,128)(2,1)S(1)}, u32[]{:S(2)}, u32[]{:S(2)}) collective-permute-start(bf16[2,192,128]{2,1,0:T(8,128)(2,1)S(1)} %pad_maximum_fusion.2.mine), channel_id=1, source_target_pairs={{0,3},{1,2},{2,1},{3,0},{4,7},{5,6},{6,5},{7,4},{8,11},{9,10},{10,... | collective-permute-start | bytes 294920 | tf_op jit(solution)/shard_map/ppermute | solution.py:182
  37.5 9.5 %collective-permute-start.15 = (bf16[2,3,48,384]{3,2,1,0:T(8,128)(2,1)S(1)}, bf16[2,3,48,384]{3,2,1,0:T(8,128)(2,1)S(1)}, u32[]{:S(2)}, u32[]{:S(2)}) collective-permute-start(bf16[2,3,48,384]{3,2,1,0:T(8,128)(2,1)S(1)} %get-tuple-element.50), channel_id=1, source_target_pairs={{0,4},{1,5},{2,6},{3,7},{4,0},{5,1},{6,2},{7,3},{8,12},{9,13},{10,... | collective-permute-start | bytes 663560 | tf_op jit(solution)/shard_map/ppermute | solution.py:182
  42.8 15.3 %collective-permute-start.14 = (bf16[2,3,48,384]{3,2,1,0:T(8,128)(2,1)S(1)}, bf16[2,3,48,384]{3,2,1,0:T(8,128)(2,1)S(1)}, u32[]{:S(2)}, u32[]{:S(2)}) collective-permute-start(bf16[2,3,48,384]{3,2,1,0:T(8,128)(2,1)S(1)} %add_convert_fusion.1), channel_id=1, source_target_pairs={{0,12},{1,13},{2,14},{3,15},{4,8},{5,9},{6,10},{7,11},{8,4},{9,5},... | collective-permute-start | bytes 663560 | tf_op jit(solution)/shard_map/ppermute | solution.py:182
  47.1 15.2 %collective-permute-start.16 = (bf16[2,3,48,384]{3,2,1,0:T(8,128)(2,1)S(1)}, bf16[2,3,48,384]{3,2,1,0:T(8,128)(2,1)S(1)}, u32[]{:S(2)}, u32[]{:S(2)}) collective-permute-start(bf16[2,3,48,384]{3,2,1,0:T(8,128)(2,1)S(1)} %add_convert_fusion), channel_id=1, source_target_pairs={{0,12},{1,13},{2,14},{3,15},{4,8},{5,9},{6,10},{7,11},{8,4},{9,5},... | collective-permute-start | bytes 663560 | tf_op jit(solution)/shard_map/ppermute | solution.py:182
  58.9 8.9 %collective-permute-start.18 = (bf16[2,3,48,384]{3,2,1,0:T(8,128)(2,1)S(1)}, bf16[2,3,48,384]{3,2,1,0:T(8,128)(2,1)S(1)}, u32[]{:S(2)}, u32[]{:S(2)}) collective-permute-start(bf16[2,3,48,384]{3,2,1,0:T(8,128)(2,1)S(1)} %get-tuple-element.48.refs_0_), channel_id=1, source_target_pairs={{0,4},{1,5},{2,6},{3,7},{4,0},{5,1},{6,2},{7,3},{8,12},{9,13},{10,... | collective-permute-start | bytes 663560 | tf_op jit(solution)/shard_map/ppermute | solution.py:182
  63.1 4.6 %collective-permute-start.17 = (f32[2,24,96]{2,1,0:T(8,128)S(1)}, f32[2,24,96]{2,1,0:T(8,128)S(1)}, u32[]{:S(2)}, u32[]{:S(2)}) collective-permute-start(f32[2,24,96]{2,1,0:T(8,128)S(1)} %pad_maximum_fusion.3), channel_id=1, source_target_pairs={{0,1},{1,0},{2,3},{3,2},{4,5},{5,4},{6,7},{7,6},{8,9},{9,8},{10,11... | collective-permute-start | bytes 55304 | tf_op jit(solution)/shard_map/ppermute | solution.py:182
  63.2 11.6 %collective-permute-start.19 = (bf16[2,3,48,384]{3,2,1,0:T(8,128)(2,1)S(1)}, bf16[2,3,48,384]{3,2,1,0:T(8,128)(2,1)S(1)}, u32[]{:S(2)}, u32[]{:S(2)}) collective-permute-start(bf16[2,3,48,384]{3,2,1,0:T(8,128)(2,1)S(1)} %get-tuple-element.51.refs_1_), channel_id=1, source_target_pairs={{0,4},{1,5},{2,6},{3,7},{4,0},{5,1},{6,2},{7,3},{8,12},{9,13},{10,... | collective-permute-start | bytes 663560 | tf_op jit(solution)/shard_map/ppermute | solution.py:182
  67.8 3.9 %collective-permute-start.20 = (f32[2,24,96]{2,1,0:T(8,128)S(1)}, f32[2,24,96]{2,1,0:T(8,128)S(1)}, u32[]{:S(2)}, u32[]{:S(2)}) collective-permute-start(f32[2,24,96]{2,1,0:T(8,128)S(1)} %fusion.1.here), channel_id=1, source_target_pairs={{0,2},{1,3},{2,0},{3,1},{4,6},{5,7},{6,4},{7,5},{8,10},{9,11},{10,... | collective-permute-start | bytes 55304 | tf_op jit(solution)/shard_map/ppermute | solution.py:182
  68.3 6.1 %collective-permute-start.21 = (f32[2,24,96]{2,1,0:T(8,128)S(1)}, f32[2,24,96]{2,1,0:T(8,128)S(1)}, u32[]{:S(2)}, u32[]{:S(2)}) collective-permute-start(f32[2,24,96]{2,1,0:T(8,128)S(1)} %fusion.1.here), channel_id=1, source_target_pairs={{0,4},{1,5},{2,6},{3,7},{4,0},{5,1},{6,2},{7,3},{8,12},{9,13},{10,... | collective-permute-start | bytes 55304 | tf_op jit(solution)/shard_map/ppermute | solution.py:182
  69.4 5.3 %collective-permute-start.22 = (f32[2,24,96]{2,1,0:T(8,128)S(1)}, f32[2,24,96]{2,1,0:T(8,128)S(1)}, u32[]{:S(2)}, u32[]{:S(2)}) collective-permute-start(f32[2,24,96]{2,1,0:T(8,128)S(1)} %fusion.1.here), channel_id=1, source_target_pairs={{0,6},{1,7},{2,4},{3,5},{4,2},{5,3},{6,0},{7,1},{8,14},{9,15},{10,... | collective-permute-start | bytes 55304 | tf_op jit(solution)/shard_map/ppermute | solution.py:182
  76.8 1.4 %collective-permute-start.23 = (bf16[2,192,128]{2,1,0:T(8,128)(2,1)S(1)}, bf16[2,192,128]{2,1,0:T(8,128)(2,1)S(1)}, u32[]{:S(2)}, u32[]{:S(2)}) collective-permute-start(bf16[2,192,128]{2,1,0:T(8,128)(2,1)S(1)} %get-tuple-element.59), channel_id=1, source_target_pairs={{0,1},{1,0},{2,3},{3,2},{4,5},{5,4},{6,7},{7,6},{8,9},{9,8},{10,11... | collective-permute-start | bytes 294920 | tf_op jit(solution)/shard_map/ppermute | solution.py:182
  78.2 4.9 %collective-permute-start.25 = (bf16[2,192,128]{2,1,0:T(8,128)(2,1)S(1)}, bf16[2,192,128]{2,1,0:T(8,128)(2,1)S(1)}, u32[]{:S(2)}, u32[]{:S(2)}) collective-permute-start(bf16[2,192,128]{2,1,0:T(8,128)(2,1)S(1)} %add_convert_fusion.2), channel_id=1, source_target_pairs={{0,2},{1,3},{2,0},{3,1},{4,6},{5,7},{6,4},{7,5},{8,10},{9,11},{10,... | collective-permute-start | bytes 294920 | tf_op jit(solution)/shard_map/ppermute | solution.py:182
  81.0 2.1 %collective-permute-start.24 = (bf16[2,192,128]{2,1,0:T(8,128)(2,1)S(1)}, bf16[2,192,128]{2,1,0:T(8,128)(2,1)S(1)}, u32[]{:S(2)}, u32[]{:S(2)}) collective-permute-start(bf16[2,192,128]{2,1,0:T(8,128)(2,1)S(1)} %get-tuple-element.65), channel_id=1, source_target_pairs={{0,1},{1,0},{2,3},{3,2},{4,5},{5,4},{6,7},{7,6},{8,9},{9,8},{10,11... | collective-permute-start | bytes 294920 | tf_op jit(solution)/shard_map/ppermute | solution.py:182

commit v8 on v7

--- a/solution.py
+++ b/solution.py
@@ -32,7 +32,7 @@
     full[:, pl.ds(pl.multiple_of((1 - half) * feats, feats), feats), :] = other[...]
 
 
-def gradients(tokens, weights, deltas, acts):
+def backward(tokens, weights, deltas, acts):
     cols, total = acts.shape
     chunk = min(512, total)
     for start in range(0, total, chunk):
@@ -44,6 +44,10 @@
         deltas[:cols, span] = (back * slope_up).astype(bf16)
         deltas[cols:, span] = (back * silu).astype(bf16)
         acts[:, span] = act.astype(bf16)
+
+
+def gradients(tokens, deltas, acts):
+    cols = acts.shape[0]
     both = contract(tokens[0], deltas[...], 1, 1)
     return both[:, :cols], both[:, cols:], contract(tokens[1], acts[...], 1, 1)
 
@@ -58,20 +62,30 @@
 
 def own_kernel(place, mine, other, weights, grads, tokens, deltas, acts):
     join(tokens, mine, other, place[2])
-    for index, grad in enumerate(gradients(tokens, weights, deltas, acts)):
+    backward(tokens, weights, deltas, acts)
+    for index, grad in enumerate(gradients(tokens, deltas, acts)):
         grads[index] = grad
 
 
-def pair_kernel(parts, place, mine, other, weights, before, *refs):
-    outs, (grads, tokens, deltas, acts) = refs[: 2 * parts], refs[2 * parts :]
+def owners_kernel(given, place, tokens, deltas, acts, before, *refs):
+    outs, picked = refs[:-1], refs[-1]
+    size = picked.shape[1] // 2
+    owners = [rows_of(place[0] ^ (3 * spot) ^ given, size) for spot in range(2)]
+    for spot, where in enumerate(owners):
+        picked[:, spot * size : (spot + 1) * size, :] = tokens[:, where, :]
+    short = size // len(outs)
+    for index, grad in enumerate(gradients(picked, deltas, acts)):
+        for spot, where in enumerate(owners):
+            total = before[index, where, :] + grad[spot * size : (spot + 1) * size]
+            for part, out in enumerate(outs):
+                out[spot, index] = total[part * short : (part + 1) * short].astype(out.dtype)
+
+
+def pair_kernel(place, mine, other, weights, before, *refs):
+    outs, (tokens, deltas, acts, picked) = refs[:-4], refs[-4:]
     join(tokens, mine, other, place[2])
-    for index, grad in enumerate(gradients(tokens, weights, deltas, acts)):
-        grads[index] = before[index] + grad
-    for index, out in enumerate(outs):
-        part, given = index % parts, index // parts
-        for spot in range(2):
-            where = rows_of((place[0] ^ ((3 * spot) ^ given)) * parts + part, out.shape[2])
-            out[spot] = grads[:, where, :].astype(out.dtype)
+    backward(tokens, weights, deltas, acts)
+    owners_kernel(1, place, tokens, deltas, acts, before, *outs, picked)
 
 
 def rows_of(owner, rows):
@@ -225,19 +239,29 @@
     )
     parts = 2
     block = (2, 3, rows // parts, cols)
-    kept_given = [jax.ShapeDtypeStruct(block, f32)] * parts + [jax.ShapeDtypeStruct(block, bf16)] * parts
-    shares = call(
-        functools.partial(pair_kernel, parts),
+    picked = pltpu.VMEM((2, 2 * rows, toks), bf16)
+    *given, pair_tokens, deltas, acts = call(
+        pair_kernel,
         (pair_tokens, swap(pair_tokens, core), weights, grads),
-        kept_given,
-        [pltpu.VMEM(whole, f32), *joined],
-        token_flops,
+        [jax.ShapeDtypeStruct(block, bf16)] * parts
+        + [jax.ShapeDtypeStruct(scratch.shape, scratch.dtype) for scratch in joined],
+        [picked],
+        token_flops * 3 // 4,
         place,
         16,
     )
-    quest, shares = lax.optimization_barrier((jnp.stack([queries.T, out_grad.T]), shares))
+    kept = call(
+        functools.partial(owners_kernel, 0),
+        (pair_tokens, deltas, acts, grads),
+        [jax.ShapeDtypeStruct(block, f32)] * parts,
+        [picked],
+        token_flops // 4,
+        place,
+        16,
+    )
+    quest, given = lax.optimization_barrier((jnp.stack([queries.T, out_grad.T]), given))
     quests = [quest] + [swap(quest, flip) for flip in (1, 2, 3)]
-    kept, came = shares[:parts], [swap(share, zed) for share in shares[parts:]]
+    came = [swap(part, zed) for part in given]
     came[0], quests = lax.optimization_barrier((came[0], quests))
     crossed = [swap((k + c.astype(f32)).astype(bf16), 3 * zed) for k, c in zip(kept, came)]
     sums, stats = zip(

time: 84 us -> 83.5 us (level)
  waiting for transfers between devices: 24.8 us -> 23.3 us
  Pallas kernels: 13.2 us -> 14.2 us
    ppermute x26, waiting for transfers between devices: 24.8 us -> 23.3 us  [swap(): return lax.ppermute(array, ('tok', 'hid'), pairs)]
    pallas_call x10 -> x11, Pallas kernels: 13.2 us -> 14.2 us  [call(): pl.pallas_call(body, out_shape=list(outs), in_specs=specs, out_specs=[pl....]
  transfers between devices with their start and end apart: 26 -> 26, of which waited for: 16 -> 16; matrix products, arithmetic and copies ran while one was open for 2% -> 2% of each run, Pallas kernels for 8% -> 10%
where the time goes in v8:
time: 83.5 us; the launch traced here: 83.3 us
  starting transfers between devices  42.5 us (51%)
  waiting for transfers between devices  23.3 us (28%)
  Pallas kernels  14.2 us (17%)
  other arithmetic  2.41 us (3%)
  between operations  0.9 us (1%)
    ppermute x26, starting transfers between devices, swap(): return lax.ppermute(array, ('tok', 'hid'), pairs)  42.5 us
    ppermute x26, waiting for transfers between devices, swap(): return lax.ppermute(array, ('tok', 'hid'), pairs)  23.3 us
    pallas_call x11, Pallas kernels, call(): pl.pallas_call(body, out_shape=list(outs), in_specs=specs, out_specs=[pl....  14.2 us
  transfers between devices with their start and end apart: 26, of which 16 were waited for; matrix products, arithmetic and copies ran while one was open for 2% of the time, Pallas kernels for 10%

profile of v8, /device:TPU:0, one launch (start us, length us, event | category | flops | bytes accessed | tf_op | source)
XLA Modules:
  0.0 83.3 jit_solution(10255295702163445892)
XLA Ops:
  0.7 1.0 %pad_maximum_fusion.1 = bf16[3,48,768]{2,1,0:T(8,128)(2,1)S(1)} fusion(bf16[1,48,768]{2,1,0:T(8,128)(2,1)} %bitcast.28, bf16[1,48,768]{2,1,0:T(8,128)(2,1)} %bitcast.29, bf16[1,48,768]{2,1,0:T(8,128)(2,1)} %bitcast.30), kind=kLoop, calls=%fused_computation.5 | loop fusion | flops 221184 | bytes 442368 | tf_op jit(solution)/shard_map/stack | solution.py:202
  1.7 3.0 %collective-permute-start = (bf16[3,48,384]{2,1,0:T(8,128)(2,1)S(1)}, bf16[3,48,384]{2,1,0:T(8,128)(2,1)S(1)}, u32[]{:S(2)}, u32[]{:S(2)}) collective-permute-start(bf16[3,48,384]{2,1,0:T(8,128)(2,1)S(1)} %get-tuple-element.73), channel_id=1, source_target_pairs={{0,2},{1,3},{2,0},{3,1},{4,6},{5,7},{6,4},{7,5},{8,10},{9,11},{10,... | collective-permute-start | bytes 331784 | tf_op jit(solution)/shard_map/ppermute | solution.py:196
  4.7 1.1 %fusion = bf16[1,192,1024]{2,1,0:T(8,128)(2,1)S(1)} fusion(bf16[1024,192]{0,1:T(8,128)(2,1)} %param.9, f32[1024]{0:T(1024)} %param.10), kind=kLoop, calls=%fused_computation.4 | loop fusion | flops 589824 | bytes 790528 | tf_op jit(solution)/shard_map/stack | solution.py:207
  5.9 1.9 %collective-permute-done.refs_4_ = bf16[3,48,384]{2,1,0:T(8,128)(2,1)S(1)} collective-permute-done((bf16[3,48,384]{2,1,0:T(8,128)(2,1)S(1)}, bf16[3,48,384]{2,1,0:T(8,128)(2,1)S(1)}, u32[]{:S(2)}, u32[]{:S(2)}) %collective-permute-start) | collective-permute-done | bytes 110624 | tf_op jit(solution)/shard_map/ppermute | solution.py:196
  7.8 1.7 %collective-permute-start.1 = (bf16[2,192,1024]{2,1,0:T(8,128)(2,1)S(1)}, bf16[2,192,1024]{2,1,0:T(8,128)(2,1)S(1)}, u32[]{:S(2)}, u32[]{:S(2)}) collective-permute-start(bf16[2,192,1024]{2,1,0:T(8,128)(2,1)S(1)} %pad_maximum_fusion.mine), channel_id=1, source_target_pairs={{0,2},{1,3},{2,0},{3,1},{4,6},{5,7},{6,4},{7,5},{8,10},{9,11},{10,... | collective-permute-start | bytes 2359304 | tf_op jit(solution)/shard_map/ppermute | solution.py:196
  9.5 2.6 %collective-permute-start.3 = (bf16[3,48,384]{2,1,0:T(8,128)(2,1)S(1)}, bf16[3,48,384]{2,1,0:T(8,128)(2,1)S(1)}, u32[]{:S(2)}, u32[]{:S(2)}) collective-permute-start(bf16[3,48,384]{2,1,0:T(8,128)(2,1)S(1)} %get-tuple-element.72.refs_0_), channel_id=1, source_target_pairs={{0,8},{1,9},{2,10},{3,11},{4,12},{5,13},{6,14},{7,15},{8,0},{9,1},... | collective-permute-start | bytes 331784 | tf_op jit(solution)/shard_map/ppermute | solution.py:196
  12.1 1.6 %collective-permute-start.2 = (bf16[3,48,384]{2,1,0:T(8,128)(2,1)S(1)}, bf16[3,48,384]{2,1,0:T(8,128)(2,1)S(1)}, u32[]{:S(2)}, u32[]{:S(2)}) collective-permute-start(bf16[3,48,384]{2,1,0:T(8,128)(2,1)S(1)} %get-tuple-element.72.refs_0_), channel_id=1, source_target_pairs={{0,4},{1,5},{2,6},{3,7},{4,0},{5,1},{6,2},{7,3},{8,12},{9,13},{10,... | collective-permute-start | bytes 331784 | tf_op jit(solution)/shard_map/ppermute | solution.py:196
  14.0 3.8 %collective-permute-done.3.refs_2_ = bf16[3,48,384]{2,1,0:T(8,128)(2,1)S(1)} collective-permute-done((bf16[3,48,384]{2,1,0:T(8,128)(2,1)S(1)}, bf16[3,48,384]{2,1,0:T(8,128)(2,1)S(1)}, u32[]{:S(2)}, u32[]{:S(2)}) %collective-permute-start.3) | collective-permute-done | bytes 110624 | tf_op jit(solution)/shard_map/ppermute | solution.py:196
  17.8 1.8 %collective-permute-start.5 = (bf16[3,48,384]{2,1,0:T(8,128)(2,1)S(1)}, bf16[3,48,384]{2,1,0:T(8,128)(2,1)S(1)}, u32[]{:S(2)}, u32[]{:S(2)}) collective-permute-start(bf16[3,48,384]{2,1,0:T(8,128)(2,1)S(1)} %collective-permute-done.refs_4_), channel_id=1, source_target_pairs={{0,4},{1,5},{2,6},{3,7},{4,0},{5,1},{6,2},{7,3},{8,12},{9,13},{10,... | collective-permute-start | bytes 331784 | tf_op jit(solution)/shard_map/ppermute | solution.py:196
  20.4 1.0 %collective-permute-done.6.refs_6_ = bf16[3,48,384]{2,1,0:T(8,128)(2,1)S(1)} collective-permute-done((bf16[3,48,384]{2,1,0:T(8,128)(2,1)S(1)}, bf16[3,48,384]{2,1,0:T(8,128)(2,1)S(1)}, u32[]{:S(2)}, u32[]{:S(2)}) %collective-permute-start.6) | collective-permute-done | bytes 110624 | tf_op jit(solution)/shard_map/ppermute | solution.py:196
  22.0 1.2 %collective-permute-done.5.refs_5_ = bf16[3,48,384]{2,1,0:T(8,128)(2,1)S(1)} collective-permute-done((bf16[3,48,384]{2,1,0:T(8,128)(2,1)S(1)}, bf16[3,48,384]{2,1,0:T(8,128)(2,1)S(1)}, u32[]{:S(2)}, u32[]{:S(2)}) %collective-permute-start.5) | collective-permute-done | bytes 110624 | tf_op jit(solution)/shard_map/ppermute | solution.py:196
  23.2 2.2 %collective-permute-done.4.refs_3_ = bf16[3,48,384]{2,1,0:T(8,128)(2,1)S(1)} collective-permute-done((bf16[3,48,384]{2,1,0:T(8,128)(2,1)S(1)}, bf16[3,48,384]{2,1,0:T(8,128)(2,1)S(1)}, u32[]{:S(2)}, u32[]{:S(2)}) %collective-permute-start.4) | collective-permute-done | bytes 110624 | tf_op jit(solution)/shard_map/ppermute | solution.py:196
  25.3 1.4 %collective-permute-done.7.refs_7_ = bf16[3,48,384]{2,1,0:T(8,128)(2,1)S(1)} collective-permute-done((bf16[3,48,384]{2,1,0:T(8,128)(2,1)S(1)}, bf16[3,48,384]{2,1,0:T(8,128)(2,1)S(1)}, u32[]{:S(2)}, u32[]{:S(2)}) %collective-permute-start.7) | collective-permute-done | bytes 110624 | tf_op jit(solution)/shard_map/ppermute | solution.py:196
  27.5 3.3 %shard_map.96.before = f32[3,384,384]{2,1,0:T(8,128)S(1)} custom-call(s32[3]{0:T(128)S(1)} %pad_add_fusion.place, bf16[2,192,1024]{2,1,0:T(8,128)(2,1)S(1)} %pad_maximum_fusion.mine, bf16[2,192,1024]{2,1,0:T(8,128)(2,1)S(1)} %collective-permute-done.9.other, bf16[3,384,384]{2,1,0:T(8,128)(2,1)S(1)} %shard_map.95.weights), custom_call_target="tpu_custom_call" | custom-call | flops 1811939328 | bytes 6684684 | tf_op jit(solution)/shard_map/pallas_call | solution.py:173
  30.9 3.1 %shard_map.97 = (bf16[2,3,48,384]{3,2,1,0:T(8,128)(2,1)S(1)}, bf16[2,3,48,384]{3,2,1,0:T(8,128)(2,1)S(1)}, bf16[2,384,1024]{2,1,0:T(8,128)(2,1)S(1)}, bf16[768,1024]{1,0:T(8,128)(2,1)S(1)}, bf16[384,1024]{1,0:T(8,128)(2,1)S(1)}) custom-call(s32[3]{0:T(128)S(1)} %pad_add_fusion.place, bf16[2,192,1024]{2,1,0:T(8,128)(2,1)S(1)} %collective-permute-done.1.mine, ...), custom_call_target="tpu_custom_call" | custom-call | flops 1358954496 | bytes 15433740 | tf_op jit(solution)/shard_map/pallas_call | solution.py:173
  34.0 1.2 %collective-permute-start.10 = (bf16[2,3,48,384]{3,2,1,0:T(8,128)(2,1)S(1)}, bf16[2,3,48,384]{3,2,1,0:T(8,128)(2,1)S(1)}, u32[]{:S(2)}, u32[]{:S(2)}) collective-permute-start(bf16[2,3,48,384]{3,2,1,0:T(8,128)(2,1)S(1)} %get-tuple-element.47), channel_id=1, source_target_pairs={{0,4},{1,5},{2,6},{3,7},{4,0},{5,1},{6,2},{7,3},{8,12},{9,13},{10,... | collective-permute-start | bytes 663560 | tf_op jit(solution)/shard_map/ppermute | solution.py:196
  37.9 1.5 %shard_map.98 = (f32[2,3,48,384]{3,2,1,0:T(8,128)S(1)}, f32[2,3,48,384]{3,2,1,0:T(8,128)S(1)}) custom-call(s32[3]{0:T(128)S(1)} %pad_add_fusion.place, bf16[2,384,1024]{2,1,0:T(8,128)(2,1)S(1)} %get-tuple-element.41.tokens, bf16[768,1024]{1,0:T(8,128)(2,1)S(1)} %get-tuple-element.42.deltas, bf16[384,1024]{1,0:T(8,128)(2,1)S(1)} %get-tuple-element.43.acts, ...), custom_call_target="tpu_custom_call" | custom-call | flops 452984832 | bytes 10518540 | tf_op jit(solution)/shard_map/pallas_call | solution.py:173
  39.4 1.6 %collective-permute-done.12.refs_6_ = bf16[2,192,128]{2,1,0:T(8,128)(2,1)S(1)} collective-permute-done((bf16[2,192,128]{2,1,0:T(8,128)(2,1)S(1)}, bf16[2,192,128]{2,1,0:T(8,128)(2,1)S(1)}, u32[]{:S(2)}, u32[]{:S(2)}) %collective-permute-start.12) | collective-permute-done | bytes 98336 | tf_op jit(solution)/shard_map/ppermute | solution.py:196
  41.0 0.9 %collective-permute-done.13.refs_7_ = bf16[2,192,128]{2,1,0:T(8,128)(2,1)S(1)} collective-permute-done((bf16[2,192,128]{2,1,0:T(8,128)(2,1)S(1)}, bf16[2,192,128]{2,1,0:T(8,128)(2,1)S(1)}, u32[]{:S(2)}, u32[]{:S(2)}) %collective-permute-start.13) | collective-permute-done | bytes 98336 | tf_op jit(solution)/shard_map/ppermute | solution.py:196
  42.3 3.8 %collective-permute-start.14 = (bf16[2,3,48,384]{3,2,1,0:T(8,128)(2,1)S(1)}, bf16[2,3,48,384]{3,2,1,0:T(8,128)(2,1)S(1)}, u32[]{:S(2)}, u32[]{:S(2)}) collective-permute-start(bf16[2,3,48,384]{3,2,1,0:T(8,128)(2,1)S(1)} %add_convert_fusion.1), channel_id=1, source_target_pairs={{0,12},{1,13},{2,14},{3,15},{4,8},{5,9},{6,10},{7,11},{8,4},{9,5},... | collective-permute-start | bytes 663560 | tf_op jit(solution)/shard_map/ppermute | solution.py:196
  46.6 10.9 %collective-permute-start.16 = (bf16[2,3,48,384]{3,2,1,0:T(8,128)(2,1)S(1)}, bf16[2,3,48,384]{3,2,1,0:T(8,128)(2,1)S(1)}, u32[]{:S(2)}, u32[]{:S(2)}) collective-permute-start(bf16[2,3,48,384]{3,2,1,0:T(8,128)(2,1)S(1)} %add_convert_fusion), channel_id=1, source_target_pairs={{0,12},{1,13},{2,14},{3,15},{4,8},{5,9},{6,10},{7,11},{8,4},{9,5},... | collective-permute-start | bytes 663560 | tf_op jit(solution)/shard_map/ppermute | solution.py:196
  58.4 1.6 %collective-permute-start.18 = (bf16[2,3,48,384]{3,2,1,0:T(8,128)(2,1)S(1)}, bf16[2,3,48,384]{3,2,1,0:T(8,128)(2,1)S(1)}, u32[]{:S(2)}, u32[]{:S(2)}) collective-permute-start(bf16[2,3,48,384]{3,2,1,0:T(8,128)(2,1)S(1)} %get-tuple-element.50.refs_0_), channel_id=1, source_target_pairs={{0,4},{1,5},{2,6},{3,7},{4,0},{5,1},{6,2},{7,3},{8,12},{9,13},{10,... | collective-permute-start | bytes 663560 | tf_op jit(solution)/shard_map/ppermute | solution.py:196
  60.0 1.9 %collective-permute-done.16.crossed = bf16[2,3,48,384]{3,2,1,0:T(8,128)(2,1)S(1)} collective-permute-done((bf16[2,3,48,384]{3,2,1,0:T(8,128)(2,1)S(1)}, bf16[2,3,48,384]{3,2,1,0:T(8,128)(2,1)S(1)}, u32[]{:S(2)}, u32[]{:S(2)}) %collective-permute-start.16) | collective-permute-done | bytes 221216 | tf_op jit(solution)/shard_map/ppermute | solution.py:196
  62.7 4.5 %collective-permute-start.19 = (bf16[2,3,48,384]{3,2,1,0:T(8,128)(2,1)S(1)}, bf16[2,3,48,384]{3,2,1,0:T(8,128)(2,1)S(1)}, u32[]{:S(2)}, u32[]{:S(2)}) collective-permute-start(bf16[2,3,48,384]{3,2,1,0:T(8,128)(2,1)S(1)} %get-tuple-element.53.refs_1_), channel_id=1, source_target_pairs={{0,4},{1,5},{2,6},{3,7},{4,0},{5,1},{6,2},{7,3},{8,12},{9,13},{10,... | collective-permute-start | bytes 663560 | tf_op jit(solution)/shard_map/ppermute | solution.py:196
  67.9 1.1 %collective-permute-start.21 = (f32[2,24,96]{2,1,0:T(8,128)S(1)}, f32[2,24,96]{2,1,0:T(8,128)S(1)}, u32[]{:S(2)}, u32[]{:S(2)}) collective-permute-start(f32[2,24,96]{2,1,0:T(8,128)S(1)} %fusion.1.here), channel_id=1, source_target_pairs={{0,4},{1,5},{2,6},{3,7},{4,0},{5,1},{6,2},{7,3},{8,12},{9,13},{10,... | collective-permute-start | bytes 55304 | tf_op jit(solution)/shard_map/ppermute | solution.py:196
  69.0 1.9 %collective-permute-start.22 = (f32[2,24,96]{2,1,0:T(8,128)S(1)}, f32[2,24,96]{2,1,0:T(8,128)S(1)}, u32[]{:S(2)}, u32[]{:S(2)}) collective-permute-start(f32[2,24,96]{2,1,0:T(8,128)S(1)} %fusion.1.here), channel_id=1, source_target_pairs={{0,6},{1,7},{2,4},{3,5},{4,2},{5,3},{6,0},{7,1},{8,14},{9,15},{10,... | collective-permute-start | bytes 55304 | tf_op jit(solution)/shard_map/ppermute | solution.py:196
  71.2 2.8 %collective-permute-done.21.here = f32[2,24,96]{2,1,0:T(8,128)S(1)} collective-permute-done((f32[2,24,96]{2,1,0:T(8,128)S(1)}, f32[2,24,96]{2,1,0:T(8,128)S(1)}, u32[]{:S(2)}, u32[]{:S(2)}) %collective-permute-start.21) | collective-permute-done | bytes 18464 | tf_op jit(solution)/shard_map/ppermute | solution.py:196
  74.3 2.0 %shard_map.103 = (bf16[3,384,384]{2,1,0:T(8,128)(2,1)S(1)}, f32[2,192,128]{2,1,0:T(8,128)S(1)}, bf16[2,192,128]{2,1,0:T(8,128)(2,1)S(1)}) custom-call(s32[3]{0:T(128)S(1)} %pad_add_fusion.place, bf16[3,384,384]{2,1,0:T(8,128)(2,1)S(1)} %shard_map.95.weights, bf16[2,3,48,384]{3,2,1,0:T(8,128)(2,1)S(1)} %get-tuple-element.50.refs_0_, ...), custom_call_target="tpu_custom_call" | custom-call | flops 226492416 | bytes 6119436 | tf_op jit(solution)/shard_map/pallas_call | solution.py:173
  76.4 1.3 %collective-permute-done.23 = bf16[2,192,128]{2,1,0:T(8,128)(2,1)S(1)} collective-permute-done((bf16[2,192,128]{2,1,0:T(8,128)(2,1)S(1)}, bf16[2,192,128]{2,1,0:T(8,128)(2,1)S(1)}, u32[]{:S(2)}, u32[]{:S(2)}) %collective-permute-start.23) | collective-permute-done | bytes 98336 | tf_op jit(solution)/shard_map/ppermute | solution.py:196
  77.8 1.5 %collective-permute-start.25 = (bf16[2,192,128]{2,1,0:T(8,128)(2,1)S(1)}, bf16[2,192,128]{2,1,0:T(8,128)(2,1)S(1)}, u32[]{:S(2)}, u32[]{:S(2)}) collective-permute-start(bf16[2,192,128]{2,1,0:T(8,128)(2,1)S(1)} %add_convert_fusion.2), channel_id=1, source_target_pairs={{0,2},{1,3},{2,0},{3,1},{4,6},{5,7},{6,4},{7,5},{8,10},{9,11},{10,... | collective-permute-start | bytes 294920 | tf_op jit(solution)/shard_map/ppermute | solution.py:196
  79.3 1.3 %shard_map.104 = (f32[2,192,128]{2,1,0:T(8,128)S(1)}, bf16[2,192,128]{2,1,0:T(8,128)(2,1)S(1)}) custom-call(s32[3]{0:T(128)S(1)} %pad_add_fusion.place, bf16[3,384,384]{2,1,0:T(8,128)(2,1)S(1)} %get-tuple-element.60.renewed, bf16[2,192,128]{2,1,0:T(8,128)(2,1)S(1)} %pad_maximum_fusion.2.mine, bf16[2,192,128]{2,1,0:T(8,128)(2,1)S(1)} %collective-permute-done.11.other), custom_call_target="tpu_custom_call" | custom-call | flops 226492416 | bytes 2555916 | tf_op jit(solution)/shard_map/pallas_call | solution.py:173
  80.6 2.1 %collective-permute-done.25.pair = bf16[2,192,128]{2,1,0:T(8,128)(2,1)S(1)} collective-permute-done((bf16[2,192,128]{2,1,0:T(8,128)(2,1)S(1)}, bf16[2,192,128]{2,1,0:T(8,128)(2,1)S(1)}, u32[]{:S(2)}, u32[]{:S(2)}) %collective-permute-start.25) | collective-permute-done | bytes 98336 | tf_op jit(solution)/shard_map/ppermute | solution.py:196
  (48 shorter events, 10.0 us)
Async XLA Ops:
  0.6 5.2 %copy-start = (bf16[1024,192]{0,1:T(8,128)(2,1)S(1)}, bf16[1024,192]{0,1:T(8,128)(2,1)}, u32[]{:S(2)}) copy-start(bf16[1024,192]{0,1:T(8,128)(2,1)} %param.8) | copy-start | bytes 1179652
  1.7 6.1 %collective-permute-start = (bf16[3,48,384]{2,1,0:T(8,128)(2,1)S(1)}, bf16[3,48,384]{2,1,0:T(8,128)(2,1)S(1)}, u32[]{:S(2)}, u32[]{:S(2)}) collective-permute-start(bf16[3,48,384]{2,1,0:T(8,128)(2,1)S(1)} %get-tuple-element.73), channel_id=1, source_target_pairs={{0,2},{1,3},{2,0},{3,1},{4,6},{5,7},{6,4},{7,5},{8,10},{9,11},{10,... | collective-permute-start | bytes 331784 | tf_op jit(solution)/shard_map/ppermute | solution.py:196
  5.8 21.6 %copy-start.1 = (bf16[128,192]{0,1:T(8,128)(2,1)S(1)}, bf16[128,192]{0,1:T(8,128)(2,1)}, u32[]{:S(2)}) copy-start(bf16[128,192]{0,1:T(8,128)(2,1)} %param.15) | copy-start | bytes 147460
  5.9 21.6 %copy-start.2 = (bf16[128,192]{0,1:T(8,128)(2,1)S(1)}, bf16[128,192]{0,1:T(8,128)(2,1)}, u32[]{:S(2)}) copy-start(bf16[128,192]{0,1:T(8,128)(2,1)} %param.14) | copy-start | bytes 147460
  7.8 19.6 %collective-permute-start.1 = (bf16[2,192,1024]{2,1,0:T(8,128)(2,1)S(1)}, bf16[2,192,1024]{2,1,0:T(8,128)(2,1)S(1)}, u32[]{:S(2)}, u32[]{:S(2)}) collective-permute-start(bf16[2,192,1024]{2,1,0:T(8,128)(2,1)S(1)} %pad_maximum_fusion.mine), channel_id=1, source_target_pairs={{0,2},{1,3},{2,0},{3,1},{4,6},{5,7},{6,4},{7,5},{8,10},{9,11},{10,... | collective-permute-start | bytes 2359304 | tf_op jit(solution)/shard_map/ppermute | solution.py:196
  9.5 8.3 %collective-permute-start.3 = (bf16[3,48,384]{2,1,0:T(8,128)(2,1)S(1)}, bf16[3,48,384]{2,1,0:T(8,128)(2,1)S(1)}, u32[]{:S(2)}, u32[]{:S(2)}) collective-permute-start(bf16[3,48,384]{2,1,0:T(8,128)(2,1)S(1)} %get-tuple-element.72.refs_0_), channel_id=1, source_target_pairs={{0,8},{1,9},{2,10},{3,11},{4,12},{5,13},{6,14},{7,15},{8,0},{9,1},... | collective-permute-start | bytes 331784 | tf_op jit(solution)/shard_map/ppermute | solution.py:196
  12.1 7.5 %collective-permute-start.2 = (bf16[3,48,384]{2,1,0:T(8,128)(2,1)S(1)}, bf16[3,48,384]{2,1,0:T(8,128)(2,1)S(1)}, u32[]{:S(2)}, u32[]{:S(2)}) collective-permute-start(bf16[3,48,384]{2,1,0:T(8,128)(2,1)S(1)} %get-tuple-element.72.refs_0_), channel_id=1, source_target_pairs={{0,4},{1,5},{2,6},{3,7},{4,0},{5,1},{6,2},{7,3},{8,12},{9,13},{10,... | collective-permute-start | bytes 331784 | tf_op jit(solution)/shard_map/ppermute | solution.py:196
  13.7 7.7 %collective-permute-start.6 = (bf16[3,48,384]{2,1,0:T(8,128)(2,1)S(1)}, bf16[3,48,384]{2,1,0:T(8,128)(2,1)S(1)}, u32[]{:S(2)}, u32[]{:S(2)}) collective-permute-start(bf16[3,48,384]{2,1,0:T(8,128)(2,1)S(1)} %collective-permute-done.refs_4_), channel_id=1, source_target_pairs={{0,8},{1,9},{2,10},{3,11},{4,12},{5,13},{6,14},{7,15},{8,0},{9,1},... | collective-permute-start | bytes 331784 | tf_op jit(solution)/shard_map/ppermute | solution.py:196
  14.0 13.5 %collective-permute-start.9 = (bf16[2,192,1024]{2,1,0:T(8,128)(2,1)S(1)}, bf16[2,192,1024]{2,1,0:T(8,128)(2,1)S(1)}, u32[]{:S(2)}, u32[]{:S(2)}) collective-permute-start(bf16[2,192,1024]{2,1,0:T(8,128)(2,1)S(1)} %pad_maximum_fusion.mine), channel_id=1, source_target_pairs={{0,1},{1,0},{2,3},{3,2},{4,5},{5,4},{6,7},{7,6},{8,9},{9,8},{10,11... | collective-permute-start | bytes 2359304 | tf_op jit(solution)/shard_map/ppermute | solution.py:196
  17.8 5.3 %collective-permute-start.5 = (bf16[3,48,384]{2,1,0:T(8,128)(2,1)S(1)}, bf16[3,48,384]{2,1,0:T(8,128)(2,1)S(1)}, u32[]{:S(2)}, u32[]{:S(2)}) collective-permute-start(bf16[3,48,384]{2,1,0:T(8,128)(2,1)S(1)} %collective-permute-done.refs_4_), channel_id=1, source_target_pairs={{0,4},{1,5},{2,6},{3,7},{4,0},{5,1},{6,2},{7,3},{8,12},{9,13},{10,... | collective-permute-start | bytes 331784 | tf_op jit(solution)/shard_map/ppermute | solution.py:196
  19.6 5.7 %collective-permute-start.4 = (bf16[3,48,384]{2,1,0:T(8,128)(2,1)S(1)}, bf16[3,48,384]{2,1,0:T(8,128)(2,1)S(1)}, u32[]{:S(2)}, u32[]{:S(2)}) collective-permute-start(bf16[3,48,384]{2,1,0:T(8,128)(2,1)S(1)} %collective-permute-done.3.refs_2_), channel_id=1, source_target_pairs={{0,4},{1,5},{2,6},{3,7},{4,0},{5,1},{6,2},{7,3},{8,12},{9,13},{10,... | collective-permute-start | bytes 331784 | tf_op jit(solution)/shard_map/ppermute | solution.py:196
  21.4 5.4 %collective-permute-start.7 = (bf16[3,48,384]{2,1,0:T(8,128)(2,1)S(1)}, bf16[3,48,384]{2,1,0:T(8,128)(2,1)S(1)}, u32[]{:S(2)}, u32[]{:S(2)}) collective-permute-start(bf16[3,48,384]{2,1,0:T(8,128)(2,1)S(1)} %collective-permute-done.6.refs_6_), channel_id=1, source_target_pairs={{0,4},{1,5},{2,6},{3,7},{4,0},{5,1},{6,2},{7,3},{8,12},{9,13},{10,... | collective-permute-start | bytes 331784 | tf_op jit(solution)/shard_map/ppermute | solution.py:196
  27.4 3.5 %collective-permute-start.8 = (bf16[2,192,1024]{2,1,0:T(8,128)(2,1)S(1)}, bf16[2,192,1024]{2,1,0:T(8,128)(2,1)S(1)}, u32[]{:S(2)}, u32[]{:S(2)}) collective-permute-start(bf16[2,192,1024]{2,1,0:T(8,128)(2,1)S(1)} %collective-permute-done.1.mine), channel_id=1, source_target_pairs={{0,1},{1,0},{2,3},{3,2},{4,5},{5,4},{6,7},{7,6},{8,9},{9,8},{10,11... | collective-permute-start | bytes 2359304 | tf_op jit(solution)/shard_map/ppermute | solution.py:196
  34.0 8.3 %collective-permute-start.10 = (bf16[2,3,48,384]{3,2,1,0:T(8,128)(2,1)S(1)}, bf16[2,3,48,384]{3,2,1,0:T(8,128)(2,1)S(1)}, u32[]{:S(2)}, u32[]{:S(2)}) collective-permute-start(bf16[2,3,48,384]{3,2,1,0:T(8,128)(2,1)S(1)} %get-tuple-element.47), channel_id=1, source_target_pairs={{0,4},{1,5},{2,6},{3,7},{4,0},{5,1},{6,2},{7,3},{8,12},{9,13},{10,... | collective-permute-start | bytes 663560 | tf_op jit(solution)/shard_map/ppermute | solution.py:196
  35.2 4.2 %collective-permute-start.11 = (bf16[2,192,128]{2,1,0:T(8,128)(2,1)S(1)}, bf16[2,192,128]{2,1,0:T(8,128)(2,1)S(1)}, u32[]{:S(2)}, u32[]{:S(2)}) collective-permute-start(bf16[2,192,128]{2,1,0:T(8,128)(2,1)S(1)} %pad_maximum_fusion.2.mine), channel_id=1, source_target_pairs={{0,1},{1,0},{2,3},{3,2},{4,5},{5,4},{6,7},{7,6},{8,9},{9,8},{10,11... | collective-permute-start | bytes 294920 | tf_op jit(solution)/shard_map/ppermute | solution.py:196
  35.4 5.6 %collective-permute-start.12 = (bf16[2,192,128]{2,1,0:T(8,128)(2,1)S(1)}, bf16[2,192,128]{2,1,0:T(8,128)(2,1)S(1)}, u32[]{:S(2)}, u32[]{:S(2)}) collective-permute-start(bf16[2,192,128]{2,1,0:T(8,128)(2,1)S(1)} %pad_maximum_fusion.2.mine), channel_id=1, source_target_pairs={{0,2},{1,3},{2,0},{3,1},{4,6},{5,7},{6,4},{7,5},{8,10},{9,11},{10,... | collective-permute-start | bytes 294920 | tf_op jit(solution)/shard_map/ppermute | solution.py:196
  36.3 5.6 %collective-permute-start.13 = (bf16[2,192,128]{2,1,0:T(8,128)(2,1)S(1)}, bf16[2,192,128]{2,1,0:T(8,128)(2,1)S(1)}, u32[]{:S(2)}, u32[]{:S(2)}) collective-permute-start(bf16[2,192,128]{2,1,0:T(8,128)(2,1)S(1)} %pad_maximum_fusion.2.mine), channel_id=1, source_target_pairs={{0,3},{1,2},{2,1},{3,0},{4,7},{5,6},{6,5},{7,4},{8,11},{9,10},{10,... | collective-permute-start | bytes 294920 | tf_op jit(solution)/shard_map/ppermute | solution.py:196
  37.1 9.5 %collective-permute-start.15 = (bf16[2,3,48,384]{3,2,1,0:T(8,128)(2,1)S(1)}, bf16[2,3,48,384]{3,2,1,0:T(8,128)(2,1)S(1)}, u32[]{:S(2)}, u32[]{:S(2)}) collective-permute-start(bf16[2,3,48,384]{3,2,1,0:T(8,128)(2,1)S(1)} %get-tuple-element.52), channel_id=1, source_target_pairs={{0,4},{1,5},{2,6},{3,7},{4,0},{5,1},{6,2},{7,3},{8,12},{9,13},{10,... | collective-permute-start | bytes 663560 | tf_op jit(solution)/shard_map/ppermute | solution.py:196
  42.3 15.3 %collective-permute-start.14 = (bf16[2,3,48,384]{3,2,1,0:T(8,128)(2,1)S(1)}, bf16[2,3,48,384]{3,2,1,0:T(8,128)(2,1)S(1)}, u32[]{:S(2)}, u32[]{:S(2)}) collective-permute-start(bf16[2,3,48,384]{3,2,1,0:T(8,128)(2,1)S(1)} %add_convert_fusion.1), channel_id=1, source_target_pairs={{0,12},{1,13},{2,14},{3,15},{4,8},{5,9},{6,10},{7,11},{8,4},{9,5},... | collective-permute-start | bytes 663560 | tf_op jit(solution)/shard_map/ppermute | solution.py:196
  46.6 15.2 %collective-permute-start.16 = (bf16[2,3,48,384]{3,2,1,0:T(8,128)(2,1)S(1)}, bf16[2,3,48,384]{3,2,1,0:T(8,128)(2,1)S(1)}, u32[]{:S(2)}, u32[]{:S(2)}) collective-permute-start(bf16[2,3,48,384]{3,2,1,0:T(8,128)(2,1)S(1)} %add_convert_fusion), channel_id=1, source_target_pairs={{0,12},{1,13},{2,14},{3,15},{4,8},{5,9},{6,10},{7,11},{8,4},{9,5},... | collective-permute-start | bytes 663560 | tf_op jit(solution)/shard_map/ppermute | solution.py:196
  58.4 8.9 %collective-permute-start.18 = (bf16[2,3,48,384]{3,2,1,0:T(8,128)(2,1)S(1)}, bf16[2,3,48,384]{3,2,1,0:T(8,128)(2,1)S(1)}, u32[]{:S(2)}, u32[]{:S(2)}) collective-permute-start(bf16[2,3,48,384]{3,2,1,0:T(8,128)(2,1)S(1)} %get-tuple-element.50.refs_0_), channel_id=1, source_target_pairs={{0,4},{1,5},{2,6},{3,7},{4,0},{5,1},{6,2},{7,3},{8,12},{9,13},{10,... | collective-permute-start | bytes 663560 | tf_op jit(solution)/shard_map/ppermute | solution.py:196
  62.7 4.6 %collective-permute-start.17 = (f32[2,24,96]{2,1,0:T(8,128)S(1)}, f32[2,24,96]{2,1,0:T(8,128)S(1)}, u32[]{:S(2)}, u32[]{:S(2)}) collective-permute-start(f32[2,24,96]{2,1,0:T(8,128)S(1)} %pad_maximum_fusion.3), channel_id=1, source_target_pairs={{0,1},{1,0},{2,3},{3,2},{4,5},{5,4},{6,7},{7,6},{8,9},{9,8},{10,11... | collective-permute-start | bytes 55304 | tf_op jit(solution)/shard_map/ppermute | solution.py:196
  62.7 11.6 %collective-permute-start.19 = (bf16[2,3,48,384]{3,2,1,0:T(8,128)(2,1)S(1)}, bf16[2,3,48,384]{3,2,1,0:T(8,128)(2,1)S(1)}, u32[]{:S(2)}, u32[]{:S(2)}) collective-permute-start(bf16[2,3,48,384]{3,2,1,0:T(8,128)(2,1)S(1)} %get-tuple-element.53.refs_1_), channel_id=1, source_target_pairs={{0,4},{1,5},{2,6},{3,7},{4,0},{5,1},{6,2},{7,3},{8,12},{9,13},{10,... | collective-permute-start | bytes 663560 | tf_op jit(solution)/shard_map/ppermute | solution.py:196
  67.3 3.9 %collective-permute-start.20 = (f32[2,24,96]{2,1,0:T(8,128)S(1)}, f32[2,24,96]{2,1,0:T(8,128)S(1)}, u32[]{:S(2)}, u32[]{:S(2)}) collective-permute-start(f32[2,24,96]{2,1,0:T(8,128)S(1)} %fusion.1.here), channel_id=1, source_target_pairs={{0,2},{1,3},{2,0},{3,1},{4,6},{5,7},{6,4},{7,5},{8,10},{9,11},{10,... | collective-permute-start | bytes 55304 | tf_op jit(solution)/shard_map/ppermute | solution.py:196
  67.9 6.1 %collective-permute-start.21 = (f32[2,24,96]{2,1,0:T(8,128)S(1)}, f32[2,24,96]{2,1,0:T(8,128)S(1)}, u32[]{:S(2)}, u32[]{:S(2)}) collective-permute-start(f32[2,24,96]{2,1,0:T(8,128)S(1)} %fusion.1.here), channel_id=1, source_target_pairs={{0,4},{1,5},{2,6},{3,7},{4,0},{5,1},{6,2},{7,3},{8,12},{9,13},{10,... | collective-permute-start | bytes 55304 | tf_op jit(solution)/shard_map/ppermute | solution.py:196
  69.0 5.3 %collective-permute-start.22 = (f32[2,24,96]{2,1,0:T(8,128)S(1)}, f32[2,24,96]{2,1,0:T(8,128)S(1)}, u32[]{:S(2)}, u32[]{:S(2)}) collective-permute-start(f32[2,24,96]{2,1,0:T(8,128)S(1)} %fusion.1.here), channel_id=1, source_target_pairs={{0,6},{1,7},{2,4},{3,5},{4,2},{5,3},{6,0},{7,1},{8,14},{9,15},{10,... | collective-permute-start | bytes 55304 | tf_op jit(solution)/shard_map/ppermute | solution.py:196
  76.4 1.4 %collective-permute-start.23 = (bf16[2,192,128]{2,1,0:T(8,128)(2,1)S(1)}, bf16[2,192,128]{2,1,0:T(8,128)(2,1)S(1)}, u32[]{:S(2)}, u32[]{:S(2)}) collective-permute-start(bf16[2,192,128]{2,1,0:T(8,128)(2,1)S(1)} %get-tuple-element.61), channel_id=1, source_target_pairs={{0,1},{1,0},{2,3},{3,2},{4,5},{5,4},{6,7},{7,6},{8,9},{9,8},{10,11... | collective-permute-start | bytes 294920 | tf_op jit(solution)/shard_map/ppermute | solution.py:196
  77.8 4.9 %collective-permute-start.25 = (bf16[2,192,128]{2,1,0:T(8,128)(2,1)S(1)}, bf16[2,192,128]{2,1,0:T(8,128)(2,1)S(1)}, u32[]{:S(2)}, u32[]{:S(2)}) collective-permute-start(bf16[2,192,128]{2,1,0:T(8,128)(2,1)S(1)} %add_convert_fusion.2), channel_id=1, source_target_pairs={{0,2},{1,3},{2,0},{3,1},{4,6},{5,7},{6,4},{7,5},{8,10},{9,11},{10,... | collective-permute-start | bytes 294920 | tf_op jit(solution)/shard_map/ppermute | solution.py:196
  80.5 2.1 %collective-permute-start.24 = (bf16[2,192,128]{2,1,0:T(8,128)(2,1)S(1)}, bf16[2,192,128]{2,1,0:T(8,128)(2,1)S(1)}, u32[]{:S(2)}, u32[]{:S(2)}) collective-permute-start(bf16[2,192,128]{2,1,0:T(8,128)(2,1)S(1)} %get-tuple-element.67), channel_id=1, source_target_pairs={{0,1},{1,0},{2,3},{3,2},{4,5},{5,4},{6,7},{7,6},{8,9},{9,8},{10,11... | collective-permute-start | bytes 294920 | tf_op jit(solution)/shard_map/ppermute | solution.py:196

commit v9 on v8

--- a/solution.py
+++ b/solution.py
@@ -92,18 +92,26 @@
     return pl.ds(pl.multiple_of(owner * rows, rows), rows)
 
 
-def sum_kernel(parts, part, place, weights, kept, came, crossed, grad_out, stats_out):
+def kept_kernel(parts, place, tokens, deltas, acts, before, weights, *refs):
+    outs, olds, picked = refs[:parts], refs[parts : 2 * parts], refs[2 * parts]
+    owners_kernel(0, place, tokens, deltas, acts, before, *outs, picked)
+    for part, old in enumerate(olds):
+        for spot in range(2):
+            where = rows_of((place[0] ^ (3 * spot)) * parts + part, old.shape[2])
+            old[spot] = weights[:, where, :]
+
+
+def sum_kernel(olds, kept, came, crossed, grad_out, stats_out):
     rows = kept.shape[2]
     lane = lax.broadcasted_iota(jnp.int32, (rows, LANES), 1)
     both = []
     for spot in range(2):
-        where = rows_of((place[0] ^ (3 * spot)) * parts + part, rows)
         stats = jnp.zeros((rows, LANES), f32)
         for index in range(3):
             near = kept[spot, index] + came[spot, index].astype(f32)
             grad = near + crossed[1 - spot, index].astype(f32)
             grad_out[spot, index] = grad.astype(bf16)
-            weight = weights[index, where, :].astype(f32)
+            weight = olds[spot, index].astype(f32)
             for slot, product in enumerate((weight * weight, weight * grad, grad * grad)):
                 row_sum = jnp.sum(product, axis=1, keepdims=True)
                 stats = jnp.where(lane == 8 * slot + index, row_sum, stats)
@@ -250,30 +258,30 @@
         place,
         16,
     )
-    kept = call(
-        functools.partial(owners_kernel, 0),
-        (pair_tokens, deltas, acts, grads),
-        [jax.ShapeDtypeStruct(block, f32)] * parts,
+    kept_olds = call(
+        functools.partial(kept_kernel, parts),
+        (pair_tokens, deltas, acts, grads, weights),
+        [jax.ShapeDtypeStruct(block, f32)] * parts + [jax.ShapeDtypeStruct(block, bf16)] * parts,
         [picked],
         token_flops // 4,
         place,
         16,
     )
+    kept, olds = kept_olds[:parts], kept_olds[parts:]
     quest, given = lax.optimization_barrier((jnp.stack([queries.T, out_grad.T]), given))
     quests = [quest] + [swap(quest, flip) for flip in (1, 2, 3)]
     came = [swap(part, zed) for part in given]
-    came[0], quests = lax.optimization_barrier((came[0], quests))
+    came[0], quests[1:3] = lax.optimization_barrier((came[0], quests[1:3]))
     crossed = [swap((k + c.astype(f32)).astype(bf16), 3 * zed) for k, c in zip(kept, came)]
     sums, stats = zip(
         *(
             call(
-                functools.partial(sum_kernel, parts, part),
-                (weights, kept[part], came[part], crossed[part]),
+                sum_kernel,
+                (olds[part], kept[part], came[part], crossed[part]),
                 (
                     jax.ShapeDtypeStruct(block, bf16),
                     jax.ShapeDtypeStruct((24, 2 * rows // parts), f32),
                 ),
-                place=place,
             )
             for part in range(parts)
         )

time: 83.5 us -> 82.7 us (level)
  waiting for transfers between devices: 23.3 us -> 27.3 us
  starting transfers between devices: 42.5 us -> 38.7 us
  Pallas kernels: 14.2 us -> 13.1 us
    ppermute x26, waiting for transfers between devices: 23.3 us -> 27.3 us  [swap(): return lax.ppermute(array, ('tok', 'hid'), pairs)]
    ppermute x26, starting transfers between devices: 42.5 us -> 38.7 us  [swap(): return lax.ppermute(array, ('tok', 'hid'), pairs)]
    pallas_call x11, Pallas kernels: 14.2 us -> 13.1 us  [call(): pl.pallas_call(body, out_shape=list(outs), in_specs=specs, out_specs=[pl....]
  transfers between devices with their start and end apart: 26 -> 26, of which waited for: 16 -> 15; matrix products, arithmetic and copies ran while one was open for 2% -> 2% of each run, Pallas kernels for 10% -> 9%
where the time goes in v9:
time: 82.7 us; the launch traced here: 82.5 us
  starting transfers between devices  38.7 us (47%)
  waiting for transfers between devices  27.3 us (33%)
  Pallas kernels  13.1 us (16%)
  other arithmetic  2.41 us (3%)
  between operations  0.91 us (1%)
    ppermute x26, starting transfers between devices, swap(): return lax.ppermute(array, ('tok', 'hid'), pairs)  38.7 us
    ppermute x26, waiting for transfers between devices, swap(): return lax.ppermute(array, ('tok', 'hid'), pairs)  27.3 us
    pallas_call x11, Pallas kernels, call(): pl.pallas_call(body, out_shape=list(outs), in_specs=specs, out_specs=[pl....  13.1 us
  transfers between devices with their start and end apart: 26, of which 15 were waited for; matrix products, arithmetic and copies ran while one was open for 2% of the time, Pallas kernels for 9%

profile of v9, /device:TPU:0, one launch (start us, length us, event | category | flops | bytes accessed | tf_op | source)
XLA Modules:
  0.0 82.5 jit_solution(6457881180914833054)
XLA Ops:
  0.7 1.0 %pad_maximum_fusion.1 = bf16[3,48,768]{2,1,0:T(8,128)(2,1)S(1)} fusion(bf16[1,48,768]{2,1,0:T(8,128)(2,1)} %bitcast.28, bf16[1,48,768]{2,1,0:T(8,128)(2,1)} %bitcast.29, bf16[1,48,768]{2,1,0:T(8,128)(2,1)} %bitcast.30), kind=kLoop, calls=%fused_computation.5 | loop fusion | flops 221184 | bytes 442368 | tf_op jit(solution)/shard_map/stack | solution.py:210
  1.7 3.0 %collective-permute-start = (bf16[3,48,384]{2,1,0:T(8,128)(2,1)S(1)}, bf16[3,48,384]{2,1,0:T(8,128)(2,1)S(1)}, u32[]{:S(2)}, u32[]{:S(2)}) collective-permute-start(bf16[3,48,384]{2,1,0:T(8,128)(2,1)S(1)} %get-tuple-element.73), channel_id=1, source_target_pairs={{0,2},{1,3},{2,0},{3,1},{4,6},{5,7},{6,4},{7,5},{8,10},{9,11},{10,... | collective-permute-start | bytes 331784 | tf_op jit(solution)/shard_map/ppermute | solution.py:204
  4.7 1.1 %fusion = bf16[1,192,1024]{2,1,0:T(8,128)(2,1)S(1)} fusion(bf16[1024,192]{0,1:T(8,128)(2,1)} %param.9, f32[1024]{0:T(1024)} %param.10), kind=kLoop, calls=%fused_computation.4 | loop fusion | flops 589824 | bytes 790528 | tf_op jit(solution)/shard_map/stack | solution.py:215
  5.9 1.9 %collective-permute-done.refs_4_ = bf16[3,48,384]{2,1,0:T(8,128)(2,1)S(1)} collective-permute-done((bf16[3,48,384]{2,1,0:T(8,128)(2,1)S(1)}, bf16[3,48,384]{2,1,0:T(8,128)(2,1)S(1)}, u32[]{:S(2)}, u32[]{:S(2)}) %collective-permute-start) | collective-permute-done | bytes 110624 | tf_op jit(solution)/shard_map/ppermute | solution.py:204
  7.8 1.7 %collective-permute-start.1 = (bf16[2,192,1024]{2,1,0:T(8,128)(2,1)S(1)}, bf16[2,192,1024]{2,1,0:T(8,128)(2,1)S(1)}, u32[]{:S(2)}, u32[]{:S(2)}) collective-permute-start(bf16[2,192,1024]{2,1,0:T(8,128)(2,1)S(1)} %pad_maximum_fusion.mine), channel_id=1, source_target_pairs={{0,2},{1,3},{2,0},{3,1},{4,6},{5,7},{6,4},{7,5},{8,10},{9,11},{10,... | collective-permute-start | bytes 2359304 | tf_op jit(solution)/shard_map/ppermute | solution.py:204
  9.5 2.6 %collective-permute-start.3 = (bf16[3,48,384]{2,1,0:T(8,128)(2,1)S(1)}, bf16[3,48,384]{2,1,0:T(8,128)(2,1)S(1)}, u32[]{:S(2)}, u32[]{:S(2)}) collective-permute-start(bf16[3,48,384]{2,1,0:T(8,128)(2,1)S(1)} %get-tuple-element.72.refs_0_), channel_id=1, source_target_pairs={{0,8},{1,9},{2,10},{3,11},{4,12},{5,13},{6,14},{7,15},{8,0},{9,1},... | collective-permute-start | bytes 331784 | tf_op jit(solution)/shard_map/ppermute | solution.py:204
  12.1 1.6 %collective-permute-start.2 = (bf16[3,48,384]{2,1,0:T(8,128)(2,1)S(1)}, bf16[3,48,384]{2,1,0:T(8,128)(2,1)S(1)}, u32[]{:S(2)}, u32[]{:S(2)}) collective-permute-start(bf16[3,48,384]{2,1,0:T(8,128)(2,1)S(1)} %get-tuple-element.72.refs_0_), channel_id=1, source_target_pairs={{0,4},{1,5},{2,6},{3,7},{4,0},{5,1},{6,2},{7,3},{8,12},{9,13},{10,... | collective-permute-start | bytes 331784 | tf_op jit(solution)/shard_map/ppermute | solution.py:204
  14.0 3.8 %collective-permute-done.3.refs_2_ = bf16[3,48,384]{2,1,0:T(8,128)(2,1)S(1)} collective-permute-done((bf16[3,48,384]{2,1,0:T(8,128)(2,1)S(1)}, bf16[3,48,384]{2,1,0:T(8,128)(2,1)S(1)}, u32[]{:S(2)}, u32[]{:S(2)}) %collective-permute-start.3) | collective-permute-done | bytes 110624 | tf_op jit(solution)/shard_map/ppermute | solution.py:204
  17.8 1.8 %collective-permute-start.5 = (bf16[3,48,384]{2,1,0:T(8,128)(2,1)S(1)}, bf16[3,48,384]{2,1,0:T(8,128)(2,1)S(1)}, u32[]{:S(2)}, u32[]{:S(2)}) collective-permute-start(bf16[3,48,384]{2,1,0:T(8,128)(2,1)S(1)} %collective-permute-done.refs_4_), channel_id=1, source_target_pairs={{0,4},{1,5},{2,6},{3,7},{4,0},{5,1},{6,2},{7,3},{8,12},{9,13},{10,... | collective-permute-start | bytes 331784 | tf_op jit(solution)/shard_map/ppermute | solution.py:204
  22.0 1.2 %collective-permute-done.5.refs_5_ = bf16[3,48,384]{2,1,0:T(8,128)(2,1)S(1)} collective-permute-done((bf16[3,48,384]{2,1,0:T(8,128)(2,1)S(1)}, bf16[3,48,384]{2,1,0:T(8,128)(2,1)S(1)}, u32[]{:S(2)}, u32[]{:S(2)}) %collective-permute-start.5) | collective-permute-done | bytes 110624 | tf_op jit(solution)/shard_map/ppermute | solution.py:204
  23.2 2.2 %collective-permute-done.4.refs_3_ = bf16[3,48,384]{2,1,0:T(8,128)(2,1)S(1)} collective-permute-done((bf16[3,48,384]{2,1,0:T(8,128)(2,1)S(1)}, bf16[3,48,384]{2,1,0:T(8,128)(2,1)S(1)}, u32[]{:S(2)}, u32[]{:S(2)}) %collective-permute-start.4) | collective-permute-done | bytes 110624 | tf_op jit(solution)/shard_map/ppermute | solution.py:204
  25.3 1.4 %collective-permute-done.7.refs_7_ = bf16[3,48,384]{2,1,0:T(8,128)(2,1)S(1)} collective-permute-done((bf16[3,48,384]{2,1,0:T(8,128)(2,1)S(1)}, bf16[3,48,384]{2,1,0:T(8,128)(2,1)S(1)}, u32[]{:S(2)}, u32[]{:S(2)}) %collective-permute-start.7) | collective-permute-done | bytes 110624 | tf_op jit(solution)/shard_map/ppermute | solution.py:204
  27.5 3.3 %shard_map.96.before = f32[3,384,384]{2,1,0:T(8,128)S(1)} custom-call(s32[3]{0:T(128)S(1)} %pad_add_fusion.place, bf16[2,192,1024]{2,1,0:T(8,128)(2,1)S(1)} %pad_maximum_fusion.mine, bf16[2,192,1024]{2,1,0:T(8,128)(2,1)S(1)} %collective-permute-done.9.other, bf16[3,384,384]{2,1,0:T(8,128)(2,1)S(1)} %shard_map.95.weights), custom_call_target="tpu_custom_call" | custom-call | flops 1811939328 | bytes 6684684 | tf_op jit(solution)/shard_map/pallas_call | solution.py:181
  30.9 3.1 %shard_map.97 = (bf16[2,3,48,384]{3,2,1,0:T(8,128)(2,1)S(1)}, bf16[2,3,48,384]{3,2,1,0:T(8,128)(2,1)S(1)}, bf16[2,384,1024]{2,1,0:T(8,128)(2,1)S(1)}, bf16[768,1024]{1,0:T(8,128)(2,1)S(1)}, bf16[384,1024]{1,0:T(8,128)(2,1)S(1)}) custom-call(s32[3]{0:T(128)S(1)} %pad_add_fusion.place, bf16[2,192,1024]{2,1,0:T(8,128)(2,1)S(1)} %collective-permute-done.1.mine, ...), custom_call_target="tpu_custom_call" | custom-call | flops 1358954496 | bytes 15433740 | tf_op jit(solution)/shard_map/pallas_call | solution.py:181
  34.0 1.2 %collective-permute-start.10 = (bf16[2,3,48,384]{3,2,1,0:T(8,128)(2,1)S(1)}, bf16[2,3,48,384]{3,2,1,0:T(8,128)(2,1)S(1)}, u32[]{:S(2)}, u32[]{:S(2)}) collective-permute-start(bf16[2,3,48,384]{3,2,1,0:T(8,128)(2,1)S(1)} %get-tuple-element.48), channel_id=1, source_target_pairs={{0,4},{1,5},{2,6},{3,7},{4,0},{5,1},{6,2},{7,3},{8,12},{9,13},{10,... | collective-permute-start | bytes 663560 | tf_op jit(solution)/shard_map/ppermute | solution.py:204
  36.8 1.5 %shard_map.98 = (f32[2,3,48,384]{3,2,1,0:T(8,128)S(1)}, f32[2,3,48,384]{3,2,1,0:T(8,128)S(1)}, bf16[2,3,48,384]{3,2,1,0:T(8,128)(2,1)S(1)}, bf16[2,3,48,384]{3,2,1,0:T(8,128)(2,1)S(1)}) custom-call(s32[3]{0:T(128)S(1)} %pad_add_fusion.place, bf16[2,384,1024]{2,1,0:T(8,128)(2,1)S(1)} %get-tuple-element.41.tokens, ...), custom_call_target="tpu_custom_call" | custom-call | flops 452984832 | bytes 13172748 | tf_op jit(solution)/shard_map/pallas_call | solution.py:181
  38.3 2.1 %collective-permute-done.12.refs_6_ = bf16[2,192,128]{2,1,0:T(8,128)(2,1)S(1)} collective-permute-done((bf16[2,192,128]{2,1,0:T(8,128)(2,1)S(1)}, bf16[2,192,128]{2,1,0:T(8,128)(2,1)S(1)}, u32[]{:S(2)}, u32[]{:S(2)}) %collective-permute-start.12) | collective-permute-done | bytes 98336 | tf_op jit(solution)/shard_map/ppermute | solution.py:204
  40.4 1.8 %collective-permute-done.10.came = bf16[2,3,48,384]{3,2,1,0:T(8,128)(2,1)S(1)} collective-permute-done((bf16[2,3,48,384]{3,2,1,0:T(8,128)(2,1)S(1)}, bf16[2,3,48,384]{3,2,1,0:T(8,128)(2,1)S(1)}, u32[]{:S(2)}, u32[]{:S(2)}) %collective-permute-start.10) | collective-permute-done | bytes 221216 | tf_op jit(solution)/shard_map/ppermute | solution.py:204
  42.3 3.8 %collective-permute-start.13 = (bf16[2,3,48,384]{3,2,1,0:T(8,128)(2,1)S(1)}, bf16[2,3,48,384]{3,2,1,0:T(8,128)(2,1)S(1)}, u32[]{:S(2)}, u32[]{:S(2)}) collective-permute-start(bf16[2,3,48,384]{3,2,1,0:T(8,128)(2,1)S(1)} %add_convert_fusion.1), channel_id=1, source_target_pairs={{0,12},{1,13},{2,14},{3,15},{4,8},{5,9},{6,10},{7,11},{8,4},{9,5},... | collective-permute-start | bytes 663560 | tf_op jit(solution)/shard_map/ppermute | solution.py:204
  46.6 10.9 %collective-permute-start.15 = (bf16[2,3,48,384]{3,2,1,0:T(8,128)(2,1)S(1)}, bf16[2,3,48,384]{3,2,1,0:T(8,128)(2,1)S(1)}, u32[]{:S(2)}, u32[]{:S(2)}) collective-permute-start(bf16[2,3,48,384]{3,2,1,0:T(8,128)(2,1)S(1)} %add_convert_fusion), channel_id=1, source_target_pairs={{0,12},{1,13},{2,14},{3,15},{4,8},{5,9},{6,10},{7,11},{8,4},{9,5},... | collective-permute-start | bytes 663560 | tf_op jit(solution)/shard_map/ppermute | solution.py:204
  57.9 1.5 %collective-permute-start.17 = (bf16[2,3,48,384]{3,2,1,0:T(8,128)(2,1)S(1)}, bf16[2,3,48,384]{3,2,1,0:T(8,128)(2,1)S(1)}, u32[]{:S(2)}, u32[]{:S(2)}) collective-permute-start(bf16[2,3,48,384]{3,2,1,0:T(8,128)(2,1)S(1)} %get-tuple-element.51.refs_0_), channel_id=1, source_target_pairs={{0,4},{1,5},{2,6},{3,7},{4,0},{5,1},{6,2},{7,3},{8,12},{9,13},{10,... | collective-permute-start | bytes 663560 | tf_op jit(solution)/shard_map/ppermute | solution.py:204
  59.3 3.6 %collective-permute-done.15.crossed = bf16[2,3,48,384]{3,2,1,0:T(8,128)(2,1)S(1)} collective-permute-done((bf16[2,3,48,384]{3,2,1,0:T(8,128)(2,1)S(1)}, bf16[2,3,48,384]{3,2,1,0:T(8,128)(2,1)S(1)}, u32[]{:S(2)}, u32[]{:S(2)}) %collective-permute-start.15) | collective-permute-done | bytes 221216 | tf_op jit(solution)/shard_map/ppermute | solution.py:204
  63.3 1.2 %collective-permute-start.22 = (bf16[2,192,128]{2,1,0:T(8,128)(2,1)S(1)}, bf16[2,192,128]{2,1,0:T(8,128)(2,1)S(1)}, u32[]{:S(2)}, u32[]{:S(2)}) collective-permute-start(bf16[2,192,128]{2,1,0:T(8,128)(2,1)S(1)} %pad_maximum_fusion.2.mine), channel_id=1, source_target_pairs={{0,3},{1,2},{2,1},{3,0},{4,7},{5,6},{6,5},{7,4},{8,11},{9,10},{10,... | collective-permute-start | bytes 294920 | tf_op jit(solution)/shard_map/ppermute | solution.py:204
  64.5 1.3 %collective-permute-start.18 = (bf16[2,3,48,384]{3,2,1,0:T(8,128)(2,1)S(1)}, bf16[2,3,48,384]{3,2,1,0:T(8,128)(2,1)S(1)}, u32[]{:S(2)}, u32[]{:S(2)}) collective-permute-start(bf16[2,3,48,384]{3,2,1,0:T(8,128)(2,1)S(1)} %get-tuple-element.55.refs_1_), channel_id=1, source_target_pairs={{0,4},{1,5},{2,6},{3,7},{4,0},{5,1},{6,2},{7,3},{8,12},{9,13},{10,... | collective-permute-start | bytes 663560 | tf_op jit(solution)/shard_map/ppermute | solution.py:204
  65.8 1.6 %collective-permute-start.19 = (f32[2,24,96]{2,1,0:T(8,128)S(1)}, f32[2,24,96]{2,1,0:T(8,128)S(1)}, u32[]{:S(2)}, u32[]{:S(2)}) collective-permute-start(f32[2,24,96]{2,1,0:T(8,128)S(1)} %fusion.1.here), channel_id=1, source_target_pairs={{0,2},{1,3},{2,0},{3,1},{4,6},{5,7},{6,4},{7,5},{8,10},{9,11},{10,... | collective-permute-start | bytes 55304 | tf_op jit(solution)/shard_map/ppermute | solution.py:204
  67.5 1.8 %collective-permute-start.21 = (f32[2,24,96]{2,1,0:T(8,128)S(1)}, f32[2,24,96]{2,1,0:T(8,128)S(1)}, u32[]{:S(2)}, u32[]{:S(2)}) collective-permute-start(f32[2,24,96]{2,1,0:T(8,128)S(1)} %fusion.1.here), channel_id=1, source_target_pairs={{0,6},{1,7},{2,4},{3,5},{4,2},{5,3},{6,0},{7,1},{8,14},{9,15},{10,... | collective-permute-start | bytes 55304 | tf_op jit(solution)/shard_map/ppermute | solution.py:204
  69.7 3.0 %collective-permute-done.20.here = f32[2,24,96]{2,1,0:T(8,128)S(1)} collective-permute-done((f32[2,24,96]{2,1,0:T(8,128)S(1)}, f32[2,24,96]{2,1,0:T(8,128)S(1)}, u32[]{:S(2)}, u32[]{:S(2)}) %collective-permute-start.20) | collective-permute-done | bytes 18464 | tf_op jit(solution)/shard_map/ppermute | solution.py:204
  73.5 2.0 %shard_map.103 = (bf16[3,384,384]{2,1,0:T(8,128)(2,1)S(1)}, f32[2,192,128]{2,1,0:T(8,128)S(1)}, bf16[2,192,128]{2,1,0:T(8,128)(2,1)S(1)}) custom-call(s32[3]{0:T(128)S(1)} %pad_add_fusion.place, bf16[3,384,384]{2,1,0:T(8,128)(2,1)S(1)} %shard_map.95.weights, bf16[2,3,48,384]{3,2,1,0:T(8,128)(2,1)S(1)} %get-tuple-element.51.refs_0_, ...), custom_call_target="tpu_custom_call" | custom-call | flops 226492416 | bytes 6119436 | tf_op jit(solution)/shard_map/pallas_call | solution.py:181
  75.6 1.3 %collective-permute-done.23 = bf16[2,192,128]{2,1,0:T(8,128)(2,1)S(1)} collective-permute-done((bf16[2,192,128]{2,1,0:T(8,128)(2,1)S(1)}, bf16[2,192,128]{2,1,0:T(8,128)(2,1)S(1)}, u32[]{:S(2)}, u32[]{:S(2)}) %collective-permute-start.23) | collective-permute-done | bytes 98336 | tf_op jit(solution)/shard_map/ppermute | solution.py:204
  77.0 1.0 %collective-permute-start.25 = (bf16[2,192,128]{2,1,0:T(8,128)(2,1)S(1)}, bf16[2,192,128]{2,1,0:T(8,128)(2,1)S(1)}, u32[]{:S(2)}, u32[]{:S(2)}) collective-permute-start(bf16[2,192,128]{2,1,0:T(8,128)(2,1)S(1)} %add_convert_fusion.2), channel_id=1, source_target_pairs={{0,2},{1,3},{2,0},{3,1},{4,6},{5,7},{6,4},{7,5},{8,10},{9,11},{10,... | collective-permute-start | bytes 294920 | tf_op jit(solution)/shard_map/ppermute | solution.py:204
  78.0 1.3 %shard_map.104 = (f32[2,192,128]{2,1,0:T(8,128)S(1)}, bf16[2,192,128]{2,1,0:T(8,128)(2,1)S(1)}) custom-call(s32[3]{0:T(128)S(1)} %pad_add_fusion.place, bf16[3,384,384]{2,1,0:T(8,128)(2,1)S(1)} %get-tuple-element.61.renewed, bf16[2,192,128]{2,1,0:T(8,128)(2,1)S(1)} %pad_maximum_fusion.2.mine, bf16[2,192,128]{2,1,0:T(8,128)(2,1)S(1)} %collective-permute-done.11.other), custom_call_target="tpu_custom_call" | custom-call | flops 226492416 | bytes 2555916 | tf_op jit(solution)/shard_map/pallas_call | solution.py:181
  79.3 2.5 %collective-permute-done.25.pair = bf16[2,192,128]{2,1,0:T(8,128)(2,1)S(1)} collective-permute-done((bf16[2,192,128]{2,1,0:T(8,128)(2,1)S(1)}, bf16[2,192,128]{2,1,0:T(8,128)(2,1)S(1)}, u32[]{:S(2)}, u32[]{:S(2)}) %collective-permute-start.25) | collective-permute-done | bytes 98336 | tf_op jit(solution)/shard_map/ppermute | solution.py:204
  (48 shorter events, 8.5 us)
Async XLA Ops:
  0.6 5.2 %copy-start = (bf16[1024,192]{0,1:T(8,128)(2,1)S(1)}, bf16[1024,192]{0,1:T(8,128)(2,1)}, u32[]{:S(2)}) copy-start(bf16[1024,192]{0,1:T(8,128)(2,1)} %param.8) | copy-start | bytes 1179652
  1.7 6.1 %collective-permute-start = (bf16[3,48,384]{2,1,0:T(8,128)(2,1)S(1)}, bf16[3,48,384]{2,1,0:T(8,128)(2,1)S(1)}, u32[]{:S(2)}, u32[]{:S(2)}) collective-permute-start(bf16[3,48,384]{2,1,0:T(8,128)(2,1)S(1)} %get-tuple-element.73), channel_id=1, source_target_pairs={{0,2},{1,3},{2,0},{3,1},{4,6},{5,7},{6,4},{7,5},{8,10},{9,11},{10,... | collective-permute-start | bytes 331784 | tf_op jit(solution)/shard_map/ppermute | solution.py:204
  5.8 21.6 %copy-start.1 = (bf16[128,192]{0,1:T(8,128)(2,1)S(1)}, bf16[128,192]{0,1:T(8,128)(2,1)}, u32[]{:S(2)}) copy-start(bf16[128,192]{0,1:T(8,128)(2,1)} %param.15) | copy-start | bytes 147460
  5.9 21.6 %copy-start.2 = (bf16[128,192]{0,1:T(8,128)(2,1)S(1)}, bf16[128,192]{0,1:T(8,128)(2,1)}, u32[]{:S(2)}) copy-start(bf16[128,192]{0,1:T(8,128)(2,1)} %param.14) | copy-start | bytes 147460
  7.8 19.6 %collective-permute-start.1 = (bf16[2,192,1024]{2,1,0:T(8,128)(2,1)S(1)}, bf16[2,192,1024]{2,1,0:T(8,128)(2,1)S(1)}, u32[]{:S(2)}, u32[]{:S(2)}) collective-permute-start(bf16[2,192,1024]{2,1,0:T(8,128)(2,1)S(1)} %pad_maximum_fusion.mine), channel_id=1, source_target_pairs={{0,2},{1,3},{2,0},{3,1},{4,6},{5,7},{6,4},{7,5},{8,10},{9,11},{10,... | collective-permute-start | bytes 2359304 | tf_op jit(solution)/shard_map/ppermute | solution.py:204
  9.5 8.3 %collective-permute-start.3 = (bf16[3,48,384]{2,1,0:T(8,128)(2,1)S(1)}, bf16[3,48,384]{2,1,0:T(8,128)(2,1)S(1)}, u32[]{:S(2)}, u32[]{:S(2)}) collective-permute-start(bf16[3,48,384]{2,1,0:T(8,128)(2,1)S(1)} %get-tuple-element.72.refs_0_), channel_id=1, source_target_pairs={{0,8},{1,9},{2,10},{3,11},{4,12},{5,13},{6,14},{7,15},{8,0},{9,1},... | collective-permute-start | bytes 331784 | tf_op jit(solution)/shard_map/ppermute | solution.py:204
  12.1 7.5 %collective-permute-start.2 = (bf16[3,48,384]{2,1,0:T(8,128)(2,1)S(1)}, bf16[3,48,384]{2,1,0:T(8,128)(2,1)S(1)}, u32[]{:S(2)}, u32[]{:S(2)}) collective-permute-start(bf16[3,48,384]{2,1,0:T(8,128)(2,1)S(1)} %get-tuple-element.72.refs_0_), channel_id=1, source_target_pairs={{0,4},{1,5},{2,6},{3,7},{4,0},{5,1},{6,2},{7,3},{8,12},{9,13},{10,... | collective-permute-start | bytes 331784 | tf_op jit(solution)/shard_map/ppermute | solution.py:204
  13.7 7.7 %collective-permute-start.6 = (bf16[3,48,384]{2,1,0:T(8,128)(2,1)S(1)}, bf16[3,48,384]{2,1,0:T(8,128)(2,1)S(1)}, u32[]{:S(2)}, u32[]{:S(2)}) collective-permute-start(bf16[3,48,384]{2,1,0:T(8,128)(2,1)S(1)} %collective-permute-done.refs_4_), channel_id=1, source_target_pairs={{0,8},{1,9},{2,10},{3,11},{4,12},{5,13},{6,14},{7,15},{8,0},{9,1},... | collective-permute-start | bytes 331784 | tf_op jit(solution)/shard_map/ppermute | solution.py:204
  14.0 13.5 %collective-permute-start.9 = (bf16[2,192,1024]{2,1,0:T(8,128)(2,1)S(1)}, bf16[2,192,1024]{2,1,0:T(8,128)(2,1)S(1)}, u32[]{:S(2)}, u32[]{:S(2)}) collective-permute-start(bf16[2,192,1024]{2,1,0:T(8,128)(2,1)S(1)} %pad_maximum_fusion.mine), channel_id=1, source_target_pairs={{0,1},{1,0},{2,3},{3,2},{4,5},{5,4},{6,7},{7,6},{8,9},{9,8},{10,11... | collective-permute-start | bytes 2359304 | tf_op jit(solution)/shard_map/ppermute | solution.py:204
  17.8 5.3 %collective-permute-start.5 = (bf16[3,48,384]{2,1,0:T(8,128)(2,1)S(1)}, bf16[3,48,384]{2,1,0:T(8,128)(2,1)S(1)}, u32[]{:S(2)}, u32[]{:S(2)}) collective-permute-start(bf16[3,48,384]{2,1,0:T(8,128)(2,1)S(1)} %collective-permute-done.refs_4_), channel_id=1, source_target_pairs={{0,4},{1,5},{2,6},{3,7},{4,0},{5,1},{6,2},{7,3},{8,12},{9,13},{10,... | collective-permute-start | bytes 331784 | tf_op jit(solution)/shard_map/ppermute | solution.py:204
  19.6 5.7 %collective-permute-start.4 = (bf16[3,48,384]{2,1,0:T(8,128)(2,1)S(1)}, bf16[3,48,384]{2,1,0:T(8,128)(2,1)S(1)}, u32[]{:S(2)}, u32[]{:S(2)}) collective-permute-start(bf16[3,48,384]{2,1,0:T(8,128)(2,1)S(1)} %collective-permute-done.3.refs_2_), channel_id=1, source_target_pairs={{0,4},{1,5},{2,6},{3,7},{4,0},{5,1},{6,2},{7,3},{8,12},{9,13},{10,... | collective-permute-start | bytes 331784 | tf_op jit(solution)/shard_map/ppermute | solution.py:204
  21.4 5.4 %collective-permute-start.7 = (bf16[3,48,384]{2,1,0:T(8,128)(2,1)S(1)}, bf16[3,48,384]{2,1,0:T(8,128)(2,1)S(1)}, u32[]{:S(2)}, u32[]{:S(2)}) collective-permute-start(bf16[3,48,384]{2,1,0:T(8,128)(2,1)S(1)} %collective-permute-done.6.refs_6_), channel_id=1, source_target_pairs={{0,4},{1,5},{2,6},{3,7},{4,0},{5,1},{6,2},{7,3},{8,12},{9,13},{10,... | collective-permute-start | bytes 331784 | tf_op jit(solution)/shard_map/ppermute | solution.py:204
  27.4 3.5 %collective-permute-start.8 = (bf16[2,192,1024]{2,1,0:T(8,128)(2,1)S(1)}, bf16[2,192,1024]{2,1,0:T(8,128)(2,1)S(1)}, u32[]{:S(2)}, u32[]{:S(2)}) collective-permute-start(bf16[2,192,1024]{2,1,0:T(8,128)(2,1)S(1)} %collective-permute-done.1.mine), channel_id=1, source_target_pairs={{0,1},{1,0},{2,3},{3,2},{4,5},{5,4},{6,7},{7,6},{8,9},{9,8},{10,11... | collective-permute-start | bytes 2359304 | tf_op jit(solution)/shard_map/ppermute | solution.py:204
  34.0 8.3 %collective-permute-start.10 = (bf16[2,3,48,384]{3,2,1,0:T(8,128)(2,1)S(1)}, bf16[2,3,48,384]{3,2,1,0:T(8,128)(2,1)S(1)}, u32[]{:S(2)}, u32[]{:S(2)}) collective-permute-start(bf16[2,3,48,384]{3,2,1,0:T(8,128)(2,1)S(1)} %get-tuple-element.48), channel_id=1, source_target_pairs={{0,4},{1,5},{2,6},{3,7},{4,0},{5,1},{6,2},{7,3},{8,12},{9,13},{10,... | collective-permute-start | bytes 663560 | tf_op jit(solution)/shard_map/ppermute | solution.py:204
  35.2 3.1 %collective-permute-start.11 = (bf16[2,192,128]{2,1,0:T(8,128)(2,1)S(1)}, bf16[2,192,128]{2,1,0:T(8,128)(2,1)S(1)}, u32[]{:S(2)}, u32[]{:S(2)}) collective-permute-start(bf16[2,192,128]{2,1,0:T(8,128)(2,1)S(1)} %pad_maximum_fusion.2.mine), channel_id=1, source_target_pairs={{0,1},{1,0},{2,3},{3,2},{4,5},{5,4},{6,7},{7,6},{8,9},{9,8},{10,11... | collective-permute-start | bytes 294920 | tf_op jit(solution)/shard_map/ppermute | solution.py:204
  35.4 5.0 %collective-permute-start.12 = (bf16[2,192,128]{2,1,0:T(8,128)(2,1)S(1)}, bf16[2,192,128]{2,1,0:T(8,128)(2,1)S(1)}, u32[]{:S(2)}, u32[]{:S(2)}) collective-permute-start(bf16[2,192,128]{2,1,0:T(8,128)(2,1)S(1)} %pad_maximum_fusion.2.mine), channel_id=1, source_target_pairs={{0,2},{1,3},{2,0},{3,1},{4,6},{5,7},{6,4},{7,5},{8,10},{9,11},{10,... | collective-permute-start | bytes 294920 | tf_op jit(solution)/shard_map/ppermute | solution.py:204
  36.3 10.3 %collective-permute-start.14 = (bf16[2,3,48,384]{3,2,1,0:T(8,128)(2,1)S(1)}, bf16[2,3,48,384]{3,2,1,0:T(8,128)(2,1)S(1)}, u32[]{:S(2)}, u32[]{:S(2)}) collective-permute-start(bf16[2,3,48,384]{3,2,1,0:T(8,128)(2,1)S(1)} %get-tuple-element.54), channel_id=1, source_target_pairs={{0,4},{1,5},{2,6},{3,7},{4,0},{5,1},{6,2},{7,3},{8,12},{9,13},{10,... | collective-permute-start | bytes 663560 | tf_op jit(solution)/shard_map/ppermute | solution.py:204
  42.3 15.2 %collective-permute-start.13 = (bf16[2,3,48,384]{3,2,1,0:T(8,128)(2,1)S(1)}, bf16[2,3,48,384]{3,2,1,0:T(8,128)(2,1)S(1)}, u32[]{:S(2)}, u32[]{:S(2)}) collective-permute-start(bf16[2,3,48,384]{3,2,1,0:T(8,128)(2,1)S(1)} %add_convert_fusion.1), channel_id=1, source_target_pairs={{0,12},{1,13},{2,14},{3,15},{4,8},{5,9},{6,10},{7,11},{8,4},{9,5},... | collective-permute-start | bytes 663560 | tf_op jit(solution)/shard_map/ppermute | solution.py:204
  46.6 16.3 %collective-permute-start.15 = (bf16[2,3,48,384]{3,2,1,0:T(8,128)(2,1)S(1)}, bf16[2,3,48,384]{3,2,1,0:T(8,128)(2,1)S(1)}, u32[]{:S(2)}, u32[]{:S(2)}) collective-permute-start(bf16[2,3,48,384]{3,2,1,0:T(8,128)(2,1)S(1)} %add_convert_fusion), channel_id=1, source_target_pairs={{0,12},{1,13},{2,14},{3,15},{4,8},{5,9},{6,10},{7,11},{8,4},{9,5},... | collective-permute-start | bytes 663560 | tf_op jit(solution)/shard_map/ppermute | solution.py:204
  57.9 7.9 %collective-permute-start.17 = (bf16[2,3,48,384]{3,2,1,0:T(8,128)(2,1)S(1)}, bf16[2,3,48,384]{3,2,1,0:T(8,128)(2,1)S(1)}, u32[]{:S(2)}, u32[]{:S(2)}) collective-permute-start(bf16[2,3,48,384]{3,2,1,0:T(8,128)(2,1)S(1)} %get-tuple-element.51.refs_0_), channel_id=1, source_target_pairs={{0,4},{1,5},{2,6},{3,7},{4,0},{5,1},{6,2},{7,3},{8,12},{9,13},{10,... | collective-permute-start | bytes 663560 | tf_op jit(solution)/shard_map/ppermute | solution.py:204
  63.2 2.6 %collective-permute-start.16 = (f32[2,24,96]{2,1,0:T(8,128)S(1)}, f32[2,24,96]{2,1,0:T(8,128)S(1)}, u32[]{:S(2)}, u32[]{:S(2)}) collective-permute-start(f32[2,24,96]{2,1,0:T(8,128)S(1)} %pad_maximum_fusion.3), channel_id=1, source_target_pairs={{0,1},{1,0},{2,3},{3,2},{4,5},{5,4},{6,7},{7,6},{8,9},{9,8},{10,11... | collective-permute-start | bytes 55304 | tf_op jit(solution)/shard_map/ppermute | solution.py:204
  63.3 10.2 %collective-permute-start.22 = (bf16[2,192,128]{2,1,0:T(8,128)(2,1)S(1)}, bf16[2,192,128]{2,1,0:T(8,128)(2,1)S(1)}, u32[]{:S(2)}, u32[]{:S(2)}) collective-permute-start(bf16[2,192,128]{2,1,0:T(8,128)(2,1)S(1)} %pad_maximum_fusion.2.mine), channel_id=1, source_target_pairs={{0,3},{1,2},{2,1},{3,0},{4,7},{5,6},{6,5},{7,4},{8,11},{9,10},{10,... | collective-permute-start | bytes 294920 | tf_op jit(solution)/shard_map/ppermute | solution.py:204
  64.5 9.0 %collective-permute-start.18 = (bf16[2,3,48,384]{3,2,1,0:T(8,128)(2,1)S(1)}, bf16[2,3,48,384]{3,2,1,0:T(8,128)(2,1)S(1)}, u32[]{:S(2)}, u32[]{:S(2)}) collective-permute-start(bf16[2,3,48,384]{3,2,1,0:T(8,128)(2,1)S(1)} %get-tuple-element.55.refs_1_), channel_id=1, source_target_pairs={{0,4},{1,5},{2,6},{3,7},{4,0},{5,1},{6,2},{7,3},{8,12},{9,13},{10,... | collective-permute-start | bytes 663560 | tf_op jit(solution)/shard_map/ppermute | solution.py:204
  65.8 3.9 %collective-permute-start.19 = (f32[2,24,96]{2,1,0:T(8,128)S(1)}, f32[2,24,96]{2,1,0:T(8,128)S(1)}, u32[]{:S(2)}, u32[]{:S(2)}) collective-permute-start(f32[2,24,96]{2,1,0:T(8,128)S(1)} %fusion.1.here), channel_id=1, source_target_pairs={{0,2},{1,3},{2,0},{3,1},{4,6},{5,7},{6,4},{7,5},{8,10},{9,11},{10,... | collective-permute-start | bytes 55304 | tf_op jit(solution)/shard_map/ppermute | solution.py:204
  67.4 5.3 %collective-permute-start.20 = (f32[2,24,96]{2,1,0:T(8,128)S(1)}, f32[2,24,96]{2,1,0:T(8,128)S(1)}, u32[]{:S(2)}, u32[]{:S(2)}) collective-permute-start(f32[2,24,96]{2,1,0:T(8,128)S(1)} %fusion.1.here), channel_id=1, source_target_pairs={{0,4},{1,5},{2,6},{3,7},{4,0},{5,1},{6,2},{7,3},{8,12},{9,13},{10,... | collective-permute-start | bytes 55304 | tf_op jit(solution)/shard_map/ppermute | solution.py:204
  67.5 5.9 %collective-permute-start.21 = (f32[2,24,96]{2,1,0:T(8,128)S(1)}, f32[2,24,96]{2,1,0:T(8,128)S(1)}, u32[]{:S(2)}, u32[]{:S(2)}) collective-permute-start(f32[2,24,96]{2,1,0:T(8,128)S(1)} %fusion.1.here), channel_id=1, source_target_pairs={{0,6},{1,7},{2,4},{3,5},{4,2},{5,3},{6,0},{7,1},{8,14},{9,15},{10,... | collective-permute-start | bytes 55304 | tf_op jit(solution)/shard_map/ppermute | solution.py:204
  75.6 1.4 %collective-permute-start.23 = (bf16[2,192,128]{2,1,0:T(8,128)(2,1)S(1)}, bf16[2,192,128]{2,1,0:T(8,128)(2,1)S(1)}, u32[]{:S(2)}, u32[]{:S(2)}) collective-permute-start(bf16[2,192,128]{2,1,0:T(8,128)(2,1)S(1)} %get-tuple-element.62), channel_id=1, source_target_pairs={{0,1},{1,0},{2,3},{3,2},{4,5},{5,4},{6,7},{7,6},{8,9},{9,8},{10,11... | collective-permute-start | bytes 294920 | tf_op jit(solution)/shard_map/ppermute | solution.py:204
  77.0 4.9 %collective-permute-start.25 = (bf16[2,192,128]{2,1,0:T(8,128)(2,1)S(1)}, bf16[2,192,128]{2,1,0:T(8,128)(2,1)S(1)}, u32[]{:S(2)}, u32[]{:S(2)}) collective-permute-start(bf16[2,192,128]{2,1,0:T(8,128)(2,1)S(1)} %add_convert_fusion.2), channel_id=1, source_target_pairs={{0,2},{1,3},{2,0},{3,1},{4,6},{5,7},{6,4},{7,5},{8,10},{9,11},{10,... | collective-permute-start | bytes 294920 | tf_op jit(solution)/shard_map/ppermute | solution.py:204
  79.2 2.6 %collective-permute-start.24 = (bf16[2,192,128]{2,1,0:T(8,128)(2,1)S(1)}, bf16[2,192,128]{2,1,0:T(8,128)(2,1)S(1)}, u32[]{:S(2)}, u32[]{:S(2)}) collective-permute-start(bf16[2,192,128]{2,1,0:T(8,128)(2,1)S(1)} %get-tuple-element.67), channel_id=1, source_target_pairs={{0,1},{1,0},{2,3},{3,2},{4,5},{5,4},{6,7},{7,6},{8,9},{9,8},{10,11... | collective-permute-start | bytes 294920 | tf_op jit(solution)/shard_map/ppermute | solution.py:204

commit v10 on v9

--- a/solution.py
+++ b/solution.py
@@ -176,7 +176,7 @@
 def call(body, operands, outs, scratch=(), flops=0, place=None, mib=4):
     specs = [pl.BlockSpec(memory_space=pltpu.VMEM)] * len(operands)
     if place is not None:
-        specs, operands = [pl.BlockSpec(memory_space=pltpu.SMEM)] + specs, (place, *operands)
+        inner, body = body, lambda *refs: inner(place(), *refs)
     moved = sum(4 * leaf.size for leaf in (*operands, *outs))
     return pl.pallas_call(
         body,
@@ -196,7 +196,11 @@
     groups = n_tok // 2
     tok, half = lax.axis_index("tok"), lax.axis_index("hid")
     group, side = tok // 2, tok % 2
-    place = jnp.stack([group, side, half]).astype(jnp.int32)
+
+    def place():
+        spot = lax.axis_index("tok")
+        return spot >> 1, spot & 1, lax.axis_index("hid")
+
     core, pair, zed = 1, 2, 4
 
     def swap(array, flip):

time: 82.7 us -> 80.6 us (0.975)
  Pallas kernels: 13.1 us -> 9.93 us
  starting transfers between devices: 38.7 us -> 39.9 us
    pallas_call x11, Pallas kernels: 13.1 us -> 9.93 us  [call(): pl.pallas_call(body, out_shape=list(outs), in_specs=specs, out_specs=[pl....]
    ppermute x26, starting transfers between devices: 38.7 us -> 39.9 us  [swap(): return lax.ppermute(array, ('tok', 'hid'), pairs)]
  transfers between devices with their start and end apart: 26 -> 26, of which waited for: 15 -> 15; matrix products, arithmetic and copies ran while one was open for 2% -> 2% of each run, Pallas kernels for 9% -> 7%
where the time goes in v10:
time: 80.6 us; the launch traced here: 80.5 us
  starting transfers between devices  39.9 us (50%)
  waiting for transfers between devices  27.4 us (34%)
  Pallas kernels  9.93 us (12%)
  other arithmetic  2.33 us (3%)
  between operations  0.9 us (1%)
    ppermute x26, starting transfers between devices, swap(): return lax.ppermute(array, ('tok', 'hid'), pairs)  39.9 us
    ppermute x26, waiting for transfers between devices, swap(): return lax.ppermute(array, ('tok', 'hid'), pairs)  27.4 us
    pallas_call x11, Pallas kernels, call(): pl.pallas_call(body, out_shape=list(outs), in_specs=specs, out_specs=[pl....  9.93 us
  transfers between devices with their start and end apart: 26, of which 15 were waited for; matrix products, arithmetic and copies ran while one was open for 2% of the time, Pallas kernels for 7%

profile of v10, /device:TPU:0, one launch (start us, length us, event | category | flops | bytes accessed | tf_op | source)
XLA Modules:
  0.0 80.5 jit_solution(14197395611756154283)
XLA Ops:
  0.7 1.0 %pad_maximum_fusion.1 = bf16[3,48,768]{2,1,0:T(8,128)(2,1)S(1)} fusion(bf16[1,48,768]{2,1,0:T(8,128)(2,1)} %bitcast.25, bf16[1,48,768]{2,1,0:T(8,128)(2,1)} %bitcast.26, bf16[1,48,768]{2,1,0:T(8,128)(2,1)} %bitcast.27), kind=kLoop, calls=%fused_computation.5 | loop fusion | flops 221184 | bytes 442368 | tf_op jit(solution)/shard_map/stack | solution.py:214
  1.7 3.0 %collective-permute-start = (bf16[3,48,384]{2,1,0:T(8,128)(2,1)S(1)}, bf16[3,48,384]{2,1,0:T(8,128)(2,1)S(1)}, u32[]{:S(2)}, u32[]{:S(2)}) collective-permute-start(bf16[3,48,384]{2,1,0:T(8,128)(2,1)S(1)} %get-tuple-element.73), channel_id=1, source_target_pairs={{0,2},{1,3},{2,0},{3,1},{4,6},{5,7},{6,4},{7,5},{8,10},{9,11},{10,... | collective-permute-start | bytes 331784 | tf_op jit(solution)/shard_map/ppermute | solution.py:208
  4.7 1.1 %fusion = bf16[1,192,1024]{2,1,0:T(8,128)(2,1)S(1)} fusion(bf16[1024,192]{0,1:T(8,128)(2,1)} %param.9, f32[1024]{0:T(1024)} %param.10), kind=kLoop, calls=%fused_computation.4 | loop fusion | flops 589824 | bytes 790528 | tf_op jit(solution)/shard_map/stack | solution.py:219
  5.9 1.9 %collective-permute-done.refs_4_ = bf16[3,48,384]{2,1,0:T(8,128)(2,1)S(1)} collective-permute-done((bf16[3,48,384]{2,1,0:T(8,128)(2,1)S(1)}, bf16[3,48,384]{2,1,0:T(8,128)(2,1)S(1)}, u32[]{:S(2)}, u32[]{:S(2)}) %collective-permute-start) | collective-permute-done | bytes 110624 | tf_op jit(solution)/shard_map/ppermute | solution.py:208
  7.8 1.7 %collective-permute-start.1 = (bf16[2,192,1024]{2,1,0:T(8,128)(2,1)S(1)}, bf16[2,192,1024]{2,1,0:T(8,128)(2,1)S(1)}, u32[]{:S(2)}, u32[]{:S(2)}) collective-permute-start(bf16[2,192,1024]{2,1,0:T(8,128)(2,1)S(1)} %pad_maximum_fusion.refs_0_), channel_id=1, source_target_pairs={{0,2},{1,3},{2,0},{3,1},{4,6},{5,7},{6,4},{7,5},{8,10},{9,11},{10,... | collective-permute-start | bytes 2359304 | tf_op jit(solution)/shard_map/ppermute | solution.py:208
  9.5 2.6 %collective-permute-start.3 = (bf16[3,48,384]{2,1,0:T(8,128)(2,1)S(1)}, bf16[3,48,384]{2,1,0:T(8,128)(2,1)S(1)}, u32[]{:S(2)}, u32[]{:S(2)}) collective-permute-start(bf16[3,48,384]{2,1,0:T(8,128)(2,1)S(1)} %get-tuple-element.72.refs_0_), channel_id=1, source_target_pairs={{0,8},{1,9},{2,10},{3,11},{4,12},{5,13},{6,14},{7,15},{8,0},{9,1},... | collective-permute-start | bytes 331784 | tf_op jit(solution)/shard_map/ppermute | solution.py:208
  12.1 1.6 %collective-permute-start.2 = (bf16[3,48,384]{2,1,0:T(8,128)(2,1)S(1)}, bf16[3,48,384]{2,1,0:T(8,128)(2,1)S(1)}, u32[]{:S(2)}, u32[]{:S(2)}) collective-permute-start(bf16[3,48,384]{2,1,0:T(8,128)(2,1)S(1)} %get-tuple-element.72.refs_0_), channel_id=1, source_target_pairs={{0,4},{1,5},{2,6},{3,7},{4,0},{5,1},{6,2},{7,3},{8,12},{9,13},{10,... | collective-permute-start | bytes 331784 | tf_op jit(solution)/shard_map/ppermute | solution.py:208
  14.0 3.8 %collective-permute-done.3.refs_2_ = bf16[3,48,384]{2,1,0:T(8,128)(2,1)S(1)} collective-permute-done((bf16[3,48,384]{2,1,0:T(8,128)(2,1)S(1)}, bf16[3,48,384]{2,1,0:T(8,128)(2,1)S(1)}, u32[]{:S(2)}, u32[]{:S(2)}) %collective-permute-start.3) | collective-permute-done | bytes 110624 | tf_op jit(solution)/shard_map/ppermute | solution.py:208
  17.8 1.8 %collective-permute-start.5 = (bf16[3,48,384]{2,1,0:T(8,128)(2,1)S(1)}, bf16[3,48,384]{2,1,0:T(8,128)(2,1)S(1)}, u32[]{:S(2)}, u32[]{:S(2)}) collective-permute-start(bf16[3,48,384]{2,1,0:T(8,128)(2,1)S(1)} %collective-permute-done.refs_4_), channel_id=1, source_target_pairs={{0,4},{1,5},{2,6},{3,7},{4,0},{5,1},{6,2},{7,3},{8,12},{9,13},{10,... | collective-permute-start | bytes 331784 | tf_op jit(solution)/shard_map/ppermute | solution.py:208
  20.4 1.0 %collective-permute-done.6.refs_6_ = bf16[3,48,384]{2,1,0:T(8,128)(2,1)S(1)} collective-permute-done((bf16[3,48,384]{2,1,0:T(8,128)(2,1)S(1)}, bf16[3,48,384]{2,1,0:T(8,128)(2,1)S(1)}, u32[]{:S(2)}, u32[]{:S(2)}) %collective-permute-start.6) | collective-permute-done | bytes 110624 | tf_op jit(solution)/shard_map/ppermute | solution.py:208
  21.9 1.3 %collective-permute-done.5.refs_5_ = bf16[3,48,384]{2,1,0:T(8,128)(2,1)S(1)} collective-permute-done((bf16[3,48,384]{2,1,0:T(8,128)(2,1)S(1)}, bf16[3,48,384]{2,1,0:T(8,128)(2,1)S(1)}, u32[]{:S(2)}, u32[]{:S(2)}) %collective-permute-start.5) | collective-permute-done | bytes 110624 | tf_op jit(solution)/shard_map/ppermute | solution.py:208
  23.1 2.2 %collective-permute-done.4.refs_3_ = bf16[3,48,384]{2,1,0:T(8,128)(2,1)S(1)} collective-permute-done((bf16[3,48,384]{2,1,0:T(8,128)(2,1)S(1)}, bf16[3,48,384]{2,1,0:T(8,128)(2,1)S(1)}, u32[]{:S(2)}, u32[]{:S(2)}) %collective-permute-start.4) | collective-permute-done | bytes 110624 | tf_op jit(solution)/shard_map/ppermute | solution.py:208
  25.3 1.4 %collective-permute-done.7.refs_7_ = bf16[3,48,384]{2,1,0:T(8,128)(2,1)S(1)} collective-permute-done((bf16[3,48,384]{2,1,0:T(8,128)(2,1)S(1)}, bf16[3,48,384]{2,1,0:T(8,128)(2,1)S(1)}, u32[]{:S(2)}, u32[]{:S(2)}) %collective-permute-start.7) | collective-permute-done | bytes 110624 | tf_op jit(solution)/shard_map/ppermute | solution.py:208
  27.0 2.9 %shard_map.96.refs_3_ = f32[3,384,384]{2,1,0:T(8,128)S(1)} custom-call(bf16[2,192,1024]{2,1,0:T(8,128)(2,1)S(1)} %pad_maximum_fusion.refs_0_, bf16[2,192,1024]{2,1,0:T(8,128)(2,1)S(1)} %collective-permute-done.9.refs_1_, bf16[3,384,384]{2,1,0:T(8,128)(2,1)S(1)} %shard_map.95.refs_2_.refs_4_.refs_0_), custom_call_target="tpu_custom_call" | custom-call | flops 1811939328 | bytes 6684672 | tf_op jit(solution)/shard_map/pallas_call | solution.py:181
  29.9 2.5 %shard_map.97 = (bf16[2,3,48,384]{3,2,1,0:T(8,128)(2,1)S(1)}, bf16[2,3,48,384]{3,2,1,0:T(8,128)(2,1)S(1)}, bf16[2,384,1024]{2,1,0:T(8,128)(2,1)S(1)}, bf16[768,1024]{1,0:T(8,128)(2,1)S(1)}, bf16[384,1024]{1,0:T(8,128)(2,1)S(1)}) custom-call(bf16[2,192,1024]{2,1,0:T(8,128)(2,1)S(1)} %collective-permute-done.1.refs_0_, ...), custom_call_target="tpu_custom_call" | custom-call | flops 1358954496 | bytes 15433728 | tf_op jit(solution)/shard_map/pallas_call | solution.py:181
  32.4 1.2 %collective-permute-start.10 = (bf16[2,3,48,384]{3,2,1,0:T(8,128)(2,1)S(1)}, bf16[2,3,48,384]{3,2,1,0:T(8,128)(2,1)S(1)}, u32[]{:S(2)}, u32[]{:S(2)}) collective-permute-start(bf16[2,3,48,384]{3,2,1,0:T(8,128)(2,1)S(1)} %get-tuple-element.48), channel_id=1, source_target_pairs={{0,4},{1,5},{2,6},{3,7},{4,0},{5,1},{6,2},{7,3},{8,12},{9,13},{10,... | collective-permute-start | bytes 663560 | tf_op jit(solution)/shard_map/ppermute | solution.py:208
  33.9 1.4 %collective-permute-start.12 = (bf16[2,192,128]{2,1,0:T(8,128)(2,1)S(1)}, bf16[2,192,128]{2,1,0:T(8,128)(2,1)S(1)}, u32[]{:S(2)}, u32[]{:S(2)}) collective-permute-start(bf16[2,192,128]{2,1,0:T(8,128)(2,1)S(1)} %pad_maximum_fusion.2.refs_1_), channel_id=1, source_target_pairs={{0,2},{1,3},{2,0},{3,1},{4,6},{5,7},{6,4},{7,5},{8,10},{9,11},{10,... | collective-permute-start | bytes 294920 | tf_op jit(solution)/shard_map/ppermute | solution.py:208
  36.7 2.1 %collective-permute-done.12.refs_7_ = bf16[2,192,128]{2,1,0:T(8,128)(2,1)S(1)} collective-permute-done((bf16[2,192,128]{2,1,0:T(8,128)(2,1)S(1)}, bf16[2,192,128]{2,1,0:T(8,128)(2,1)S(1)}, u32[]{:S(2)}, u32[]{:S(2)}) %collective-permute-start.12) | collective-permute-done | bytes 98336 | tf_op jit(solution)/shard_map/ppermute | solution.py:208
  38.8 1.8 %collective-permute-done.10.came = bf16[2,3,48,384]{3,2,1,0:T(8,128)(2,1)S(1)} collective-permute-done((bf16[2,3,48,384]{3,2,1,0:T(8,128)(2,1)S(1)}, bf16[2,3,48,384]{3,2,1,0:T(8,128)(2,1)S(1)}, u32[]{:S(2)}, u32[]{:S(2)}) %collective-permute-start.10) | collective-permute-done | bytes 221216 | tf_op jit(solution)/shard_map/ppermute | solution.py:208
  40.7 3.8 %collective-permute-start.13 = (bf16[2,3,48,384]{3,2,1,0:T(8,128)(2,1)S(1)}, bf16[2,3,48,384]{3,2,1,0:T(8,128)(2,1)S(1)}, u32[]{:S(2)}, u32[]{:S(2)}) collective-permute-start(bf16[2,3,48,384]{3,2,1,0:T(8,128)(2,1)S(1)} %add_convert_fusion.1), channel_id=1, source_target_pairs={{0,12},{1,13},{2,14},{3,15},{4,8},{5,9},{6,10},{7,11},{8,4},{9,5},... | collective-permute-start | bytes 663560 | tf_op jit(solution)/shard_map/ppermute | solution.py:208
  45.1 10.9 %collective-permute-start.15 = (bf16[2,3,48,384]{3,2,1,0:T(8,128)(2,1)S(1)}, bf16[2,3,48,384]{3,2,1,0:T(8,128)(2,1)S(1)}, u32[]{:S(2)}, u32[]{:S(2)}) collective-permute-start(bf16[2,3,48,384]{3,2,1,0:T(8,128)(2,1)S(1)} %add_convert_fusion), channel_id=1, source_target_pairs={{0,12},{1,13},{2,14},{3,15},{4,8},{5,9},{6,10},{7,11},{8,4},{9,5},... | collective-permute-start | bytes 663560 | tf_op jit(solution)/shard_map/ppermute | solution.py:208
  56.3 1.4 %collective-permute-start.17 = (bf16[2,3,48,384]{3,2,1,0:T(8,128)(2,1)S(1)}, bf16[2,3,48,384]{3,2,1,0:T(8,128)(2,1)S(1)}, u32[]{:S(2)}, u32[]{:S(2)}) collective-permute-start(bf16[2,3,48,384]{3,2,1,0:T(8,128)(2,1)S(1)} %get-tuple-element.51.refs_1_), channel_id=1, source_target_pairs={{0,4},{1,5},{2,6},{3,7},{4,0},{5,1},{6,2},{7,3},{8,12},{9,13},{10,... | collective-permute-start | bytes 663560 | tf_op jit(solution)/shard_map/ppermute | solution.py:208
  57.7 3.6 %collective-permute-done.15.crossed = bf16[2,3,48,384]{3,2,1,0:T(8,128)(2,1)S(1)} collective-permute-done((bf16[2,3,48,384]{3,2,1,0:T(8,128)(2,1)S(1)}, bf16[2,3,48,384]{3,2,1,0:T(8,128)(2,1)S(1)}, u32[]{:S(2)}, u32[]{:S(2)}) %collective-permute-start.15) | collective-permute-done | bytes 221216 | tf_op jit(solution)/shard_map/ppermute | solution.py:208
  61.7 1.3 %collective-permute-start.22 = (bf16[2,192,128]{2,1,0:T(8,128)(2,1)S(1)}, bf16[2,192,128]{2,1,0:T(8,128)(2,1)S(1)}, u32[]{:S(2)}, u32[]{:S(2)}) collective-permute-start(bf16[2,192,128]{2,1,0:T(8,128)(2,1)S(1)} %pad_maximum_fusion.2.refs_1_), channel_id=1, source_target_pairs={{0,3},{1,2},{2,1},{3,0},{4,7},{5,6},{6,5},{7,4},{8,11},{9,10},{10,... | collective-permute-start | bytes 294920 | tf_op jit(solution)/shard_map/ppermute | solution.py:208
  63.1 1.7 %collective-permute-start.18 = (bf16[2,3,48,384]{3,2,1,0:T(8,128)(2,1)S(1)}, bf16[2,3,48,384]{3,2,1,0:T(8,128)(2,1)S(1)}, u32[]{:S(2)}, u32[]{:S(2)}) collective-permute-start(bf16[2,3,48,384]{3,2,1,0:T(8,128)(2,1)S(1)} %get-tuple-element.55.refs_2_), channel_id=1, source_target_pairs={{0,4},{1,5},{2,6},{3,7},{4,0},{5,1},{6,2},{7,3},{8,12},{9,13},{10,... | collective-permute-start | bytes 663560 | tf_op jit(solution)/shard_map/ppermute | solution.py:208
  64.8 1.1 %collective-permute-start.19 = (f32[2,24,96]{2,1,0:T(8,128)S(1)}, f32[2,24,96]{2,1,0:T(8,128)S(1)}, u32[]{:S(2)}, u32[]{:S(2)}) collective-permute-start(f32[2,24,96]{2,1,0:T(8,128)S(1)} %fusion.1.here), channel_id=1, source_target_pairs={{0,2},{1,3},{2,0},{3,1},{4,6},{5,7},{6,4},{7,5},{8,10},{9,11},{10,... | collective-permute-start | bytes 55304 | tf_op jit(solution)/shard_map/ppermute | solution.py:208
  66.0 2.4 %collective-permute-start.21 = (f32[2,24,96]{2,1,0:T(8,128)S(1)}, f32[2,24,96]{2,1,0:T(8,128)S(1)}, u32[]{:S(2)}, u32[]{:S(2)}) collective-permute-start(f32[2,24,96]{2,1,0:T(8,128)S(1)} %fusion.1.here), channel_id=1, source_target_pairs={{0,6},{1,7},{2,4},{3,5},{4,2},{5,3},{6,0},{7,1},{8,14},{9,15},{10,... | collective-permute-start | bytes 55304 | tf_op jit(solution)/shard_map/ppermute | solution.py:208
  68.7 2.5 %collective-permute-done.20.here = f32[2,24,96]{2,1,0:T(8,128)S(1)} collective-permute-done((f32[2,24,96]{2,1,0:T(8,128)S(1)}, f32[2,24,96]{2,1,0:T(8,128)S(1)}, u32[]{:S(2)}, u32[]{:S(2)}) %collective-permute-start.20) | collective-permute-done | bytes 18464 | tf_op jit(solution)/shard_map/ppermute | solution.py:208
  72.0 1.5 %shard_map.103 = (bf16[3,384,384]{2,1,0:T(8,128)(2,1)S(1)}, f32[2,192,128]{2,1,0:T(8,128)S(1)}, bf16[2,192,128]{2,1,0:T(8,128)(2,1)S(1)}) custom-call(bf16[3,384,384]{2,1,0:T(8,128)(2,1)S(1)} %shard_map.95.refs_2_.refs_4_.refs_0_, bf16[2,3,48,384]{3,2,1,0:T(8,128)(2,1)S(1)} %get-tuple-element.51.refs_1_, ...), custom_call_target="tpu_custom_call" | custom-call | flops 226492416 | bytes 6119424 | tf_op jit(solution)/shard_map/pallas_call | solution.py:181
  73.6 1.3 %collective-permute-done.23 = bf16[2,192,128]{2,1,0:T(8,128)(2,1)S(1)} collective-permute-done((bf16[2,192,128]{2,1,0:T(8,128)(2,1)S(1)}, bf16[2,192,128]{2,1,0:T(8,128)(2,1)S(1)}, u32[]{:S(2)}, u32[]{:S(2)}) %collective-permute-start.23) | collective-permute-done | bytes 98336 | tf_op jit(solution)/shard_map/ppermute | solution.py:208
  74.9 1.1 %collective-permute-start.25 = (bf16[2,192,128]{2,1,0:T(8,128)(2,1)S(1)}, bf16[2,192,128]{2,1,0:T(8,128)(2,1)S(1)}, u32[]{:S(2)}, u32[]{:S(2)}) collective-permute-start(bf16[2,192,128]{2,1,0:T(8,128)(2,1)S(1)} %add_convert_fusion.2), channel_id=1, source_target_pairs={{0,2},{1,3},{2,0},{3,1},{4,6},{5,7},{6,4},{7,5},{8,10},{9,11},{10,... | collective-permute-start | bytes 294920 | tf_op jit(solution)/shard_map/ppermute | solution.py:208
  76.8 3.0 %collective-permute-done.25.pair = bf16[2,192,128]{2,1,0:T(8,128)(2,1)S(1)} collective-permute-done((bf16[2,192,128]{2,1,0:T(8,128)(2,1)S(1)}, bf16[2,192,128]{2,1,0:T(8,128)(2,1)S(1)}, u32[]{:S(2)}, u32[]{:S(2)}) %collective-permute-start.25) | collective-permute-done | bytes 98336 | tf_op jit(solution)/shard_map/ppermute | solution.py:208
  (47 shorter events, 7.6 us)
Async XLA Ops:
  0.6 5.2 %copy-start = (bf16[1024,192]{0,1:T(8,128)(2,1)S(1)}, bf16[1024,192]{0,1:T(8,128)(2,1)}, u32[]{:S(2)}) copy-start(bf16[1024,192]{0,1:T(8,128)(2,1)} %param.8) | copy-start | bytes 1179652
  1.7 6.1 %collective-permute-start = (bf16[3,48,384]{2,1,0:T(8,128)(2,1)S(1)}, bf16[3,48,384]{2,1,0:T(8,128)(2,1)S(1)}, u32[]{:S(2)}, u32[]{:S(2)}) collective-permute-start(bf16[3,48,384]{2,1,0:T(8,128)(2,1)S(1)} %get-tuple-element.73), channel_id=1, source_target_pairs={{0,2},{1,3},{2,0},{3,1},{4,6},{5,7},{6,4},{7,5},{8,10},{9,11},{10,... | collective-permute-start | bytes 331784 | tf_op jit(solution)/shard_map/ppermute | solution.py:208
  5.8 21.1 %copy-start.1 = (bf16[128,192]{0,1:T(8,128)(2,1)S(1)}, bf16[128,192]{0,1:T(8,128)(2,1)}, u32[]{:S(2)}) copy-start(bf16[128,192]{0,1:T(8,128)(2,1)} %param.15) | copy-start | bytes 147460
  5.8 21.1 %copy-start.2 = (bf16[128,192]{0,1:T(8,128)(2,1)S(1)}, bf16[128,192]{0,1:T(8,128)(2,1)}, u32[]{:S(2)}) copy-start(bf16[128,192]{0,1:T(8,128)(2,1)} %param.14) | copy-start | bytes 147460
  7.8 19.0 %collective-permute-start.1 = (bf16[2,192,1024]{2,1,0:T(8,128)(2,1)S(1)}, bf16[2,192,1024]{2,1,0:T(8,128)(2,1)S(1)}, u32[]{:S(2)}, u32[]{:S(2)}) collective-permute-start(bf16[2,192,1024]{2,1,0:T(8,128)(2,1)S(1)} %pad_maximum_fusion.refs_0_), channel_id=1, source_target_pairs={{0,2},{1,3},{2,0},{3,1},{4,6},{5,7},{6,4},{7,5},{8,10},{9,11},{10,... | collective-permute-start | bytes 2359304 | tf_op jit(solution)/shard_map/ppermute | solution.py:208
  9.5 8.3 %collective-permute-start.3 = (bf16[3,48,384]{2,1,0:T(8,128)(2,1)S(1)}, bf16[3,48,384]{2,1,0:T(8,128)(2,1)S(1)}, u32[]{:S(2)}, u32[]{:S(2)}) collective-permute-start(bf16[3,48,384]{2,1,0:T(8,128)(2,1)S(1)} %get-tuple-element.72.refs_0_), channel_id=1, source_target_pairs={{0,8},{1,9},{2,10},{3,11},{4,12},{5,13},{6,14},{7,15},{8,0},{9,1},... | collective-permute-start | bytes 331784 | tf_op jit(solution)/shard_map/ppermute | solution.py:208
  12.1 7.5 %collective-permute-start.2 = (bf16[3,48,384]{2,1,0:T(8,128)(2,1)S(1)}, bf16[3,48,384]{2,1,0:T(8,128)(2,1)S(1)}, u32[]{:S(2)}, u32[]{:S(2)}) collective-permute-start(bf16[3,48,384]{2,1,0:T(8,128)(2,1)S(1)} %get-tuple-element.72.refs_0_), channel_id=1, source_target_pairs={{0,4},{1,5},{2,6},{3,7},{4,0},{5,1},{6,2},{7,3},{8,12},{9,13},{10,... | collective-permute-start | bytes 331784 | tf_op jit(solution)/shard_map/ppermute | solution.py:208
  13.7 7.7 %collective-permute-start.6 = (bf16[3,48,384]{2,1,0:T(8,128)(2,1)S(1)}, bf16[3,48,384]{2,1,0:T(8,128)(2,1)S(1)}, u32[]{:S(2)}, u32[]{:S(2)}) collective-permute-start(bf16[3,48,384]{2,1,0:T(8,128)(2,1)S(1)} %collective-permute-done.refs_4_), channel_id=1, source_target_pairs={{0,8},{1,9},{2,10},{3,11},{4,12},{5,13},{6,14},{7,15},{8,0},{9,1},... | collective-permute-start | bytes 331784 | tf_op jit(solution)/shard_map/ppermute | solution.py:208
  14.0 12.9 %collective-permute-start.9 = (bf16[2,192,1024]{2,1,0:T(8,128)(2,1)S(1)}, bf16[2,192,1024]{2,1,0:T(8,128)(2,1)S(1)}, u32[]{:S(2)}, u32[]{:S(2)}) collective-permute-start(bf16[2,192,1024]{2,1,0:T(8,128)(2,1)S(1)} %pad_maximum_fusion.refs_0_), channel_id=1, source_target_pairs={{0,1},{1,0},{2,3},{3,2},{4,5},{5,4},{6,7},{7,6},{8,9},{9,8},{10,11... | collective-permute-start | bytes 2359304 | tf_op jit(solution)/shard_map/ppermute | solution.py:208
  17.8 5.3 %collective-permute-start.5 = (bf16[3,48,384]{2,1,0:T(8,128)(2,1)S(1)}, bf16[3,48,384]{2,1,0:T(8,128)(2,1)S(1)}, u32[]{:S(2)}, u32[]{:S(2)}) collective-permute-start(bf16[3,48,384]{2,1,0:T(8,128)(2,1)S(1)} %collective-permute-done.refs_4_), channel_id=1, source_target_pairs={{0,4},{1,5},{2,6},{3,7},{4,0},{5,1},{6,2},{7,3},{8,12},{9,13},{10,... | collective-permute-start | bytes 331784 | tf_op jit(solution)/shard_map/ppermute | solution.py:208
  19.6 5.7 %collective-permute-start.4 = (bf16[3,48,384]{2,1,0:T(8,128)(2,1)S(1)}, bf16[3,48,384]{2,1,0:T(8,128)(2,1)S(1)}, u32[]{:S(2)}, u32[]{:S(2)}) collective-permute-start(bf16[3,48,384]{2,1,0:T(8,128)(2,1)S(1)} %collective-permute-done.3.refs_2_), channel_id=1, source_target_pairs={{0,4},{1,5},{2,6},{3,7},{4,0},{5,1},{6,2},{7,3},{8,12},{9,13},{10,... | collective-permute-start | bytes 331784 | tf_op jit(solution)/shard_map/ppermute | solution.py:208
  21.4 5.4 %collective-permute-start.7 = (bf16[3,48,384]{2,1,0:T(8,128)(2,1)S(1)}, bf16[3,48,384]{2,1,0:T(8,128)(2,1)S(1)}, u32[]{:S(2)}, u32[]{:S(2)}) collective-permute-start(bf16[3,48,384]{2,1,0:T(8,128)(2,1)S(1)} %collective-permute-done.6.refs_6_), channel_id=1, source_target_pairs={{0,4},{1,5},{2,6},{3,7},{4,0},{5,1},{6,2},{7,3},{8,12},{9,13},{10,... | collective-permute-start | bytes 331784 | tf_op jit(solution)/shard_map/ppermute | solution.py:208
  26.9 3.0 %collective-permute-start.8 = (bf16[2,192,1024]{2,1,0:T(8,128)(2,1)S(1)}, bf16[2,192,1024]{2,1,0:T(8,128)(2,1)S(1)}, u32[]{:S(2)}, u32[]{:S(2)}) collective-permute-start(bf16[2,192,1024]{2,1,0:T(8,128)(2,1)S(1)} %collective-permute-done.1.refs_0_), channel_id=1, source_target_pairs={{0,1},{1,0},{2,3},{3,2},{4,5},{5,4},{6,7},{7,6},{8,9},{9,8},{10,11... | collective-permute-start | bytes 2359304 | tf_op jit(solution)/shard_map/ppermute | solution.py:208
  32.4 8.3 %collective-permute-start.10 = (bf16[2,3,48,384]{3,2,1,0:T(8,128)(2,1)S(1)}, bf16[2,3,48,384]{3,2,1,0:T(8,128)(2,1)S(1)}, u32[]{:S(2)}, u32[]{:S(2)}) collective-permute-start(bf16[2,3,48,384]{3,2,1,0:T(8,128)(2,1)S(1)} %get-tuple-element.48), channel_id=1, source_target_pairs={{0,4},{1,5},{2,6},{3,7},{4,0},{5,1},{6,2},{7,3},{8,12},{9,13},{10,... | collective-permute-start | bytes 663560 | tf_op jit(solution)/shard_map/ppermute | solution.py:208
  33.6 3.1 %collective-permute-start.11 = (bf16[2,192,128]{2,1,0:T(8,128)(2,1)S(1)}, bf16[2,192,128]{2,1,0:T(8,128)(2,1)S(1)}, u32[]{:S(2)}, u32[]{:S(2)}) collective-permute-start(bf16[2,192,128]{2,1,0:T(8,128)(2,1)S(1)} %pad_maximum_fusion.2.refs_1_), channel_id=1, source_target_pairs={{0,1},{1,0},{2,3},{3,2},{4,5},{5,4},{6,7},{7,6},{8,9},{9,8},{10,11... | collective-permute-start | bytes 294920 | tf_op jit(solution)/shard_map/ppermute | solution.py:208
  33.9 5.0 %collective-permute-start.12 = (bf16[2,192,128]{2,1,0:T(8,128)(2,1)S(1)}, bf16[2,192,128]{2,1,0:T(8,128)(2,1)S(1)}, u32[]{:S(2)}, u32[]{:S(2)}) collective-permute-start(bf16[2,192,128]{2,1,0:T(8,128)(2,1)S(1)} %pad_maximum_fusion.2.refs_1_), channel_id=1, source_target_pairs={{0,2},{1,3},{2,0},{3,1},{4,6},{5,7},{6,4},{7,5},{8,10},{9,11},{10,... | collective-permute-start | bytes 294920 | tf_op jit(solution)/shard_map/ppermute | solution.py:208
  35.3 9.7 %collective-permute-start.14 = (bf16[2,3,48,384]{3,2,1,0:T(8,128)(2,1)S(1)}, bf16[2,3,48,384]{3,2,1,0:T(8,128)(2,1)S(1)}, u32[]{:S(2)}, u32[]{:S(2)}) collective-permute-start(bf16[2,3,48,384]{3,2,1,0:T(8,128)(2,1)S(1)} %get-tuple-element.54), channel_id=1, source_target_pairs={{0,4},{1,5},{2,6},{3,7},{4,0},{5,1},{6,2},{7,3},{8,12},{9,13},{10,... | collective-permute-start | bytes 663560 | tf_op jit(solution)/shard_map/ppermute | solution.py:208
  40.7 15.3 %collective-permute-start.13 = (bf16[2,3,48,384]{3,2,1,0:T(8,128)(2,1)S(1)}, bf16[2,3,48,384]{3,2,1,0:T(8,128)(2,1)S(1)}, u32[]{:S(2)}, u32[]{:S(2)}) collective-permute-start(bf16[2,3,48,384]{3,2,1,0:T(8,128)(2,1)S(1)} %add_convert_fusion.1), channel_id=1, source_target_pairs={{0,12},{1,13},{2,14},{3,15},{4,8},{5,9},{6,10},{7,11},{8,4},{9,5},... | collective-permute-start | bytes 663560 | tf_op jit(solution)/shard_map/ppermute | solution.py:208
  45.1 16.3 %collective-permute-start.15 = (bf16[2,3,48,384]{3,2,1,0:T(8,128)(2,1)S(1)}, bf16[2,3,48,384]{3,2,1,0:T(8,128)(2,1)S(1)}, u32[]{:S(2)}, u32[]{:S(2)}) collective-permute-start(bf16[2,3,48,384]{3,2,1,0:T(8,128)(2,1)S(1)} %add_convert_fusion), channel_id=1, source_target_pairs={{0,12},{1,13},{2,14},{3,15},{4,8},{5,9},{6,10},{7,11},{8,4},{9,5},... | collective-permute-start | bytes 663560 | tf_op jit(solution)/shard_map/ppermute | solution.py:208
  56.3 8.5 %collective-permute-start.17 = (bf16[2,3,48,384]{3,2,1,0:T(8,128)(2,1)S(1)}, bf16[2,3,48,384]{3,2,1,0:T(8,128)(2,1)S(1)}, u32[]{:S(2)}, u32[]{:S(2)}) collective-permute-start(bf16[2,3,48,384]{3,2,1,0:T(8,128)(2,1)S(1)} %get-tuple-element.51.refs_1_), channel_id=1, source_target_pairs={{0,4},{1,5},{2,6},{3,7},{4,0},{5,1},{6,2},{7,3},{8,12},{9,13},{10,... | collective-permute-start | bytes 663560 | tf_op jit(solution)/shard_map/ppermute | solution.py:208
  61.7 3.1 %collective-permute-start.16 = (f32[2,24,96]{2,1,0:T(8,128)S(1)}, f32[2,24,96]{2,1,0:T(8,128)S(1)}, u32[]{:S(2)}, u32[]{:S(2)}) collective-permute-start(f32[2,24,96]{2,1,0:T(8,128)S(1)} %pad_maximum_fusion.3), channel_id=1, source_target_pairs={{0,1},{1,0},{2,3},{3,2},{4,5},{5,4},{6,7},{7,6},{8,9},{9,8},{10,11... | collective-permute-start | bytes 55304 | tf_op jit(solution)/shard_map/ppermute | solution.py:208
  61.7 10.3 %collective-permute-start.22 = (bf16[2,192,128]{2,1,0:T(8,128)(2,1)S(1)}, bf16[2,192,128]{2,1,0:T(8,128)(2,1)S(1)}, u32[]{:S(2)}, u32[]{:S(2)}) collective-permute-start(bf16[2,192,128]{2,1,0:T(8,128)(2,1)S(1)} %pad_maximum_fusion.2.refs_1_), channel_id=1, source_target_pairs={{0,3},{1,2},{2,1},{3,0},{4,7},{5,6},{6,5},{7,4},{8,11},{9,10},{10,... | collective-permute-start | bytes 294920 | tf_op jit(solution)/shard_map/ppermute | solution.py:208
  63.1 8.9 %collective-permute-start.18 = (bf16[2,3,48,384]{3,2,1,0:T(8,128)(2,1)S(1)}, bf16[2,3,48,384]{3,2,1,0:T(8,128)(2,1)S(1)}, u32[]{:S(2)}, u32[]{:S(2)}) collective-permute-start(bf16[2,3,48,384]{3,2,1,0:T(8,128)(2,1)S(1)} %get-tuple-element.55.refs_2_), channel_id=1, source_target_pairs={{0,4},{1,5},{2,6},{3,7},{4,0},{5,1},{6,2},{7,3},{8,12},{9,13},{10,... | collective-permute-start | bytes 663560 | tf_op jit(solution)/shard_map/ppermute | solution.py:208
  64.8 3.9 %collective-permute-start.19 = (f32[2,24,96]{2,1,0:T(8,128)S(1)}, f32[2,24,96]{2,1,0:T(8,128)S(1)}, u32[]{:S(2)}, u32[]{:S(2)}) collective-permute-start(f32[2,24,96]{2,1,0:T(8,128)S(1)} %fusion.1.here), channel_id=1, source_target_pairs={{0,2},{1,3},{2,0},{3,1},{4,6},{5,7},{6,4},{7,5},{8,10},{9,11},{10,... | collective-permute-start | bytes 55304 | tf_op jit(solution)/shard_map/ppermute | solution.py:208
  65.9 5.4 %collective-permute-start.20 = (f32[2,24,96]{2,1,0:T(8,128)S(1)}, f32[2,24,96]{2,1,0:T(8,128)S(1)}, u32[]{:S(2)}, u32[]{:S(2)}) collective-permute-start(f32[2,24,96]{2,1,0:T(8,128)S(1)} %fusion.1.here), channel_id=1, source_target_pairs={{0,4},{1,5},{2,6},{3,7},{4,0},{5,1},{6,2},{7,3},{8,12},{9,13},{10,... | collective-permute-start | bytes 55304 | tf_op jit(solution)/shard_map/ppermute | solution.py:208
  66.0 6.0 %collective-permute-start.21 = (f32[2,24,96]{2,1,0:T(8,128)S(1)}, f32[2,24,96]{2,1,0:T(8,128)S(1)}, u32[]{:S(2)}, u32[]{:S(2)}) collective-permute-start(f32[2,24,96]{2,1,0:T(8,128)S(1)} %fusion.1.here), channel_id=1, source_target_pairs={{0,6},{1,7},{2,4},{3,5},{4,2},{5,3},{6,0},{7,1},{8,14},{9,15},{10,... | collective-permute-start | bytes 55304 | tf_op jit(solution)/shard_map/ppermute | solution.py:208
  73.5 1.4 %collective-permute-start.23 = (bf16[2,192,128]{2,1,0:T(8,128)(2,1)S(1)}, bf16[2,192,128]{2,1,0:T(8,128)(2,1)S(1)}, u32[]{:S(2)}, u32[]{:S(2)}) collective-permute-start(bf16[2,192,128]{2,1,0:T(8,128)(2,1)S(1)} %get-tuple-element.62), channel_id=1, source_target_pairs={{0,1},{1,0},{2,3},{3,2},{4,5},{5,4},{6,7},{7,6},{8,9},{9,8},{10,11... | collective-permute-start | bytes 294920 | tf_op jit(solution)/shard_map/ppermute | solution.py:208
  74.9 4.9 %collective-permute-start.25 = (bf16[2,192,128]{2,1,0:T(8,128)(2,1)S(1)}, bf16[2,192,128]{2,1,0:T(8,128)(2,1)S(1)}, u32[]{:S(2)}, u32[]{:S(2)}) collective-permute-start(bf16[2,192,128]{2,1,0:T(8,128)(2,1)S(1)} %add_convert_fusion.2), channel_id=1, source_target_pairs={{0,2},{1,3},{2,0},{3,1},{4,6},{5,7},{6,4},{7,5},{8,10},{9,11},{10,... | collective-permute-start | bytes 294920 | tf_op jit(solution)/shard_map/ppermute | solution.py:208
  76.7 3.1 %collective-permute-start.24 = (bf16[2,192,128]{2,1,0:T(8,128)(2,1)S(1)}, bf16[2,192,128]{2,1,0:T(8,128)(2,1)S(1)}, u32[]{:S(2)}, u32[]{:S(2)}) collective-permute-start(bf16[2,192,128]{2,1,0:T(8,128)(2,1)S(1)} %get-tuple-element.67), channel_id=1, source_target_pairs={{0,1},{1,0},{2,3},{3,2},{4,5},{5,4},{6,7},{7,6},{8,9},{9,8},{10,11... | collective-permute-start | bytes 294920 | tf_op jit(solution)/shard_map/ppermute | solution.py:208

commit v11 on v10

--- a/solution.py
+++ b/solution.py
@@ -20,9 +20,9 @@
 
 
 def gated(gate, up):
-    sigma = jax.nn.sigmoid(gate)
+    sigma = 0.5 * jnp.tanh(0.5 * gate) + 0.5
     silu = gate * sigma
-    slope = sigma * (1.0 + gate * (1.0 - sigma))
+    slope = sigma + silu * (1.0 - sigma)
     return silu, slope * up, silu * up
 
 

time: 80.6 us -> 80.5 us (level)
  no operation moved by 1% of the time
where the time goes in v11:
time: 80.5 us; the launch traced here: 80.3 us
  starting transfers between devices  40 us (50%)
  waiting for transfers between devices  27.2 us (34%)
  Pallas kernels  9.81 us (12%)
  other arithmetic  2.33 us (3%)
  between operations  0.9 us (1%)
    ppermute x26, starting transfers between devices, swap(): return lax.ppermute(array, ('tok', 'hid'), pairs)  40 us
    ppermute x26, waiting for transfers between devices, swap(): return lax.ppermute(array, ('tok', 'hid'), pairs)  27.2 us
    pallas_call x11, Pallas kernels, call(): pl.pallas_call(body, out_shape=list(outs), in_specs=specs, out_specs=[pl....  9.81 us
  transfers between devices with their start and end apart: 26, of which 15 were waited for; matrix products, arithmetic and copies ran while one was open for 2% of the time, Pallas kernels for 7%

profile of v11, /device:TPU:0, one launch (start us, length us, event | category | flops | bytes accessed | tf_op | source)
XLA Modules:
  0.0 80.3 jit_solution(7694047827062095829)
XLA Ops:
  0.7 1.0 %pad_maximum_fusion.1 = bf16[3,48,768]{2,1,0:T(8,128)(2,1)S(1)} fusion(bf16[1,48,768]{2,1,0:T(8,128)(2,1)} %bitcast.25, bf16[1,48,768]{2,1,0:T(8,128)(2,1)} %bitcast.26, bf16[1,48,768]{2,1,0:T(8,128)(2,1)} %bitcast.27), kind=kLoop, calls=%fused_computation.5 | loop fusion | flops 221184 | bytes 442368 | tf_op jit(solution)/shard_map/stack | solution.py:214
  1.7 3.0 %collective-permute-start = (bf16[3,48,384]{2,1,0:T(8,128)(2,1)S(1)}, bf16[3,48,384]{2,1,0:T(8,128)(2,1)S(1)}, u32[]{:S(2)}, u32[]{:S(2)}) collective-permute-start(bf16[3,48,384]{2,1,0:T(8,128)(2,1)S(1)} %get-tuple-element.73), channel_id=1, source_target_pairs={{0,2},{1,3},{2,0},{3,1},{4,6},{5,7},{6,4},{7,5},{8,10},{9,11},{10,... | collective-permute-start | bytes 331784 | tf_op jit(solution)/shard_map/ppermute | solution.py:208
  4.7 1.1 %fusion = bf16[1,192,1024]{2,1,0:T(8,128)(2,1)S(1)} fusion(bf16[1024,192]{0,1:T(8,128)(2,1)} %param.9, f32[1024]{0:T(1024)} %param.10), kind=kLoop, calls=%fused_computation.4 | loop fusion | flops 589824 | bytes 790528 | tf_op jit(solution)/shard_map/stack | solution.py:219
  5.9 1.9 %collective-permute-done.refs_4_ = bf16[3,48,384]{2,1,0:T(8,128)(2,1)S(1)} collective-permute-done((bf16[3,48,384]{2,1,0:T(8,128)(2,1)S(1)}, bf16[3,48,384]{2,1,0:T(8,128)(2,1)S(1)}, u32[]{:S(2)}, u32[]{:S(2)}) %collective-permute-start) | collective-permute-done | bytes 110624 | tf_op jit(solution)/shard_map/ppermute | solution.py:208
  7.8 1.7 %collective-permute-start.1 = (bf16[2,192,1024]{2,1,0:T(8,128)(2,1)S(1)}, bf16[2,192,1024]{2,1,0:T(8,128)(2,1)S(1)}, u32[]{:S(2)}, u32[]{:S(2)}) collective-permute-start(bf16[2,192,1024]{2,1,0:T(8,128)(2,1)S(1)} %pad_maximum_fusion.refs_0_), channel_id=1, source_target_pairs={{0,2},{1,3},{2,0},{3,1},{4,6},{5,7},{6,4},{7,5},{8,10},{9,11},{10,... | collective-permute-start | bytes 2359304 | tf_op jit(solution)/shard_map/ppermute | solution.py:208
  9.5 2.6 %collective-permute-start.3 = (bf16[3,48,384]{2,1,0:T(8,128)(2,1)S(1)}, bf16[3,48,384]{2,1,0:T(8,128)(2,1)S(1)}, u32[]{:S(2)}, u32[]{:S(2)}) collective-permute-start(bf16[3,48,384]{2,1,0:T(8,128)(2,1)S(1)} %get-tuple-element.72.refs_0_), channel_id=1, source_target_pairs={{0,8},{1,9},{2,10},{3,11},{4,12},{5,13},{6,14},{7,15},{8,0},{9,1},... | collective-permute-start | bytes 331784 | tf_op jit(solution)/shard_map/ppermute | solution.py:208
  12.1 1.6 %collective-permute-start.2 = (bf16[3,48,384]{2,1,0:T(8,128)(2,1)S(1)}, bf16[3,48,384]{2,1,0:T(8,128)(2,1)S(1)}, u32[]{:S(2)}, u32[]{:S(2)}) collective-permute-start(bf16[3,48,384]{2,1,0:T(8,128)(2,1)S(1)} %get-tuple-element.72.refs_0_), channel_id=1, source_target_pairs={{0,4},{1,5},{2,6},{3,7},{4,0},{5,1},{6,2},{7,3},{8,12},{9,13},{10,... | collective-permute-start | bytes 331784 | tf_op jit(solution)/shard_map/ppermute | solution.py:208
  14.0 3.8 %collective-permute-done.3.refs_2_ = bf16[3,48,384]{2,1,0:T(8,128)(2,1)S(1)} collective-permute-done((bf16[3,48,384]{2,1,0:T(8,128)(2,1)S(1)}, bf16[3,48,384]{2,1,0:T(8,128)(2,1)S(1)}, u32[]{:S(2)}, u32[]{:S(2)}) %collective-permute-start.3) | collective-permute-done | bytes 110624 | tf_op jit(solution)/shard_map/ppermute | solution.py:208
  17.8 1.8 %collective-permute-start.5 = (bf16[3,48,384]{2,1,0:T(8,128)(2,1)S(1)}, bf16[3,48,384]{2,1,0:T(8,128)(2,1)S(1)}, u32[]{:S(2)}, u32[]{:S(2)}) collective-permute-start(bf16[3,48,384]{2,1,0:T(8,128)(2,1)S(1)} %collective-permute-done.refs_4_), channel_id=1, source_target_pairs={{0,4},{1,5},{2,6},{3,7},{4,0},{5,1},{6,2},{7,3},{8,12},{9,13},{10,... | collective-permute-start | bytes 331784 | tf_op jit(solution)/shard_map/ppermute | solution.py:208
  20.4 1.0 %collective-permute-done.6.refs_6_ = bf16[3,48,384]{2,1,0:T(8,128)(2,1)S(1)} collective-permute-done((bf16[3,48,384]{2,1,0:T(8,128)(2,1)S(1)}, bf16[3,48,384]{2,1,0:T(8,128)(2,1)S(1)}, u32[]{:S(2)}, u32[]{:S(2)}) %collective-permute-start.6) | collective-permute-done | bytes 110624 | tf_op jit(solution)/shard_map/ppermute | solution.py:208
  21.9 1.3 %collective-permute-done.5.refs_5_ = bf16[3,48,384]{2,1,0:T(8,128)(2,1)S(1)} collective-permute-done((bf16[3,48,384]{2,1,0:T(8,128)(2,1)S(1)}, bf16[3,48,384]{2,1,0:T(8,128)(2,1)S(1)}, u32[]{:S(2)}, u32[]{:S(2)}) %collective-permute-start.5) | collective-permute-done | bytes 110624 | tf_op jit(solution)/shard_map/ppermute | solution.py:208
  23.1 2.2 %collective-permute-done.4.refs_3_ = bf16[3,48,384]{2,1,0:T(8,128)(2,1)S(1)} collective-permute-done((bf16[3,48,384]{2,1,0:T(8,128)(2,1)S(1)}, bf16[3,48,384]{2,1,0:T(8,128)(2,1)S(1)}, u32[]{:S(2)}, u32[]{:S(2)}) %collective-permute-start.4) | collective-permute-done | bytes 110624 | tf_op jit(solution)/shard_map/ppermute | solution.py:208
  25.3 1.4 %collective-permute-done.7.refs_7_ = bf16[3,48,384]{2,1,0:T(8,128)(2,1)S(1)} collective-permute-done((bf16[3,48,384]{2,1,0:T(8,128)(2,1)S(1)}, bf16[3,48,384]{2,1,0:T(8,128)(2,1)S(1)}, u32[]{:S(2)}, u32[]{:S(2)}) %collective-permute-start.7) | collective-permute-done | bytes 110624 | tf_op jit(solution)/shard_map/ppermute | solution.py:208
  27.0 2.8 %shard_map.96.refs_3_ = f32[3,384,384]{2,1,0:T(8,128)S(1)} custom-call(bf16[2,192,1024]{2,1,0:T(8,128)(2,1)S(1)} %pad_maximum_fusion.refs_0_, bf16[2,192,1024]{2,1,0:T(8,128)(2,1)S(1)} %collective-permute-done.9.refs_1_, bf16[3,384,384]{2,1,0:T(8,128)(2,1)S(1)} %shard_map.95.refs_2_.refs_4_.refs_0_), custom_call_target="tpu_custom_call" | custom-call | flops 1811939328 | bytes 6684672 | tf_op jit(solution)/shard_map/pallas_call | solution.py:181
  29.8 2.4 %shard_map.97 = (bf16[2,3,48,384]{3,2,1,0:T(8,128)(2,1)S(1)}, bf16[2,3,48,384]{3,2,1,0:T(8,128)(2,1)S(1)}, bf16[2,384,1024]{2,1,0:T(8,128)(2,1)S(1)}, bf16[768,1024]{1,0:T(8,128)(2,1)S(1)}, bf16[384,1024]{1,0:T(8,128)(2,1)S(1)}) custom-call(bf16[2,192,1024]{2,1,0:T(8,128)(2,1)S(1)} %collective-permute-done.1.refs_0_, ...), custom_call_target="tpu_custom_call" | custom-call | flops 1358954496 | bytes 15433728 | tf_op jit(solution)/shard_map/pallas_call | solution.py:181
  32.3 1.2 %collective-permute-start.10 = (bf16[2,3,48,384]{3,2,1,0:T(8,128)(2,1)S(1)}, bf16[2,3,48,384]{3,2,1,0:T(8,128)(2,1)S(1)}, u32[]{:S(2)}, u32[]{:S(2)}) collective-permute-start(bf16[2,3,48,384]{3,2,1,0:T(8,128)(2,1)S(1)} %get-tuple-element.48), channel_id=1, source_target_pairs={{0,4},{1,5},{2,6},{3,7},{4,0},{5,1},{6,2},{7,3},{8,12},{9,13},{10,... | collective-permute-start | bytes 663560 | tf_op jit(solution)/shard_map/ppermute | solution.py:208
  33.7 1.4 %collective-permute-start.12 = (bf16[2,192,128]{2,1,0:T(8,128)(2,1)S(1)}, bf16[2,192,128]{2,1,0:T(8,128)(2,1)S(1)}, u32[]{:S(2)}, u32[]{:S(2)}) collective-permute-start(bf16[2,192,128]{2,1,0:T(8,128)(2,1)S(1)} %pad_maximum_fusion.2.refs_1_), channel_id=1, source_target_pairs={{0,2},{1,3},{2,0},{3,1},{4,6},{5,7},{6,4},{7,5},{8,10},{9,11},{10,... | collective-permute-start | bytes 294920 | tf_op jit(solution)/shard_map/ppermute | solution.py:208
  36.6 2.1 %collective-permute-done.12.refs_7_ = bf16[2,192,128]{2,1,0:T(8,128)(2,1)S(1)} collective-permute-done((bf16[2,192,128]{2,1,0:T(8,128)(2,1)S(1)}, bf16[2,192,128]{2,1,0:T(8,128)(2,1)S(1)}, u32[]{:S(2)}, u32[]{:S(2)}) %collective-permute-start.12) | collective-permute-done | bytes 98336 | tf_op jit(solution)/shard_map/ppermute | solution.py:208
  38.7 1.8 %collective-permute-done.10.came = bf16[2,3,48,384]{3,2,1,0:T(8,128)(2,1)S(1)} collective-permute-done((bf16[2,3,48,384]{3,2,1,0:T(8,128)(2,1)S(1)}, bf16[2,3,48,384]{3,2,1,0:T(8,128)(2,1)S(1)}, u32[]{:S(2)}, u32[]{:S(2)}) %collective-permute-start.10) | collective-permute-done | bytes 221216 | tf_op jit(solution)/shard_map/ppermute | solution.py:208
  40.6 3.8 %collective-permute-start.13 = (bf16[2,3,48,384]{3,2,1,0:T(8,128)(2,1)S(1)}, bf16[2,3,48,384]{3,2,1,0:T(8,128)(2,1)S(1)}, u32[]{:S(2)}, u32[]{:S(2)}) collective-permute-start(bf16[2,3,48,384]{3,2,1,0:T(8,128)(2,1)S(1)} %add_convert_fusion.1), channel_id=1, source_target_pairs={{0,12},{1,13},{2,14},{3,15},{4,8},{5,9},{6,10},{7,11},{8,4},{9,5},... | collective-permute-start | bytes 663560 | tf_op jit(solution)/shard_map/ppermute | solution.py:208
  45.0 10.9 %collective-permute-start.15 = (bf16[2,3,48,384]{3,2,1,0:T(8,128)(2,1)S(1)}, bf16[2,3,48,384]{3,2,1,0:T(8,128)(2,1)S(1)}, u32[]{:S(2)}, u32[]{:S(2)}) collective-permute-start(bf16[2,3,48,384]{3,2,1,0:T(8,128)(2,1)S(1)} %add_convert_fusion), channel_id=1, source_target_pairs={{0,12},{1,13},{2,14},{3,15},{4,8},{5,9},{6,10},{7,11},{8,4},{9,5},... | collective-permute-start | bytes 663560 | tf_op jit(solution)/shard_map/ppermute | solution.py:208
  56.2 1.4 %collective-permute-start.17 = (bf16[2,3,48,384]{3,2,1,0:T(8,128)(2,1)S(1)}, bf16[2,3,48,384]{3,2,1,0:T(8,128)(2,1)S(1)}, u32[]{:S(2)}, u32[]{:S(2)}) collective-permute-start(bf16[2,3,48,384]{3,2,1,0:T(8,128)(2,1)S(1)} %get-tuple-element.51.refs_1_), channel_id=1, source_target_pairs={{0,4},{1,5},{2,6},{3,7},{4,0},{5,1},{6,2},{7,3},{8,12},{9,13},{10,... | collective-permute-start | bytes 663560 | tf_op jit(solution)/shard_map/ppermute | solution.py:208
  57.6 3.6 %collective-permute-done.15.crossed = bf16[2,3,48,384]{3,2,1,0:T(8,128)(2,1)S(1)} collective-permute-done((bf16[2,3,48,384]{3,2,1,0:T(8,128)(2,1)S(1)}, bf16[2,3,48,384]{3,2,1,0:T(8,128)(2,1)S(1)}, u32[]{:S(2)}, u32[]{:S(2)}) %collective-permute-start.15) | collective-permute-done | bytes 221216 | tf_op jit(solution)/shard_map/ppermute | solution.py:208
  61.6 1.4 %collective-permute-start.22 = (bf16[2,192,128]{2,1,0:T(8,128)(2,1)S(1)}, bf16[2,192,128]{2,1,0:T(8,128)(2,1)S(1)}, u32[]{:S(2)}, u32[]{:S(2)}) collective-permute-start(bf16[2,192,128]{2,1,0:T(8,128)(2,1)S(1)} %pad_maximum_fusion.2.refs_1_), channel_id=1, source_target_pairs={{0,3},{1,2},{2,1},{3,0},{4,7},{5,6},{6,5},{7,4},{8,11},{9,10},{10,... | collective-permute-start | bytes 294920 | tf_op jit(solution)/shard_map/ppermute | solution.py:208
  63.0 1.7 %collective-permute-start.18 = (bf16[2,3,48,384]{3,2,1,0:T(8,128)(2,1)S(1)}, bf16[2,3,48,384]{3,2,1,0:T(8,128)(2,1)S(1)}, u32[]{:S(2)}, u32[]{:S(2)}) collective-permute-start(bf16[2,3,48,384]{3,2,1,0:T(8,128)(2,1)S(1)} %get-tuple-element.55.refs_2_), channel_id=1, source_target_pairs={{0,4},{1,5},{2,6},{3,7},{4,0},{5,1},{6,2},{7,3},{8,12},{9,13},{10,... | collective-permute-start | bytes 663560 | tf_op jit(solution)/shard_map/ppermute | solution.py:208
  64.7 1.1 %collective-permute-start.19 = (f32[2,24,96]{2,1,0:T(8,128)S(1)}, f32[2,24,96]{2,1,0:T(8,128)S(1)}, u32[]{:S(2)}, u32[]{:S(2)}) collective-permute-start(f32[2,24,96]{2,1,0:T(8,128)S(1)} %fusion.1.here), channel_id=1, source_target_pairs={{0,2},{1,3},{2,0},{3,1},{4,6},{5,7},{6,4},{7,5},{8,10},{9,11},{10,... | collective-permute-start | bytes 55304 | tf_op jit(solution)/shard_map/ppermute | solution.py:208
  65.9 2.4 %collective-permute-start.21 = (f32[2,24,96]{2,1,0:T(8,128)S(1)}, f32[2,24,96]{2,1,0:T(8,128)S(1)}, u32[]{:S(2)}, u32[]{:S(2)}) collective-permute-start(f32[2,24,96]{2,1,0:T(8,128)S(1)} %fusion.1.here), channel_id=1, source_target_pairs={{0,6},{1,7},{2,4},{3,5},{4,2},{5,3},{6,0},{7,1},{8,14},{9,15},{10,... | collective-permute-start | bytes 55304 | tf_op jit(solution)/shard_map/ppermute | solution.py:208
  68.6 2.6 %collective-permute-done.20.here = f32[2,24,96]{2,1,0:T(8,128)S(1)} collective-permute-done((f32[2,24,96]{2,1,0:T(8,128)S(1)}, f32[2,24,96]{2,1,0:T(8,128)S(1)}, u32[]{:S(2)}, u32[]{:S(2)}) %collective-permute-start.20) | collective-permute-done | bytes 18464 | tf_op jit(solution)/shard_map/ppermute | solution.py:208
  71.9 1.5 %shard_map.103 = (bf16[3,384,384]{2,1,0:T(8,128)(2,1)S(1)}, f32[2,192,128]{2,1,0:T(8,128)S(1)}, bf16[2,192,128]{2,1,0:T(8,128)(2,1)S(1)}) custom-call(bf16[3,384,384]{2,1,0:T(8,128)(2,1)S(1)} %shard_map.95.refs_2_.refs_4_.refs_0_, bf16[2,3,48,384]{3,2,1,0:T(8,128)(2,1)S(1)} %get-tuple-element.51.refs_1_, ...), custom_call_target="tpu_custom_call" | custom-call | flops 226492416 | bytes 6119424 | tf_op jit(solution)/shard_map/pallas_call | solution.py:181
  73.4 1.3 %collective-permute-done.23 = bf16[2,192,128]{2,1,0:T(8,128)(2,1)S(1)} collective-permute-done((bf16[2,192,128]{2,1,0:T(8,128)(2,1)S(1)}, bf16[2,192,128]{2,1,0:T(8,128)(2,1)S(1)}, u32[]{:S(2)}, u32[]{:S(2)}) %collective-permute-start.23) | collective-permute-done | bytes 98336 | tf_op jit(solution)/shard_map/ppermute | solution.py:208
  74.7 1.2 %collective-permute-start.25 = (bf16[2,192,128]{2,1,0:T(8,128)(2,1)S(1)}, bf16[2,192,128]{2,1,0:T(8,128)(2,1)S(1)}, u32[]{:S(2)}, u32[]{:S(2)}) collective-permute-start(bf16[2,192,128]{2,1,0:T(8,128)(2,1)S(1)} %add_convert_fusion.2), channel_id=1, source_target_pairs={{0,2},{1,3},{2,0},{3,1},{4,6},{5,7},{6,4},{7,5},{8,10},{9,11},{10,... | collective-permute-start | bytes 294920 | tf_op jit(solution)/shard_map/ppermute | solution.py:208
  76.8 2.9 %collective-permute-done.25.pair = bf16[2,192,128]{2,1,0:T(8,128)(2,1)S(1)} collective-permute-done((bf16[2,192,128]{2,1,0:T(8,128)(2,1)S(1)}, bf16[2,192,128]{2,1,0:T(8,128)(2,1)S(1)}, u32[]{:S(2)}, u32[]{:S(2)}) %collective-permute-start.25) | collective-permute-done | bytes 98336 | tf_op jit(solution)/shard_map/ppermute | solution.py:208
  (47 shorter events, 7.5 us)
Async XLA Ops:
  0.6 5.2 %copy-start = (bf16[1024,192]{0,1:T(8,128)(2,1)S(1)}, bf16[1024,192]{0,1:T(8,128)(2,1)}, u32[]{:S(2)}) copy-start(bf16[1024,192]{0,1:T(8,128)(2,1)} %param.8) | copy-start | bytes 1179652
  1.7 6.1 %collective-permute-start = (bf16[3,48,384]{2,1,0:T(8,128)(2,1)S(1)}, bf16[3,48,384]{2,1,0:T(8,128)(2,1)S(1)}, u32[]{:S(2)}, u32[]{:S(2)}) collective-permute-start(bf16[3,48,384]{2,1,0:T(8,128)(2,1)S(1)} %get-tuple-element.73), channel_id=1, source_target_pairs={{0,2},{1,3},{2,0},{3,1},{4,6},{5,7},{6,4},{7,5},{8,10},{9,11},{10,... | collective-permute-start | bytes 331784 | tf_op jit(solution)/shard_map/ppermute | solution.py:208
  5.8 21.1 %copy-start.1 = (bf16[128,192]{0,1:T(8,128)(2,1)S(1)}, bf16[128,192]{0,1:T(8,128)(2,1)}, u32[]{:S(2)}) copy-start(bf16[128,192]{0,1:T(8,128)(2,1)} %param.15) | copy-start | bytes 147460
  5.8 21.1 %copy-start.2 = (bf16[128,192]{0,1:T(8,128)(2,1)S(1)}, bf16[128,192]{0,1:T(8,128)(2,1)}, u32[]{:S(2)}) copy-start(bf16[128,192]{0,1:T(8,128)(2,1)} %param.14) | copy-start | bytes 147460
  7.8 19.0 %collective-permute-start.1 = (bf16[2,192,1024]{2,1,0:T(8,128)(2,1)S(1)}, bf16[2,192,1024]{2,1,0:T(8,128)(2,1)S(1)}, u32[]{:S(2)}, u32[]{:S(2)}) collective-permute-start(bf16[2,192,1024]{2,1,0:T(8,128)(2,1)S(1)} %pad_maximum_fusion.refs_0_), channel_id=1, source_target_pairs={{0,2},{1,3},{2,0},{3,1},{4,6},{5,7},{6,4},{7,5},{8,10},{9,11},{10,... | collective-permute-start | bytes 2359304 | tf_op jit(solution)/shard_map/ppermute | solution.py:208
  9.5 8.3 %collective-permute-start.3 = (bf16[3,48,384]{2,1,0:T(8,128)(2,1)S(1)}, bf16[3,48,384]{2,1,0:T(8,128)(2,1)S(1)}, u32[]{:S(2)}, u32[]{:S(2)}) collective-permute-start(bf16[3,48,384]{2,1,0:T(8,128)(2,1)S(1)} %get-tuple-element.72.refs_0_), channel_id=1, source_target_pairs={{0,8},{1,9},{2,10},{3,11},{4,12},{5,13},{6,14},{7,15},{8,0},{9,1},... | collective-permute-start | bytes 331784 | tf_op jit(solution)/shard_map/ppermute | solution.py:208
  12.1 7.5 %collective-permute-start.2 = (bf16[3,48,384]{2,1,0:T(8,128)(2,1)S(1)}, bf16[3,48,384]{2,1,0:T(8,128)(2,1)S(1)}, u32[]{:S(2)}, u32[]{:S(2)}) collective-permute-start(bf16[3,48,384]{2,1,0:T(8,128)(2,1)S(1)} %get-tuple-element.72.refs_0_), channel_id=1, source_target_pairs={{0,4},{1,5},{2,6},{3,7},{4,0},{5,1},{6,2},{7,3},{8,12},{9,13},{10,... | collective-permute-start | bytes 331784 | tf_op jit(solution)/shard_map/ppermute | solution.py:208
  13.7 7.7 %collective-permute-start.6 = (bf16[3,48,384]{2,1,0:T(8,128)(2,1)S(1)}, bf16[3,48,384]{2,1,0:T(8,128)(2,1)S(1)}, u32[]{:S(2)}, u32[]{:S(2)}) collective-permute-start(bf16[3,48,384]{2,1,0:T(8,128)(2,1)S(1)} %collective-permute-done.refs_4_), channel_id=1, source_target_pairs={{0,8},{1,9},{2,10},{3,11},{4,12},{5,13},{6,14},{7,15},{8,0},{9,1},... | collective-permute-start | bytes 331784 | tf_op jit(solution)/shard_map/ppermute | solution.py:208
  14.0 12.9 %collective-permute-start.9 = (bf16[2,192,1024]{2,1,0:T(8,128)(2,1)S(1)}, bf16[2,192,1024]{2,1,0:T(8,128)(2,1)S(1)}, u32[]{:S(2)}, u32[]{:S(2)}) collective-permute-start(bf16[2,192,1024]{2,1,0:T(8,128)(2,1)S(1)} %pad_maximum_fusion.refs_0_), channel_id=1, source_target_pairs={{0,1},{1,0},{2,3},{3,2},{4,5},{5,4},{6,7},{7,6},{8,9},{9,8},{10,11... | collective-permute-start | bytes 2359304 | tf_op jit(solution)/shard_map/ppermute | solution.py:208
  17.8 5.3 %collective-permute-start.5 = (bf16[3,48,384]{2,1,0:T(8,128)(2,1)S(1)}, bf16[3,48,384]{2,1,0:T(8,128)(2,1)S(1)}, u32[]{:S(2)}, u32[]{:S(2)}) collective-permute-start(bf16[3,48,384]{2,1,0:T(8,128)(2,1)S(1)} %collective-permute-done.refs_4_), channel_id=1, source_target_pairs={{0,4},{1,5},{2,6},{3,7},{4,0},{5,1},{6,2},{7,3},{8,12},{9,13},{10,... | collective-permute-start | bytes 331784 | tf_op jit(solution)/shard_map/ppermute | solution.py:208
  19.6 5.7 %collective-permute-start.4 = (bf16[3,48,384]{2,1,0:T(8,128)(2,1)S(1)}, bf16[3,48,384]{2,1,0:T(8,128)(2,1)S(1)}, u32[]{:S(2)}, u32[]{:S(2)}) collective-permute-start(bf16[3,48,384]{2,1,0:T(8,128)(2,1)S(1)} %collective-permute-done.3.refs_2_), channel_id=1, source_target_pairs={{0,4},{1,5},{2,6},{3,7},{4,0},{5,1},{6,2},{7,3},{8,12},{9,13},{10,... | collective-permute-start | bytes 331784 | tf_op jit(solution)/shard_map/ppermute | solution.py:208
  21.4 5.4 %collective-permute-start.7 = (bf16[3,48,384]{2,1,0:T(8,128)(2,1)S(1)}, bf16[3,48,384]{2,1,0:T(8,128)(2,1)S(1)}, u32[]{:S(2)}, u32[]{:S(2)}) collective-permute-start(bf16[3,48,384]{2,1,0:T(8,128)(2,1)S(1)} %collective-permute-done.6.refs_6_), channel_id=1, source_target_pairs={{0,4},{1,5},{2,6},{3,7},{4,0},{5,1},{6,2},{7,3},{8,12},{9,13},{10,... | collective-permute-start | bytes 331784 | tf_op jit(solution)/shard_map/ppermute | solution.py:208
  26.9 3.0 %collective-permute-start.8 = (bf16[2,192,1024]{2,1,0:T(8,128)(2,1)S(1)}, bf16[2,192,1024]{2,1,0:T(8,128)(2,1)S(1)}, u32[]{:S(2)}, u32[]{:S(2)}) collective-permute-start(bf16[2,192,1024]{2,1,0:T(8,128)(2,1)S(1)} %collective-permute-done.1.refs_0_), channel_id=1, source_target_pairs={{0,1},{1,0},{2,3},{3,2},{4,5},{5,4},{6,7},{7,6},{8,9},{9,8},{10,11... | collective-permute-start | bytes 2359304 | tf_op jit(solution)/shard_map/ppermute | solution.py:208
  32.3 8.3 %collective-permute-start.10 = (bf16[2,3,48,384]{3,2,1,0:T(8,128)(2,1)S(1)}, bf16[2,3,48,384]{3,2,1,0:T(8,128)(2,1)S(1)}, u32[]{:S(2)}, u32[]{:S(2)}) collective-permute-start(bf16[2,3,48,384]{3,2,1,0:T(8,128)(2,1)S(1)} %get-tuple-element.48), channel_id=1, source_target_pairs={{0,4},{1,5},{2,6},{3,7},{4,0},{5,1},{6,2},{7,3},{8,12},{9,13},{10,... | collective-permute-start | bytes 663560 | tf_op jit(solution)/shard_map/ppermute | solution.py:208
  33.5 3.1 %collective-permute-start.11 = (bf16[2,192,128]{2,1,0:T(8,128)(2,1)S(1)}, bf16[2,192,128]{2,1,0:T(8,128)(2,1)S(1)}, u32[]{:S(2)}, u32[]{:S(2)}) collective-permute-start(bf16[2,192,128]{2,1,0:T(8,128)(2,1)S(1)} %pad_maximum_fusion.2.refs_1_), channel_id=1, source_target_pairs={{0,1},{1,0},{2,3},{3,2},{4,5},{5,4},{6,7},{7,6},{8,9},{9,8},{10,11... | collective-permute-start | bytes 294920 | tf_op jit(solution)/shard_map/ppermute | solution.py:208
  33.7 5.0 %collective-permute-start.12 = (bf16[2,192,128]{2,1,0:T(8,128)(2,1)S(1)}, bf16[2,192,128]{2,1,0:T(8,128)(2,1)S(1)}, u32[]{:S(2)}, u32[]{:S(2)}) collective-permute-start(bf16[2,192,128]{2,1,0:T(8,128)(2,1)S(1)} %pad_maximum_fusion.2.refs_1_), channel_id=1, source_target_pairs={{0,2},{1,3},{2,0},{3,1},{4,6},{5,7},{6,4},{7,5},{8,10},{9,11},{10,... | collective-permute-start | bytes 294920 | tf_op jit(solution)/shard_map/ppermute | solution.py:208
  35.2 9.7 %collective-permute-start.14 = (bf16[2,3,48,384]{3,2,1,0:T(8,128)(2,1)S(1)}, bf16[2,3,48,384]{3,2,1,0:T(8,128)(2,1)S(1)}, u32[]{:S(2)}, u32[]{:S(2)}) collective-permute-start(bf16[2,3,48,384]{3,2,1,0:T(8,128)(2,1)S(1)} %get-tuple-element.54), channel_id=1, source_target_pairs={{0,4},{1,5},{2,6},{3,7},{4,0},{5,1},{6,2},{7,3},{8,12},{9,13},{10,... | collective-permute-start | bytes 663560 | tf_op jit(solution)/shard_map/ppermute | solution.py:208
  40.6 15.3 %collective-permute-start.13 = (bf16[2,3,48,384]{3,2,1,0:T(8,128)(2,1)S(1)}, bf16[2,3,48,384]{3,2,1,0:T(8,128)(2,1)S(1)}, u32[]{:S(2)}, u32[]{:S(2)}) collective-permute-start(bf16[2,3,48,384]{3,2,1,0:T(8,128)(2,1)S(1)} %add_convert_fusion.1), channel_id=1, source_target_pairs={{0,12},{1,13},{2,14},{3,15},{4,8},{5,9},{6,10},{7,11},{8,4},{9,5},... | collective-permute-start | bytes 663560 | tf_op jit(solution)/shard_map/ppermute | solution.py:208
  45.0 16.3 %collective-permute-start.15 = (bf16[2,3,48,384]{3,2,1,0:T(8,128)(2,1)S(1)}, bf16[2,3,48,384]{3,2,1,0:T(8,128)(2,1)S(1)}, u32[]{:S(2)}, u32[]{:S(2)}) collective-permute-start(bf16[2,3,48,384]{3,2,1,0:T(8,128)(2,1)S(1)} %add_convert_fusion), channel_id=1, source_target_pairs={{0,12},{1,13},{2,14},{3,15},{4,8},{5,9},{6,10},{7,11},{8,4},{9,5},... | collective-permute-start | bytes 663560 | tf_op jit(solution)/shard_map/ppermute | solution.py:208
  56.2 8.5 %collective-permute-start.17 = (bf16[2,3,48,384]{3,2,1,0:T(8,128)(2,1)S(1)}, bf16[2,3,48,384]{3,2,1,0:T(8,128)(2,1)S(1)}, u32[]{:S(2)}, u32[]{:S(2)}) collective-permute-start(bf16[2,3,48,384]{3,2,1,0:T(8,128)(2,1)S(1)} %get-tuple-element.51.refs_1_), channel_id=1, source_target_pairs={{0,4},{1,5},{2,6},{3,7},{4,0},{5,1},{6,2},{7,3},{8,12},{9,13},{10,... | collective-permute-start | bytes 663560 | tf_op jit(solution)/shard_map/ppermute | solution.py:208
  61.6 3.1 %collective-permute-start.16 = (f32[2,24,96]{2,1,0:T(8,128)S(1)}, f32[2,24,96]{2,1,0:T(8,128)S(1)}, u32[]{:S(2)}, u32[]{:S(2)}) collective-permute-start(f32[2,24,96]{2,1,0:T(8,128)S(1)} %pad_maximum_fusion.3), channel_id=1, source_target_pairs={{0,1},{1,0},{2,3},{3,2},{4,5},{5,4},{6,7},{7,6},{8,9},{9,8},{10,11... | collective-permute-start | bytes 55304 | tf_op jit(solution)/shard_map/ppermute | solution.py:208
  61.6 10.2 %collective-permute-start.22 = (bf16[2,192,128]{2,1,0:T(8,128)(2,1)S(1)}, bf16[2,192,128]{2,1,0:T(8,128)(2,1)S(1)}, u32[]{:S(2)}, u32[]{:S(2)}) collective-permute-start(bf16[2,192,128]{2,1,0:T(8,128)(2,1)S(1)} %pad_maximum_fusion.2.refs_1_), channel_id=1, source_target_pairs={{0,3},{1,2},{2,1},{3,0},{4,7},{5,6},{6,5},{7,4},{8,11},{9,10},{10,... | collective-permute-start | bytes 294920 | tf_op jit(solution)/shard_map/ppermute | solution.py:208
  63.0 8.8 %collective-permute-start.18 = (bf16[2,3,48,384]{3,2,1,0:T(8,128)(2,1)S(1)}, bf16[2,3,48,384]{3,2,1,0:T(8,128)(2,1)S(1)}, u32[]{:S(2)}, u32[]{:S(2)}) collective-permute-start(bf16[2,3,48,384]{3,2,1,0:T(8,128)(2,1)S(1)} %get-tuple-element.55.refs_2_), channel_id=1, source_target_pairs={{0,4},{1,5},{2,6},{3,7},{4,0},{5,1},{6,2},{7,3},{8,12},{9,13},{10,... | collective-permute-start | bytes 663560 | tf_op jit(solution)/shard_map/ppermute | solution.py:208
  64.7 3.9 %collective-permute-start.19 = (f32[2,24,96]{2,1,0:T(8,128)S(1)}, f32[2,24,96]{2,1,0:T(8,128)S(1)}, u32[]{:S(2)}, u32[]{:S(2)}) collective-permute-start(f32[2,24,96]{2,1,0:T(8,128)S(1)} %fusion.1.here), channel_id=1, source_target_pairs={{0,2},{1,3},{2,0},{3,1},{4,6},{5,7},{6,4},{7,5},{8,10},{9,11},{10,... | collective-permute-start | bytes 55304 | tf_op jit(solution)/shard_map/ppermute | solution.py:208
  65.8 5.5 %collective-permute-start.20 = (f32[2,24,96]{2,1,0:T(8,128)S(1)}, f32[2,24,96]{2,1,0:T(8,128)S(1)}, u32[]{:S(2)}, u32[]{:S(2)}) collective-permute-start(f32[2,24,96]{2,1,0:T(8,128)S(1)} %fusion.1.here), channel_id=1, source_target_pairs={{0,4},{1,5},{2,6},{3,7},{4,0},{5,1},{6,2},{7,3},{8,12},{9,13},{10,... | collective-permute-start | bytes 55304 | tf_op jit(solution)/shard_map/ppermute | solution.py:208
  65.9 6.0 %collective-permute-start.21 = (f32[2,24,96]{2,1,0:T(8,128)S(1)}, f32[2,24,96]{2,1,0:T(8,128)S(1)}, u32[]{:S(2)}, u32[]{:S(2)}) collective-permute-start(f32[2,24,96]{2,1,0:T(8,128)S(1)} %fusion.1.here), channel_id=1, source_target_pairs={{0,6},{1,7},{2,4},{3,5},{4,2},{5,3},{6,0},{7,1},{8,14},{9,15},{10,... | collective-permute-start | bytes 55304 | tf_op jit(solution)/shard_map/ppermute | solution.py:208
  73.3 1.4 %collective-permute-start.23 = (bf16[2,192,128]{2,1,0:T(8,128)(2,1)S(1)}, bf16[2,192,128]{2,1,0:T(8,128)(2,1)S(1)}, u32[]{:S(2)}, u32[]{:S(2)}) collective-permute-start(bf16[2,192,128]{2,1,0:T(8,128)(2,1)S(1)} %get-tuple-element.62), channel_id=1, source_target_pairs={{0,1},{1,0},{2,3},{3,2},{4,5},{5,4},{6,7},{7,6},{8,9},{9,8},{10,11... | collective-permute-start | bytes 294920 | tf_op jit(solution)/shard_map/ppermute | solution.py:208
  74.7 4.9 %collective-permute-start.25 = (bf16[2,192,128]{2,1,0:T(8,128)(2,1)S(1)}, bf16[2,192,128]{2,1,0:T(8,128)(2,1)S(1)}, u32[]{:S(2)}, u32[]{:S(2)}) collective-permute-start(bf16[2,192,128]{2,1,0:T(8,128)(2,1)S(1)} %add_convert_fusion.2), channel_id=1, source_target_pairs={{0,2},{1,3},{2,0},{3,1},{4,6},{5,7},{6,4},{7,5},{8,10},{9,11},{10,... | collective-permute-start | bytes 294920 | tf_op jit(solution)/shard_map/ppermute | solution.py:208
  76.7 3.0 %collective-permute-start.24 = (bf16[2,192,128]{2,1,0:T(8,128)(2,1)S(1)}, bf16[2,192,128]{2,1,0:T(8,128)(2,1)S(1)}, u32[]{:S(2)}, u32[]{:S(2)}) collective-permute-start(bf16[2,192,128]{2,1,0:T(8,128)(2,1)S(1)} %get-tuple-element.67), channel_id=1, source_target_pairs={{0,1},{1,0},{2,3},{3,2},{4,5},{5,4},{6,7},{7,6},{8,9},{9,8},{10,11... | collective-permute-start | bytes 294920 | tf_op jit(solution)/shard_map/ppermute | solution.py:208

commit v12 on v11

--- a/solution.py
+++ b/solution.py
@@ -127,6 +127,11 @@
     factor = jnp.sqrt(wsq) / jnp.sqrt(msq + epsilon)
     factors[:, :8] = factor
     factors[:, 8:] = scale * factor
+
+
+def factors_kernel(hidden, here, there, near, near_there, own, others):
+    factor_kernel(hidden, here, there, own)
+    factor_kernel(hidden, near, near_there, others)
 
 
 def answer(renewed, query, quests, half, kept, given):
@@ -294,17 +299,12 @@
     stats = jnp.stack(stats)
     there, backs[0] = lax.optimization_barrier((swap(stats, core), backs[0]))
     stats = stats + there
-    factors = [
-        call(
-            functools.partial(factor_kernel, 2 * n_hid * cols),
-            (here, there),
-            (jax.ShapeDtypeStruct((parts, 16, 2 * rows // parts), f32),),
-        )[0]
-        for here, there in (
-            (stats, swap(stats, pair)),
-            (swap(stats, zed), swap(stats, zed + pair)),
-        )
-    ]
+    shared = jax.ShapeDtypeStruct((parts, 16, 2 * rows // parts), f32)
+    factors = call(
+        functools.partial(factors_kernel, 2 * n_hid * cols),
+        (stats, swap(stats, pair), swap(stats, zed), swap(stats, zed + pair)),
+        (shared, shared),
+    )
 
     count = queries.shape[0]
     piece = (2, feats, count)

time: 80.5 us -> 80.5 us (level)
    pallas_call x11 -> x10, Pallas kernels: 9.81 us -> 9.8 us  [call(): pl.pallas_call(body, out_shape=list(outs), in_specs=specs, out_specs=[pl....]
where the time goes in v12:
time: 80.5 us; the launch traced here: 80.3 us
  starting transfers between devices  40 us (50%)
  waiting for transfers between devices  27.3 us (34%)
  Pallas kernels  9.8 us (12%)
  other arithmetic  2.33 us (3%)
  between operations  0.88 us (1%)
    ppermute x26, starting transfers between devices, swap(): return lax.ppermute(array, ('tok', 'hid'), pairs)  40 us
    ppermute x26, waiting for transfers between devices, swap(): return lax.ppermute(array, ('tok', 'hid'), pairs)  27.3 us
    pallas_call x10, Pallas kernels, call(): pl.pallas_call(body, out_shape=list(outs), in_specs=specs, out_specs=[pl....  9.8 us
  transfers between devices with their start and end apart: 26, of which 15 were waited for; matrix products, arithmetic and copies ran while one was open for 2% of the time, Pallas kernels for 7%

profile of v12, /device:TPU:0, one launch (start us, length us, event | category | flops | bytes accessed | tf_op | source)
XLA Modules:
  0.0 80.3 jit_solution(2650604531960754470)
XLA Ops:
  0.7 1.0 %pad_maximum_fusion.1 = bf16[3,48,768]{2,1,0:T(8,128)(2,1)S(1)} fusion(bf16[1,48,768]{2,1,0:T(8,128)(2,1)} %bitcast.25, bf16[1,48,768]{2,1,0:T(8,128)(2,1)} %bitcast.26, bf16[1,48,768]{2,1,0:T(8,128)(2,1)} %bitcast.27), kind=kLoop, calls=%fused_computation.5 | loop fusion | flops 221184 | bytes 442368 | tf_op jit(solution)/shard_map/stack | solution.py:219
  1.7 3.0 %collective-permute-start = (bf16[3,48,384]{2,1,0:T(8,128)(2,1)S(1)}, bf16[3,48,384]{2,1,0:T(8,128)(2,1)S(1)}, u32[]{:S(2)}, u32[]{:S(2)}) collective-permute-start(bf16[3,48,384]{2,1,0:T(8,128)(2,1)S(1)} %get-tuple-element.77), channel_id=1, source_target_pairs={{0,2},{1,3},{2,0},{3,1},{4,6},{5,7},{6,4},{7,5},{8,10},{9,11},{10,... | collective-permute-start | bytes 331784 | tf_op jit(solution)/shard_map/ppermute | solution.py:213
  4.7 1.1 %fusion = bf16[1,192,1024]{2,1,0:T(8,128)(2,1)S(1)} fusion(bf16[1024,192]{0,1:T(8,128)(2,1)} %param.9, f32[1024]{0:T(1024)} %param.10), kind=kLoop, calls=%fused_computation.4 | loop fusion | flops 589824 | bytes 790528 | tf_op jit(solution)/shard_map/stack | solution.py:224
  5.9 1.9 %collective-permute-done.refs_4_ = bf16[3,48,384]{2,1,0:T(8,128)(2,1)S(1)} collective-permute-done((bf16[3,48,384]{2,1,0:T(8,128)(2,1)S(1)}, bf16[3,48,384]{2,1,0:T(8,128)(2,1)S(1)}, u32[]{:S(2)}, u32[]{:S(2)}) %collective-permute-start) | collective-permute-done | bytes 110624 | tf_op jit(solution)/shard_map/ppermute | solution.py:213
  7.8 1.7 %collective-permute-start.1 = (bf16[2,192,1024]{2,1,0:T(8,128)(2,1)S(1)}, bf16[2,192,1024]{2,1,0:T(8,128)(2,1)S(1)}, u32[]{:S(2)}, u32[]{:S(2)}) collective-permute-start(bf16[2,192,1024]{2,1,0:T(8,128)(2,1)S(1)} %pad_maximum_fusion.refs_0_), channel_id=1, source_target_pairs={{0,2},{1,3},{2,0},{3,1},{4,6},{5,7},{6,4},{7,5},{8,10},{9,11},{10,... | collective-permute-start | bytes 2359304 | tf_op jit(solution)/shard_map/ppermute | solution.py:213
  9.5 2.6 %collective-permute-start.3 = (bf16[3,48,384]{2,1,0:T(8,128)(2,1)S(1)}, bf16[3,48,384]{2,1,0:T(8,128)(2,1)S(1)}, u32[]{:S(2)}, u32[]{:S(2)}) collective-permute-start(bf16[3,48,384]{2,1,0:T(8,128)(2,1)S(1)} %get-tuple-element.76.refs_0_), channel_id=1, source_target_pairs={{0,8},{1,9},{2,10},{3,11},{4,12},{5,13},{6,14},{7,15},{8,0},{9,1},... | collective-permute-start | bytes 331784 | tf_op jit(solution)/shard_map/ppermute | solution.py:213
  12.1 1.6 %collective-permute-start.2 = (bf16[3,48,384]{2,1,0:T(8,128)(2,1)S(1)}, bf16[3,48,384]{2,1,0:T(8,128)(2,1)S(1)}, u32[]{:S(2)}, u32[]{:S(2)}) collective-permute-start(bf16[3,48,384]{2,1,0:T(8,128)(2,1)S(1)} %get-tuple-element.76.refs_0_), channel_id=1, source_target_pairs={{0,4},{1,5},{2,6},{3,7},{4,0},{5,1},{6,2},{7,3},{8,12},{9,13},{10,... | collective-permute-start | bytes 331784 | tf_op jit(solution)/shard_map/ppermute | solution.py:213
  14.0 3.8 %collective-permute-done.3.refs_2_ = bf16[3,48,384]{2,1,0:T(8,128)(2,1)S(1)} collective-permute-done((bf16[3,48,384]{2,1,0:T(8,128)(2,1)S(1)}, bf16[3,48,384]{2,1,0:T(8,128)(2,1)S(1)}, u32[]{:S(2)}, u32[]{:S(2)}) %collective-permute-start.3) | collective-permute-done | bytes 110624 | tf_op jit(solution)/shard_map/ppermute | solution.py:213
  17.8 1.8 %collective-permute-start.5 = (bf16[3,48,384]{2,1,0:T(8,128)(2,1)S(1)}, bf16[3,48,384]{2,1,0:T(8,128)(2,1)S(1)}, u32[]{:S(2)}, u32[]{:S(2)}) collective-permute-start(bf16[3,48,384]{2,1,0:T(8,128)(2,1)S(1)} %collective-permute-done.refs_4_), channel_id=1, source_target_pairs={{0,4},{1,5},{2,6},{3,7},{4,0},{5,1},{6,2},{7,3},{8,12},{9,13},{10,... | collective-permute-start | bytes 331784 | tf_op jit(solution)/shard_map/ppermute | solution.py:213
  20.4 1.0 %collective-permute-done.6.refs_6_ = bf16[3,48,384]{2,1,0:T(8,128)(2,1)S(1)} collective-permute-done((bf16[3,48,384]{2,1,0:T(8,128)(2,1)S(1)}, bf16[3,48,384]{2,1,0:T(8,128)(2,1)S(1)}, u32[]{:S(2)}, u32[]{:S(2)}) %collective-permute-start.6) | collective-permute-done | bytes 110624 | tf_op jit(solution)/shard_map/ppermute | solution.py:213
  21.9 1.3 %collective-permute-done.5.refs_5_ = bf16[3,48,384]{2,1,0:T(8,128)(2,1)S(1)} collective-permute-done((bf16[3,48,384]{2,1,0:T(8,128)(2,1)S(1)}, bf16[3,48,384]{2,1,0:T(8,128)(2,1)S(1)}, u32[]{:S(2)}, u32[]{:S(2)}) %collective-permute-start.5) | collective-permute-done | bytes 110624 | tf_op jit(solution)/shard_map/ppermute | solution.py:213
  23.1 2.2 %collective-permute-done.4.refs_3_ = bf16[3,48,384]{2,1,0:T(8,128)(2,1)S(1)} collective-permute-done((bf16[3,48,384]{2,1,0:T(8,128)(2,1)S(1)}, bf16[3,48,384]{2,1,0:T(8,128)(2,1)S(1)}, u32[]{:S(2)}, u32[]{:S(2)}) %collective-permute-start.4) | collective-permute-done | bytes 110624 | tf_op jit(solution)/shard_map/ppermute | solution.py:213
  25.3 1.4 %collective-permute-done.7.refs_7_ = bf16[3,48,384]{2,1,0:T(8,128)(2,1)S(1)} collective-permute-done((bf16[3,48,384]{2,1,0:T(8,128)(2,1)S(1)}, bf16[3,48,384]{2,1,0:T(8,128)(2,1)S(1)}, u32[]{:S(2)}, u32[]{:S(2)}) %collective-permute-start.7) | collective-permute-done | bytes 110624 | tf_op jit(solution)/shard_map/ppermute | solution.py:213
  27.0 2.8 %shard_map.96.refs_3_ = f32[3,384,384]{2,1,0:T(8,128)S(1)} custom-call(bf16[2,192,1024]{2,1,0:T(8,128)(2,1)S(1)} %pad_maximum_fusion.refs_0_, bf16[2,192,1024]{2,1,0:T(8,128)(2,1)S(1)} %collective-permute-done.9.refs_1_, bf16[3,384,384]{2,1,0:T(8,128)(2,1)S(1)} %shard_map.95.refs_2_.refs_4_.refs_0_), custom_call_target="tpu_custom_call" | custom-call | flops 1811939328 | bytes 6684672 | tf_op jit(solution)/shard_map/pallas_call | solution.py:186
  29.8 2.4 %shard_map.97 = (bf16[2,3,48,384]{3,2,1,0:T(8,128)(2,1)S(1)}, bf16[2,3,48,384]{3,2,1,0:T(8,128)(2,1)S(1)}, bf16[2,384,1024]{2,1,0:T(8,128)(2,1)S(1)}, bf16[768,1024]{1,0:T(8,128)(2,1)S(1)}, bf16[384,1024]{1,0:T(8,128)(2,1)S(1)}) custom-call(bf16[2,192,1024]{2,1,0:T(8,128)(2,1)S(1)} %collective-permute-done.1.refs_0_, ...), custom_call_target="tpu_custom_call" | custom-call | flops 1358954496 | bytes 15433728 | tf_op jit(solution)/shard_map/pallas_call | solution.py:186
  32.3 1.2 %collective-permute-start.10 = (bf16[2,3,48,384]{3,2,1,0:T(8,128)(2,1)S(1)}, bf16[2,3,48,384]{3,2,1,0:T(8,128)(2,1)S(1)}, u32[]{:S(2)}, u32[]{:S(2)}) collective-permute-start(bf16[2,3,48,384]{3,2,1,0:T(8,128)(2,1)S(1)} %get-tuple-element.50), channel_id=1, source_target_pairs={{0,4},{1,5},{2,6},{3,7},{4,0},{5,1},{6,2},{7,3},{8,12},{9,13},{10,... | collective-permute-start | bytes 663560 | tf_op jit(solution)/shard_map/ppermute | solution.py:213
  33.7 1.4 %collective-permute-start.12 = (bf16[2,192,128]{2,1,0:T(8,128)(2,1)S(1)}, bf16[2,192,128]{2,1,0:T(8,128)(2,1)S(1)}, u32[]{:S(2)}, u32[]{:S(2)}) collective-permute-start(bf16[2,192,128]{2,1,0:T(8,128)(2,1)S(1)} %pad_maximum_fusion.2.refs_1_), channel_id=1, source_target_pairs={{0,2},{1,3},{2,0},{3,1},{4,6},{5,7},{6,4},{7,5},{8,10},{9,11},{10,... | collective-permute-start | bytes 294920 | tf_op jit(solution)/shard_map/ppermute | solution.py:213
  36.6 2.1 %collective-permute-done.12.refs_7_ = bf16[2,192,128]{2,1,0:T(8,128)(2,1)S(1)} collective-permute-done((bf16[2,192,128]{2,1,0:T(8,128)(2,1)S(1)}, bf16[2,192,128]{2,1,0:T(8,128)(2,1)S(1)}, u32[]{:S(2)}, u32[]{:S(2)}) %collective-permute-start.12) | collective-permute-done | bytes 98336 | tf_op jit(solution)/shard_map/ppermute | solution.py:213
  38.7 1.8 %collective-permute-done.10.came = bf16[2,3,48,384]{3,2,1,0:T(8,128)(2,1)S(1)} collective-permute-done((bf16[2,3,48,384]{3,2,1,0:T(8,128)(2,1)S(1)}, bf16[2,3,48,384]{3,2,1,0:T(8,128)(2,1)S(1)}, u32[]{:S(2)}, u32[]{:S(2)}) %collective-permute-start.10) | collective-permute-done | bytes 221216 | tf_op jit(solution)/shard_map/ppermute | solution.py:213
  40.6 3.8 %collective-permute-start.13 = (bf16[2,3,48,384]{3,2,1,0:T(8,128)(2,1)S(1)}, bf16[2,3,48,384]{3,2,1,0:T(8,128)(2,1)S(1)}, u32[]{:S(2)}, u32[]{:S(2)}) collective-permute-start(bf16[2,3,48,384]{3,2,1,0:T(8,128)(2,1)S(1)} %add_convert_fusion.1), channel_id=1, source_target_pairs={{0,12},{1,13},{2,14},{3,15},{4,8},{5,9},{6,10},{7,11},{8,4},{9,5},... | collective-permute-start | bytes 663560 | tf_op jit(solution)/shard_map/ppermute | solution.py:213
  45.0 10.9 %collective-permute-start.15 = (bf16[2,3,48,384]{3,2,1,0:T(8,128)(2,1)S(1)}, bf16[2,3,48,384]{3,2,1,0:T(8,128)(2,1)S(1)}, u32[]{:S(2)}, u32[]{:S(2)}) collective-permute-start(bf16[2,3,48,384]{3,2,1,0:T(8,128)(2,1)S(1)} %add_convert_fusion), channel_id=1, source_target_pairs={{0,12},{1,13},{2,14},{3,15},{4,8},{5,9},{6,10},{7,11},{8,4},{9,5},... | collective-permute-start | bytes 663560 | tf_op jit(solution)/shard_map/ppermute | solution.py:213
  56.2 1.4 %collective-permute-start.17 = (bf16[2,3,48,384]{3,2,1,0:T(8,128)(2,1)S(1)}, bf16[2,3,48,384]{3,2,1,0:T(8,128)(2,1)S(1)}, u32[]{:S(2)}, u32[]{:S(2)}) collective-permute-start(bf16[2,3,48,384]{3,2,1,0:T(8,128)(2,1)S(1)} %get-tuple-element.53.refs_1_), channel_id=1, source_target_pairs={{0,4},{1,5},{2,6},{3,7},{4,0},{5,1},{6,2},{7,3},{8,12},{9,13},{10,... | collective-permute-start | bytes 663560 | tf_op jit(solution)/shard_map/ppermute | solution.py:213
  57.6 3.6 %collective-permute-done.15.crossed = bf16[2,3,48,384]{3,2,1,0:T(8,128)(2,1)S(1)} collective-permute-done((bf16[2,3,48,384]{3,2,1,0:T(8,128)(2,1)S(1)}, bf16[2,3,48,384]{3,2,1,0:T(8,128)(2,1)S(1)}, u32[]{:S(2)}, u32[]{:S(2)}) %collective-permute-start.15) | collective-permute-done | bytes 221216 | tf_op jit(solution)/shard_map/ppermute | solution.py:213
  61.6 1.4 %collective-permute-start.22 = (bf16[2,192,128]{2,1,0:T(8,128)(2,1)S(1)}, bf16[2,192,128]{2,1,0:T(8,128)(2,1)S(1)}, u32[]{:S(2)}, u32[]{:S(2)}) collective-permute-start(bf16[2,192,128]{2,1,0:T(8,128)(2,1)S(1)} %pad_maximum_fusion.2.refs_1_), channel_id=1, source_target_pairs={{0,3},{1,2},{2,1},{3,0},{4,7},{5,6},{6,5},{7,4},{8,11},{9,10},{10,... | collective-permute-start | bytes 294920 | tf_op jit(solution)/shard_map/ppermute | solution.py:213
  63.0 1.7 %collective-permute-start.18 = (bf16[2,3,48,384]{3,2,1,0:T(8,128)(2,1)S(1)}, bf16[2,3,48,384]{3,2,1,0:T(8,128)(2,1)S(1)}, u32[]{:S(2)}, u32[]{:S(2)}) collective-permute-start(bf16[2,3,48,384]{3,2,1,0:T(8,128)(2,1)S(1)} %get-tuple-element.57.refs_2_), channel_id=1, source_target_pairs={{0,4},{1,5},{2,6},{3,7},{4,0},{5,1},{6,2},{7,3},{8,12},{9,13},{10,... | collective-permute-start | bytes 663560 | tf_op jit(solution)/shard_map/ppermute | solution.py:213
  64.7 1.1 %collective-permute-start.19 = (f32[2,24,96]{2,1,0:T(8,128)S(1)}, f32[2,24,96]{2,1,0:T(8,128)S(1)}, u32[]{:S(2)}, u32[]{:S(2)}) collective-permute-start(f32[2,24,96]{2,1,0:T(8,128)S(1)} %fusion.1.here), channel_id=1, source_target_pairs={{0,2},{1,3},{2,0},{3,1},{4,6},{5,7},{6,4},{7,5},{8,10},{9,11},{10,... | collective-permute-start | bytes 55304 | tf_op jit(solution)/shard_map/ppermute | solution.py:213
  65.9 2.4 %collective-permute-start.21 = (f32[2,24,96]{2,1,0:T(8,128)S(1)}, f32[2,24,96]{2,1,0:T(8,128)S(1)}, u32[]{:S(2)}, u32[]{:S(2)}) collective-permute-start(f32[2,24,96]{2,1,0:T(8,128)S(1)} %fusion.1.here), channel_id=1, source_target_pairs={{0,6},{1,7},{2,4},{3,5},{4,2},{5,3},{6,0},{7,1},{8,14},{9,15},{10,... | collective-permute-start | bytes 55304 | tf_op jit(solution)/shard_map/ppermute | solution.py:213
  68.6 2.6 %collective-permute-done.20.near = f32[2,24,96]{2,1,0:T(8,128)S(1)} collective-permute-done((f32[2,24,96]{2,1,0:T(8,128)S(1)}, f32[2,24,96]{2,1,0:T(8,128)S(1)}, u32[]{:S(2)}, u32[]{:S(2)}) %collective-permute-start.20) | collective-permute-done | bytes 18464 | tf_op jit(solution)/shard_map/ppermute | solution.py:213
  71.9 1.5 %shard_map.102 = (bf16[3,384,384]{2,1,0:T(8,128)(2,1)S(1)}, f32[2,192,128]{2,1,0:T(8,128)S(1)}, bf16[2,192,128]{2,1,0:T(8,128)(2,1)S(1)}) custom-call(bf16[3,384,384]{2,1,0:T(8,128)(2,1)S(1)} %shard_map.95.refs_2_.refs_4_.refs_0_, bf16[2,3,48,384]{3,2,1,0:T(8,128)(2,1)S(1)} %get-tuple-element.53.refs_1_, ...), custom_call_target="tpu_custom_call" | custom-call | flops 226492416 | bytes 6119424 | tf_op jit(solution)/shard_map/pallas_call | solution.py:186
  73.4 1.3 %collective-permute-done.23 = bf16[2,192,128]{2,1,0:T(8,128)(2,1)S(1)} collective-permute-done((bf16[2,192,128]{2,1,0:T(8,128)(2,1)S(1)}, bf16[2,192,128]{2,1,0:T(8,128)(2,1)S(1)}, u32[]{:S(2)}, u32[]{:S(2)}) %collective-permute-start.23) | collective-permute-done | bytes 98336 | tf_op jit(solution)/shard_map/ppermute | solution.py:213
  74.7 1.2 %collective-permute-start.25 = (bf16[2,192,128]{2,1,0:T(8,128)(2,1)S(1)}, bf16[2,192,128]{2,1,0:T(8,128)(2,1)S(1)}, u32[]{:S(2)}, u32[]{:S(2)}) collective-permute-start(bf16[2,192,128]{2,1,0:T(8,128)(2,1)S(1)} %add_convert_fusion.2), channel_id=1, source_target_pairs={{0,2},{1,3},{2,0},{3,1},{4,6},{5,7},{6,4},{7,5},{8,10},{9,11},{10,... | collective-permute-start | bytes 294920 | tf_op jit(solution)/shard_map/ppermute | solution.py:213
  76.8 2.9 %collective-permute-done.25.pair = bf16[2,192,128]{2,1,0:T(8,128)(2,1)S(1)} collective-permute-done((bf16[2,192,128]{2,1,0:T(8,128)(2,1)S(1)}, bf16[2,192,128]{2,1,0:T(8,128)(2,1)S(1)}, u32[]{:S(2)}, u32[]{:S(2)}) %collective-permute-start.25) | collective-permute-done | bytes 98336 | tf_op jit(solution)/shard_map/ppermute | solution.py:213
  (46 shorter events, 7.5 us)
Async XLA Ops:
  0.6 5.2 %copy-start = (bf16[1024,192]{0,1:T(8,128)(2,1)S(1)}, bf16[1024,192]{0,1:T(8,128)(2,1)}, u32[]{:S(2)}) copy-start(bf16[1024,192]{0,1:T(8,128)(2,1)} %param.8) | copy-start | bytes 1179652
  1.7 6.1 %collective-permute-start = (bf16[3,48,384]{2,1,0:T(8,128)(2,1)S(1)}, bf16[3,48,384]{2,1,0:T(8,128)(2,1)S(1)}, u32[]{:S(2)}, u32[]{:S(2)}) collective-permute-start(bf16[3,48,384]{2,1,0:T(8,128)(2,1)S(1)} %get-tuple-element.77), channel_id=1, source_target_pairs={{0,2},{1,3},{2,0},{3,1},{4,6},{5,7},{6,4},{7,5},{8,10},{9,11},{10,... | collective-permute-start | bytes 331784 | tf_op jit(solution)/shard_map/ppermute | solution.py:213
  5.8 21.1 %copy-start.1 = (bf16[128,192]{0,1:T(8,128)(2,1)S(1)}, bf16[128,192]{0,1:T(8,128)(2,1)}, u32[]{:S(2)}) copy-start(bf16[128,192]{0,1:T(8,128)(2,1)} %param.15) | copy-start | bytes 147460
  5.8 21.1 %copy-start.2 = (bf16[128,192]{0,1:T(8,128)(2,1)S(1)}, bf16[128,192]{0,1:T(8,128)(2,1)}, u32[]{:S(2)}) copy-start(bf16[128,192]{0,1:T(8,128)(2,1)} %param.14) | copy-start | bytes 147460
  7.8 19.0 %collective-permute-start.1 = (bf16[2,192,1024]{2,1,0:T(8,128)(2,1)S(1)}, bf16[2,192,1024]{2,1,0:T(8,128)(2,1)S(1)}, u32[]{:S(2)}, u32[]{:S(2)}) collective-permute-start(bf16[2,192,1024]{2,1,0:T(8,128)(2,1)S(1)} %pad_maximum_fusion.refs_0_), channel_id=1, source_target_pairs={{0,2},{1,3},{2,0},{3,1},{4,6},{5,7},{6,4},{7,5},{8,10},{9,11},{10,... | collective-permute-start | bytes 2359304 | tf_op jit(solution)/shard_map/ppermute | solution.py:213
  9.5 8.3 %collective-permute-start.3 = (bf16[3,48,384]{2,1,0:T(8,128)(2,1)S(1)}, bf16[3,48,384]{2,1,0:T(8,128)(2,1)S(1)}, u32[]{:S(2)}, u32[]{:S(2)}) collective-permute-start(bf16[3,48,384]{2,1,0:T(8,128)(2,1)S(1)} %get-tuple-element.76.refs_0_), channel_id=1, source_target_pairs={{0,8},{1,9},{2,10},{3,11},{4,12},{5,13},{6,14},{7,15},{8,0},{9,1},... | collective-permute-start | bytes 331784 | tf_op jit(solution)/shard_map/ppermute | solution.py:213
  12.1 7.5 %collective-permute-start.2 = (bf16[3,48,384]{2,1,0:T(8,128)(2,1)S(1)}, bf16[3,48,384]{2,1,0:T(8,128)(2,1)S(1)}, u32[]{:S(2)}, u32[]{:S(2)}) collective-permute-start(bf16[3,48,384]{2,1,0:T(8,128)(2,1)S(1)} %get-tuple-element.76.refs_0_), channel_id=1, source_target_pairs={{0,4},{1,5},{2,6},{3,7},{4,0},{5,1},{6,2},{7,3},{8,12},{9,13},{10,... | collective-permute-start | bytes 331784 | tf_op jit(solution)/shard_map/ppermute | solution.py:213
  13.7 7.7 %collective-permute-start.6 = (bf16[3,48,384]{2,1,0:T(8,128)(2,1)S(1)}, bf16[3,48,384]{2,1,0:T(8,128)(2,1)S(1)}, u32[]{:S(2)}, u32[]{:S(2)}) collective-permute-start(bf16[3,48,384]{2,1,0:T(8,128)(2,1)S(1)} %collective-permute-done.refs_4_), channel_id=1, source_target_pairs={{0,8},{1,9},{2,10},{3,11},{4,12},{5,13},{6,14},{7,15},{8,0},{9,1},... | collective-permute-start | bytes 331784 | tf_op jit(solution)/shard_map/ppermute | solution.py:213
  14.0 12.9 %collective-permute-start.9 = (bf16[2,192,1024]{2,1,0:T(8,128)(2,1)S(1)}, bf16[2,192,1024]{2,1,0:T(8,128)(2,1)S(1)}, u32[]{:S(2)}, u32[]{:S(2)}) collective-permute-start(bf16[2,192,1024]{2,1,0:T(8,128)(2,1)S(1)} %pad_maximum_fusion.refs_0_), channel_id=1, source_target_pairs={{0,1},{1,0},{2,3},{3,2},{4,5},{5,4},{6,7},{7,6},{8,9},{9,8},{10,11... | collective-permute-start | bytes 2359304 | tf_op jit(solution)/shard_map/ppermute | solution.py:213
  17.8 5.3 %collective-permute-start.5 = (bf16[3,48,384]{2,1,0:T(8,128)(2,1)S(1)}, bf16[3,48,384]{2,1,0:T(8,128)(2,1)S(1)}, u32[]{:S(2)}, u32[]{:S(2)}) collective-permute-start(bf16[3,48,384]{2,1,0:T(8,128)(2,1)S(1)} %collective-permute-done.refs_4_), channel_id=1, source_target_pairs={{0,4},{1,5},{2,6},{3,7},{4,0},{5,1},{6,2},{7,3},{8,12},{9,13},{10,... | collective-permute-start | bytes 331784 | tf_op jit(solution)/shard_map/ppermute | solution.py:213
  19.6 5.7 %collective-permute-start.4 = (bf16[3,48,384]{2,1,0:T(8,128)(2,1)S(1)}, bf16[3,48,384]{2,1,0:T(8,128)(2,1)S(1)}, u32[]{:S(2)}, u32[]{:S(2)}) collective-permute-start(bf16[3,48,384]{2,1,0:T(8,128)(2,1)S(1)} %collective-permute-done.3.refs_2_), channel_id=1, source_target_pairs={{0,4},{1,5},{2,6},{3,7},{4,0},{5,1},{6,2},{7,3},{8,12},{9,13},{10,... | collective-permute-start | bytes 331784 | tf_op jit(solution)/shard_map/ppermute | solution.py:213
  21.4 5.4 %collective-permute-start.7 = (bf16[3,48,384]{2,1,0:T(8,128)(2,1)S(1)}, bf16[3,48,384]{2,1,0:T(8,128)(2,1)S(1)}, u32[]{:S(2)}, u32[]{:S(2)}) collective-permute-start(bf16[3,48,384]{2,1,0:T(8,128)(2,1)S(1)} %collective-permute-done.6.refs_6_), channel_id=1, source_target_pairs={{0,4},{1,5},{2,6},{3,7},{4,0},{5,1},{6,2},{7,3},{8,12},{9,13},{10,... | collective-permute-start | bytes 331784 | tf_op jit(solution)/shard_map/ppermute | solution.py:213
  26.9 3.0 %collective-permute-start.8 = (bf16[2,192,1024]{2,1,0:T(8,128)(2,1)S(1)}, bf16[2,192,1024]{2,1,0:T(8,128)(2,1)S(1)}, u32[]{:S(2)}, u32[]{:S(2)}) collective-permute-start(bf16[2,192,1024]{2,1,0:T(8,128)(2,1)S(1)} %collective-permute-done.1.refs_0_), channel_id=1, source_target_pairs={{0,1},{1,0},{2,3},{3,2},{4,5},{5,4},{6,7},{7,6},{8,9},{9,8},{10,11... | collective-permute-start | bytes 2359304 | tf_op jit(solution)/shard_map/ppermute | solution.py:213
  32.3 8.3 %collective-permute-start.10 = (bf16[2,3,48,384]{3,2,1,0:T(8,128)(2,1)S(1)}, bf16[2,3,48,384]{3,2,1,0:T(8,128)(2,1)S(1)}, u32[]{:S(2)}, u32[]{:S(2)}) collective-permute-start(bf16[2,3,48,384]{3,2,1,0:T(8,128)(2,1)S(1)} %get-tuple-element.50), channel_id=1, source_target_pairs={{0,4},{1,5},{2,6},{3,7},{4,0},{5,1},{6,2},{7,3},{8,12},{9,13},{10,... | collective-permute-start | bytes 663560 | tf_op jit(solution)/shard_map/ppermute | solution.py:213
  33.5 3.1 %collective-permute-start.11 = (bf16[2,192,128]{2,1,0:T(8,128)(2,1)S(1)}, bf16[2,192,128]{2,1,0:T(8,128)(2,1)S(1)}, u32[]{:S(2)}, u32[]{:S(2)}) collective-permute-start(bf16[2,192,128]{2,1,0:T(8,128)(2,1)S(1)} %pad_maximum_fusion.2.refs_1_), channel_id=1, source_target_pairs={{0,1},{1,0},{2,3},{3,2},{4,5},{5,4},{6,7},{7,6},{8,9},{9,8},{10,11... | collective-permute-start | bytes 294920 | tf_op jit(solution)/shard_map/ppermute | solution.py:213
  33.7 5.0 %collective-permute-start.12 = (bf16[2,192,128]{2,1,0:T(8,128)(2,1)S(1)}, bf16[2,192,128]{2,1,0:T(8,128)(2,1)S(1)}, u32[]{:S(2)}, u32[]{:S(2)}) collective-permute-start(bf16[2,192,128]{2,1,0:T(8,128)(2,1)S(1)} %pad_maximum_fusion.2.refs_1_), channel_id=1, source_target_pairs={{0,2},{1,3},{2,0},{3,1},{4,6},{5,7},{6,4},{7,5},{8,10},{9,11},{10,... | collective-permute-start | bytes 294920 | tf_op jit(solution)/shard_map/ppermute | solution.py:213
  35.2 9.7 %collective-permute-start.14 = (bf16[2,3,48,384]{3,2,1,0:T(8,128)(2,1)S(1)}, bf16[2,3,48,384]{3,2,1,0:T(8,128)(2,1)S(1)}, u32[]{:S(2)}, u32[]{:S(2)}) collective-permute-start(bf16[2,3,48,384]{3,2,1,0:T(8,128)(2,1)S(1)} %get-tuple-element.56), channel_id=1, source_target_pairs={{0,4},{1,5},{2,6},{3,7},{4,0},{5,1},{6,2},{7,3},{8,12},{9,13},{10,... | collective-permute-start | bytes 663560 | tf_op jit(solution)/shard_map/ppermute | solution.py:213
  40.6 15.3 %collective-permute-start.13 = (bf16[2,3,48,384]{3,2,1,0:T(8,128)(2,1)S(1)}, bf16[2,3,48,384]{3,2,1,0:T(8,128)(2,1)S(1)}, u32[]{:S(2)}, u32[]{:S(2)}) collective-permute-start(bf16[2,3,48,384]{3,2,1,0:T(8,128)(2,1)S(1)} %add_convert_fusion.1), channel_id=1, source_target_pairs={{0,12},{1,13},{2,14},{3,15},{4,8},{5,9},{6,10},{7,11},{8,4},{9,5},... | collective-permute-start | bytes 663560 | tf_op jit(solution)/shard_map/ppermute | solution.py:213
  45.0 16.3 %collective-permute-start.15 = (bf16[2,3,48,384]{3,2,1,0:T(8,128)(2,1)S(1)}, bf16[2,3,48,384]{3,2,1,0:T(8,128)(2,1)S(1)}, u32[]{:S(2)}, u32[]{:S(2)}) collective-permute-start(bf16[2,3,48,384]{3,2,1,0:T(8,128)(2,1)S(1)} %add_convert_fusion), channel_id=1, source_target_pairs={{0,12},{1,13},{2,14},{3,15},{4,8},{5,9},{6,10},{7,11},{8,4},{9,5},... | collective-permute-start | bytes 663560 | tf_op jit(solution)/shard_map/ppermute | solution.py:213
  56.2 8.5 %collective-permute-start.17 = (bf16[2,3,48,384]{3,2,1,0:T(8,128)(2,1)S(1)}, bf16[2,3,48,384]{3,2,1,0:T(8,128)(2,1)S(1)}, u32[]{:S(2)}, u32[]{:S(2)}) collective-permute-start(bf16[2,3,48,384]{3,2,1,0:T(8,128)(2,1)S(1)} %get-tuple-element.53.refs_1_), channel_id=1, source_target_pairs={{0,4},{1,5},{2,6},{3,7},{4,0},{5,1},{6,2},{7,3},{8,12},{9,13},{10,... | collective-permute-start | bytes 663560 | tf_op jit(solution)/shard_map/ppermute | solution.py:213
  61.6 3.1 %collective-permute-start.16 = (f32[2,24,96]{2,1,0:T(8,128)S(1)}, f32[2,24,96]{2,1,0:T(8,128)S(1)}, u32[]{:S(2)}, u32[]{:S(2)}) collective-permute-start(f32[2,24,96]{2,1,0:T(8,128)S(1)} %pad_maximum_fusion.3), channel_id=1, source_target_pairs={{0,1},{1,0},{2,3},{3,2},{4,5},{5,4},{6,7},{7,6},{8,9},{9,8},{10,11... | collective-permute-start | bytes 55304 | tf_op jit(solution)/shard_map/ppermute | solution.py:213
  61.6 10.3 %collective-permute-start.22 = (bf16[2,192,128]{2,1,0:T(8,128)(2,1)S(1)}, bf16[2,192,128]{2,1,0:T(8,128)(2,1)S(1)}, u32[]{:S(2)}, u32[]{:S(2)}) collective-permute-start(bf16[2,192,128]{2,1,0:T(8,128)(2,1)S(1)} %pad_maximum_fusion.2.refs_1_), channel_id=1, source_target_pairs={{0,3},{1,2},{2,1},{3,0},{4,7},{5,6},{6,5},{7,4},{8,11},{9,10},{10,... | collective-permute-start | bytes 294920 | tf_op jit(solution)/shard_map/ppermute | solution.py:213
  63.0 8.8 %collective-permute-start.18 = (bf16[2,3,48,384]{3,2,1,0:T(8,128)(2,1)S(1)}, bf16[2,3,48,384]{3,2,1,0:T(8,128)(2,1)S(1)}, u32[]{:S(2)}, u32[]{:S(2)}) collective-permute-start(bf16[2,3,48,384]{3,2,1,0:T(8,128)(2,1)S(1)} %get-tuple-element.57.refs_2_), channel_id=1, source_target_pairs={{0,4},{1,5},{2,6},{3,7},{4,0},{5,1},{6,2},{7,3},{8,12},{9,13},{10,... | collective-permute-start | bytes 663560 | tf_op jit(solution)/shard_map/ppermute | solution.py:213
  64.7 3.9 %collective-permute-start.19 = (f32[2,24,96]{2,1,0:T(8,128)S(1)}, f32[2,24,96]{2,1,0:T(8,128)S(1)}, u32[]{:S(2)}, u32[]{:S(2)}) collective-permute-start(f32[2,24,96]{2,1,0:T(8,128)S(1)} %fusion.1.here), channel_id=1, source_target_pairs={{0,2},{1,3},{2,0},{3,1},{4,6},{5,7},{6,4},{7,5},{8,10},{9,11},{10,... | collective-permute-start | bytes 55304 | tf_op jit(solution)/shard_map/ppermute | solution.py:213
  65.8 5.5 %collective-permute-start.20 = (f32[2,24,96]{2,1,0:T(8,128)S(1)}, f32[2,24,96]{2,1,0:T(8,128)S(1)}, u32[]{:S(2)}, u32[]{:S(2)}) collective-permute-start(f32[2,24,96]{2,1,0:T(8,128)S(1)} %fusion.1.here), channel_id=1, source_target_pairs={{0,4},{1,5},{2,6},{3,7},{4,0},{5,1},{6,2},{7,3},{8,12},{9,13},{10,... | collective-permute-start | bytes 55304 | tf_op jit(solution)/shard_map/ppermute | solution.py:213
  65.9 6.0 %collective-permute-start.21 = (f32[2,24,96]{2,1,0:T(8,128)S(1)}, f32[2,24,96]{2,1,0:T(8,128)S(1)}, u32[]{:S(2)}, u32[]{:S(2)}) collective-permute-start(f32[2,24,96]{2,1,0:T(8,128)S(1)} %fusion.1.here), channel_id=1, source_target_pairs={{0,6},{1,7},{2,4},{3,5},{4,2},{5,3},{6,0},{7,1},{8,14},{9,15},{10,... | collective-permute-start | bytes 55304 | tf_op jit(solution)/shard_map/ppermute | solution.py:213
  73.3 1.4 %collective-permute-start.23 = (bf16[2,192,128]{2,1,0:T(8,128)(2,1)S(1)}, bf16[2,192,128]{2,1,0:T(8,128)(2,1)S(1)}, u32[]{:S(2)}, u32[]{:S(2)}) collective-permute-start(bf16[2,192,128]{2,1,0:T(8,128)(2,1)S(1)} %get-tuple-element.66), channel_id=1, source_target_pairs={{0,1},{1,0},{2,3},{3,2},{4,5},{5,4},{6,7},{7,6},{8,9},{9,8},{10,11... | collective-permute-start | bytes 294920 | tf_op jit(solution)/shard_map/ppermute | solution.py:213
  74.7 4.9 %collective-permute-start.25 = (bf16[2,192,128]{2,1,0:T(8,128)(2,1)S(1)}, bf16[2,192,128]{2,1,0:T(8,128)(2,1)S(1)}, u32[]{:S(2)}, u32[]{:S(2)}) collective-permute-start(bf16[2,192,128]{2,1,0:T(8,128)(2,1)S(1)} %add_convert_fusion.2), channel_id=1, source_target_pairs={{0,2},{1,3},{2,0},{3,1},{4,6},{5,7},{6,4},{7,5},{8,10},{9,11},{10,... | collective-permute-start | bytes 294920 | tf_op jit(solution)/shard_map/ppermute | solution.py:213
  76.7 3.0 %collective-permute-start.24 = (bf16[2,192,128]{2,1,0:T(8,128)(2,1)S(1)}, bf16[2,192,128]{2,1,0:T(8,128)(2,1)S(1)}, u32[]{:S(2)}, u32[]{:S(2)}) collective-permute-start(bf16[2,192,128]{2,1,0:T(8,128)(2,1)S(1)} %get-tuple-element.71), channel_id=1, source_target_pairs={{0,1},{1,0},{2,3},{3,2},{4,5},{5,4},{6,7},{7,6},{8,9},{9,8},{10,11... | collective-permute-start | bytes 294920 | tf_op jit(solution)/shard_map/ppermute | solution.py:213
